TPU v7x, 32 devices: a whole 2x2x4 slice. The times are simulated.
32 devices in a mesh: dp: 4 (over y, core), row: 2 (over x), col: 4 (over z).
Axes of the slice: x: 2, y: 2, z: 4, core: 2. Of those that a mesh axis runs over, the one named last changes fastest.
Arguments:
- tokens: bfloat16 [16384, 1536], P(('dp', 'row', 'col')), may hold values from -6 to 6
- attention_gain: float32 [1536], replicated, may hold values from 0.25 to 1.75
- feedforward_gain: float32 [1536], replicated, may hold values from 0.25 to 1.75
- query_weight: bfloat16 [1536, 1536], P('row', 'col'), may hold values from -0.15625 to 0.15625
- key_value_matrix: bfloat16 [1536, 2, 768], P('row', None, 'col'), may hold values from -0.15625 to 0.15625
- projection_weight: bfloat16 [1536, 1536], P('col', 'row'), may hold values from -2.5 to 2.5
- gate_up_weight: bfloat16 [1536, 2, 4096], P('row', None, 'col'), may hold values from -0.15625 to 0.15625
- down_weight: bfloat16 [4096, 1536], P('col', 'row'), may hold values from -0.09375 to 0.09375
- cotangent: bfloat16 [16384, 1536], P(('dp', 'row', 'col')), may hold values from -6 to 6
Outputs:
- output: bfloat16 [16384, 1536], P(('dp', 'row', 'col'))
- input_grad: bfloat16 [16384, 1536], P(('dp', 'row', 'col'))
- attention_gain_grad: float32 [1536], replicated
- feedforward_gain_grad: float32 [1536], replicated
- query_grad: float32 [1536, 1536], P('row', 'col')
- key_value_grad: float32 [1536, 2, 768], P('row', None, 'col')
- projection_grad: float32 [1536, 1536], P('col', 'row')
- gate_up_grad: float32 [1536, 2, 4096], P('row', None, 'col')
- down_grad: float32 [4096, 1536], P('col', 'row')
All inputs are finite; a program needn't handle non-finite values.
Results may differ from a plain program's by a relative error of at most 0.018.
Values may be sent and summed in bfloat16 or wider, within the bound.
No kernel may reach another device: no remote copies, remote signals or barrier semaphores. Data moves between devices by JAX's collectives and lax.ppermute only.
A program may use at most 192 MiB of HBM per device.

v0:
```python
import math

import jax
import jax.numpy as jnp
from jax import lax
from jax.sharding import PartitionSpec as P

QUERY_HEADS = 16
KEY_VALUE_HEADS = 8
HEAD_DIM = 96
SEQUENCE_TOKENS = 1024


eps = 1e-05
rope_base = 100000.0


def norm_rows(field, gain_vec):
    return field * lax.rsqrt(jnp.mean(field * field, axis=-1, keepdims=True) + eps) * gain_vec


def apply_rotary(field, seq_len):
    half_size = field.shape[-1] // 2
    positions = (jnp.arange(field.shape[0]) % seq_len).astype(jnp.float32)
    inverse_freq = jnp.exp(
        jnp.arange(half_size).astype(jnp.float32) * (-2.0 * math.log(rope_base) / field.shape[-1])
    )
    angles = positions[:, None] * inverse_freq[None, :]
    cosine = jnp.cos(angles)[:, None, :]
    sine_part = jnp.sin(angles)[:, None, :]
    first_half = field[..., :half_size]
    second_half = field[..., half_size:]
    return jnp.concatenate(
        [
            first_half * cosine - second_half * sine_part,
            second_half * cosine + first_half * sine_part,
        ],
        axis=-1,
    )


def contract(left, right, left_dim, right_dim):
    return lax.dot_general(
        left, right, (((left_dim,), (right_dim,)), ((), ())), preferred_element_type=jnp.float32
    )


def block_scores(query_rot, key_rot, block_index, block_size):
    per_seq = SEQUENCE_TOKENS // block_size
    query_block = lax.dynamic_slice_in_dim(query_rot, block_index * block_size, block_size, 0)
    first_key = block_index // per_seq * SEQUENCE_TOKENS
    key_block = lax.dynamic_slice_in_dim(key_rot, first_key, SEQUENCE_TOKENS, 0)
    scores = jnp.einsum(
        "qkgd,skd->kgqs", query_block, key_block, preferred_element_type=jnp.float32
    ) * HEAD_DIM ** (-0.5)
    query_pos = block_index % per_seq * block_size + jnp.arange(block_size)
    causal = jnp.arange(SEQUENCE_TOKENS)[None, :] <= query_pos[:, None]
    return (query_block, first_key, jnp.where(causal, scores, -1e30))


def attend_forward(query_rot, key_rot, value_rot):
    block_size = min(512, SEQUENCE_TOKENS)
    block_count = query_rot.shape[0] // block_size

    def one_block(block_index):
        query_block, first_key, scores = block_scores(query_rot, key_rot, block_index, block_size)
        value_block = lax.dynamic_slice_in_dim(value_rot, first_key, SEQUENCE_TOKENS, 0)
        row_max = jnp.max(scores, axis=-1, keepdims=True)
        shifted = jnp.exp(scores - row_max)
        exp_total = jnp.sum(shifted, axis=-1, keepdims=True)
        attn_probs = (shifted / exp_total).astype(jnp.bfloat16)
        result = jnp.einsum(
            "kgqs,skd->qkgd", attn_probs, value_block, preferred_element_type=jnp.float32
        )
        return (result.astype(jnp.bfloat16), row_max + jnp.log(exp_total))

    return lax.map(one_block, jnp.arange(block_count))


def attend_backward(query_rot, key_rot, value_rot, grad_attended, log_totals):
    block_size = min(512, SEQUENCE_TOKENS)
    block_count = query_rot.shape[0] // block_size
    scaling = HEAD_DIM ** (-0.5)

    def one_block(running, block_index):
        grad_keys, grad_values = running
        query_block, first_key, scores = block_scores(query_rot, key_rot, block_index, block_size)
        key_block = lax.dynamic_slice_in_dim(key_rot, first_key, SEQUENCE_TOKENS, 0)
        value_block = lax.dynamic_slice_in_dim(value_rot, first_key, SEQUENCE_TOKENS, 0)
        grad_block = lax.dynamic_slice_in_dim(
            grad_attended, block_index * block_size, block_size, 0
        )
        attn_probs = jnp.exp(scores - log_totals[block_index])
        grad_probs = jnp.einsum(
            "qkgd,skd->kgqs", grad_block, value_block, preferred_element_type=jnp.float32
        )
        delta_sum = jnp.sum(attn_probs * grad_probs, axis=-1, keepdims=True)
        grad_scores = (attn_probs * (grad_probs - delta_sum)).astype(jnp.bfloat16)
        grad_query = (
            jnp.einsum("kgqs,skd->qkgd", grad_scores, key_block, preferred_element_type=jnp.float32)
            * scaling
        )
        part_keys = (
            jnp.einsum(
                "kgqs,qkgd->skd", grad_scores, query_block, preferred_element_type=jnp.float32
            )
            * scaling
        )
        part_values = jnp.einsum(
            "kgqs,qkgd->skd",
            attn_probs.astype(jnp.bfloat16),
            grad_block,
            preferred_element_type=jnp.float32,
        )
        grad_keys = lax.dynamic_update_slice_in_dim(
            grad_keys,
            lax.dynamic_slice_in_dim(grad_keys, first_key, SEQUENCE_TOKENS, 0) + part_keys,
            first_key,
            0,
        )
        grad_values = lax.dynamic_update_slice_in_dim(
            grad_values,
            lax.dynamic_slice_in_dim(grad_values, first_key, SEQUENCE_TOKENS, 0) + part_values,
            first_key,
            0,
        )
        return ((grad_keys, grad_values), grad_query)

    empty = jnp.zeros(key_rot.shape, jnp.float32)
    (grad_keys, grad_values), grad_query = lax.scan(
        one_block, (empty, empty), jnp.arange(block_count)
    )
    return (grad_query, grad_keys, grad_values)


def per_device(
    tokens,
    attention_gain,
    feedforward_gain,
    query_weight,
    key_value_matrix,
    projection_weight,
    gate_up_weight,
    down_weight,
    cotangent,
):
    full_query, full_key_value, full_projection, full_gate_up, full_down = (
        lax.all_gather(query_weight, "row", axis=0, tiled=True),
        lax.all_gather(key_value_matrix, "row", axis=0, tiled=True),
        lax.all_gather(projection_weight, "row", axis=1, tiled=True),
        lax.all_gather(gate_up_weight, "row", axis=0, tiled=True),
        lax.all_gather(down_weight, "row", axis=1, tiled=True),
    )
    model_width = tokens.shape[1]
    kv_heads = full_key_value.shape[2] // HEAD_DIM
    group_width = QUERY_HEADS // KEY_VALUE_HEADS
    inputs = tokens.astype(jnp.float32)
    normalized_rows = norm_rows(inputs, attention_gain).astype(jnp.bfloat16)
    normed_all = lax.all_gather(normalized_rows, "col", axis=0, tiled=True)
    grouped_tokens = normed_all.shape[0]
    query_pre = jnp.dot(normed_all, full_query, preferred_element_type=jnp.float32).reshape(
        grouped_tokens, kv_heads * group_width, HEAD_DIM
    )
    key_value_pair = jnp.dot(
        normed_all, full_key_value.reshape(model_width, -1), preferred_element_type=jnp.float32
    ).reshape(grouped_tokens, 2, kv_heads, HEAD_DIM)
    key_pre = key_value_pair[:, 0]
    query_rot = (
        apply_rotary(query_pre, SEQUENCE_TOKENS)
        .astype(jnp.bfloat16)
        .reshape(grouped_tokens, kv_heads, group_width, HEAD_DIM)
    )
    key_rot = apply_rotary(key_pre, SEQUENCE_TOKENS).astype(jnp.bfloat16)
    value_rot = key_value_pair[:, 1].astype(jnp.bfloat16)
    attended, log_totals = attend_forward(query_rot, key_rot, value_rot)
    attended = attended.reshape(grouped_tokens, -1)
    middle = inputs + lax.psum_scatter(
        jnp.dot(attended, full_projection, preferred_element_type=jnp.float32),
        "col",
        scatter_dimension=0,
        tiled=True,
    )
    normed_two = norm_rows(middle, feedforward_gain).astype(jnp.bfloat16)
    normed_two_all = lax.all_gather(normed_two, "col", axis=0, tiled=True)
    gate_up = jnp.dot(
        normed_two_all, full_gate_up.reshape(model_width, -1), preferred_element_type=jnp.float32
    ).reshape(grouped_tokens, 2, -1)
    hidden = (jax.nn.silu(gate_up[:, 0]) * gate_up[:, 1]).astype(jnp.bfloat16)
    output = middle + lax.psum_scatter(
        jnp.dot(hidden, full_down, preferred_element_type=jnp.float32).astype(jnp.bfloat16),
        "col",
        scatter_dimension=0,
        tiled=True,
    ).astype(jnp.float32)
    grad_out_all = lax.all_gather(cotangent, "col", axis=0, tiled=True)
    grad_hidden = contract(grad_out_all, full_down, 1, 1)
    down_grad = contract(hidden, grad_out_all, 0, 0)
    unused_value, swiglu_pull = jax.vjp(
        lambda gate_in, up_in: jax.nn.silu(gate_in) * up_in, gate_up[:, 0], gate_up[:, 1]
    )
    grad_gate, grad_up = swiglu_pull(grad_hidden)
    grad_gate_up = (
        jnp.stack([grad_gate, grad_up], axis=1).astype(jnp.bfloat16).reshape(grouped_tokens, -1)
    )
    gate_up_grad = contract(normed_two_all, grad_gate_up, 0, 0).reshape(model_width, 2, -1)
    grad_normed_two = lax.psum_scatter(
        contract(grad_gate_up, full_gate_up.reshape(model_width, -1), 1, 1),
        "col",
        scatter_dimension=0,
        tiled=True,
    )
    unused_norm, norm_pull = jax.vjp(norm_rows, middle, feedforward_gain)
    grad_middle, feedforward_term = norm_pull(grad_normed_two)
    grad_middle = grad_middle + cotangent.astype(jnp.float32)
    grad_branch_all = lax.all_gather(grad_middle.astype(jnp.bfloat16), "col", axis=0, tiled=True)
    grad_attended = contract(grad_branch_all, full_projection, 1, 1).astype(jnp.bfloat16)
    projection_grad = contract(attended, grad_branch_all, 0, 0)
    grad_query_rot, grad_key_rot, grad_values = attend_backward(
        query_rot,
        key_rot,
        value_rot,
        grad_attended.reshape(grouped_tokens, kv_heads, group_width, HEAD_DIM),
        log_totals,
    )
    unused_query, query_pull = jax.vjp(
        lambda field: apply_rotary(field, SEQUENCE_TOKENS), query_pre
    )
    (grad_query_pre,) = query_pull(grad_query_rot.reshape(grouped_tokens, -1, HEAD_DIM))
    unused_key, key_pull = jax.vjp(lambda field: apply_rotary(field, SEQUENCE_TOKENS), key_pre)
    (grad_key_pre,) = key_pull(grad_key_rot)
    grad_query_flat = grad_query_pre.reshape(grouped_tokens, -1).astype(jnp.bfloat16)
    grad_key_value = jnp.concatenate(
        [grad_key_pre.reshape(grouped_tokens, -1), grad_values.reshape(grouped_tokens, -1)], axis=1
    ).astype(jnp.bfloat16)
    query_grad = contract(normed_all, grad_query_flat, 0, 0)
    key_value_grad = contract(normed_all, grad_key_value, 0, 0).reshape(model_width, 2, -1)
    query_part = contract(grad_query_flat, full_query, 1, 1)
    pair_part = contract(grad_key_value, full_key_value.reshape(model_width, -1), 1, 1)
    grad_normed = lax.psum_scatter(query_part + pair_part, "col", scatter_dimension=0, tiled=True)
    unused_first, first_pull = jax.vjp(norm_rows, inputs, attention_gain)
    grad_inputs, attention_term = first_pull(grad_normed)
    grad_inputs = grad_inputs + grad_middle
    attention_gain_grad, feedforward_gain_grad = lax.psum(
        (attention_term, feedforward_term), ("dp", "row", "col")
    )
    row_blocks = (
        lax.psum_scatter(
            query_grad.astype(jnp.bfloat16), "row", scatter_dimension=0, tiled=True
        ).astype(jnp.float32),
        lax.psum_scatter(
            key_value_grad.astype(jnp.bfloat16), "row", scatter_dimension=0, tiled=True
        ).astype(jnp.float32),
        lax.psum_scatter(
            projection_grad.astype(jnp.bfloat16), "row", scatter_dimension=1, tiled=True
        ).astype(jnp.float32),
        lax.psum_scatter(
            gate_up_grad.astype(jnp.bfloat16), "row", scatter_dimension=0, tiled=True
        ).astype(jnp.float32),
        lax.psum_scatter(
            down_grad.astype(jnp.bfloat16), "row", scatter_dimension=1, tiled=True
        ).astype(jnp.float32),
    )
    weight_grads = (
        lax.psum(row_blocks[0].astype(jnp.bfloat16), "dp").astype(jnp.float32),
        lax.psum(row_blocks[1].astype(jnp.bfloat16), "dp").astype(jnp.float32),
        lax.psum(row_blocks[2].astype(jnp.bfloat16), "dp").astype(jnp.float32),
        lax.psum(row_blocks[3].astype(jnp.bfloat16), "dp").astype(jnp.float32),
        lax.psum(row_blocks[4].astype(jnp.bfloat16), "dp").astype(jnp.float32),
    )
    return (
        output.astype(jnp.bfloat16),
        grad_inputs.astype(jnp.bfloat16),
        attention_gain_grad,
        feedforward_gain_grad,
        weight_grads[0],
        weight_grads[1],
        weight_grads[2],
        weight_grads[3],
        weight_grads[4],
    )


def solution(mesh):
    return jax.shard_map(
        per_device,
        mesh=mesh,
        in_specs=(
            P(("dp", "row", "col"), None),
            P(),
            P(),
            P("row", "col"),
            P("row", None, "col"),
            P("col", "row"),
            P("row", None, "col"),
            P("col", "row"),
            P(("dp", "row", "col"), None),
        ),
        out_specs=(
            P(("dp", "row", "col"), None),
            P(("dp", "row", "col"), None),
            P(),
            P(),
            P("row", "col"),
            P("row", None, "col"),
            P("col", "row"),
            P("row", None, "col"),
            P("col", "row"),
        ),
        check_vma=False,
    )
```

profile of v0, /device:TPU:0, one launch (start us, length us, event | category | flops | bytes accessed | tf_op | source)
XLA Modules:
  0.0 1884.1 jit_solution(2831046348147661463)
XLA Ops:
  16.1 19.0 %all-gather.12.cloned.1.call-done = bf16[1536,2,192]{0,2,1:T(8,128)(2,1)} async-done(((bf16[768,2,192]{0,2,1:T(8,128)(2,1)}), bf16[1536,2,192]{0,2,1:T(8,128)(2,1)}) %all-gather.12.cloned.1.call-update) | async-done | bytes 1179664 | tf_op jit(solution)/shard_map/all_gather | solution.py:149
  35.1 117.5 %all-gather.10.cloned.1.call-done = bf16[2048,1536]{1,0:T(8,128)(2,1)} async-done(((bf16[512,1536]{1,0:T(8,128)(2,1)}), bf16[2048,1536]{1,0:T(8,128)(2,1)}) %all-gather.10.cloned.1.call-update) | async-done | bytes 6291472 | tf_op jit(solution)/shard_map/all_gather | solution.py:159
  152.6 5.1 fusion.66
  159.0 16.2 all-gather.14.cloned.1.call-done
  175.2 5.1 fusion.96
  181.1 51.0 %while.30 = (s32[]{:T(128)}, bf16[4,512,2,2,96]{1,4,3,2,0:T(8,128)(2,1)}, f32[4,2,2,512,1]{3,2,1,4,0:T(2,128)}, s32[4]{0:T(128)S(1)}, bf16[2048,2,96]{0,2,1:T(8,...) while((s32[]{:T(128)}, ...), condition=%wide.region_4.5_spmd, body=%wide.region_1.4_spmd.sunk | while | flops 831191552 | bytes 28905940 | solution.py:77
  189.0 4.2 fusion.144
  201.7 4.2 fusion.144
  214.4 4.2 fusion.144
  227.1 4.2 fusion.144
  232.1 3.5 copy.30
  237.2 9.8 fusion.97
  248.9 2.6 copy.31
  251.6 207.4 %reduce-scatter.10.cloned.1.call-done = f32[512,1536]{1,0:T(8,128)} async-done(((f32[2048,1536]{1,0:T(8,128)}), f32[512,1536]{1,0:T(8,128)}) %reduce-scatter.10.cloned.1.call-update) | async-done | bytes 3145744 | tf_op jit(solution)/shard_map/reduce_scatter | solution.py:177
  459.1 2.8 multiply_reduce_fusion.2
  465.2 77.3 %all-gather.20.cloned.1.call-done = bf16[1536,2,1024]{2,0,1:T(8,128)(2,1)} async-done(((bf16[768,2,1024]{2,0,1:T(8,128)(2,1)}), bf16[1536,2,1024]{2,0,1:T(8,128)(2,1)}) %all-gather.20.cloned.1.call-update) | async-done | bytes 6291472 | tf_op jit(solution)/shard_map/all_gather | solution.py:151
  542.5 8.8 copy.32
  551.3 108.2 %all-gather.18.cloned.1.call-done = bf16[2048,1536]{1,0:T(8,128)(2,1)} async-done(((bf16[512,1536]{1,0:T(8,128)(2,1)}), bf16[2048,1536]{1,0:T(8,128)(2,1)}) %all-gather.18.cloned.1.call-update) | async-done | bytes 6291472 | tf_op jit(solution)/shard_map/all_gather | solution.py:184
  659.4 19.6 %fusion.64 = f32[2048,2,1024]{0,2,1:T(8,128)} fusion(bf16[1536,2,1024]{0,2,1:T(8,128)(2,1)} %copy.32, bf16[2048,1536]{1,0:T(8,128)(2,1)} %all-gather.18.cloned.1.call-done), kind=kOutput, calls=%fused_computation.81 | convolution fusion | flops 12884901888 | bytes 29360128 | tf_op jit(solution)/shard_map/dot_general | solution.py:185
  679.0 25.2 %all-gather.22.cloned.1.call-done = bf16[1024,1536]{1,0:T(8,128)(2,1)} async-done(((bf16[1024,768]{1,0:T(8,128)(2,1)}), bf16[1024,1536]{1,0:T(8,128)(2,1)}) %all-gather.22.cloned.1.call-update) | async-done | bytes 3145744 | tf_op jit(solution)/shard_map/all_gather | solution.py:152
  704.2 117.0 %all-gather.24.cloned.1.call-done = bf16[2048,1536]{1,0:T(8,128)(2,1)} async-done(((bf16[512,1536]{1,0:T(8,128)(2,1)}), bf16[2048,1536]{1,0:T(8,128)(2,1)}) %all-gather.24.cloned.1.call-update) | async-done | bytes 6291472 | tf_op jit(solution)/shard_map/all_gather | solution.py:195
  821.1 15.8 fusion.60
  840.2 18.0 convolution_bitcast_fusion.1
  858.7 209.8 %reduce-scatter.14.cloned.1.call-done = f32[512,1536]{1,0:T(8,128)} async-done(((f32[2048,1536]{1,0:T(8,128)}), f32[512,1536]{1,0:T(8,128)}) %reduce-scatter.14.cloned.1.call-update) | async-done | bytes 3145744 | tf_op jit(solution)/shard_map/reduce_scatter | solution.py:206
  1068.5 3.4 multiply_reduce_fusion
  1074.6 7.1 multiply_convert_fusion
  1083.8 10.3 convolution_convert_fusion.1
  1094.1 19.1 %fusion.70 = bf16[1536,2,1024]{2,0,1:T(8,128)(2,1)} fusion(bf16[2048,1536]{1,0:T(8,128)(2,1)} %all-gather.18.cloned.1.call-done, bf16[2048,1,1024]{0,2,1:T(8,128)(2,1)} %copy-done.40, bf16[2048,1,1024]{0,2,1:T(8,128)(2,1)} %copy-done.39), kind=kOutput, calls=%fused_computation.92 | convolution fusion | flops 12904824832 | bytes 20971520 | tf_op jit(solution)/shard_map/dot_general | solution.py:43
  1113.5 77.6 %all-gather.26.cloned.1.call-done = bf16[2048,1536]{1,0:T(8,128)(2,1)} async-done(((bf16[512,1536]{1,0:T(8,128)(2,1)}), bf16[2048,1536]{1,0:T(8,128)(2,1)}) %all-gather.26.cloned.1.call-update) | async-done | bytes 6291472 | tf_op jit(solution)/shard_map/all_gather | solution.py:215
  1191.1 6.4 convolution_convert_fusion.3
  1197.6 8.5 convolution_convert_fusion.5
  1207.5 154.1 %while.31 = (s32[]{:T(128)}, f32[2048,2,96]{0,2,1:T(8,128)S(1)}, f32[2048,2,96]{0,2,1:T(8,128)}, f32[4,512,2,2,96]{1,0,4,3,2:T(4,128)}, s32[4]{0:T(128)S(1)}, /*...) while((s32[]{:T(128)}, f32[2048,2,96]{0,2,1:T(8,128)S(1)}, ...), condition=%wide.region_12.13_spmd, body=%wide.region_10.12_spmd.sunk | while | flops 2046032384 | bytes 93778552 | solution.py:130
  1216.3 2.6 fusion.157
  1218.9 4.3 fusion.154
  1223.1 2.7 fusion.155
  1229.9 16.2 dynamic_update_slice.46
  1254.8 2.6 fusion.157
  1257.4 4.3 fusion.154
  1261.7 2.7 fusion.155
  1268.4 16.1 dynamic_update_slice.46
  1293.3 2.6 fusion.157
  1295.9 4.3 fusion.154
  1300.2 2.7 fusion.155
  1306.9 16.1 dynamic_update_slice.46
  1329.2 2.5 fusion.153
  1331.7 2.6 fusion.157
  1334.3 4.3 fusion.154
  1338.6 2.7 fusion.155
  1345.3 16.1 dynamic_update_slice.46
  1366.6 3.6 convolution_convert_fusion.2
  1370.3 3.9 reshape.211
  1376.0 7.3 convolution_convert_fusion.4
  1383.4 7.4 reduce-scatter.20.cloned.1.call-done
  1390.8 24.5 %reduce-scatter.18.cloned.1.call-done = bf16[768,384]{1,0:T(8,128)(2,1)} async-done(((bf16[1536,384]{1,0:T(8,128)(2,1)}), bf16[768,384]{1,0:T(8,128)(2,1)}) %reduce-scatter.18.cloned.1.call-update) | async-done | bytes 589840 | tf_op jit(solution)/shard_map/reduce_scatter | solution.py:247
  1415.4 4.9 fusion.98
  1420.4 7.3 convolution_add_fusion
  1429.5 11.0 convolution_convert_fusion
  1440.6 101.0 %all-reduce.8.cloned.1.call-done = (bf16[768,2,1024]{2,0,1:T(8,128)(2,1)}, bf16[768,384]{1,0:T(8,128)(2,1)}, bf16[768,2,192]{0,2,1:T(8,128)(2,1)}, bf16[384,768]{1,0:T(8,128)(2,1)}, bf16[1024,768]{1,0:T(8,128)(2,1)}) async-done(((bf16[768,2,1024]{2,0,1:T(8,128)(2,1)}, bf16[768,384]{1,0:T(8,128)(2,1)}, bf16[768,2,192]{0,2,1:T(8,128)(2,1)}, bf16[384,768]{1,0:T(8,128)(2,1)}, bf16[1024,768]{1,0:T(8,128)(2,1)}), ...) | async-done | bytes 6488080 | tf_op jit(solution)/shard_map/psum | solution.py:267
  1548.2 5.9 copy.36
  1556.1 199.8 %reduce-scatter.16.cloned.1.call-done = f32[512,1536]{1,0:T(8,128)} async-done(((f32[2048,1536]{1,0:T(8,128)}), f32[512,1536]{1,0:T(8,128)}) %reduce-scatter.16.cloned.1.call-update) | async-done | bytes 3145744 | tf_op jit(solution)/shard_map/reduce_scatter | solution.py:239
  1755.9 3.3 fusion.78
  1759.2 49.6 %all-reduce.4 = (f32[1536]{0:T(1024)}, f32[1536]{0:T(1024)}) all-reduce(f32[1536]{0:T(1024)S(1)} %get-tuple-element.257, f32[1536]{0:T(1024)S(1)} %copy-done.30), channel_id=1, replica_groups=mesh['dp'=4,'row'=2,'col'=4] {'dp','row','col'}, use_global_device_ids=true, to_apply=%region_16.17 | all-reduce | flops 3072 | bytes 24576 | tf_op jit(solution)/shard_map/psum | solution.py:243
  1808.8 62.2 %reduce-scatter.12.cloned.1.call-done = bf16[512,1536]{1,0:T(8,128)(2,1)} async-done(((bf16[2048,1536]{1,0:T(8,128)(2,1)}), bf16[512,1536]{1,0:T(8,128)(2,1)}) %reduce-scatter.12.cloned.1.call-update) | async-done | bytes 1572880 | tf_op jit(solution)/shard_map/reduce_scatter | solution.py:189
  1871.0 6.1 fusion.81
  (231 shorter events, 96.4 us)
Async XLA Ops:
  7.2 3.8 copy-start.2
  7.2 27.9 %all-gather.12.cloned.1.call-start = ((), (), s32[]{:S(2)}) async-start(), calls=%async_computation.10 | async-start | bytes 1769472 | tf_op jit(solution)/shard_map/all_gather | solution.py:149
  7.9 144.7 %all-gather.10.cloned.1.call-start = ((), (), s32[]{:S(2)}) async-start(), calls=%async_computation.9 | async-start | bytes 7864320 | tf_op jit(solution)/shard_map/all_gather | solution.py:159
  13.2 162.0 %all-gather.14.cloned.1.call-start = ((), (), s32[]{:S(2)}) async-start(), calls=%async_computation.11 | async-start | bytes 1769472 | tf_op jit(solution)/shard_map/all_gather | solution.py:148
  14.0 223.3 %all-gather.16.cloned.1.call-start = ((), (), s32[]{:S(2)}) async-start(), calls=%async_computation.12 | async-start | bytes 1769472 | tf_op jit(solution)/shard_map/all_gather | solution.py:150
  14.5 444.5 %reduce-scatter.10.cloned.1.call-start = ((), (), s32[]{:S(2)}) async-start(), calls=%async_computation.13 | async-start | bytes 15728640 | tf_op jit(solution)/shard_map/reduce_scatter | solution.py:177
  16.1 164.3 %copy-start.8 = (f32[2048,48]{0,1:T(8,128)}, f32[2048,48]{0,1:T(8,128)S(1)}, u32[]{:S(2)}) copy-start(f32[2048,48]{0,1:T(8,128)S(1)} %get-tuple-element.318) | copy-start | bytes 1179652
  16.1 164.3 %copy-start.10 = (f32[2048,48]{0,1:T(8,128)}, f32[2048,48]{0,1:T(8,128)S(1)}, u32[]{:S(2)}) copy-start(f32[2048,48]{0,1:T(8,128)S(1)} %get-tuple-element.319) | copy-start | bytes 1179652
  232.1 5.1 copy-start.3
  232.1 5.1 copy-start.6
  247.0 1.9 copy-start.15
  247.0 295.4 %all-gather.20.cloned.1.call-start = ((), (), s32[]{:S(2)}) async-start(), calls=%async_computation.15 | async-start | bytes 9437184 | tf_op jit(solution)/shard_map/all_gather | solution.py:151
  251.6 210.4 %copy-start.25 = (f32[1536]{0:T(1024)S(1)}, f32[1536]{0:T(1024)}, u32[]{:S(2)}) copy-start(f32[1536]{0:T(1024)} %param.15) | copy-start | bytes 18436
  251.6 407.9 %all-gather.18.cloned.1.call-start = ((), (), s32[]{:S(2)}) async-start(), calls=%async_computation.14 | async-start | bytes 7864320 | tf_op jit(solution)/shard_map/all_gather | solution.py:184
  461.9 610.0 %copy-start = (f32[512,1536]{1,0:T(8,128)}, f32[512,1536]{1,0:T(8,128)S(1)}, u32[]{:S(2)}) copy-start(f32[512,1536]{1,0:T(8,128)S(1)} %get-tuple-element.301) | copy-start | bytes 9437188
  461.9 610.0 %copy-start.28 = (f32[512]{0:T(512)}, f32[512]{0:T(512)S(1)}, u32[]{:S(2)}) copy-start(f32[512]{0:T(512)S(1)} %fusion.90) | copy-start | bytes 6148
  463.7 240.5 %all-gather.22.cloned.1.call-start = ((), (), s32[]{:S(2)}) async-start(), calls=%async_computation.16 | async-start | bytes 4718592 | tf_op jit(solution)/shard_map/all_gather | solution.py:152
  464.4 356.7 %all-gather.24.cloned.1.call-start = ((), (), s32[]{:S(2)}) async-start(), calls=%async_computation.18 | async-start | bytes 7864320 | tf_op jit(solution)/shard_map/all_gather | solution.py:195
  465.2 603.3 %reduce-scatter.14.cloned.1.call-start = ((), (), s32[]{:S(2)}) async-start(), calls=%async_computation.19 | async-start | bytes 15728640 | tf_op jit(solution)/shard_map/reduce_scatter | solution.py:206
  837.0 2.0 copy-start.39
  837.0 3.2 copy-start.40
  858.2 332.9 %all-gather.26.cloned.1.call-start = ((), (), s32[]{:S(2)}) async-start(), calls=%async_computation.20 | async-start | bytes 7864320 | tf_op jit(solution)/shard_map/all_gather | solution.py:215
  1068.5 4.0 copy-start.5
  1068.5 4.0 copy-start.7
  1074.6 308.8 %reduce-scatter.26.cloned.1.call-start = ((), (), s32[]{:S(2)}) async-start(), calls=%async_computation.26 | async-start | bytes 4718592 | tf_op jit(solution)/shard_map/reduce_scatter | solution.py:259
  1081.7 2.1 copy-start.14
  1094.1 289.3 %reduce-scatter.24.cloned.1.call-start = ((), (), s32[]{:S(2)}) async-start(), calls=%async_computation.25 | async-start | bytes 9437184 | tf_op jit(solution)/shard_map/reduce_scatter | solution.py:256
  1113.2 77.9 %copy-start.11 = (bf16[48,8,4,512]{3,1,2,0:T(8,128)(2,1)S(1)}, bf16[48,8,4,512]{3,1,2,0:T(8,128)(2,1)}, u32[]{:S(2)}) copy-start(bf16[48,8,4,512]{3,1,2,0:T(8,128)(2,1)} %copy.63) | copy-start | bytes 4718596
  1113.2 270.2 %reduce-scatter.22.cloned.1.call-start = ((), (), s32[]{:S(2)}) async-start(), calls=%async_computation.24 | async-start | bytes 1769472 | tf_op jit(solution)/shard_map/reduce_scatter | solution.py:253
  1113.5 84.1 %copy-start.24 = (bf16[384,1536]{1,0:T(8,128)(2,1)S(1)}, bf16[384,1536]{1,0:T(8,128)(2,1)}, u32[]{:S(2)}) copy-start(bf16[384,1536]{1,0:T(8,128)(2,1)} %all-gather.16.cloned.1.call-done) | copy-start | bytes 3538948
  1197.5 193.3 %reduce-scatter.20.cloned.1.call-start = ((), (), s32[]{:S(2)}) async-start(), calls=%async_computation.23 | async-start | bytes 1769472 | tf_op jit(solution)/shard_map/reduce_scatter | solution.py:250
  1207.5 155.6 %copy-start.9 = (f32[2048,48]{0,1:T(8,128)S(1)}, f32[2048,48]{0,1:T(8,128)}, u32[]{:S(2)}) copy-start(f32[2048,48]{0,1:T(8,128)} %copy-done.8) | copy-start | bytes 1179652
  1213.8 2.5 copy-start.12
  1213.8 2.5 copy-start.21
  1218.9 4.3 copy-start.13
  1252.3 2.5 copy-start.12
  1252.3 2.5 copy-start.21
  1257.4 4.3 copy-start.13
  1290.8 2.5 copy-start.12
  1290.8 2.5 copy-start.21
  1295.9 4.3 copy-start.13
  1329.2 2.5 copy-start.12
  1329.2 2.5 copy-start.21
  1334.3 4.3 copy-start.13
  1363.1 3.5 copy-start.37
  1364.8 5.4 copy-start.19
  1370.3 45.0 %reduce-scatter.18.cloned.1.call-start = ((), (), s32[]{:S(2)}) async-start(), calls=%async_computation.22 | async-start | bytes 1769472 | tf_op jit(solution)/shard_map/reduce_scatter | solution.py:247
  1383.3 158.3 %all-reduce.8.cloned.1.call-start = ((), (), s32[]{:S(2)}) async-start(), calls=%async_computation.27 | async-start | bytes 12976128 | tf_op jit(solution)/shard_map/psum | solution.py:267
  1415.3 5.0 copy-start.18
  1415.3 5.0 copy-start.20
  1415.3 340.5 %reduce-scatter.16.cloned.1.call-start = ((), (), s32[]{:S(2)}) async-start(), calls=%async_computation.21 | async-start | bytes 15728640 | tf_op jit(solution)/shard_map/reduce_scatter | solution.py:239
  1415.4 5.0 copy-start.23
  1427.6 1.9 copy-start.38
  1427.7 443.3 %reduce-scatter.12.cloned.1.call-start = ((), (), s32[]{:S(2)}) async-start(), calls=%async_computation.17 | async-start | bytes 7864320 | tf_op jit(solution)/shard_map/reduce_scatter | solution.py:189
  1541.6 6.6 copy-start.16
  1548.2 5.9 copy-start.22
  1554.2 201.7 %copy-start.27 = (f32[1536]{0:T(1024)S(1)}, f32[1536]{0:T(1024)}, u32[]{:S(2)}) copy-start(f32[1536]{0:T(1024)} %param.14) | copy-start | bytes 18436
  1554.2 201.7 %copy-start.32 = (f32[512]{0:T(512)S(1)}, f32[512]{0:T(512)}, u32[]{:S(2)}) copy-start(f32[512]{0:T(512)} %copy-done.31) | copy-start | bytes 6148
  1556.1 203.1 %copy-start.30 = (f32[1536]{0:T(1024)S(1)}, f32[1536]{0:T(1024)}, u32[]{:S(2)}) copy-start(f32[1536]{0:T(1024)} %get-tuple-element.255) | copy-start | bytes 18436
  1556.1 252.7 %copy-start.36 = (f32[512]{0:T(512)S(1)}, f32[512]{0:T(512)}, u32[]{:S(2)}) copy-start(f32[512]{0:T(512)} %copy-done.35) | copy-start | bytes 6148
  1556.1 314.9 %copy-start.1 = (f32[512,1536]{1,0:T(8,128)S(1)}, f32[512,1536]{1,0:T(8,128)}, u32[]{:S(2)}) copy-start(f32[512,1536]{1,0:T(8,128)} %copy-done) | copy-start | bytes 9437188
  1556.1 314.9 %copy-start.26 = (f32[1536]{0:T(1024)S(1)}, f32[1536]{0:T(1024)}, u32[]{:S(2)}) copy-start(f32[1536]{0:T(1024)} %param.15) | copy-start | bytes 18436
  1556.1 314.9 %copy-start.29 = (f32[512]{0:T(512)S(1)}, f32[512]{0:T(512)}, u32[]{:S(2)}) copy-start(f32[512]{0:T(512)} %copy-done.28) | copy-start | bytes 6148
  1556.1 314.9 %copy-start.34 = (f32[512]{0:T(512)S(1)}, f32[512]{0:T(512)}, u32[]{:S(2)}) copy-start(f32[512]{0:T(512)} %copy-done.33) | copy-start | bytes 6148
  (5 other events, 5.0 us)
Sparse Core Ops, SparseCore 0:
  9.6 25.4 all-gather.11
  37.2 115.3 all-gather.9
  154.2 20.9 all-gather.13
  176.6 22.7 all-gather.15
  247.2 211.8 reduce-scatter.9
  461.0 81.3 all-gather.19
  544.0 115.3 all-gather.17
  661.0 43.1 all-gather.21
  705.7 115.3 all-gather.23
  858.3 210.0 reduce-scatter.13
  1074.7 116.3 all-gather.25
  1193.2 41.5 reduce-scatter.25
  1237.8 77.0 reduce-scatter.23
  1317.5 21.7 reduce-scatter.21
  1370.4 20.3 reduce-scatter.19
  1393.5 21.7 reduce-scatter.17
  1418.0 123.5 all-reduce.7
  1543.8 211.9 reduce-scatter.15
  1758.1 112.8 reduce-scatter.11
where the time goes:
time: 1900 us; the launch traced here: 1880 us
  waiting for transfers between devices  1370 us (72%)
  matrix products  226 us (12%)
  local copies, waits for them, and re-layouts  117 us (6%)
  other arithmetic  70.1 us (4%)
  blocking collectives  49.6 us (3%)
  loops' own time  32.2 us (2%)
    reduce_scatter x1, waiting for transfers between devices, per_device(): lax.psum_scatter(contract(grad_gate_up, full_gate_up.reshape(model_width,...  210 us
    reduce_scatter x1, waiting for transfers between devices, per_device(): lax.psum_scatter(jnp.dot(attended, full_projection, preferred_element_typ...  207 us
    reduce_scatter x1, waiting for transfers between devices, per_device(): lax.psum_scatter(query_part + pair_part, 'col', scatter_dimension=0, tile...  200 us
    all_gather x1, waiting for transfers between devices, per_device(): normed_all = lax.all_gather(normalized_rows, 'col', axis=0, tiled=True)  118 us
    all_gather x1, waiting for transfers between devices, per_device(): grad_out_all = lax.all_gather(cotangent, 'col', axis=0, tiled=True)  117 us
    all_gather x1, waiting for transfers between devices, per_device(): normed_two_all = lax.all_gather(normed_two, 'col', axis=0, tiled=True)  108 us
    dot_general x10, matrix products, contract(): lax.dot_general(left, right, (((left_dim,), (right_dim,)), ((), ())), pre...  101 us
    psum x1, waiting for transfers between devices, per_device(): lax.psum(row_blocks[3].astype(jnp.bfloat16), 'dp').astype(jnp.float32)  101 us
  transfers between devices with their start and end apart: 19, of which 15 were waited for; matrix products, arithmetic and copies ran while one was open for 18% of the time, Pallas kernels for 0%

commit v1 on v0

v1 whole, which is shorter than its diff:
```python
import functools
import math

import jax
import jax.numpy as jnp
from jax import lax
from jax.experimental import pallas as pl
from jax.experimental.pallas import tpu as pltpu
from jax.sharding import PartitionSpec as P

QUERY_HEADS = 16
KEY_VALUE_HEADS = 8
HEAD_DIM = 96
SEQUENCE_TOKENS = 1024

eps = 1e-05
rope_base = 100000.0

BF = jnp.bfloat16
F32 = jnp.float32

HALF = HEAD_DIM // 2
LANES = 128
GROUP = 4 * HEAD_DIM
GROUP_LANES = 4 * LANES
BLOCK = 256
SCALE = HEAD_DIM ** (-0.5)
PARTS = 2
SPLIT_MODEL = 768


def dot(a, b):
    return lax.dot_general(a, b, (((1,), (0,)), ((), ())), preferred_element_type=F32)


def dot_nt(a, b):
    return lax.dot_general(a, b, (((1,), (1,)), ((), ())), preferred_element_type=F32)


def dot_tn(a, b):
    return lax.dot_general(a, b, (((0,), (0,)), ((), ())), preferred_element_type=F32)


def scores_t(keys, queries, block):
    s = dot_nt(keys, queries)
    length = s.shape[0]
    key_pos = lax.broadcasted_iota(jnp.int32, s.shape, 0)
    query_pos = lax.broadcasted_iota(jnp.int32, s.shape, 1) + block * BLOCK
    s = jnp.where(key_pos <= query_pos, s, -1e30)
    top = jnp.max(s, axis=0, keepdims=True)
    e = jnp.exp2((s - top) * (SCALE * math.log2(math.e)))
    return e * (1.0 / jnp.sum(e, axis=0, keepdims=True))


def attention_forward_kernel(n1_ref, w_ref, spread_ref, cos_ref, sin_ref, qkv_ref, o_ref):
    w = dot(w_ref[...], spread_ref[...]).astype(BF)
    h = dot(n1_ref[...], w)
    cos, sin = cos_ref[...], sin_ref[...]
    for part in range(4):
        c = h[:, part * LANES : (part + 1) * LANES]
        if part < 3:
            c = c * cos + pltpu.roll(c, LANES // 2, 1) * sin
        qkv_ref[:, part * LANES : (part + 1) * LANES] = c.astype(BF)
    v_t = h[:, 3 * LANES :].T.astype(BF)
    for head in range(2):
        lanes = slice(head * LANES, (head + 1) * LANES)
        for block in range(SEQUENCE_TOKENS // BLOCK):
            rows = slice(block * BLOCK, (block + 1) * BLOCK)
            length = (block + 1) * BLOCK
            p = scores_t(qkv_ref[:length, 2 * LANES : 3 * LANES], qkv_ref[rows, lanes], block)
            o_t = dot(v_t[:, :length], p.astype(BF))
            o_ref[rows, lanes] = o_t.T.astype(BF)


def attention_backward_kernel(qkv_ref, do_ref, gather_ref, cos_ref, sin_ref, out_ref, dk_ref, dv_ref, dq_ref, d_ref):
    cos, sin = cos_ref[...], sin_ref[...]

    def unrotate(c):
        c = c * SCALE
        return (c * cos - pltpu.roll(c, LANES // 2, 1) * sin).astype(BF)

    k_t = qkv_ref[:, 2 * LANES : 3 * LANES].astype(F32).T.astype(BF)
    dk_ref[...] = jnp.zeros_like(dk_ref)
    dv_ref[...] = jnp.zeros_like(dv_ref)
    for head in range(2):
        lanes = slice(head * LANES, (head + 1) * LANES)
        for block in range(SEQUENCE_TOKENS // BLOCK):
            rows = slice(block * BLOCK, (block + 1) * BLOCK)
            length = (block + 1) * BLOCK
            q = qkv_ref[rows, lanes]
            do = do_ref[rows, lanes]
            p = scores_t(qkv_ref[:length, 2 * LANES : 3 * LANES], q, block)
            dp = dot_nt(qkv_ref[:length, 3 * LANES :], do)
            ds = (p * (dp - jnp.sum(p * dp, axis=0, keepdims=True))).astype(BF)
            dv_ref[:length, :] += dot(p.astype(BF), do)
            dk_ref[:length, :] += dot(ds, q)
            dq_ref[rows, :] = dot(k_t[:, :length], ds).T
        d_ref[:, lanes] = unrotate(dq_ref[...])
    d_ref[:, 2 * LANES : 3 * LANES] = unrotate(dk_ref[...])
    d_ref[:, 3 * LANES :] = dv_ref[...].astype(BF)
    out_ref[...] = dot(d_ref[...], gather_ref[...]).astype(BF)


def rotary_tables():
    positions = jnp.arange(SEQUENCE_TOKENS).astype(F32)
    inverse_freq = jnp.exp(jnp.arange(HALF).astype(F32) * (-2.0 * math.log(rope_base) / HEAD_DIM))
    angles = positions[:, None] * inverse_freq[None, :]
    gap = ((0, 0), (0, LANES // 2 - HALF))
    cos, sin = jnp.pad(jnp.cos(angles), gap), jnp.pad(jnp.sin(angles), gap)
    return jnp.concatenate([cos, cos], axis=1), jnp.concatenate([-sin, sin], axis=1)


def spread_matrix():
    src = lax.broadcasted_iota(jnp.int32, (GROUP, GROUP_LANES), 0)
    lane = lax.broadcasted_iota(jnp.int32, (GROUP, GROUP_LANES), 1)
    head, comp = src // HEAD_DIM, src % HEAD_DIM
    place = head * LANES + jnp.where(comp < HALF, comp, comp + LANES // 2 - HALF)
    return (place == lane).astype(BF)


def attention_forward(n1, w, spread, cos, sin):
    tokens, width = n1.shape
    groups = w.shape[1] // GROUP
    whole = lambda a: pl.BlockSpec(a.shape, lambda j: (0, 0))
    return pl.pallas_call(
        attention_forward_kernel,
        grid=(groups,),
        in_specs=[
            whole(n1),
            pl.BlockSpec((width, GROUP), lambda j: (0, j)),
            whole(spread),
            whole(cos),
            whole(sin),
        ],
        out_specs=[
            pl.BlockSpec((tokens, GROUP_LANES), lambda j: (0, j)),
            pl.BlockSpec((tokens, 2 * LANES), lambda j: (0, j)),
        ],
        out_shape=[
            jax.ShapeDtypeStruct((tokens, groups * GROUP_LANES), BF),
            jax.ShapeDtypeStruct((tokens, groups * 2 * LANES), BF),
        ],
        compiler_params=pltpu.CompilerParams(vmem_limit_bytes=48 * 1024 * 1024),
        cost_estimate=pl.CostEstimate(
            flops=2 * tokens * width * groups * GROUP_LANES * 2, bytes_accessed=16 << 20, transcendentals=tokens * tokens * groups * 2
        ),
        name="attention_forward",
    )(n1, w, spread, cos, sin)


def attention_backward(qkv, do, gather, cos, sin):
    tokens = qkv.shape[0]
    groups = qkv.shape[1] // GROUP_LANES
    whole = lambda a: pl.BlockSpec(a.shape, lambda j: (0, 0))
    return pl.pallas_call(
        attention_backward_kernel,
        grid=(groups,),
        in_specs=[
            pl.BlockSpec((tokens, GROUP_LANES), lambda j: (0, j)),
            pl.BlockSpec((tokens, 2 * LANES), lambda j: (0, j)),
            whole(gather),
            whole(cos),
            whole(sin),
        ],
        out_specs=pl.BlockSpec((tokens, GROUP), lambda j: (0, j)),
        out_shape=jax.ShapeDtypeStruct((tokens, groups * GROUP), BF),
        scratch_shapes=[
            pltpu.VMEM((tokens, LANES), F32),
            pltpu.VMEM((tokens, LANES), F32),
            pltpu.VMEM((tokens, LANES), F32),
            pltpu.VMEM((tokens, GROUP_LANES), BF),
        ],
        compiler_params=pltpu.CompilerParams(vmem_limit_bytes=48 * 1024 * 1024),
        cost_estimate=pl.CostEstimate(
            flops=10 * tokens * tokens * LANES * groups * 2, bytes_accessed=16 << 20, transcendentals=tokens * tokens * groups * 2
        ),
        name="attention_backward",
    )(qkv, do, gather, cos, sin)


def feedforward_kernel(col_step, sub, rows_of, n2_ref, cot_ref, *refs):
    take = iter(refs)
    grid_of = lambda: [[next(take) for _ in range(rows_of)] for _ in range(2)]
    gate_up, down, gate_up_grad, down_grad = grid_of(), grid_of(), grid_of(), grid_of()
    out_ref, dn2_ref, n2_t_ref, h_ref, dgu_ref = take
    step, half = pl.program_id(0), pl.num_programs(0) // 2
    width = n2_ref.shape[1] // rows_of
    cut = [slice(i * width, (i + 1) * width) for i in range(rows_of)]

    @pl.when(step == 0)
    def _():
        n2_t_ref[...] = n2_ref[...].T
        out_ref[...] = jnp.zeros_like(out_ref)
        dn2_ref[...] = jnp.zeros_like(dn2_ref)

    def work(whose):
        weights = [r[...].reshape(col_step * sub, width) for r in down[whose]]
        dh = sum(dot_nt(cot_ref[:, cut[i]], weights[i]) for i in range(rows_of))
        for c in range(col_step):
            gu = sum(dot(n2_ref[:, cut[i]], gate_up[whose][i][c]) for i in range(rows_of))
            gate, up = gu[:, :sub], gu[:, sub:]
            sig = jax.nn.sigmoid(gate)
            silu = gate * sig
            lanes = slice(c * sub, (c + 1) * sub)
            part = dh[:, lanes]
            h_ref[:, lanes] = (silu * up).astype(BF)
            dgu_ref[c, :, :sub] = (part * up * (sig + silu * (1 - sig))).astype(BF)
            dgu_ref[c, :, sub:] = (part * silu).astype(BF)
        hidden_t = h_ref[...].T
        for i in range(rows_of):
            out_ref[:, cut[i]] += dot(h_ref[...], weights[i])
            g = dot(hidden_t, cot_ref[:, cut[i]])
            down_grad[whose][i][...] = g.astype(BF).reshape(col_step, sub, width)
            for c in range(col_step):
                gate_up_grad[whose][i][c] = dot(n2_t_ref[cut[i], :], dgu_ref[c]).astype(BF)
            dn2_ref[:, cut[i]] += sum(dot_nt(dgu_ref[c], gate_up[whose][i][c]) for c in range(col_step))

    pl.when(step < half)(lambda: work(1))
    pl.when(step >= half)(lambda: work(0))


def feedforward(n2, cot, gate_up, down, col_step):
    tokens, model = n2.shape
    rows_of = len(down[0])
    columns, sub, width = down[0][0].shape
    half = columns // col_step
    once = lambda a: pl.BlockSpec(a.shape, lambda s: (0, 0), pipeline_mode=pl.Buffered(1))
    place = [lambda s: (jnp.maximum(s - half, 0), 0, 0), lambda s: (jnp.minimum(s, half - 1), 0, 0)]
    spec = lambda a, whose: pl.BlockSpec((col_step,) + a.shape[1:], place[whose])
    flat = [a for side in gate_up for a in side] + [a for side in down for a in side]
    specs = [spec(a, w) for w, side in enumerate(gate_up) for a in side]
    specs += [spec(a, w) for w, side in enumerate(down) for a in side]
    total = jax.ShapeDtypeStruct((tokens, model), F32)
    flops = 18 * tokens * model * 2 * columns * sub
    outs = pl.pallas_call(
        functools.partial(feedforward_kernel, col_step, sub, rows_of),
        grid=(2 * half,),
        in_specs=[once(n2), once(cot)] + specs,
        out_specs=specs + [once(total), once(total)],
        out_shape=[jax.ShapeDtypeStruct(a.shape, BF) for a in flat] + [total, total],
        scratch_shapes=[
            pltpu.VMEM((model, tokens), BF),
            pltpu.VMEM((tokens, col_step * sub), BF),
            pltpu.VMEM((col_step, tokens, 2 * sub), BF),
        ],
        compiler_params=pltpu.CompilerParams(vmem_limit_bytes=60 * 1024 * 1024),
        cost_estimate=pl.CostEstimate(flops=flops, bytes_accessed=48 << 20, transcendentals=tokens * 2 * columns * sub),
        name="feedforward",
    )(n2, cot, *flat)
    n = rows_of
    sides = lambda k: [list(outs[k : k + n]), list(outs[k + n : k + 2 * n])]
    return sides(0), sides(2 * n), outs[4 * n], outs[4 * n + 1]


def inverse_rms(field):
    return lax.rsqrt(jnp.mean(field * field, axis=-1, keepdims=True) + eps)


def norm_back(field, gain, grad):
    r = inverse_rms(field)
    scaled = gain * grad
    inner = jnp.mean(field * scaled, axis=-1, keepdims=True)
    return r * scaled - field * (r * r * r * inner), jnp.sum(grad * field * r, axis=0)


def halves(first_is_mine, mine, other, axis):
    return jnp.where(
        first_is_mine, jnp.concatenate([mine, other], axis), jnp.concatenate([other, mine], axis)
    )


def per_device(
    tokens,
    attention_gain,
    feedforward_gain,
    query_weight,
    key_value_matrix,
    projection_weight,
    gate_up_weight,
    down_weight,
    cotangent,
    *,
    sizes,
):
    dp_size, row_size, col_size = sizes
    x, z, d = lax.axis_index("row"), lax.axis_index("col"), lax.axis_index("dp")
    core, y, parity = d % 2, d // 2, z % 2
    model = tokens.shape[1]
    own = tokens.shape[0]
    block = model // row_size
    hidden_block = down_weight.shape[0]
    sub = hidden_block // 4 // PARTS

    def swap(a, axis, bit):
        n = {"dp": dp_size, "col": col_size}[axis]
        return lax.ppermute(a, axis, [(i, i ^ bit) for i in range(n)])

    def to_core(a):
        return swap(a, "dp", 1)

    def to_y(a):
        return swap(a, "dp", 2)

    def to_pair(a):
        return swap(a, "col", 1)

    def shift(a, axis, by):
        n = {"row": row_size, "col": col_size}[axis]
        return lax.ppermute(a, axis, [(i, (i + by) % n) for i in range(n)])

    def rel(a):
        if row_size == 2:
            return jnp.where(x == 0, a, jnp.concatenate([a[..., block:], a[..., :block]], axis=-1))
        return lax.dynamic_slice_in_dim(jnp.concatenate([a, a], axis=-1), x * block, model, a.ndim - 1)

    def unrel(a):
        if row_size == 2:
            return rel(a)
        return lax.dynamic_slice_in_dim(
            jnp.concatenate([a, a], axis=-1), (row_size - x) % row_size * block, model, a.ndim - 1
        )

    def gather_rows(piece):
        return [piece] + [shift(piece, "row", -i) for i in range(1, row_size)]

    def gather(piece_of):
        mine = [piece_of(parity ^ (j & 1)) for j in range(col_size)]
        along = [mine[0]] + [shift(mine[j], "col", j) for j in range(1, col_size)]
        return [gather_rows(piece) for piece in along]

    def pick(a, index, axis):
        return lax.dynamic_index_in_dim(a, index, axis, keepdims=False)

    query_blocks = query_weight.reshape(block, 2, 2 * HEAD_DIM)
    pair_blocks = key_value_matrix.reshape(block, 2, 2, HEAD_DIM)
    packed = jnp.concatenate([query_blocks, pair_blocks[:, 0], pair_blocks[:, 1]], axis=-1)
    packed = lax.dynamic_slice_in_dim(packed, core * (block // 2), block // 2, 0)
    got = got_qkv = gather(lambda which: pick(packed, which, 1))
    mine = jnp.stack([jnp.concatenate([got[j][i] for j in range(col_size)], axis=1) for i in range(row_size)])
    weight_qkv = halves(core == 0, mine[:, None], to_core(mine)[:, None], 1).reshape(model, -1)

    head_rows = projection_weight.reshape(2, 2, HEAD_DIM, block)
    head_rows = pick(head_rows, core, 1)
    got = gather(lambda which: pick(head_rows, which, 0))
    mine = jnp.stack([jnp.concatenate(got[j], axis=1) for j in range(col_size)])
    heads = halves(core == 0, mine[:, None], to_core(mine)[:, None], 1)
    gap = jnp.zeros(heads.shape[:2] + (LANES // 2 - HALF, model), BF)
    weight_projection = jnp.concatenate(
        [heads[:, :, :HALF], gap, heads[:, :, HALF:], gap], axis=2
    ).reshape(-1, model)

    def after(a, *earlier):
        return lax.optimization_barrier((a,) + earlier)[0]

    def both_cores(rows, axis):
        rows = rows if len(rows) * SPLIT_MODEL <= model else [jnp.concatenate(rows, axis=axis)]
        return [rows, [to_core(r) for r in rows]]

    weights_two = []
    for part in range(PARTS):
        start = ((2 * y + core) * PARTS + part) * sub
        piece = lax.dynamic_slice_in_dim(gate_up_weight, start, sub, 2).reshape(block, 2 * sub)
        piece = after(piece, got_qkv[-1][0])
        gate_up = both_cores(gather_rows(lax.all_gather(piece, "col")), 1)
        piece = after(lax.dynamic_slice_in_dim(down_weight, start, sub, 0), got_qkv[-1][0])
        down = both_cores(gather_rows(lax.all_gather(piece, "col")), 2)
        weights_two.append((gate_up, down))

    def in_sequence(a, other):
        return halves(parity == 0, a, other, 0)

    def over_pair(product, a):
        theirs = lax.dynamic_slice_in_dim(a, (1 - parity) * own, own, 0)
        arrived = to_pair(product(theirs).astype(BF))
        return product(lax.dynamic_slice_in_dim(a, parity * own, own, 0)) + arrived.astype(F32)

    gain_one, gain_two = rel(attention_gain), rel(feedforward_gain)
    inputs = rel(tokens).astype(F32)
    grad_out = rel(cotangent)
    grad_out_all = jnp.concatenate([grad_out, to_y(grad_out)], axis=0)
    normed = (inputs * inverse_rms(inputs) * gain_one).astype(BF)
    normed_all = in_sequence(normed, to_pair(normed))
    cos, sin = rotary_tables()
    spread = spread_matrix()
    qkv, attended = attention_forward(normed_all, weight_qkv, spread, cos, sin)
    middle = inputs + over_pair(lambda a: dot(a, weight_projection), attended)
    normed_two = (middle * inverse_rms(middle) * gain_two).astype(BF)
    normed_two_all = jnp.concatenate([normed_two, to_y(normed_two)], axis=0)

    grads_two, outs, dn2s = [], [], []
    for gate_up, down in weights_two:
        gate_up_grad, down_grad, out, dn2 = feedforward(normed_two_all, grad_out_all, gate_up, down, PARTS)
        grads_two.append((gate_up_grad, down_grad))
        outs.append(out)
        dn2s.append(dn2)

    def over_y(parts):
        kept, sent = (functools.reduce(jnp.add, [p[rows] for p in parts]) for rows in (slice(own), slice(own, None)))
        return kept + to_y(sent.astype(BF)).astype(F32)

    grad_two = over_y(dn2s)
    output = middle + over_y(outs)
    grad_middle, gain_two_term = norm_back(middle, gain_two, grad_two)
    grad_middle = grad_middle + grad_out.astype(F32)

    branch = grad_middle.astype(BF)
    branch_all = in_sequence(branch, to_pair(branch))
    grad_attended = dot_nt(branch_all, weight_projection).astype(BF)
    projection_grad = dot_tn(attended, branch_all).astype(BF)
    grad_qkv = attention_backward(qkv, grad_attended, spread.T, cos, sin)
    qkv_grad = dot_tn(normed_all, grad_qkv).astype(BF)
    grad_one = over_pair(lambda a: dot_nt(a, weight_qkv), grad_qkv)
    grad_inputs, gain_one_term = norm_back(inputs, gain_one, grad_one)
    grad_inputs = grad_inputs + grad_middle

    def total(*parts):
        return sum(part.astype(F32) for part in parts)

    def reduce_rows(blocks):
        return total(blocks[0], *[shift(blocks[i], "row", i) for i in range(1, row_size)]).astype(BF)

    def reduce_columns(parts):
        return [parts[0]] + [shift(parts[j], "col", -j) for j in range(1, col_size)]

    def by_core(a, axis):
        mine, other = pick(a, core, axis), pick(a, 1 - core, axis)
        return total(mine, to_core(other)).astype(BF)

    def by_parity(arrived, axis):
        same = total(*arrived[0::2]).astype(BF)
        cross = total(*arrived[1::2]).astype(BF)
        both = halves(parity == 0, jnp.expand_dims(same, axis), jnp.expand_dims(cross, axis), axis)
        return total(both, to_y(both)).astype(BF)

    g = qkv_grad.reshape(row_size, 2, block // 2, col_size * GROUP)
    g = reduce_rows(by_core(g, 1))
    g = reduce_columns([g[:, j * GROUP : (j + 1) * GROUP] for j in range(col_size)])
    g = by_parity(g, 1)
    g = halves(core == 0, g, to_core(g), 0).astype(F32)
    query_grad = g[:, :, : 2 * HEAD_DIM].reshape(block, -1)
    key_value_grad = jnp.stack(
        [
            g[:, :, 2 * HEAD_DIM : 3 * HEAD_DIM].reshape(block, -1),
            g[:, :, 3 * HEAD_DIM :].reshape(block, -1),
        ],
        axis=1,
    )

    g = projection_grad.reshape(col_size, 2, LANES, model)
    g = jnp.concatenate([g[:, :, :HALF], g[:, :, LANES // 2 : LANES // 2 + HALF]], axis=2)
    g = by_core(g, 1)
    g = reduce_rows([g[:, :, i * block : (i + 1) * block] for i in range(row_size)])
    g = by_parity(reduce_columns([g[j] for j in range(col_size)]), 0)[:, None]
    projection_grad = halves(core == 0, g, to_core(g), 1).astype(F32).reshape(-1, block)

    def by_y_and_core(a, axis):
        a = jnp.expand_dims(a, (axis, axis + 1))
        a = halves(y == 0, a, to_y(a), axis)
        return halves(core == 0, a, to_core(a), axis + 1)

    def reduce_part(mine, other, axis):
        if len(mine) < row_size:
            mine, other = ([r for r in jnp.split(a[0], row_size, axis=axis)] for a in (mine, other))
        arrived = [to_core(r) for r in other]
        rows = [shift(total(mine[i], arrived[i]).astype(BF), "row", i) for i in range(1, row_size)]
        g = total(mine[0], arrived[0], *rows).astype(BF)
        return lax.psum_scatter(g, "col", scatter_dimension=0)

    gate_up_parts, down_parts = [], []
    for gate_up, down in grads_two:
        g = reduce_part(*gate_up, 1).reshape(block, 2, sub)
        gate_up_parts.append(by_y_and_core(g, 2))
        down_parts.append(by_y_and_core(reduce_part(*down, 2), 0))
    gate_up_grad = jnp.stack(gate_up_parts, axis=4).astype(F32).reshape(block, 2, -1)
    down_grad = jnp.stack(down_parts, axis=2).astype(F32).reshape(-1, block)

    gains = unrel(jnp.stack([gain_one_term, gain_two_term]))
    for axis, n in (("dp", dp_size), ("row", row_size), ("col", col_size)):
        bit = 1
        while bit < n:
            gains = gains + lax.ppermute(gains, axis, [(i, i ^ bit) for i in range(n)])
            bit *= 2
    attention_gain_grad, feedforward_gain_grad = gains[0], gains[1]
    return (
        unrel(output.astype(BF)),
        unrel(grad_inputs.astype(BF)),
        attention_gain_grad,
        feedforward_gain_grad,
        query_grad,
        key_value_grad,
        projection_grad,
        gate_up_grad,
        down_grad,
    )


def solution(mesh):
    sizes = tuple(mesh.shape[name] for name in ("dp", "row", "col"))
    return jax.shard_map(
        functools.partial(per_device, sizes=sizes),
        mesh=mesh,
        in_specs=(
            P(("dp", "row", "col"), None),
            P(),
            P(),
            P("row", "col"),
            P("row", None, "col"),
            P("col", "row"),
            P("row", None, "col"),
            P("col", "row"),
            P(("dp", "row", "col"), None),
        ),
        out_specs=(
            P(("dp", "row", "col"), None),
            P(("dp", "row", "col"), None),
            P(),
            P(),
            P("row", "col"),
            P("row", None, "col"),
            P("col", "row"),
            P("row", None, "col"),
            P("col", "row"),
        ),
        check_vma=False,
    )
```

time: 1900 us -> 771 us (0.41)
  waiting for transfers between devices: 1370 us -> 241 us
  matrix products: 226 us -> 37.3 us
  Pallas kernels: 0 us -> 158 us
  starting transfers between devices: 1.34 us -> 62.9 us
  local copies, waits for them, and re-layouts: 117 us -> 55.6 us
  blocking collectives: 49.6 us -> 86.3 us
  other arithmetic: 70.1 us -> 106 us
  loops' own time: 32.2 us -> 0 us
    reduce_scatter x9 -> x4, waiting for transfers between devices: 711 us -> 0.02 us  [reduce_part(): return lax.psum_scatter(g, 'col', scatter_dimension=0)]
    all_gather x9 -> x2, waiting for transfers between devices: 558 us -> 0.01 us  [per_device(): gate_up = both_cores(gather_rows(lax.all_gather(piece, 'col')), 1)]
    ppermute x0 -> x75, waiting for transfers between devices: none -> 241 us  [the longest x30 151 us: shift(): return lax.ppermute(a, axis, [(i, (i + by) % n) for i in range(n)])]
    dot_general x43 -> x7, matrix products: 226 us -> 37.3 us  [the longest x3 15.8 us: dot_nt(): lax.dot_general(a, b, (((1,), (1,)), ((), ())), preferred_element_type=F32)]
    pallas_call x0 -> x4, Pallas kernels: none -> 158 us  [the longest x2 98.6 us: feedforward(): pl.pallas_call(functools.partial(feedforward_kernel, col_step, sub, rows_...]
    psum x1 -> x0, waiting for transfers between devices: 101 us -> none  [per_device(): lax.psum(row_blocks[3].astype(jnp.bfloat16), 'dp').astype(jnp.float32)]
    all_gather x0 -> x2, blocking collectives: none -> 86.3 us  [per_device(): down = both_cores(gather_rows(lax.all_gather(piece, 'col')), 2)]
    dynamic_update_slice x8 -> x0, local copies, waits for them, and re-layouts: 67.7 us -> none  [attend_backward(): lax.scan(one_block, (empty, empty), jnp.arange(block_count))]
  transfers between devices with their start and end apart: 19 -> 81, of which waited for: 15 -> 23; matrix products, arithmetic and copies ran while one was open for 18% -> 25% of each run, Pallas kernels for 0% -> 21%
where the time goes in v1:
time: 771 us; the launch traced here: 763 us
  waiting for transfers between devices  241 us (31%)
  Pallas kernels  158 us (20%)
  other arithmetic  106 us (14%)
  blocking collectives  86.3 us (11%)
  starting transfers between devices  62.9 us (8%)
  local copies, waits for them, and re-layouts  55.6 us (7%)
  matrix products  37.3 us (5%)
  between operations  15.8 us (2%)
    ppermute x30, waiting for transfers between devices, shift(): return lax.ppermute(a, axis, [(i, (i + by) % n) for i in range(n)])  151 us
    pallas_call x2, Pallas kernels, feedforward(): pl.pallas_call(functools.partial(feedforward_kernel, col_step, sub, rows_...  98.6 us
    all_gather x2, blocking collectives, per_device(): down = both_cores(gather_rows(lax.all_gather(piece, 'col')), 2)  86.3 us
    ppermute x40, waiting for transfers between devices, swap(): return lax.ppermute(a, axis, [(i, i ^ bit) for i in range(n)])  81.4 us
    ppermute x30, starting transfers between devices, shift(): return lax.ppermute(a, axis, [(i, (i + by) % n) for i in range(n)])  41.9 us
    pallas_call x1, Pallas kernels, attention_backward(): pl.pallas_call(attention_backward_kernel, grid=(groups,), in_specs=[pl.Bl...  29.7 us
    pallas_call x1, Pallas kernels, attention_forward(): pl.pallas_call(attention_forward_kernel, grid=(groups,), in_specs=[whole(...  29.6 us
    unnamed x100, local copies, waits for them, and re-layouts  21.3 us
  transfers between devices with their start and end apart: 81, of which 23 were waited for; matrix products, arithmetic and copies ran while one was open for 25% of the time, Pallas kernels for 21%

profile of v1, /device:TPU:0, one launch (start us, length us, event | category | flops | bytes accessed | tf_op | source)
XLA Modules:
  0.0 763.3 jit_solution(16056828471154472005)
XLA Ops:
  8.9 5.0 collective-permute-start.14
  20.2 2.8 collective-permute-start.3
  33.2 4.0 collective-permute-done.15
  40.0 4.0 collective-permute-done.11
  45.9 3.5 collective-permute-done.13
  57.8 3.8 collective-permute-done.7
  61.6 4.2 collective-permute-done.5
  65.8 3.2 collective-permute-done.6
  74.0 2.9 maximum_select_fusion.3
  77.5 15.0 %collective-permute-done = bf16[512,1536]{1,0:T(8,128)(2,1)} collective-permute-done((bf16[512,1536]{1,0:T(8,128)(2,1)S(1)}, bf16[512,1536]{1,0:T(8,128)(2,1)}, u32[]{:S(2)}, u32[]{:S(2)}) %collective-permute-start) | collective-permute-done | bytes 1572896 | tf_op jit(solution)/shard_map/ppermute | solution.py:296
  92.6 3.5 maximum_select_fusion.1.n1_ref
  96.1 3.3 maximum_select_fusion
  101.9 29.6 %attention_forward.1 = (bf16[1024,2048]{1,0:T(8,128)(2,1)}, bf16[1024,1024]{1,0:T(8,128)(2,1)S(1)}) custom-call(bf16[1024,1536]{1,0:T(8,128)(2,1)} %maximum_select_fusion.1.n1_ref, bf16[1536,1536]{1,0:T(8,128)(2,1)} %bitcast.121, bf16[384,512]{1,0:T(8,128)(2,1)S(1)} %fusion.32.spread_ref, f32[1024,128]{1,0:T(8,128)S(1)} %get-tuple-element.154.cos_ref, ...), custom_call_target="tpu_custom_call" | custom-call | flops 12884901888 | bytes 16777216 | tf_op jit(solution)/shard_map/attention_forward/pallas_call | solution.py:125
  131.5 2.9 convolution_convert_fusion.3
  139.6 68.1 %all-gather.3 = bf16[512,768]{1,0:T(8,128)(2,1)} all-gather(bf16[128,768]{1,0:T(8,128)(2,1)S(1)} %get-tuple-element.40), channel_id=5, replica_groups=mesh['dp'=4,'row'=2,'col'=4] {'col'}, dimensions={0}, use_global_device_ids=true | all-gather | bytes 983040 | tf_op jit(solution)/shard_map/all_gather | solution.py:366
  207.7 2.6 collective-permute-start.26
  210.3 4.8 multiply_reduce_fusion.2
  219.0 43.5 %collective-permute-done.29.refs_5_ = bf16[4,128,768]{2,1,0:T(8,128)(2,1)} collective-permute-done((bf16[4,128,768]{2,1,0:T(8,128)(2,1)}, bf16[4,128,768]{2,1,0:T(8,128)(2,1)}, u32[]{:S(2)}, u32[]{:S(2)}) %collective-permute-start.29) | collective-permute-done | bytes 786464 | tf_op jit(solution)/shard_map/ppermute | solution.py:309
  264.2 18.2 %all-gather.1 = bf16[512,768]{1,0:T(8,128)(2,1)} all-gather(bf16[128,768]{1,0:T(8,128)(2,1)S(1)} %get-tuple-element.37), channel_id=3, replica_groups=mesh['dp'=4,'row'=2,'col'=4] {'col'}, dimensions={0}, use_global_device_ids=true | all-gather | bytes 983040 | tf_op jit(solution)/shard_map/all_gather | solution.py:366
  282.7 3.7 pad_maximum_fusion.2.cot_ref
  286.4 3.8 pad_maximum_fusion.1.n2_ref
  290.2 25.6 %collective-permute-done.23.refs_5_ = bf16[4,128,768]{2,1,0:T(8,128)(2,1)} collective-permute-done((bf16[4,128,768]{2,1,0:T(8,128)(2,1)}, bf16[4,128,768]{2,1,0:T(8,128)(2,1)}, u32[]{:S(2)}, u32[]{:S(2)}) %collective-permute-start.23) | collective-permute-done | bytes 786464 | tf_op jit(solution)/shard_map/ppermute | solution.py:309
  316.8 49.2 %feedforward.3 = (bf16[4,768,256]{2,1,0:T(8,128)(2,1)}, bf16[4,768,256]{2,1,0:T(8,128)(2,1)}, bf16[4,768,256]{2,1,0:T(8,128)(2,1)}, bf16[4,768,256]{2,1,0:T(8,12...) custom-call(bf16[1024,1536]{1,0:T(8,128)(2,1)} %pad_maximum_fusion.1, ...), custom_call_target="tpu_custom_call" | custom-call | flops 28991029248 | bytes 50331648 | tf_op jit(solution)/shard_map/feedforward/pallas_call | solution.py:235
  366.7 49.4 %feedforward.2 = (bf16[4,768,256]{2,1,0:T(8,128)(2,1)}, bf16[4,768,256]{2,1,0:T(8,128)(2,1)}, bf16[4,768,256]{2,1,0:T(8,128)(2,1)}, bf16[4,768,256]{2,1,0:T(8,12...) custom-call(bf16[1024,1536]{1,0:T(8,128)(2,1)} %pad_maximum_fusion.1, ...), custom_call_target="tpu_custom_call" | custom-call | flops 28991029248 | bytes 50331648 | tf_op jit(solution)/shard_map/feedforward/pallas_call | solution.py:235
  416.6 4.6 add_convert_fusion.4
  426.5 2.5 add_convert_fusion.10
  429.5 15.1 %collective-permute-done.72 = bf16[4,128,768]{2,1,0:T(8,128)(2,1)} collective-permute-done((bf16[4,128,768]{2,1,0:T(8,128)(2,1)}, bf16[4,128,768]{2,1,0:T(8,128)(2,1)}, u32[]{:S(2)}, u32[]{:S(2)}) %collective-permute-start.72) | collective-permute-done | bytes 786464 | tf_op jit(solution)/shard_map/ppermute | solution.py:309
  444.6 2.6 add_convert_fusion.7
  448.8 3.6 add_convert_fusion.1
  452.4 5.5 collective-permute-done.33
  459.4 4.5 multiply_reduce_fusion
  463.9 4.5 fusion.59
  471.8 4.6 add_convert_fusion.6
  478.6 2.9 add_convert_fusion.3
  482.0 19.6 %collective-permute-done.62 = bf16[4,768,256]{2,1,0:T(8,128)(2,1)} collective-permute-done((bf16[4,768,256]{2,1,0:T(8,128)(2,1)}, bf16[4,768,256]{2,1,0:T(8,128)(2,1)}, u32[]{:S(2)}, u32[]{:S(2)}) %collective-permute-start.62) | collective-permute-done | bytes 1572896 | tf_op jit(solution)/shard_map/ppermute | solution.py:309
  502.0 4.1 add_convert_fusion
  506.2 15.5 %collective-permute-done.34 = bf16[512,1536]{1,0:T(8,128)(2,1)} collective-permute-done((bf16[512,1536]{1,0:T(8,128)(2,1)}, bf16[512,1536]{1,0:T(8,128)(2,1)}, u32[]{:S(2)}, u32[]{:S(2)}) %collective-permute-start.34) | collective-permute-done | bytes 1572896 | tf_op jit(solution)/shard_map/ppermute | solution.py:296
  521.7 2.8 collective-permute-start.68
  524.5 7.4 convolution_convert_fusion.4.do_ref
  531.9 29.7 %attention_backward.1 = bf16[1024,1536]{1,0:T(8,128)(2,1)} custom-call(bf16[1024,2048]{1,0:T(8,128)(2,1)} %get-tuple-element.42.qkv_ref, bf16[1024,1024]{1,0:T(8,128)(2,1)S(1)} %convolution_convert_fusion.4.do_ref, bf16[512,384]{1,0:T(8,128)(2,1)S(1)} %fusion.31.gather_ref, f32[1024,128]{1,0:T(8,128)S(1)} %get-tuple-element.154.cos_ref, ...), custom_call_target="tpu_custom_call" | custom-call | flops 10737418240 | bytes 16777216 | tf_op jit(solution)/shard_map/attention_backward/pallas_call | solution.py:155
  561.6 6.4 convolution_convert_fusion.1
  570.5 3.8 convolution_convert_fusion.2
  574.3 7.3 convolution_convert_fusion
  581.7 3.7 add_convert_fusion.2
  590.0 4.8 constant_dynamic-slice_fusion.1
  594.8 4.3 copy.83
  599.1 4.3 copy.68
  612.1 29.0 %collective-permute-done.35 = bf16[512,1536]{1,0:T(8,128)(2,1)} collective-permute-done((bf16[512,1536]{1,0:T(8,128)(2,1)}, bf16[512,1536]{1,0:T(8,128)(2,1)}, u32[]{:S(2)}, u32[]{:S(2)}) %collective-permute-start.35) | collective-permute-done | bytes 1572896 | tf_op jit(solution)/shard_map/ppermute | solution.py:296
  641.1 4.6 fusion.9
  646.0 4.4 fusion.7
  650.7 3.6 collective-permute-done.37
  658.2 3.6 collective-permute-done.39
  664.5 3.0 collective-permute-start.50
  669.1 3.8 collective-permute-start.51
  672.9 3.7 collective-permute-done.50
  676.6 12.6 %collective-permute-done.42 = bf16[384,1536]{0,1:T(8,128)(2,1)S(1)} collective-permute-done((bf16[384,1536]{0,1:T(8,128)(2,1)S(1)}, bf16[384,1536]{0,1:T(8,128)(2,1)S(1)}, u32[]{:S(2)}, u32[]{:S(2)}) %collective-permute-start.42) | collective-permute-done | bytes 1179680 | tf_op jit(solution)/shard_map/ppermute | solution.py:309
  690.3 2.6 collective-permute-start.43
  693.3 3.5 collective-permute-start.44
  702.0 7.2 collective-permute-done.43
  715.1 6.1 collective-permute-done.58
  722.6 10.2 %collective-permute-done.46 = bf16[384,2,384]{0,2,1:T(8,128)(2,1)S(1)} collective-permute-done((bf16[384,2,384]{0,2,1:T(8,128)(2,1)S(1)}, bf16[384,2,384]{0,2,1:T(8,128)(2,1)S(1)}, u32[]{:S(2)}, u32[]{:S(2)}) %collective-permute-start.46) | collective-permute-done | bytes 589856 | tf_op jit(solution)/shard_map/ppermute | solution.py:296
  733.5 3.0 maximum_convert_fusion
  736.5 6.6 copy.78
  743.1 10.3 %copy.82 = f32[768,2,1024]{2,1,0:T(2,128)} copy(f32[768,2,1024]{0,2,1:T(8,128)} %bitcast.118) | data formatting | bytes 12582912
  (342 shorter events, 109.1 us)
Async XLA Ops:
  7.2 200.5 %all-gather.9.cloned.1.call-start = ((), (), s32[]{:S(2)}) async-start(), calls=%async_computation.9 | async-start | bytes 1966080 | tf_op jit(solution)/shard_map/all_gather | solution.py:364
  8.9 20.5 %collective-permute-start.14 = (bf16[96,768]{1,0:T(8,128)(2,1)}, bf16[96,768]{1,0:T(8,128)(2,1)}, u32[]{:S(2)}, u32[]{:S(2)}) collective-permute-start(bf16[96,768]{1,0:T(8,128)(2,1)} %get-tuple-element.134), channel_id=1, source_target_pairs={{0,3},{1,0},{2,1},{3,2},{4,7},{5,4},{6,5},{7,6},{8,11},{9,8},{10,9... | collective-permute-start | bytes 442376 | tf_op jit(solution)/shard_map/ppermute | solution.py:309
  14.0 17.6 %collective-permute-start.10 = (bf16[96,768]{1,0:T(8,128)(2,1)}, bf16[96,768]{1,0:T(8,128)(2,1)}, u32[]{:S(2)}, u32[]{:S(2)}) collective-permute-start(bf16[96,768]{1,0:T(8,128)(2,1)} %get-tuple-element.134), channel_id=1, source_target_pairs={{0,1},{1,2},{2,3},{3,0},{4,5},{5,6},{6,7},{7,4},{8,9},{9,10},{10,1... | collective-permute-start | bytes 442376 | tf_op jit(solution)/shard_map/ppermute | solution.py:309
  14.0 24.5 %collective-permute-start.12 = (bf16[96,768]{1,0:T(8,128)(2,1)S(1)}, bf16[96,768]{1,0:T(8,128)(2,1)}, u32[]{:S(2)}, u32[]{:S(2)}) collective-permute-start(bf16[96,768]{1,0:T(8,128)(2,1)S(1)} %get-tuple-element.133), channel_id=1, source_target_pairs={{0,2},{1,3},{2,0},{3,1},{4,6},{5,7},{6,4},{7,5},{8,10},{9,11},{10,... | collective-permute-start | bytes 442376 | tf_op jit(solution)/shard_map/ppermute | solution.py:309
  15.0 15.1 %collective-permute-start.9 = (bf16[96,768]{1,0:T(8,128)(2,1)S(1)}, bf16[96,768]{1,0:T(8,128)(2,1)}, u32[]{:S(2)}, u32[]{:S(2)}) collective-permute-start(bf16[96,768]{1,0:T(8,128)(2,1)S(1)} %get-tuple-element.133), channel_id=1, source_target_pairs={{0,4},{4,0},{1,5},{5,1},{2,6},{6,2},{3,7},{7,3},{8,12},{12,8},{9,1... | collective-permute-start | bytes 442376 | tf_op jit(solution)/shard_map/ppermute | solution.py:309
  20.2 31.2 %collective-permute-start.3 = (bf16[384,384]{1,0:T(8,128)(2,1)}, bf16[384,384]{1,0:T(8,128)(2,1)}, u32[]{:S(2)}, u32[]{:S(2)}) collective-permute-start(bf16[384,384]{1,0:T(8,128)(2,1)} %bitcast.5), channel_id=1, source_target_pairs={{0,3},{1,0},{2,1},{3,2},{4,7},{5,4},{6,5},{7,6},{8,11},{9,8},{10,9... | collective-permute-start | bytes 884744 | tf_op jit(solution)/shard_map/ppermute | solution.py:309
  29.5 22.5 %collective-permute-start.1 = (bf16[384,384]{1,0:T(8,128)(2,1)}, bf16[384,384]{1,0:T(8,128)(2,1)S(1)}, u32[]{:S(2)}, u32[]{:S(2)}) collective-permute-start(bf16[384,384]{1,0:T(8,128)(2,1)} %bitcast.5), channel_id=1, source_target_pairs={{0,1},{1,2},{2,3},{3,0},{4,5},{5,6},{6,7},{7,4},{8,9},{9,10},{10,1... | collective-permute-start | bytes 884744 | tf_op jit(solution)/shard_map/ppermute | solution.py:309
  31.6 26.1 %collective-permute-start.4 = (bf16[384,384]{1,0:T(8,128)(2,1)S(1)}, bf16[384,384]{1,0:T(8,128)(2,1)S(1)}, u32[]{:S(2)}, u32[]{:S(2)}) collective-permute-start(bf16[384,384]{1,0:T(8,128)(2,1)S(1)} %bitcast.143), channel_id=1, source_target_pairs={{0,4},{4,0},{1,5},{5,1},{2,6},{6,2},{3,7},{7,3},{8,12},{12,8},{9,1... | collective-permute-start | bytes 884744 | tf_op jit(solution)/shard_map/ppermute | solution.py:309
  38.5 15.9 %collective-permute-start.2 = (bf16[384,384]{1,0:T(8,128)(2,1)S(1)}, bf16[384,384]{1,0:T(8,128)(2,1)S(1)}, u32[]{:S(2)}, u32[]{:S(2)}) collective-permute-start(bf16[384,384]{1,0:T(8,128)(2,1)S(1)} %bitcast.144), channel_id=1, source_target_pairs={{0,2},{1,3},{2,0},{3,1},{4,6},{5,7},{6,4},{7,5},{8,10},{9,11},{10,... | collective-permute-start | bytes 884744 | tf_op jit(solution)/shard_map/ppermute | solution.py:309
  49.4 43.2 %collective-permute-start = (bf16[512,1536]{1,0:T(8,128)(2,1)S(1)}, bf16[512,1536]{1,0:T(8,128)(2,1)}, u32[]{:S(2)}, u32[]{:S(2)}) collective-permute-start(bf16[512,1536]{1,0:T(8,128)(2,1)S(1)} %fusion.3), channel_id=1, source_target_pairs={{0,1},{1,0},{2,3},{3,2},{4,5},{5,4},{6,7},{7,6},{8,9},{9,8},{10,11... | collective-permute-start | bytes 4718600 | tf_op jit(solution)/shard_map/ppermute | solution.py:296
  57.7 16.4 %collective-permute-start.16 = (bf16[4,96,1536]{2,1,0:T(8,128)(2,1)}, bf16[4,96,1536]{2,1,0:T(8,128)(2,1)}, u32[]{:S(2)}, u32[]{:S(2)}) collective-permute-start(bf16[4,96,1536]{2,1,0:T(8,128)(2,1)} %get-tuple-element.127), channel_id=1, source_target_pairs={{0,8},{8,0},{16,24},{24,16},{1,9},{9,1},{17,25},{25,17},{2,10},{10... | collective-permute-start | bytes 3538952 | tf_op jit(solution)/shard_map/ppermute | solution.py:296
  71.6 24.6 %collective-permute-start.8 = (bf16[2,384,1536]{2,1,0:T(8,128)(2,1)}, bf16[2,384,1536]{2,1,0:T(8,128)(2,1)}, u32[]{:S(2)}, u32[]{:S(2)}) collective-permute-start(bf16[2,384,1536]{2,1,0:T(8,128)(2,1)} %get-tuple-element.108), channel_id=1, source_target_pairs={{0,8},{8,0},{16,24},{24,16},{1,9},{9,1},{17,25},{25,17},{2,10},{10... | collective-permute-start | bytes 7077896 | tf_op jit(solution)/shard_map/ppermute | solution.py:296
  73.5 188.9 %all-gather.7.cloned.1.call-start = ((), (), s32[]{:S(2)}) async-start(), calls=%async_computation.8 | async-start | bytes 1966080 | tf_op jit(solution)/shard_map/all_gather | solution.py:364
  134.5 75.8 %collective-permute-start.17 = (bf16[512,1536]{1,0:T(8,128)(2,1)}, bf16[512,1536]{1,0:T(8,128)(2,1)}, u32[]{:S(2)}, u32[]{:S(2)}) collective-permute-start(bf16[512,1536]{1,0:T(8,128)(2,1)} %convolution_convert_fusion.3), channel_id=1, source_target_pairs={{0,1},{1,0},{2,3},{3,2},{4,5},{5,4},{6,7},{7,6},{8,9},{9,8},{10,11... | collective-permute-start | bytes 4718600 | tf_op jit(solution)/shard_map/ppermute | solution.py:296
  136.1 146.3 %collective-permute-start.19 = (bf16[512,1536]{1,0:T(8,128)(2,1)}, bf16[512,1536]{1,0:T(8,128)(2,1)}, u32[]{:S(2)}, u32[]{:S(2)}) collective-permute-start(bf16[512,1536]{1,0:T(8,128)(2,1)} %maximum_select_fusion.5), channel_id=1, source_target_pairs={{0,16},{8,24},{16,0},{24,8},{1,17},{9,25},{17,1},{25,9},{2,18},{10... | collective-permute-start | bytes 4718600 | tf_op jit(solution)/shard_map/ppermute | solution.py:296
  139.6 342.4 %reduce-scatter.11.cloned.1.call-start = ((), (), s32[]{:S(2)}) async-start(), calls=%async_computation.7 | async-start | bytes 983040 | tf_op jit(solution)/shard_map/reduce_scatter | solution.py:467
  207.7 56.5 %collective-permute-start.26 = (bf16[4,768,256]{2,1,0:T(8,128)(2,1)}, bf16[4,768,256]{2,1,0:T(8,128)(2,1)}, u32[]{:S(2)}, u32[]{:S(2)}) collective-permute-start(bf16[4,768,256]{2,1,0:T(8,128)(2,1)} %bitcast.23.refs_0_), channel_id=1, source_target_pairs={{0,4},{4,0},{1,5},{5,1},{2,6},{6,2},{3,7},{7,3},{8,12},{12,8},{9,1... | collective-permute-start | bytes 4718600 | tf_op jit(solution)/shard_map/ppermute | solution.py:309
  217.3 65.4 %collective-permute-start.18 = (bf16[512,1536]{1,0:T(8,128)(2,1)}, bf16[512,1536]{1,0:T(8,128)(2,1)}, u32[]{:S(2)}, u32[]{:S(2)}) collective-permute-start(bf16[512,1536]{1,0:T(8,128)(2,1)} %multiply_convert_fusion), channel_id=1, source_target_pairs={{0,16},{8,24},{16,0},{24,8},{1,17},{9,25},{17,1},{25,9},{2,18},{10... | collective-permute-start | bytes 4718600 | tf_op jit(solution)/shard_map/ppermute | solution.py:296
  218.9 43.5 %collective-permute-start.29 = (bf16[4,128,768]{2,1,0:T(8,128)(2,1)}, bf16[4,128,768]{2,1,0:T(8,128)(2,1)}, u32[]{:S(2)}, u32[]{:S(2)}) collective-permute-start(bf16[4,128,768]{2,1,0:T(8,128)(2,1)} %bitcast.24.refs_4_), channel_id=1, source_target_pairs={{0,4},{4,0},{1,5},{5,1},{2,6},{6,2},{3,7},{7,3},{8,12},{12,8},{9,1... | collective-permute-start | bytes 2359304 | tf_op jit(solution)/shard_map/ppermute | solution.py:309
  219.0 97.3 %collective-permute-start.27 = (bf16[4,768,256]{2,1,0:T(8,128)(2,1)}, bf16[4,768,256]{2,1,0:T(8,128)(2,1)}, u32[]{:S(2)}, u32[]{:S(2)}) collective-permute-start(bf16[4,768,256]{2,1,0:T(8,128)(2,1)} %bitcast.23.refs_0_), channel_id=1, source_target_pairs={{0,8},{8,0},{16,24},{24,16},{1,9},{9,1},{17,25},{25,17},{2,10},{10... | collective-permute-start | bytes 4718600 | tf_op jit(solution)/shard_map/ppermute | solution.py:296
  262.4 53.9 %collective-permute-start.20 = (bf16[4,768,256]{2,1,0:T(8,128)(2,1)}, bf16[4,768,256]{2,1,0:T(8,128)(2,1)}, u32[]{:S(2)}, u32[]{:S(2)}) collective-permute-start(bf16[4,768,256]{2,1,0:T(8,128)(2,1)} %bitcast.21.refs_0_), channel_id=1, source_target_pairs={{0,4},{4,0},{1,5},{5,1},{2,6},{6,2},{3,7},{7,3},{8,12},{12,8},{9,1... | collective-permute-start | bytes 4718600 | tf_op jit(solution)/shard_map/ppermute | solution.py:309
  264.2 52.6 %collective-permute-start.28 = (bf16[4,768,256]{2,1,0:T(8,128)(2,1)}, bf16[4,768,256]{2,1,0:T(8,128)(2,1)}, u32[]{:S(2)}, u32[]{:S(2)}) collective-permute-start(bf16[4,768,256]{2,1,0:T(8,128)(2,1)} %collective-permute-done.26.refs_1_), channel_id=1, source_target_pairs={{0,8},{8,0},{16,24},{24,16},{1,9},{9,1},{17,25},{25,17},{2,10},{10... | collective-permute-start | bytes 4718600 | tf_op jit(solution)/shard_map/ppermute | solution.py:296
  282.4 33.4 %collective-permute-start.23 = (bf16[4,128,768]{2,1,0:T(8,128)(2,1)}, bf16[4,128,768]{2,1,0:T(8,128)(2,1)}, u32[]{:S(2)}, u32[]{:S(2)}) collective-permute-start(bf16[4,128,768]{2,1,0:T(8,128)(2,1)} %bitcast.22.refs_4_), channel_id=1, source_target_pairs={{0,4},{4,0},{1,5},{5,1},{2,6},{6,2},{3,7},{7,3},{8,12},{12,8},{9,1... | collective-permute-start | bytes 2359304 | tf_op jit(solution)/shard_map/ppermute | solution.py:309
  282.7 33.1 %collective-permute-start.31 = (bf16[4,128,768]{2,1,0:T(8,128)(2,1)}, bf16[4,128,768]{2,1,0:T(8,128)(2,1)}, u32[]{:S(2)}, u32[]{:S(2)}) collective-permute-start(bf16[4,128,768]{2,1,0:T(8,128)(2,1)} %collective-permute-done.29.refs_5_), channel_id=1, source_target_pairs={{0,8},{8,0},{16,24},{24,16},{1,9},{9,1},{17,25},{25,17},{2,10},{10... | collective-permute-start | bytes 2359304 | tf_op jit(solution)/shard_map/ppermute | solution.py:296
  315.8 50.4 %collective-permute-start.24 = (bf16[4,128,768]{2,1,0:T(8,128)(2,1)}, bf16[4,128,768]{2,1,0:T(8,128)(2,1)}, u32[]{:S(2)}, u32[]{:S(2)}) collective-permute-start(bf16[4,128,768]{2,1,0:T(8,128)(2,1)} %bitcast.22.refs_4_), channel_id=1, source_target_pairs={{0,8},{8,0},{16,24},{24,16},{1,9},{9,1},{17,25},{25,17},{2,10},{10... | collective-permute-start | bytes 2359304 | tf_op jit(solution)/shard_map/ppermute | solution.py:296
  315.8 50.8 %collective-permute-start.25 = (bf16[4,128,768]{2,1,0:T(8,128)(2,1)}, bf16[4,128,768]{2,1,0:T(8,128)(2,1)}, u32[]{:S(2)}, u32[]{:S(2)}) collective-permute-start(bf16[4,128,768]{2,1,0:T(8,128)(2,1)} %collective-permute-done.23.refs_5_), channel_id=1, source_target_pairs={{0,8},{8,0},{16,24},{24,16},{1,9},{9,1},{17,25},{25,17},{2,10},{10... | collective-permute-start | bytes 2359304 | tf_op jit(solution)/shard_map/ppermute | solution.py:296
  316.3 50.4 %collective-permute-start.21 = (bf16[4,768,256]{2,1,0:T(8,128)(2,1)}, bf16[4,768,256]{2,1,0:T(8,128)(2,1)}, u32[]{:S(2)}, u32[]{:S(2)}) collective-permute-start(bf16[4,768,256]{2,1,0:T(8,128)(2,1)} %bitcast.21.refs_0_), channel_id=1, source_target_pairs={{0,8},{8,0},{16,24},{24,16},{1,9},{9,1},{17,25},{25,17},{2,10},{10... | collective-permute-start | bytes 4718600 | tf_op jit(solution)/shard_map/ppermute | solution.py:296
  316.4 50.3 %collective-permute-start.22 = (bf16[4,768,256]{2,1,0:T(8,128)(2,1)}, bf16[4,768,256]{2,1,0:T(8,128)(2,1)}, u32[]{:S(2)}, u32[]{:S(2)}) collective-permute-start(bf16[4,768,256]{2,1,0:T(8,128)(2,1)} %collective-permute-done.20.refs_1_), channel_id=1, source_target_pairs={{0,8},{8,0},{16,24},{24,16},{1,9},{9,1},{17,25},{25,17},{2,10},{10... | collective-permute-start | bytes 4718600 | tf_op jit(solution)/shard_map/ppermute | solution.py:296
  366.0 63.0 %collective-permute-start.70 = (bf16[4,128,768]{2,1,0:T(8,128)(2,1)}, bf16[4,128,768]{2,1,0:T(8,128)(2,1)}, u32[]{:S(2)}, u32[]{:S(2)}) collective-permute-start(bf16[4,128,768]{2,1,0:T(8,128)(2,1)} %get-tuple-element.58), channel_id=1, source_target_pairs={{0,8},{8,0},{16,24},{24,16},{1,9},{9,1},{17,25},{25,17},{2,10},{10... | collective-permute-start | bytes 2359304 | tf_op jit(solution)/shard_map/ppermute | solution.py:296
  366.2 56.6 %collective-permute-start.71 = (bf16[4,128,768]{2,1,0:T(8,128)(2,1)}, bf16[4,128,768]{2,1,0:T(8,128)(2,1)}, u32[]{:S(2)}, u32[]{:S(2)}) collective-permute-start(bf16[4,128,768]{2,1,0:T(8,128)(2,1)} %get-tuple-element.60), channel_id=1, source_target_pairs={{0,8},{8,0},{16,24},{24,16},{1,9},{9,1},{17,25},{25,17},{2,10},{10... | collective-permute-start | bytes 2359304 | tf_op jit(solution)/shard_map/ppermute | solution.py:296
  366.6 80.6 %collective-permute-start.61 = (bf16[4,768,256]{2,1,0:T(8,128)(2,1)}, bf16[4,768,256]{2,1,0:T(8,128)(2,1)}, u32[]{:S(2)}, u32[]{:S(2)}) collective-permute-start(bf16[4,768,256]{2,1,0:T(8,128)(2,1)} %get-tuple-element.52), channel_id=1, source_target_pairs={{0,8},{8,0},{16,24},{24,16},{1,9},{9,1},{17,25},{25,17},{2,10},{10... | collective-permute-start | bytes 4718600 | tf_op jit(solution)/shard_map/ppermute | solution.py:296
  421.2 36.7 %collective-permute-start.33 = (bf16[512,1536]{1,0:T(8,128)(2,1)}, bf16[512,1536]{1,0:T(8,128)(2,1)}, u32[]{:S(2)}, u32[]{:S(2)}) collective-permute-start(bf16[512,1536]{1,0:T(8,128)(2,1)} %add_convert_fusion.4), channel_id=1, source_target_pairs={{0,16},{8,24},{16,0},{24,8},{1,17},{9,25},{17,1},{25,9},{2,18},{10... | collective-permute-start | bytes 4718600 | tf_op jit(solution)/shard_map/ppermute | solution.py:296
  425.0 19.6 %collective-permute-start.72 = (bf16[4,128,768]{2,1,0:T(8,128)(2,1)}, bf16[4,128,768]{2,1,0:T(8,128)(2,1)}, u32[]{:S(2)}, u32[]{:S(2)}) collective-permute-start(bf16[4,128,768]{2,1,0:T(8,128)(2,1)} %add_convert_fusion.8), channel_id=1, source_target_pairs={{0,4},{4,0},{1,5},{5,1},{2,6},{6,2},{3,7},{7,3},{8,12},{12,8},{9,1... | collective-permute-start | bytes 2359304 | tf_op jit(solution)/shard_map/ppermute | solution.py:309
  426.5 55.0 %collective-permute-start.60 = (bf16[4,768,256]{2,1,0:T(8,128)(2,1)}, bf16[4,768,256]{2,1,0:T(8,128)(2,1)}, u32[]{:S(2)}, u32[]{:S(2)}) collective-permute-start(bf16[4,768,256]{2,1,0:T(8,128)(2,1)} %get-tuple-element.50), channel_id=1, source_target_pairs={{0,8},{8,0},{16,24},{24,16},{1,9},{9,1},{17,25},{25,17},{2,10},{10... | collective-permute-start | bytes 4718600 | tf_op jit(solution)/shard_map/ppermute | solution.py:296
  429.1 39.3 %collective-permute-start.65 = (bf16[4,128,768]{2,1,0:T(8,128)(2,1)}, bf16[4,128,768]{2,1,0:T(8,128)(2,1)}, u32[]{:S(2)}, u32[]{:S(2)}) collective-permute-start(bf16[4,128,768]{2,1,0:T(8,128)(2,1)} %get-tuple-element.54), channel_id=1, source_target_pairs={{0,8},{8,0},{16,24},{24,16},{1,9},{9,1},{17,25},{25,17},{2,10},{10... | collective-permute-start | bytes 2359304 | tf_op jit(solution)/shard_map/ppermute | solution.py:296
  444.6 34.0 %collective-permute-start.56 = (bf16[4,768,256]{2,1,0:T(8,128)(2,1)}, bf16[4,768,256]{2,1,0:T(8,128)(2,1)}, u32[]{:S(2)}, u32[]{:S(2)}) collective-permute-start(bf16[4,768,256]{2,1,0:T(8,128)(2,1)} %get-tuple-element.48), channel_id=1, source_target_pairs={{0,8},{8,0},{16,24},{24,16},{1,9},{9,1},{17,25},{25,17},{2,10},{10... | collective-permute-start | bytes 4718600 | tf_op jit(solution)/shard_map/ppermute | solution.py:296
  447.1 59.0 %reduce-scatter.9.cloned.1.call-start = ((), (), s32[]{:S(2)}) async-start(), calls=%async_computation.6 | async-start | bytes 983040 | tf_op jit(solution)/shard_map/reduce_scatter | solution.py:467
  447.2 21.3 %collective-permute-start.67 = (bf16[4,128,768]{2,1,0:T(8,128)(2,1)}, bf16[4,128,768]{2,1,0:T(8,128)(2,1)S(1)}, u32[]{:S(2)}, u32[]{:S(2)}) collective-permute-start(bf16[4,128,768]{2,1,0:T(8,128)(2,1)} %add_convert_fusion.10), channel_id=1, source_target_pairs={{0,4},{4,0},{1,5},{5,1},{2,6},{6,2},{3,7},{7,3},{8,12},{12,8},{9,1... | collective-permute-start | bytes 2359304 | tf_op jit(solution)/shard_map/ppermute | solution.py:309
  457.9 43.8 %collective-permute-start.62 = (bf16[4,768,256]{2,1,0:T(8,128)(2,1)}, bf16[4,768,256]{2,1,0:T(8,128)(2,1)}, u32[]{:S(2)}, u32[]{:S(2)}) collective-permute-start(bf16[4,768,256]{2,1,0:T(8,128)(2,1)} %add_convert_fusion.1), channel_id=1, source_target_pairs={{0,4},{4,0},{1,5},{5,1},{2,6},{6,2},{3,7},{7,3},{8,12},{12,8},{9,1... | collective-permute-start | bytes 4718600 | tf_op jit(solution)/shard_map/ppermute | solution.py:309
  468.4 53.3 %collective-permute-start.34 = (bf16[512,1536]{1,0:T(8,128)(2,1)}, bf16[512,1536]{1,0:T(8,128)(2,1)}, u32[]{:S(2)}, u32[]{:S(2)}) collective-permute-start(bf16[512,1536]{1,0:T(8,128)(2,1)} %fusion.59), channel_id=1, source_target_pairs={{0,1},{1,0},{2,3},{3,2},{4,5},{5,4},{6,7},{7,6},{8,9},{9,8},{10,11... | collective-permute-start | bytes 4718600 | tf_op jit(solution)/shard_map/ppermute | solution.py:296
  470.9 227.0 %reduce-scatter.7.cloned.1.call-start = ((), (), s32[]{:S(2)}) async-start(), calls=%async_computation.5 | async-start | bytes 1966080 | tf_op jit(solution)/shard_map/reduce_scatter | solution.py:467
  476.3 169.6 %collective-permute-start.32 = (bf16[512,1536]{1,0:T(8,128)(2,1)}, bf16[512,1536]{1,0:T(8,128)(2,1)}, u32[]{:S(2)}, u32[]{:S(2)}) collective-permute-start(bf16[512,1536]{1,0:T(8,128)(2,1)} %add_convert_fusion.6), channel_id=1, source_target_pairs={{0,16},{8,24},{16,0},{24,8},{1,17},{9,25},{17,1},{25,9},{2,18},{10... | collective-permute-start | bytes 4718600 | tf_op jit(solution)/shard_map/ppermute | solution.py:296
  478.6 103.1 %collective-permute-start.55 = (bf16[4,768,256]{2,1,0:T(8,128)(2,1)}, bf16[4,768,256]{2,1,0:T(8,128)(2,1)}, u32[]{:S(2)}, u32[]{:S(2)}) collective-permute-start(bf16[4,768,256]{2,1,0:T(8,128)(2,1)} %get-tuple-element.46), channel_id=1, source_target_pairs={{0,8},{8,0},{16,24},{24,16},{1,9},{9,1},{17,25},{25,17},{2,10},{10... | collective-permute-start | bytes 4718600 | tf_op jit(solution)/shard_map/ppermute | solution.py:296
  481.5 100.1 %collective-permute-start.57 = (bf16[4,768,256]{2,1,0:T(8,128)(2,1)}, bf16[4,768,256]{2,1,0:T(8,128)(2,1)}, u32[]{:S(2)}, u32[]{:S(2)}) collective-permute-start(bf16[4,768,256]{2,1,0:T(8,128)(2,1)} %add_convert_fusion.3), channel_id=1, source_target_pairs={{0,4},{4,0},{1,5},{5,1},{2,6},{6,2},{3,7},{7,3},{8,12},{12,8},{9,1... | collective-permute-start | bytes 4718600 | tf_op jit(solution)/shard_map/ppermute | solution.py:309
  501.6 83.8 %collective-permute-start.73 = (bf16[1,1,128,768]{3,2,1,0:T(8,128)(2,1)}, bf16[1,1,128,768]{3,2,1,0:T(8,128)(2,1)}, u32[]{:S(2)}, u32[]{:S(2)}) collective-permute-start(bf16[1,1,128,768]{3,2,1,0:T(8,128)(2,1)} %bitcast.148), channel_id=1, source_target_pairs={{0,16},{8,24},{16,0},{24,8},{1,17},{9,25},{17,1},{25,9},{2,18},{10... | collective-permute-start | bytes 589832 | tf_op jit(solution)/shard_map/ppermute | solution.py:296
  506.1 194.7 %reduce-scatter.5.cloned.1.call-start = ((), (), s32[]{:S(2)}) async-start(), calls=%async_computation.4 | async-start | bytes 1966080 | tf_op jit(solution)/shard_map/reduce_scatter | solution.py:467
  521.7 66.1 %collective-permute-start.68 = (bf16[1,1,128,768]{3,2,0,1:T(8,128)(2,1)}, bf16[1,1,128,768]{3,2,0,1:T(8,128)(2,1)}, u32[]{:S(2)}, u32[]{:S(2)}) collective-permute-start(bf16[1,1,128,768]{3,2,0,1:T(8,128)(2,1)} %bitcast.151), channel_id=1, source_target_pairs={{0,16},{8,24},{16,0},{24,8},{1,17},{9,25},{17,1},{25,9},{2,18},{10... | collective-permute-start | bytes 589832 | tf_op jit(solution)/shard_map/ppermute | solution.py:296
  581.6 29.9 %collective-permute-start.48 = (bf16[4,96,1536]{2,1,0:T(8,128)(2,1)}, bf16[4,96,1536]{2,1,0:T(8,128)(2,1)S(1)}, u32[]{:S(2)}, u32[]{:S(2)}) collective-permute-start(bf16[4,96,1536]{2,1,0:T(8,128)(2,1)} %fusion.18), channel_id=1, source_target_pairs={{0,8},{8,0},{16,24},{24,16},{1,9},{9,1},{17,25},{25,17},{2,10},{10... | collective-permute-start | bytes 3538952 | tf_op jit(solution)/shard_map/ppermute | solution.py:296
  581.6 59.4 %collective-permute-start.35 = (bf16[512,1536]{1,0:T(8,128)(2,1)}, bf16[512,1536]{1,0:T(8,128)(2,1)}, u32[]{:S(2)}, u32[]{:S(2)}) collective-permute-start(bf16[512,1536]{1,0:T(8,128)(2,1)} %convolution_convert_fusion.2), channel_id=1, source_target_pairs={{0,1},{1,0},{2,3},{3,2},{4,5},{5,4},{6,7},{7,6},{8,9},{9,8},{10,11... | collective-permute-start | bytes 4718600 | tf_op jit(solution)/shard_map/ppermute | solution.py:296
  587.4 18.6 %collective-permute-start.74 = (bf16[2,1,128,768]{3,2,1,0:T(8,128)(2,1)}, bf16[2,1,128,768]{3,2,1,0:T(8,128)(2,1)}, u32[]{:S(2)}, u32[]{:S(2)}) collective-permute-start(bf16[2,1,128,768]{3,2,1,0:T(8,128)(2,1)} %bitcast_select_fusion), channel_id=1, source_target_pairs={{0,8},{8,0},{16,24},{24,16},{1,9},{9,1},{17,25},{25,17},{2,10},{10... | collective-permute-start | bytes 1179656 | tf_op jit(solution)/shard_map/ppermute | solution.py:296
  589.9 18.0 %collective-permute-start.69 = (bf16[2,1,128,768]{3,2,0,1:T(8,128)(2,1)}, bf16[2,1,128,768]{3,2,0,1:T(8,128)(2,1)}, u32[]{:S(2)}, u32[]{:S(2)}) collective-permute-start(bf16[2,1,128,768]{3,2,0,1:T(8,128)(2,1)} %maximum_select_fusion.19), channel_id=1, source_target_pairs={{0,8},{8,0},{16,24},{24,16},{1,9},{9,1},{17,25},{25,17},{2,10},{10... | collective-permute-start | bytes 1179656 | tf_op jit(solution)/shard_map/ppermute | solution.py:296
  606.0 55.8 %collective-permute-start.41 = (bf16[2,384,1536]{1,2,0:T(8,128)(2,1)}, bf16[2,384,1536]{1,2,0:T(8,128)(2,1)}, u32[]{:S(2)}, u32[]{:S(2)}) collective-permute-start(bf16[2,384,1536]{1,2,0:T(8,128)(2,1)} %bitcast.134), channel_id=1, source_target_pairs={{0,8},{8,0},{16,24},{24,16},{1,9},{9,1},{17,25},{25,17},{2,10},{10... | collective-permute-start | bytes 7077896 | tf_op jit(solution)/shard_map/ppermute | solution.py:296
  612.0 52.4 %collective-permute-start.49 = (bf16[4,96,768]{2,1,0:T(8,128)(2,1)S(1)}, bf16[4,96,768]{2,1,0:T(8,128)(2,1)S(1)}, u32[]{:S(2)}, u32[]{:S(2)}) collective-permute-start(bf16[4,96,768]{2,1,0:T(8,128)(2,1)S(1)} %slice.206), channel_id=1, source_target_pairs={{0,4},{4,0},{1,5},{5,1},{2,6},{6,2},{3,7},{7,3},{8,12},{12,8},{9,1... | collective-permute-start | bytes 1769480 | tf_op jit(solution)/shard_map/ppermute | solution.py:309
  664.3 25.0 %collective-permute-start.42 = (bf16[384,1536]{0,1:T(8,128)(2,1)S(1)}, bf16[384,1536]{0,1:T(8,128)(2,1)S(1)}, u32[]{:S(2)}, u32[]{:S(2)}) collective-permute-start(bf16[384,1536]{0,1:T(8,128)(2,1)S(1)} %slice_bitcast_fusion), channel_id=1, source_target_pairs={{0,4},{4,0},{1,5},{5,1},{2,6},{6,2},{3,7},{7,3},{8,12},{12,8},{9,1... | collective-permute-start | bytes 3538952 | tf_op jit(solution)/shard_map/ppermute | solution.py:309
  669.0 23.9 %collective-permute-start.52 = (bf16[96,768]{1,0:T(8,128)(2,1)S(1)}, bf16[96,768]{1,0:T(8,128)(2,1)S(1)}, u32[]{:S(2)}, u32[]{:S(2)}) collective-permute-start(bf16[96,768]{1,0:T(8,128)(2,1)S(1)} %get-tuple-element.129), channel_id=1, source_target_pairs={{0,1},{1,2},{2,3},{3,0},{4,5},{5,6},{6,7},{7,4},{8,9},{9,10},{10,1... | collective-permute-start | bytes 442376 | tf_op jit(solution)/shard_map/ppermute | solution.py:309
  669.1 23.9 %collective-permute-start.51 = (bf16[96,768]{1,0:T(8,128)(2,1)S(1)}, bf16[96,768]{1,0:T(8,128)(2,1)S(1)}, u32[]{:S(2)}, u32[]{:S(2)}) collective-permute-start(bf16[96,768]{1,0:T(8,128)(2,1)S(1)} %get-tuple-element.130), channel_id=1, source_target_pairs={{0,3},{1,0},{2,1},{3,2},{4,7},{5,4},{6,5},{7,6},{8,11},{9,8},{10,9... | collective-permute-start | bytes 442376 | tf_op jit(solution)/shard_map/ppermute | solution.py:309
  690.3 18.9 %collective-permute-start.43 = (bf16[384,384]{0,1:T(8,128)(2,1)}, bf16[384,384]{0,1:T(8,128)(2,1)S(1)}, u32[]{:S(2)}, u32[]{:S(2)}) collective-permute-start(bf16[384,384]{0,1:T(8,128)(2,1)} %get-tuple-element.121), channel_id=1, source_target_pairs={{0,2},{1,3},{2,0},{3,1},{4,6},{5,7},{6,4},{7,5},{8,10},{9,11},{10,... | collective-permute-start | bytes 884744 | tf_op jit(solution)/shard_map/ppermute | solution.py:309
  693.0 16.9 %collective-permute-start.45 = (bf16[384,384]{0,1:T(8,128)(2,1)S(1)}, bf16[384,384]{0,1:T(8,128)(2,1)}, u32[]{:S(2)}, u32[]{:S(2)}) collective-permute-start(bf16[384,384]{0,1:T(8,128)(2,1)S(1)} %get-tuple-element.122), channel_id=1, source_target_pairs={{0,1},{1,2},{2,3},{3,0},{4,5},{5,6},{6,7},{7,4},{8,9},{9,10},{10,1... | collective-permute-start | bytes 884744 | tf_op jit(solution)/shard_map/ppermute | solution.py:309
  693.3 17.1 %collective-permute-start.44 = (bf16[384,384]{0,1:T(8,128)(2,1)S(1)}, bf16[384,384]{0,1:T(8,128)(2,1)}, u32[]{:S(2)}, u32[]{:S(2)}) collective-permute-start(bf16[384,384]{0,1:T(8,128)(2,1)S(1)} %get-tuple-element.123), channel_id=1, source_target_pairs={{0,3},{1,0},{2,1},{3,2},{4,7},{5,4},{6,5},{7,6},{8,11},{9,8},{10,9... | collective-permute-start | bytes 884744 | tf_op jit(solution)/shard_map/ppermute | solution.py:309
  697.6 15.1 %collective-permute-start.53 = (bf16[2,96,768]{2,1,0:T(8,128)(2,1)}, bf16[2,96,768]{2,1,0:T(8,128)(2,1)}, u32[]{:S(2)}, u32[]{:S(2)}) collective-permute-start(bf16[2,96,768]{2,1,0:T(8,128)(2,1)} %maximum_select_fusion.20), channel_id=1, source_target_pairs={{0,16},{8,24},{16,0},{24,8},{1,17},{9,25},{17,1},{25,9},{2,18},{10... | collective-permute-start | bytes 884744 | tf_op jit(solution)/shard_map/ppermute | solution.py:296
  699.1 15.4 %collective-permute-start.63 = (bf16[768,2,1,1,128]{4,0,2,1,3:T(8,128)(2,1)S(1)}, bf16[768,2,1,1,128]{4,0,2,1,3:T(8,128)(2,1)S(1)}, u32[]{:S(2)}, u32[]{:S(2)}) collective-permute-start(bf16[768,2,1,1,128]{4,0,2,1,3:T(8,128)(2,1)S(1)} %copy.74), channel_id=1, source_target_pairs={{0,16},{8,24},{16,0},{24,8},{1,17},{9,25},{17,1},{25,9},{2,18},{10... | collective-permute-start | bytes 1179656 | tf_op jit(solution)/shard_map/ppermute | solution.py:296
  711.7 21.1 %collective-permute-start.46 = (bf16[384,2,384]{0,2,1:T(8,128)(2,1)S(1)}, bf16[384,2,384]{0,2,1:T(8,128)(2,1)S(1)}, u32[]{:S(2)}, u32[]{:S(2)}) collective-permute-start(bf16[384,2,384]{0,2,1:T(8,128)(2,1)S(1)} %maximum_select_fusion.15), channel_id=1, source_target_pairs={{0,16},{8,24},{16,0},{24,8},{1,17},{9,25},{17,1},{25,9},{2,18},{10... | collective-permute-start | bytes 1769480 | tf_op jit(solution)/shard_map/ppermute | solution.py:296
  714.5 18.8 %collective-permute-start.64 = (bf16[768,2,2,1,128]{4,0,2,1,3:T(8,128)(2,1)S(1)}, bf16[768,2,2,1,128]{4,0,2,1,3:T(8,128)(2,1)S(1)}, u32[]{:S(2)}, u32[]{:S(2)}) collective-permute-start(bf16[768,2,2,1,128]{4,0,2,1,3:T(8,128)(2,1)S(1)} %maximum_select_fusion.12), channel_id=1, source_target_pairs={{0,8},{8,0},{16,24},{24,16},{1,9},{9,1},{17,25},{25,17},{2,10},{10... | collective-permute-start | bytes 2359304 | tf_op jit(solution)/shard_map/ppermute | solution.py:296
  733.0 20.4 %collective-permute-start.47 = (bf16[384,2,384]{0,2,1:T(8,128)(2,1)S(1)}, bf16[384,2,384]{0,2,1:T(8,128)(2,1)S(1)}, u32[]{:S(2)}, u32[]{:S(2)}) collective-permute-start(bf16[384,2,384]{0,2,1:T(8,128)(2,1)S(1)} %add_convert_fusion.12), channel_id=1, source_target_pairs={{0,8},{8,0},{16,24},{24,16},{1,9},{9,1},{17,25},{25,17},{2,10},{10... | collective-permute-start | bytes 1769480 | tf_op jit(solution)/shard_map/ppermute | solution.py:296
  (64 other events, 1247.7 us)
Sparse Core Ops, SparseCore 0:
  73.6 37.6 all-gather.8
  139.7 56.5 all-gather.6
  447.3 21.4 reduce-scatter.10
  471.5 34.3 reduce-scatter.8
  508.0 34.8 reduce-scatter.6
  603.6 41.3 reduce-scatter.4

commit v2 on v1

v2 whole, which is shorter than its diff:
```python
import functools
import math

import jax
import jax.numpy as jnp
from jax import lax
from jax.experimental import pallas as pl
from jax.experimental.pallas import tpu as pltpu
from jax.sharding import PartitionSpec as P

QUERY_HEADS = 16
KEY_VALUE_HEADS = 8
HEAD_DIM = 96
SEQUENCE_TOKENS = 1024

eps = 1e-05
rope_base = 100000.0

BF = jnp.bfloat16
F32 = jnp.float32

HALF = HEAD_DIM // 2
LANES = 128
GROUP = 4 * HEAD_DIM
GROUP_LANES = 4 * LANES
BLOCK = 256
SCALE = HEAD_DIM ** (-0.5)
PARTS = 2
QUICK = pl.CostEstimate(flops=1, bytes_accessed=1, transcendentals=0)
SPLIT_MODEL = 768


def dot(a, b):
    return lax.dot_general(a, b, (((1,), (0,)), ((), ())), preferred_element_type=F32)


def dot_nt(a, b):
    return lax.dot_general(a, b, (((1,), (1,)), ((), ())), preferred_element_type=F32)


def dot_tn(a, b):
    return lax.dot_general(a, b, (((0,), (0,)), ((), ())), preferred_element_type=F32)


def scores_t(keys, queries, block):
    s = dot_nt(keys, queries)
    length = s.shape[0]
    key_pos = lax.broadcasted_iota(jnp.int32, s.shape, 0)
    query_pos = lax.broadcasted_iota(jnp.int32, s.shape, 1) + block * BLOCK
    s = jnp.where(key_pos <= query_pos, s, -1e30)
    top = jnp.max(s, axis=0, keepdims=True)
    e = jnp.exp2((s - top) * (SCALE * math.log2(math.e)))
    return e * (1.0 / jnp.sum(e, axis=0, keepdims=True))


def attention_forward_kernel(n1_ref, w_ref, spread_ref, cos_ref, sin_ref, qkv_ref, o_ref):
    w = dot(w_ref[...], spread_ref[...]).astype(BF)
    h = dot(n1_ref[...], w)
    cos, sin = cos_ref[...], sin_ref[...]
    for part in range(4):
        c = h[:, part * LANES : (part + 1) * LANES]
        if part < 3:
            c = c * cos + pltpu.roll(c, LANES // 2, 1) * sin
        qkv_ref[:, part * LANES : (part + 1) * LANES] = c.astype(BF)
    v_t = h[:, 3 * LANES :].T.astype(BF)
    for head in range(2):
        lanes = slice(head * LANES, (head + 1) * LANES)
        for block in range(SEQUENCE_TOKENS // BLOCK):
            rows = slice(block * BLOCK, (block + 1) * BLOCK)
            length = (block + 1) * BLOCK
            p = scores_t(qkv_ref[:length, 2 * LANES : 3 * LANES], qkv_ref[rows, lanes], block)
            o_t = dot(v_t[:, :length], p.astype(BF))
            o_ref[rows, lanes] = o_t.T.astype(BF)


def attention_backward_kernel(qkv_ref, do_ref, gather_ref, cos_ref, sin_ref, out_ref, dk_ref, dv_ref, dq_ref, d_ref):
    cos, sin = cos_ref[...], sin_ref[...]

    def unrotate(c):
        c = c * SCALE
        return (c * cos - pltpu.roll(c, LANES // 2, 1) * sin).astype(BF)

    k_t = qkv_ref[:, 2 * LANES : 3 * LANES].astype(F32).T.astype(BF)
    dk_ref[...] = jnp.zeros_like(dk_ref)
    dv_ref[...] = jnp.zeros_like(dv_ref)
    for head in range(2):
        lanes = slice(head * LANES, (head + 1) * LANES)
        for block in range(SEQUENCE_TOKENS // BLOCK):
            rows = slice(block * BLOCK, (block + 1) * BLOCK)
            length = (block + 1) * BLOCK
            q = qkv_ref[rows, lanes]
            do = do_ref[rows, lanes]
            p = scores_t(qkv_ref[:length, 2 * LANES : 3 * LANES], q, block)
            dp = dot_nt(qkv_ref[:length, 3 * LANES :], do)
            ds = (p * (dp - jnp.sum(p * dp, axis=0, keepdims=True))).astype(BF)
            dv_ref[:length, :] += dot(p.astype(BF), do)
            dk_ref[:length, :] += dot(ds, q)
            dq_ref[rows, :] = dot(k_t[:, :length], ds).T
        d_ref[:, lanes] = unrotate(dq_ref[...])
    d_ref[:, 2 * LANES : 3 * LANES] = unrotate(dk_ref[...])
    d_ref[:, 3 * LANES :] = dv_ref[...].astype(BF)
    out_ref[...] = dot(d_ref[...], gather_ref[...]).astype(BF)


def rotary_tables():
    positions = jnp.arange(SEQUENCE_TOKENS).astype(F32)
    inverse_freq = jnp.exp(jnp.arange(HALF).astype(F32) * (-2.0 * math.log(rope_base) / HEAD_DIM))
    angles = positions[:, None] * inverse_freq[None, :]
    gap = ((0, 0), (0, LANES // 2 - HALF))
    cos, sin = jnp.pad(jnp.cos(angles), gap), jnp.pad(jnp.sin(angles), gap)
    return jnp.concatenate([cos, cos], axis=1), jnp.concatenate([-sin, sin], axis=1)


def spread_matrix():
    src = lax.broadcasted_iota(jnp.int32, (GROUP, GROUP_LANES), 0)
    lane = lax.broadcasted_iota(jnp.int32, (GROUP, GROUP_LANES), 1)
    head, comp = src // HEAD_DIM, src % HEAD_DIM
    place = head * LANES + jnp.where(comp < HALF, comp, comp + LANES // 2 - HALF)
    return (place == lane).astype(BF)


def attention_forward(n1, w, spread, cos, sin):
    tokens, width = n1.shape
    groups = w.shape[1] // GROUP
    whole = lambda a: pl.BlockSpec(a.shape, lambda j: (0, 0))
    return pl.pallas_call(
        attention_forward_kernel,
        grid=(groups,),
        in_specs=[
            whole(n1),
            pl.BlockSpec((width, GROUP), lambda j: (0, j)),
            whole(spread),
            whole(cos),
            whole(sin),
        ],
        out_specs=[
            pl.BlockSpec((tokens, GROUP_LANES), lambda j: (0, j)),
            pl.BlockSpec((tokens, 2 * LANES), lambda j: (0, j)),
        ],
        out_shape=[
            jax.ShapeDtypeStruct((tokens, groups * GROUP_LANES), BF),
            jax.ShapeDtypeStruct((tokens, groups * 2 * LANES), BF),
        ],
        compiler_params=pltpu.CompilerParams(vmem_limit_bytes=48 * 1024 * 1024),
        cost_estimate=QUICK,
        name="attention_forward",
    )(n1, w, spread, cos, sin)


def attention_backward(qkv, do, gather, cos, sin, first, groups):
    tokens = qkv.shape[0]
    whole = lambda a: pl.BlockSpec(a.shape, lambda j: (0, 0))
    return pl.pallas_call(
        attention_backward_kernel,
        grid=(groups,),
        in_specs=[
            pl.BlockSpec((tokens, GROUP_LANES), lambda j: (0, first + j)),
            pl.BlockSpec((tokens, 2 * LANES), lambda j: (0, first + j)),
            whole(gather),
            whole(cos),
            whole(sin),
        ],
        out_specs=pl.BlockSpec((tokens, GROUP), lambda j: (0, j)),
        out_shape=jax.ShapeDtypeStruct((tokens, groups * GROUP), BF),
        scratch_shapes=[
            pltpu.VMEM((tokens, LANES), F32),
            pltpu.VMEM((tokens, LANES), F32),
            pltpu.VMEM((tokens, LANES), F32),
            pltpu.VMEM((tokens, GROUP_LANES), BF),
        ],
        compiler_params=pltpu.CompilerParams(vmem_limit_bytes=48 * 1024 * 1024),
        cost_estimate=QUICK,
        name="attention_backward",
    )(qkv, do, gather, cos, sin)


def feedforward_kernel(col_step, sub, rows_of, n2_ref, cot_ref, *refs):
    *blocks, out_ref, dn2_ref, h_ref, dgu_ref = refs
    sides = [blocks[k : k + rows_of] for k in range(0, len(blocks), rows_of)]
    weights, earlier, grads = sides[:2], sides[2:-2], sides[-2:]
    step, half = pl.program_id(0), pl.num_programs(0) // 2
    width = n2_ref.shape[1] // rows_of
    cut = [slice(i * width, (i + 1) * width) for i in range(rows_of)]

    @pl.when(step == 0)
    def _():
        out_ref[...] = jnp.zeros_like(out_ref)
        dn2_ref[...] = jnp.zeros_like(dn2_ref)

    def rows(ref, first, last):
        return jnp.concatenate([ref[c, first:last] for c in range(col_step)], axis=0)

    def work(whose):
        gate_up = [rows(r, 0, 2 * sub) for r in weights[whose]]
        down = [rows(r, 2 * sub, 3 * sub) for r in weights[whose]]
        dh = sum(dot_nt(cot_ref[:, cut[i]], down[i]) for i in range(rows_of))
        gu = sum(dot_nt(n2_ref[:, cut[i]], gate_up[i]) for i in range(rows_of))
        for c in range(col_step):
            gate, up = (gu[:, (2 * c + k) * sub : (2 * c + k + 1) * sub] for k in range(2))
            sig = jax.nn.sigmoid(gate)
            silu = gate * sig
            lanes = slice(c * sub, (c + 1) * sub)
            part = dh[:, lanes]
            h_ref[:, lanes] = (silu * up).astype(BF)
            dgu_ref[:, 2 * c * sub : (2 * c + 1) * sub] = (part * up * (sig + silu * (1 - sig))).astype(BF)
            dgu_ref[:, (2 * c + 1) * sub : (2 * c + 2) * sub] = (part * silu).astype(BF)
        hidden, dgu = h_ref[...], dgu_ref[...]
        hidden_t, dgu_t = hidden.T, dgu.T
        for i in range(rows_of):
            dn2_ref[:, cut[i]] += dot(dgu, gate_up[i])
            out_ref[:, cut[i]] += dot(hidden, down[i])
            gate_up_grad = dot(dgu_t, n2_ref[:, cut[i]])
            down_grad = dot(hidden_t, cot_ref[:, cut[i]])
            for c in range(col_step):
                new = (gate_up_grad[2 * c * sub : 2 * (c + 1) * sub], down_grad[c * sub : (c + 1) * sub])
                for part, here in zip(new, (slice(2 * sub), slice(2 * sub, None))):
                    if earlier:
                        part = part + earlier[whose][i][c, here].astype(F32)
                    grads[whose][i][c, here] = part.astype(BF)

    pl.when(step < half)(lambda: work(1))
    pl.when(step >= half)(lambda: work(0))


def feedforward(n2, cot, weights, col_step, earlier=()):
    tokens, model = n2.shape
    rows_of = len(weights[0])
    columns, rows, width = weights[0][0].shape
    sub = rows // 3
    half = columns // col_step
    once = lambda a: pl.BlockSpec(a.shape, lambda s: (0, 0), pipeline_mode=pl.Buffered(1))
    place = [lambda s: (jnp.maximum(s - half, 0), 0, 0), lambda s: (jnp.minimum(s, half - 1), 0, 0)]
    flat = [a for side in weights for a in side]
    specs = [pl.BlockSpec((col_step, rows, width), place[whose]) for whose in range(2) for _ in range(rows_of)]
    earlier = [a for side in earlier for a in side]
    total = jax.ShapeDtypeStruct((tokens, model), F32)
    outs = pl.pallas_call(
        functools.partial(feedforward_kernel, col_step, sub, rows_of),
        grid=(2 * half,),
        in_specs=[once(n2), once(cot)] + specs + (specs if earlier else []),
        out_specs=specs + [once(total), once(total)],
        out_shape=[jax.ShapeDtypeStruct(a.shape, BF) for a in flat] + [total, total],
        scratch_shapes=[
            pltpu.VMEM((tokens, col_step * sub), BF),
            pltpu.VMEM((tokens, 2 * col_step * sub), BF),
        ],
        compiler_params=pltpu.CompilerParams(vmem_limit_bytes=60 * 1024 * 1024),
        cost_estimate=QUICK,
        name="feedforward",
    )(n2, cot, *flat, *earlier)
    return [list(outs[:rows_of]), list(outs[rows_of : 2 * rows_of])], outs[2 * rows_of], outs[2 * rows_of + 1]


def place_kernel(*refs):
    parts, (gate_up_ref, down_ref) = refs[:-2], refs[-2:]
    sub, block = parts[0].shape[2] // 3, parts[0].shape[3]
    tiles = 4 * len(parts)
    for y in range(2):
        for core in range(2):
            for k, part in enumerate(parts):
                tile = (2 * y + core) * len(parts) + k
                for half in range(2):
                    piece = part[y, core, half * sub : (half + 1) * sub].astype(F32)
                    gate_up_ref[pl.ds(2 * tile + half, block, stride=2 * tiles), :] = piece.T
                down_ref[tile * sub : (tile + 1) * sub] = part[y, core, 2 * sub :].astype(F32)


def place(parts):
    sub, block = parts[0].shape[2] // 3, parts[0].shape[3]
    tiles = 4 * len(parts)
    gate_up, down = pl.pallas_call(
        place_kernel,
        out_shape=[
            jax.ShapeDtypeStruct((block * tiles * 2, sub), F32),
            jax.ShapeDtypeStruct((tiles * sub, block), F32),
        ],
        compiler_params=pltpu.CompilerParams(vmem_limit_bytes=48 * 1024 * 1024),
        cost_estimate=QUICK,
        name="place",
    )(*parts)
    return gate_up.reshape(block, tiles, 2, sub).transpose(0, 2, 1, 3).reshape(block, 2, -1), down


def place_attention_kernel(*refs):
    cores, (query_ref, pair_ref, projection_ref) = refs[:2], refs[2:]
    block = query_ref.shape[0]
    rows = block // 2
    for core, ref in enumerate(cores):
        here = slice(core * rows, (core + 1) * rows)
        for parity in range(2):
            g = ref[parity, :rows].astype(F32)
            query_ref[here, 2 * parity * HEAD_DIM : 2 * (parity + 1) * HEAD_DIM] = g[:, : 2 * HEAD_DIM]
            g = g.T
            for k in range(2):
                pair_ref[k, parity * HEAD_DIM : (parity + 1) * HEAD_DIM, here] = g[(2 + k) * HEAD_DIM : (3 + k) * HEAD_DIM]
            head = slice((2 * parity + core) * HEAD_DIM, (2 * parity + core + 1) * HEAD_DIM)
            for k in range(block // GROUP):
                piece = ref[parity, rows + k * HEAD_DIM : rows + (k + 1) * HEAD_DIM]
                projection_ref[head, k * GROUP : (k + 1) * GROUP] = piece.astype(F32)


def place_attention(first, second, block):
    folded = block % GROUP != 0
    query, pair, projection = pl.pallas_call(
        place_attention_kernel,
        out_shape=[
            jax.ShapeDtypeStruct((block, 4 * HEAD_DIM), F32),
            jax.ShapeDtypeStruct((2, 2 * HEAD_DIM, block), F32),
            jax.ShapeDtypeStruct((4 * HEAD_DIM, block), F32),
        ],
        compiler_params=pltpu.CompilerParams(vmem_limit_bytes=32 * 1024 * 1024),
        cost_estimate=QUICK,
        name="place_attention",
    )(first, second)
    if folded:
        both = jnp.stack([a[:, block // 2 :].reshape(2, HEAD_DIM, block) for a in (first, second)], axis=1)
        projection = both.astype(F32).reshape(-1, block)
    return query, pair.transpose(2, 0, 1), projection


def inverse_rms(field):
    return lax.rsqrt(jnp.mean(field * field, axis=-1, keepdims=True) + eps)


def norm_back(field, gain, grad):
    r = inverse_rms(field)
    scaled = gain * grad
    inner = jnp.mean(field * scaled, axis=-1, keepdims=True)
    return r * scaled - field * (r * r * r * inner), jnp.sum(grad * field * r, axis=0)


def halves(first_is_mine, mine, other, axis):
    return jnp.where(
        first_is_mine, jnp.concatenate([mine, other], axis), jnp.concatenate([other, mine], axis)
    )


def per_device(
    tokens,
    attention_gain,
    feedforward_gain,
    query_weight,
    key_value_matrix,
    projection_weight,
    gate_up_weight,
    down_weight,
    cotangent,
    *,
    sizes,
):
    dp_size, row_size, col_size = sizes
    x, z, d = lax.axis_index("row"), lax.axis_index("col"), lax.axis_index("dp")
    core, y, parity = d % 2, d // 2, z % 2
    model = tokens.shape[1]
    own = tokens.shape[0]
    block = model // row_size
    hidden_block = down_weight.shape[0]
    sub = hidden_block // 4 // PARTS

    def swap(a, axis, bit):
        n = {"dp": dp_size, "col": col_size}[axis]
        return lax.ppermute(a, axis, [(i, i ^ bit) for i in range(n)])

    def to_core(a):
        return swap(a, "dp", 1)

    def to_y(a):
        return swap(a, "dp", 2)

    def to_pair(a):
        return swap(a, "col", 1)

    def shift(a, axis, by):
        n = {"row": row_size, "col": col_size}[axis]
        return lax.ppermute(a, axis, [(i, (i + by) % n) for i in range(n)])

    def rel(a):
        if row_size == 2:
            return jnp.where(x == 0, a, jnp.concatenate([a[..., block:], a[..., :block]], axis=-1))
        return lax.dynamic_slice_in_dim(jnp.concatenate([a, a], axis=-1), x * block, model, a.ndim - 1)

    def unrel(a):
        if row_size == 2:
            return rel(a)
        return lax.dynamic_slice_in_dim(
            jnp.concatenate([a, a], axis=-1), (row_size - x) % row_size * block, model, a.ndim - 1
        )

    def gather_rows(piece):
        return [piece] + [shift(piece, "row", -i) for i in range(1, row_size)]

    def gather_columns(piece_of):
        return [piece_of(0)] + [shift(piece_of(j & 1), "col", j) for j in range(1, col_size)]

    def pick(a, index, axis):
        return lax.dynamic_index_in_dim(a, index, axis, keepdims=False)

    def merge(rows):
        return rows if len(rows) * SPLIT_MODEL <= model else [jnp.concatenate(rows, axis=2)]

    def by_rows(blocks):
        return list(blocks) if len(blocks) == row_size else jnp.split(blocks[0], row_size, axis=2)

    def reduce_columns(parts, first=0):
        return [shift(part, "col", -j) if j else part for j, part in enumerate(parts, first)]

    def by_core(a, axis):
        mine, other = pick(a, core, axis), pick(a, 1 - core, axis)
        return small(mine, to_core(other))

    def by_parity(arrived):
        return halves(parity == 0, small(*arrived[0::2])[None], small(*arrived[1::2])[None], 0)

    fence = lax.optimization_barrier

    def fold(a):
        if block % GROUP:
            return a.reshape(-1, GROUP)
        return jnp.concatenate([a[:, k : k + GROUP] for k in range(0, block, GROUP)])

    def unfold(a):
        if block % GROUP:
            return a.reshape(a.shape[:-2] + (HEAD_DIM, block))
        return jnp.concatenate([a[..., k : k + HEAD_DIM, :] for k in range(0, a.shape[-2], HEAD_DIM)], axis=-1)

    near, far = slice(1, None, 2), slice(2, None, 2)

    def total(*parts):
        return sum(part.astype(F32) for part in parts)

    def small(*parts):
        return total(*parts).astype(BF)

    def in_sequence(a, other):
        return halves(parity == 0, a, other, 0)

    def rows_of(a, first):
        return lax.dynamic_slice_in_dim(a, first, own, 0)

    query_blocks = query_weight.reshape(block, 2, 2 * HEAD_DIM)
    pair_blocks = key_value_matrix.reshape(block, 2, 2, HEAD_DIM)
    packed = jnp.concatenate([query_blocks, pair_blocks[:, 0], pair_blocks[:, 1]], axis=-1)
    packed = lax.dynamic_slice_in_dim(packed, core * (block // 2), block // 2, 0)
    head_rows = pick(projection_weight.reshape(2, 2, HEAD_DIM, block), core, 1)
    packed = fence(
        [jnp.concatenate([pick(packed, p, 1), fold(pick(head_rows, p, 0))]) for p in (parity, 1 - parity)]
    )
    along = gather_columns(lambda which: packed[which])
    own_packed = gather_rows(packed[0])

    pieces = []
    for part in range(PARTS):
        start = ((2 * y + core) * PARTS + part) * sub
        gate_up = lax.dynamic_slice_in_dim(gate_up_weight, start, sub, 2).transpose(1, 2, 0).reshape(2 * sub, block)
        pieces.append(jnp.concatenate([gate_up, lax.dynamic_slice_in_dim(down_weight, start, sub, 0)]))
    own_rows = gather_rows(jnp.stack(pieces))

    gain_one, gain_two = rel(attention_gain), rel(feedforward_gain)
    inputs = rel(tokens)
    grad_out = rel(cotangent)
    wide_inputs = inputs.astype(F32)
    normed = (wide_inputs * inverse_rms(wide_inputs) * gain_one).astype(BF)
    tables = rotary_tables()
    spread = spread_matrix()
    spread_back = spread.T
    along, own_packed, own_rows, pieces, normed, inputs, grad_out, tables, spread, spread_back = fence(
        (along, own_packed, own_rows, pieces, normed, inputs, grad_out, tables, spread, spread_back)
    )

    normed_other = to_pair(normed)
    got = gather_rows(jnp.stack(along[1:]))
    grad_out_other = to_y(grad_out)
    others = [None, shift(pieces[0], "col", 2), None]
    mine = [jnp.concatenate([own_packed[0][None], got[0]])]
    mine_other = [to_core(mine[0])]
    got, own_packed, normed, normed_other, own_rows, pieces, grad_out, grad_out_other, others, mine, mine_other = fence(
        (got, own_packed, normed, normed_other, own_rows, pieces, grad_out, grad_out_other, others, mine, mine_other)
    )

    mine += [jnp.concatenate([a[None], b]) for a, b in zip(own_packed[1:], got[1:])]
    mine[1:] = fence(mine[1:])
    mine_other += [to_core(a) for a in mine[1:]]
    normed_all = in_sequence(normed, normed_other)
    others = [shift(pieces[0], "col", 1), others[1], shift(pieces[0], "col", 3)]
    late_others = [shift(pieces[1], "col", 1)]
    pairs = [halves(core == 0, a[:, None], b[:, None], 1) for a, b in zip(mine, mine_other)]
    split = block // 2
    weight_qkv = jnp.concatenate([jnp.concatenate([p[j, :, :split] for j in range(col_size)], axis=-1) for p in pairs])
    weight_qkv = weight_qkv.reshape(model, -1)
    heads = jnp.concatenate([unfold(p[:, :, split:]) for p in pairs], axis=-1)
    gap = jnp.zeros(heads.shape[:2] + (LANES // 2 - HALF, model), BF)
    weight_projection = jnp.concatenate(
        [heads[:, :, :HALF], gap, heads[:, :, HALF:], gap], axis=2
    ).reshape(-1, model)
    weight_qkv, weight_projection, normed_all, grad_out, grad_out_other = fence(
        (weight_qkv, weight_projection, normed_all, grad_out, grad_out_other)
    )

    qkv, attended = attention_forward(normed_all, weight_qkv, spread, *tables)
    qkv, attended, others, late_others, grad_out, grad_out_other, weight_projection = fence(
        (qkv, attended, others, late_others, grad_out, grad_out_other, weight_projection)
    )

    sent = dot(rows_of(attended, (1 - parity) * own), weight_projection).astype(BF)
    stacked = jnp.stack(others)
    sent, stacked, attended, weight_projection = fence((sent, stacked, attended, weight_projection))
    arrived = to_pair(sent)
    rest = gather_rows(stacked)
    kept = dot(rows_of(attended, parity * own), weight_projection)
    kept, arrived, rest, pieces, own_rows = fence((kept, arrived, rest, pieces, own_rows))

    middle = inputs.astype(F32) + kept + arrived.astype(F32)
    normed_two = (middle * inverse_rms(middle) * gain_two).astype(BF)
    mine = merge([jnp.concatenate([a[None], b]) for a, b in zip([a[0] for a in own_rows], rest)])
    normed_two, middle, mine = fence((normed_two, middle, mine))
    normed_two_other = to_y(normed_two)
    others = [shift(pieces[1], "col", j) for j in (2, 3)]
    weights = [mine, [to_core(a) for a in mine]]
    weights, normed_two = fence((weights, normed_two))

    rest = [gather_rows(late_others[0])]
    grads, *sums = feedforward(normed_two, grad_out, weights, PARTS)
    grads, sums, rest, others, normed_two_other, weights, middle, late_others = fence(
        (grads, sums, rest, others, normed_two_other, weights, middle, late_others)
    )
    own_sums = [sums]
    stacked = jnp.stack(others)
    early = (
        [jnp.concatenate([own_rows[0][1:], late_others[0][None], stacked])] if row_size * SPLIT_MODEL <= model else []
    )
    stacked, early, own_rows = fence((stacked, early, own_rows))
    rest.append(gather_rows(stacked))
    early_other = [to_core(a) for a in early]
    grads, *sums = feedforward(normed_two_other, grad_out_other, weights, PARTS, grads)
    grads, sums, rest, early, early_other, own_rows = fence((grads, sums, rest, early, early_other, own_rows))
    other_sums = [sums]
    n = len(early)
    late = merge([jnp.concatenate([a[1:], b[None], c]) for a, b, c in zip(own_rows[n:], rest[0][n:], rest[1][n:])])
    mine, other = by_rows(grads[0]), by_rows(grads[1])
    late, other[1:] = fence((late, other[1:]))
    late_other = [to_core(a) for a in late]
    arrived = [to_core(a) for a in other[1:]]
    mine, other[0], late, late_other, arrived = fence((mine, other[0], late, late_other, arrived))
    weights = [early + late, early_other + late_other]
    cut = col_size // 2
    sent = [small(*pair) for pair in zip(mine[1:], arrived)]
    weights, mine[0], other[0], sent, normed_two_other = fence((weights, mine[0], other[0], sent, normed_two_other))
    rows = [shift(a[:cut], "row", i) for i, a in enumerate(sent, 1)]
    arrived = to_core(other[0])
    grads, *sums = feedforward(normed_two_other, grad_out_other, weights, PARTS)
    grads, sums, rows, mine[0], arrived, sent, weights = fence((grads, sums, rows, mine[0], arrived, sent, weights))
    other_sums.append(sums)

    blocks = [small(mine[0][j], arrived[j], *[r[j] for r in rows]) for j in range(cut)]
    sums = small(*[p[1] for p in other_sums])
    sums, blocks, grads, other_sums, own_sums = fence((sums, blocks, grads, other_sums, own_sums))
    grad_two_other = to_y(sums)
    rows = [shift(a[cut:], "row", i) for i, a in enumerate(sent, 1)]
    along = [blocks[0]] + [shift(blocks[j], "col", -j) for j in range(1, cut)]
    grads, *sums = feedforward(normed_two, grad_out, weights, PARTS, grads)
    grads, sums, rows, along, mine[0], arrived, grad_two_other = fence(
        (grads, sums, rows, along, mine[0], arrived, grad_two_other)
    )
    own_sums.append(sums)
    last, other = by_rows(grads[0]), by_rows(grads[1])
    last_rows = [to_core(a) for a in other[1:]]
    kept = total(grad_two_other, *[p[1] for p in own_sums])
    grad_middle, gain_two_term = norm_back(middle, gain_two, kept)
    grad_middle = grad_middle + grad_out.astype(F32)
    branch = grad_middle.astype(BF)
    last_rows, branch, grad_middle, gain_two_term, last, other[0] = fence(
        (last_rows, branch, grad_middle, gain_two_term, last, other[0])
    )
    branch_other = to_pair(branch)
    sent = [small(*pair) for pair in zip(last[1:], last_rows)]
    last_rows = [shift(a, "row", i) for i, a in enumerate(sent, 1)]
    last_core = to_core(other[0])
    out_kept = middle + total(*[p[0] for p in own_sums])
    out_sent = small(*[p[0] for p in other_sums])
    blocks = [small(mine[0][j], arrived[j], *[r[j - cut] for r in rows]) for j in range(cut, col_size)]
    branch, branch_other, last_core, out_kept, out_sent, blocks, grad_middle, gain_two_term = fence(
        (branch, branch_other, last_core, out_kept, out_sent, blocks, grad_middle, gain_two_term)
    )

    along += [shift(blocks[j - cut], "col", -j) for j in range(cut, col_size)]
    branch_all = in_sequence(branch, branch_other)
    grad_attended = dot_nt(branch_all, weight_projection).astype(BF)
    g = dot_tn(attended, branch_all).astype(BF).reshape(col_size, 2, LANES, model)
    projection_halves = jnp.concatenate([g[:, :, :HALF], g[:, :, LANES // 2 : LANES // 2 + HALF]], axis=2)
    projection_halves = [pick(projection_halves, which, 1) for which in (core, 1 - core)]
    projection_other = to_core(projection_halves[1])
    blocks = [small(last[0][j], last_core[j], *[r[j] for r in last_rows]) for j in range(col_size)]

    count = col_size // 2
    wide = count * GROUP
    to_rows = lambda g: [shift(g[i], "row", i) for i in range(1, row_size)]
    qkv_halves = lambda part: dot_tn(normed_all, part).astype(BF).reshape(row_size, 2, block // 2, wide)
    by_halves = lambda g: [pick(g, which, 1) for which in (core, 1 - core)]

    first = attention_backward(qkv, grad_attended, spread_back, *tables, 0, count)
    first, along, projection_halves, projection_other, blocks, grad_attended = fence(
        (first, along, projection_halves, projection_other, blocks, grad_attended)
    )
    last_along = [blocks[0]] + [shift(blocks[j], "col", -j) if j & 1 else blocks[j] for j in range(1, col_size)]
    first_halves = by_halves(qkv_halves(first))
    first_other = to_core(first_halves[1])
    g = small(projection_halves[0], projection_other)
    projection_rows = [g[:, :, i * block : (i + 1) * block] for i in range(row_size)]
    projection_rows[1:] = to_rows(projection_rows)
    second = attention_backward(qkv, grad_attended, spread_back, *tables, count, count)
    second, last_along, first_other, projection_rows, along, first_halves = fence(
        (second, last_along, first_other, projection_rows, along, first_halves)
    )

    product = lambda rows: sum(
        dot_nt(rows(part), weight_qkv[:, k * wide : (k + 1) * wide]) for k, part in enumerate((first, second))
    )
    sent = product(lambda a: rows_of(a, (1 - parity) * own)).astype(BF)
    second_halves = by_halves(qkv_halves(second))
    first_rows = small(first_halves[0], first_other)
    g = small(*projection_rows)
    sent, second, second_halves, first_rows, g, along, out_sent = fence(
        (sent, second, second_halves, first_rows, g, along, out_sent)
    )
    grad_one_other = to_pair(sent)
    first_rows = [first_rows[0]] + to_rows(first_rows)
    second_other = to_core(second_halves[1])
    first_part = small(*along)
    second_halves, second_other, g, first_part = fence((second_halves, second_other, g, first_part))
    second_rows = small(second_halves[0], second_other)
    second_rows = [second_rows[0]] + to_rows(second_rows)
    last_along[far] = [shift(last_along[j], "col", -j) for j in range(2, col_size, 2)]
    first_part_other = to_y(first_part)
    kept = product(lambda a: rows_of(a, parity * own))
    second_rows, first_rows, grad_one_other, kept, first_part, first_part_other, last_along = fence(
        (second_rows, first_rows, grad_one_other, kept, first_part, first_part_other, last_along)
    )

    columns = lambda g, first: reduce_columns([g[:, j * GROUP : (j + 1) * GROUP] for j in range(count)], first)
    blocks = [small(*first_rows), small(*second_rows)]
    last_part = small(*last_along)
    blocks, last_part = fence((blocks, last_part))
    arrived = columns(blocks[1], count) + columns(blocks[0], 0)
    arrived = arrived[count:] + arrived[:count]
    last_part_other = to_y(last_part)
    grad_inputs, gain_one_term = norm_back(inputs.astype(F32), gain_one, kept + grad_one_other.astype(F32))
    grad_inputs = unrel((grad_inputs + grad_middle).astype(BF))
    gains = unrel(jnp.stack([gain_one_term, gain_two_term]))
    first_part = halves(y == 0, first_part[None], first_part_other[None], 0)[:, None]
    first_part_other = to_core(first_part)
    arrived, gains, grad_inputs, first_part, first_part_other, last_part, last_part_other = fence(
        (arrived, gains, grad_inputs, first_part, first_part_other, last_part, last_part_other)
    )
    projection_along = reduce_columns([g[j] for j in range(col_size)])
    out_other = to_y(out_sent)
    gains = gains + swap(gains, "dp", 1)
    gains = gains + swap(gains, "dp", 2)
    last_part = halves(y == 0, last_part[None], last_part_other[None], 0)[:, None]
    arrived = by_parity(arrived)
    gains, last_part, projection_along, arrived, out_other, first_part = fence(
        (gains, last_part, projection_along, arrived, out_other, first_part)
    )

    both = jnp.concatenate([arrived, jnp.stack([fold(p) for p in by_parity(projection_along)])], axis=1)
    both, gains, last_part = fence((both, gains, last_part))
    both_other = to_y(both)
    last_part_other = to_core(last_part)
    for axis, n in (("row", row_size), ("col", col_size)):
        bit = 1
        while bit < n:
            gains = gains + lax.ppermute(gains, axis, [(i, i ^ bit) for i in range(n)])
            bit *= 2
    attention_gain_grad, feedforward_gain_grad = gains[0], gains[1]
    output = unrel((out_kept + out_other.astype(F32)).astype(BF))
    sides = [halves(core == 0, a, b, 1) for a, b in ((first_part, first_part_other), (last_part, last_part_other))]
    gate_up_grad, down_grad = place(sides)
    both, both_other, gate_up_grad, down_grad, gains, output = fence(
        (both, both_other, gate_up_grad, down_grad, gains, output)
    )
    both = small(both, both_other)
    both_other = to_core(both)
    query_grad, key_value_grad, projection_grad = place_attention(
        jnp.where(core == 0, both, both_other), jnp.where(core == 0, both_other, both), block
    )
    return (
        output,
        grad_inputs,
        attention_gain_grad,
        feedforward_gain_grad,
        query_grad,
        key_value_grad,
        projection_grad,
        gate_up_grad,
        down_grad,
    )


def solution(mesh):
    sizes = tuple(mesh.shape[name] for name in ("dp", "row", "col"))
    return jax.shard_map(
        functools.partial(per_device, sizes=sizes),
        mesh=mesh,
        in_specs=(
            P(("dp", "row", "col"), None),
            P(),
            P(),
            P("row", "col"),
            P("row", None, "col"),
            P("col", "row"),
            P("row", None, "col"),
            P("col", "row"),
            P(("dp", "row", "col"), None),
        ),
        out_specs=(
            P(("dp", "row", "col"), None),
            P(("dp", "row", "col"), None),
            P(),
            P(),
            P("row", "col"),
            P("row", None, "col"),
            P("col", "row"),
            P("row", None, "col"),
            P("col", "row"),
        ),
        check_vma=False,
    )
```

time: 771 us -> 651 us (0.84)
  blocking collectives: 86.3 us -> 0 us
  Pallas kernels: 158 us -> 180 us
  local copies, waits for them, and re-layouts: 55.6 us -> 34 us
  between operations: 15.8 us -> 2.57 us
  waiting for transfers between devices: 241 us -> 231 us
  other arithmetic: 106 us -> 97.8 us
    all_gather x2 -> x0, blocking collectives: 86.3 us -> none  [per_device(): down = both_cores(gather_rows(lax.all_gather(piece, 'col')), 2)]
    ppermute x30 -> x33, waiting for transfers between devices: 151 us -> 129 us  [shift(): return lax.ppermute(a, axis, [(i, (i + by) % n) for i in range(n)])]
    ppermute x40 -> x29, waiting for transfers between devices: 81.4 us -> 96.2 us  [swap(): return lax.ppermute(a, axis, [(i, i ^ bit) for i in range(n)])]
    pallas_call x2 -> x4, Pallas kernels: 98.6 us -> 111 us  [feedforward(): pl.pallas_call(functools.partial(feedforward_kernel, col_step, sub, rows_...]
    dynamic_slice x5 -> x3, local copies, waits for them, and re-layouts: 10.5 us -> 0.72 us  [pick(): return lax.dynamic_index_in_dim(a, index, axis, keepdims=False)]
    convert_element_type x3 -> x0, local copies, waits for them, and re-layouts: 9.65 us -> none  [the longest x1 6.58 us: per_device(): jnp.stack(gate_up_parts, axis=4).astype(F32).reshape(block, 2, -1)]
    concatenate x6 -> x12, other arithmetic: 10.2 us -> 19.5 us  [the longest x3 6.63 us: per_device(): jnp.concatenate([a[None], b])]
    convert_element_type x21 -> x19, other arithmetic: 44.5 us -> 35.2 us  [the longest x16 33.4 us: small(): return total(*parts).astype(BF)]
  transfers between devices with their start and end apart: 81 -> 65, of which waited for: 23 -> 27; matrix products, arithmetic and copies ran while one was open for 25% -> 15% of each run, Pallas kernels for 21% -> 28%
where the time goes in v2:
time: 651 us; the launch traced here: 643 us
  waiting for transfers between devices  231 us (35%)
  Pallas kernels  180 us (28%)
  other arithmetic  97.8 us (15%)
  starting transfers between devices  63.9 us (10%)
  local copies, waits for them, and re-layouts  34 us (5%)
  matrix products  33.1 us (5%)
    ppermute x33, waiting for transfers between devices, shift(): return lax.ppermute(a, axis, [(i, (i + by) % n) for i in range(n)])  129 us
    pallas_call x4, Pallas kernels, feedforward(): pl.pallas_call(functools.partial(feedforward_kernel, col_step, sub, rows_...  111 us
    ppermute x29, waiting for transfers between devices, swap(): return lax.ppermute(a, axis, [(i, i ^ bit) for i in range(n)])  96.2 us
    ppermute x33, starting transfers between devices, shift(): return lax.ppermute(a, axis, [(i, (i + by) % n) for i in range(n)])  46.3 us
    convert_element_type x16, other arithmetic, small(): return total(*parts).astype(BF)  33.4 us
    pallas_call x2, Pallas kernels, attention_backward(): pl.pallas_call(attention_backward_kernel, grid=(groups,), in_specs=[pl.Bl...  30.3 us
    pallas_call x1, Pallas kernels, attention_forward(): pl.pallas_call(attention_forward_kernel, grid=(groups,), in_specs=[whole(...  29.7 us
    dot_general x5, matrix products, dot_nt(): lax.dot_general(a, b, (((1,), (1,)), ((), ())), preferred_element_type=F32)  14.4 us
  transfers between devices with their start and end apart: 65, of which 27 were waited for; matrix products, arithmetic and copies ran while one was open for 15% of the time, Pallas kernels for 28%

profile of v2, /device:TPU:0, one launch (start us, length us, event | category | flops | bytes accessed | tf_op | source)
XLA Modules:
  0.0 642.9 jit_solution(12445850124338312457)
XLA Ops:
  5.8 5.0 collective-permute-start.2
  26.6 5.6 collective-permute-done
  32.3 16.7 %collective-permute-done.1 = bf16[576,384]{1,0:T(8,128)(2,1)} collective-permute-done((bf16[576,384]{1,0:T(8,128)(2,1)}, bf16[576,384]{1,0:T(8,128)(2,1)}, u32[]{:S(2)}, u32[]{:S(2)}) %collective-permute-start.1) | collective-permute-done | bytes 442400 | tf_op jit(solution)/shard_map/ppermute | solution.py:375
  55.5 3.2 collective-permute-start.8
  58.7 39.7 %collective-permute-done.8 = bf16[384,768]{1,0:T(8,128)(2,1)S(1)} collective-permute-done((bf16[384,768]{1,0:T(8,128)(2,1)S(1)}, bf16[384,768]{1,0:T(8,128)(2,1)S(1)}, u32[]{:S(2)}, u32[]{:S(2)}) %collective-permute-start.8) | collective-permute-done | bytes 589856 | tf_op jit(solution)/shard_map/ppermute | solution.py:375
  102.7 2.4 pad_maximum_fusion.7
  105.1 2.7 collective-permute-start.12
  109.1 3.7 maximum_select_fusion
  114.8 2.1 maximum_select_fusion.2.n1_ref
  116.9 3.7 maximum_select_fusion.1
  122.0 3.2 maximum_maximum_fusion
  125.2 29.7 %attention_forward.1 = (bf16[1024,2048]{1,0:T(8,128)(2,1)}, bf16[1024,1024]{1,0:T(8,128)(2,1)S(1)}) custom-call(bf16[1024,1536]{1,0:T(8,128)(2,1)} %maximum_select_fusion.2.n1_ref, bf16[1536,1536]{1,0:T(8,128)(2,1)} %bitcast.164, bf16[384,512]{1,0:T(8,128)(2,1)S(1)} %fusion.34.spread_ref, f32[1024,128]{1,0:T(8,128)S(1)} %get-tuple-element.310.cos_ref, ...), custom_call_target="tpu_custom_call" | custom-call | flops 1 | bytes 1 | tf_op jit(solution)/shard_map/attention_forward/pallas_call | solution.py:126
  154.9 3.4 pad_maximum_fusion.8
  158.3 2.9 convolution_convert_fusion.3
  163.0 4.0 fusion.22
  167.0 31.7 %collective-permute-done.14 = bf16[512,1536]{1,0:T(8,128)(2,1)} collective-permute-done((bf16[512,1536]{1,0:T(8,128)(2,1)}, bf16[512,1536]{1,0:T(8,128)(2,1)}, u32[]{:S(2)}, u32[]{:S(2)}) %collective-permute-start.14) | collective-permute-done | bytes 1572896 | tf_op jit(solution)/shard_map/ppermute | solution.py:362
  198.7 3.0 collective-permute-done.15
  201.7 2.4 multiply_reduce_fusion.3
  205.7 2.1 fusion.79
  209.5 2.5 pad_maximum_fusion.2.refs_0_
  217.0 3.1 collective-permute-start.20
  222.1 3.3 collective-permute-start.19
  225.4 27.0 %feedforward.4 = (bf16[4,384,768]{2,1,0:T(8,128)(2,1)}, bf16[4,384,768]{2,1,0:T(8,128)(2,1)}, bf16[4,384,768]{2,1,0:T(8,128)(2,1)}, bf16[4,384,768]{2,1,0:T(8,12...) custom-call(bf16[512,1536]{1,0:T(8,128)(2,1)} %copy-done.12, bf16[512,1536]{1,0:T(8,128)(2,1)} %copy-done.7, ...), custom_call_target="tpu_custom_call" | custom-call | flops 1 | bytes 1 | tf_op jit(solution)/shard_map/feedforward/pallas_call | solution.py:237
  252.5 6.4 collective-permute-done.19
  260.3 3.1 pad_maximum_fusion.4.refs_0_
  263.9 28.7 %feedforward.5 = (bf16[4,384,768]{2,1,0:T(8,128)(2,1)}, bf16[4,384,768]{2,1,0:T(8,128)(2,1)}, bf16[4,384,768]{2,1,0:T(8,128)(2,1)}, bf16[4,384,768]{2,1,0:T(8,12...) custom-call(bf16[512,1536]{1,0:T(8,128)(2,1)} %collective-permute-done.21.n2_ref, bf16[512,1536]{1,0:T(8,128)(2,1)} %copy-done.25, ...), custom_call_target="tpu_custom_call" | custom-call | flops 1 | bytes 1 | tf_op jit(solution)/shard_map/feedforward/pallas_call | solution.py:237
  297.6 2.9 collective-permute-done.25
  300.5 3.5 collective-permute-done.24.refs_3_
  307.6 27.0 %feedforward.6 = (bf16[4,384,768]{2,1,0:T(8,128)(2,1)}, bf16[4,384,768]{2,1,0:T(8,128)(2,1)}, bf16[4,384,768]{2,1,0:T(8,128)(2,1)}, bf16[4,384,768]{2,1,0:T(8,12...) custom-call(bf16[512,1536]{1,0:T(8,128)(2,1)} %collective-permute-done.21.n2_ref, bf16[512,1536]{1,0:T(8,128)(2,1)} %copy-done.25, ...), custom_call_target="tpu_custom_call" | custom-call | flops 1 | bytes 1 | tf_op jit(solution)/shard_map/feedforward/pallas_call | solution.py:237
  334.6 4.6 add_convert_fusion.4
  339.2 3.2 fusion.36
  345.2 3.3 collective-permute-start.29
  348.5 28.7 %feedforward.7 = (bf16[4,384,768]{2,1,0:T(8,128)(2,1)}, bf16[4,384,768]{2,1,0:T(8,128)(2,1)}, bf16[4,384,768]{2,1,0:T(8,128)(2,1)}, bf16[4,384,768]{2,1,0:T(8,12...) custom-call(bf16[512,1536]{1,0:T(8,128)(2,1)} %copy-done.12, bf16[512,1536]{1,0:T(8,128)(2,1)} %copy-done.7, ...), custom_call_target="tpu_custom_call" | custom-call | flops 1 | bytes 1 | tf_op jit(solution)/shard_map/feedforward/pallas_call | solution.py:237
  378.8 2.2 multiply_reduce_fusion.2
  381.0 7.3 %multiply_reduce_fusion = (f32[1536]{0:T(1024)S(1)}, f32[512]{0:T(512)S(1)}, f32[512,1536]{1,0:T(8,128)S(1)}, f32[512,1536]{1,0:T(8,128)}) fusion(f32[512,1536]{1,0:T(8,128)S(1)} %copy-done.4, f32[512]{0:T(512)S(1)} %add_rsqrt_fusion.1, f32[1536]{0:T(1024)S(1)} %maximum_select_fusion.17, f32[512,1536]{1,0:T(8,128)} %get-tuple-element.446, ...), kind=kLoop, calls=%fused_computation.35 | loop fusion | flops 8648704 | bytes 23609344 | tf_op jit(solution)/shard_map/reduce_sum | solution.py:329
  388.4 2.4 fusion.68
  391.8 4.6 add_convert_fusion.3
  396.4 3.2 fusion.38
  399.6 2.4 add_convert_fusion
  402.6 25.1 %collective-permute-done.32 = bf16[512,1536]{1,0:T(8,128)(2,1)} collective-permute-done((bf16[512,1536]{1,0:T(8,128)(2,1)S(1)}, bf16[512,1536]{1,0:T(8,128)(2,1)}, u32[]{:S(2)}, u32[]{:S(2)}) %collective-permute-start.32) | collective-permute-done | bytes 1572896 | tf_op jit(solution)/shard_map/ppermute | solution.py:362
  427.7 5.5 convolution_convert_fusion
  434.6 2.1 collective-permute-start.34
  438.4 5.4 convolution_convert_fusion.4.do_ref
  443.9 15.2 %attention_backward.2 = bf16[1024,768]{1,0:T(8,128)(2,1)S(1)} custom-call(bf16[1024,2048]{1,0:T(8,128)(2,1)} %get-tuple-element.320.qkv_ref, bf16[1024,1024]{1,0:T(8,128)(2,1)S(1)} %convolution_convert_fusion.4.do_ref, bf16[512,384]{1,0:T(8,128)(2,1)S(1)} %fusion.33.gather_ref, f32[1024,128]{1,0:T(8,128)S(1)} %get-tuple-element.310.cos_ref, ...), custom_call_target="tpu_custom_call" | custom-call | flops 1 | bytes 1 | tf_op jit(solution)/shard_map/attention_backward/pallas_call | solution.py:153
  459.1 4.5 fusion.42
  463.7 13.0 %collective-permute-done.34 = bf16[384,768]{1,0:T(8,128)(2,1)S(1)} collective-permute-done((bf16[384,768]{1,0:T(8,128)(2,1)}, bf16[384,768]{1,0:T(8,128)(2,1)S(1)}, u32[]{:S(2)}, u32[]{:S(2)}) %collective-permute-start.34) | collective-permute-done | bytes 589856 | tf_op jit(solution)/shard_map/ppermute | solution.py:375
  476.8 2.0 collective-permute-start.39
  478.8 3.1 convolution_convert_fusion.2
  486.7 15.1 %attention_backward.3 = bf16[1024,768]{1,0:T(8,128)(2,1)S(1)} custom-call(bf16[1024,2048]{1,0:T(8,128)(2,1)} %get-tuple-element.320.qkv_ref, bf16[1024,1024]{1,0:T(8,128)(2,1)S(1)} %convolution_convert_fusion.4.do_ref, bf16[512,384]{1,0:T(8,128)(2,1)S(1)} %fusion.33.gather_ref, f32[1024,128]{1,0:T(8,128)S(1)} %get-tuple-element.310.cos_ref, ...), custom_call_target="tpu_custom_call" | custom-call | flops 1 | bytes 1 | tf_op jit(solution)/shard_map/attention_backward/pallas_call | solution.py:153
  501.8 4.8 collective-permute-done.39
  507.5 3.2 convolution_convert_fusion.1
  513.7 2.6 fusion.11
  516.2 2.7 add_convert_fusion.6
  522.8 3.5 fusion.12
  533.4 14.1 %collective-permute-done.47 = bf16[384,768]{1,0:T(8,128)(2,1)S(1)} collective-permute-done((bf16[384,768]{1,0:T(8,128)(2,1)}, bf16[384,768]{1,0:T(8,128)(2,1)S(1)}, u32[]{:S(2)}, u32[]{:S(2)}) %collective-permute-start.47) | collective-permute-done | bytes 589856 | tf_op jit(solution)/shard_map/ppermute | solution.py:375
  548.3 23.0 %collective-permute-done.45 = bf16[512,1536]{1,0:T(8,128)(2,1)S(1)} collective-permute-done((bf16[512,1536]{1,0:T(8,128)(2,1)S(1)}, bf16[512,1536]{1,0:T(8,128)(2,1)S(1)}, u32[]{:S(2)}, u32[]{:S(2)}) %collective-permute-start.45) | collective-permute-done | bytes 1572896 | tf_op jit(solution)/shard_map/ppermute | solution.py:362
  580.7 8.4 %collective-permute-done.48 = bf16[384,384]{1,0:T(8,128)(2,1)S(1)} collective-permute-done((bf16[384,384]{1,0:T(8,128)(2,1)S(1)}, bf16[384,384]{1,0:T(8,128)(2,1)S(1)}, u32[]{:S(2)}, u32[]{:S(2)}) %collective-permute-start.48) | collective-permute-done | bytes 294944 | tf_op jit(solution)/shard_map/ppermute | solution.py:375
  592.7 12.5 %collective-permute-done.49 = bf16[384,384]{1,0:T(8,128)(2,1)S(1)} collective-permute-done((bf16[384,384]{1,0:T(8,128)(2,1)S(1)}, bf16[384,384]{1,0:T(8,128)(2,1)S(1)}, u32[]{:S(2)}, u32[]{:S(2)}) %collective-permute-start.49) | collective-permute-done | bytes 294944 | tf_op jit(solution)/shard_map/ppermute | solution.py:375
  607.2 2.0 collective-permute-start.54
  616.2 2.3 collective-permute-start.59
  622.3 2.1 collective-permute-done.62
  625.5 3.5 collective-permute-done.63
  629.1 6.8 %place.1 = (f32[12288,128]{1,0:T(8,128)}, f32[1024,768]{1,0:T(8,128)}) custom-call(bf16[2,2,384,768]{3,2,1,0:T(8,128)(2,1)S(1)} %maximum_select_fusion.4.refs_0_, bf16[2,2,384,768]{3,2,1,0:T(8,128)(2,1)S(1)} %maximum_select_fusion.5.refs_1_), custom_call_target="tpu_custom_call" | custom-call | flops 1 | bytes 1 | tf_op jit(solution)/shard_map/place/pallas_call | solution.py:271
  640.3 2.0 place_attention.1
  (341 shorter events, 118.9 us)
Async XLA Ops:
  5.8 20.8 %collective-permute-start.2 = (bf16[576,384]{1,0:T(8,128)(2,1)}, bf16[576,384]{1,0:T(8,128)(2,1)}, u32[]{:S(2)}, u32[]{:S(2)}) collective-permute-start(bf16[576,384]{1,0:T(8,128)(2,1)} %pad_maximum_fusion.18), channel_id=1, source_target_pairs={{0,3},{1,0},{2,1},{3,2},{4,7},{5,4},{6,5},{7,6},{8,11},{9,8},{10,9... | collective-permute-start | bytes 1327112 | tf_op jit(solution)/shard_map/ppermute | solution.py:375
  10.9 21.4 %collective-permute-start = (bf16[576,384]{1,0:T(8,128)(2,1)}, bf16[576,384]{1,0:T(8,128)(2,1)}, u32[]{:S(2)}, u32[]{:S(2)}) collective-permute-start(bf16[576,384]{1,0:T(8,128)(2,1)} %pad_maximum_fusion.18), channel_id=1, source_target_pairs={{0,1},{1,2},{2,3},{3,0},{4,5},{5,6},{6,7},{7,4},{8,9},{9,10},{10,1... | collective-permute-start | bytes 1327112 | tf_op jit(solution)/shard_map/ppermute | solution.py:375
  10.9 21.4 %collective-permute-start.3 = (bf16[576,384]{1,0:T(8,128)(2,1)}, bf16[576,384]{1,0:T(8,128)(2,1)}, u32[]{:S(2)}, u32[]{:S(2)}) collective-permute-start(bf16[576,384]{1,0:T(8,128)(2,1)} %pad_maximum_fusion.17), channel_id=1, source_target_pairs={{0,4},{4,0},{1,5},{5,1},{2,6},{6,2},{3,7},{7,3},{8,12},{12,8},{9,1... | collective-permute-start | bytes 1327112 | tf_op jit(solution)/shard_map/ppermute | solution.py:375
  12.4 36.6 %collective-permute-start.1 = (bf16[576,384]{1,0:T(8,128)(2,1)}, bf16[576,384]{1,0:T(8,128)(2,1)}, u32[]{:S(2)}, u32[]{:S(2)}) collective-permute-start(bf16[576,384]{1,0:T(8,128)(2,1)} %pad_maximum_fusion.17), channel_id=1, source_target_pairs={{0,2},{1,3},{2,0},{3,1},{4,6},{5,7},{6,4},{7,5},{8,10},{9,11},{10,... | collective-permute-start | bytes 1327112 | tf_op jit(solution)/shard_map/ppermute | solution.py:375
  19.3 29.7 %collective-permute-start.4 = (bf16[2,384,768]{2,1,0:T(8,128)(2,1)}, bf16[2,384,768]{2,1,0:T(8,128)(2,1)}, u32[]{:S(2)}, u32[]{:S(2)}) collective-permute-start(bf16[2,384,768]{2,1,0:T(8,128)(2,1)} %pad_maximum_fusion.11), channel_id=1, source_target_pairs={{0,4},{4,0},{1,5},{5,1},{2,6},{6,2},{3,7},{7,3},{8,12},{12,8},{9,1... | collective-permute-start | bytes 3538952 | tf_op jit(solution)/shard_map/ppermute | solution.py:375
  50.7 49.6 %collective-permute-start.9 = (bf16[4,576,384]{2,1,0:T(8,128)(2,1)S(1)}, bf16[4,576,384]{2,1,0:T(8,128)(2,1)S(1)}, u32[]{:S(2)}, u32[]{:S(2)}) collective-permute-start(bf16[4,576,384]{2,1,0:T(8,128)(2,1)S(1)} %pad_maximum_fusion.6), channel_id=1, source_target_pairs={{0,8},{8,0},{16,24},{24,16},{1,9},{9,1},{17,25},{25,17},{2,10},{10... | collective-permute-start | bytes 5308424 | tf_op jit(solution)/shard_map/ppermute | solution.py:362
  50.8 49.4 %collective-permute-start.6 = (bf16[512,1536]{1,0:T(8,128)(2,1)S(1)}, bf16[512,1536]{1,0:T(8,128)(2,1)S(1)}, u32[]{:S(2)}, u32[]{:S(2)}) collective-permute-start(bf16[512,1536]{1,0:T(8,128)(2,1)S(1)} %fusion.2), channel_id=1, source_target_pairs={{0,1},{1,0},{2,3},{3,2},{4,5},{5,4},{6,7},{7,6},{8,9},{9,8},{10,11... | collective-permute-start | bytes 4718600 | tf_op jit(solution)/shard_map/ppermute | solution.py:362
  51.5 48.8 %collective-permute-start.7 = (bf16[512,1536]{1,0:T(8,128)(2,1)S(1)}, bf16[512,1536]{1,0:T(8,128)(2,1)S(1)}, u32[]{:S(2)}, u32[]{:S(2)}) collective-permute-start(bf16[512,1536]{1,0:T(8,128)(2,1)S(1)} %maximum_select_fusion.7.cot_ref), channel_id=1, source_target_pairs={{0,16},{8,24},{16,0},{24,8},{1,17},{9,25},{17,1},{25,9},{2,18},{10... | collective-permute-start | bytes 4718600 | tf_op jit(solution)/shard_map/ppermute | solution.py:362
  54.5 43.9 %collective-permute-start.5 = (bf16[3,576,384]{2,1,0:T(8,128)(2,1)S(1)}, bf16[3,576,384]{2,1,0:T(8,128)(2,1)S(1)}, u32[]{:S(2)}, u32[]{:S(2)}) collective-permute-start(bf16[3,576,384]{2,1,0:T(8,128)(2,1)S(1)} %pad_maximum_fusion.9), channel_id=1, source_target_pairs={{0,4},{4,0},{1,5},{5,1},{2,6},{6,2},{3,7},{7,3},{8,12},{12,8},{9,1... | collective-permute-start | bytes 3981320 | tf_op jit(solution)/shard_map/ppermute | solution.py:375
  55.5 42.9 %collective-permute-start.8 = (bf16[384,768]{1,0:T(8,128)(2,1)S(1)}, bf16[384,768]{1,0:T(8,128)(2,1)S(1)}, u32[]{:S(2)}, u32[]{:S(2)}) collective-permute-start(bf16[384,768]{1,0:T(8,128)(2,1)S(1)} %copy-done.44), channel_id=1, source_target_pairs={{0,2},{1,3},{2,0},{3,1},{4,6},{5,7},{6,4},{7,5},{8,10},{9,11},{10,... | collective-permute-start | bytes 1769480 | tf_op jit(solution)/shard_map/ppermute | solution.py:375
  105.1 11.8 %collective-permute-start.10 = (bf16[4,576,384]{2,1,0:T(8,128)(2,1)}, bf16[4,576,384]{2,1,0:T(8,128)(2,1)}, u32[]{:S(2)}, u32[]{:S(2)}) collective-permute-start(bf16[4,576,384]{2,1,0:T(8,128)(2,1)} %pad_maximum_fusion.7), channel_id=1, source_target_pairs={{0,8},{8,0},{16,24},{24,16},{1,9},{9,1},{17,25},{25,17},{2,10},{10... | collective-permute-start | bytes 5308424 | tf_op jit(solution)/shard_map/ppermute | solution.py:362
  105.1 49.7 %collective-permute-start.12 = (bf16[384,768]{1,0:T(8,128)(2,1)}, bf16[384,768]{1,0:T(8,128)(2,1)}, u32[]{:S(2)}, u32[]{:S(2)}) collective-permute-start(bf16[384,768]{1,0:T(8,128)(2,1)} %get-tuple-element.314), channel_id=1, source_target_pairs={{0,3},{1,0},{2,1},{3,2},{4,7},{5,4},{6,5},{7,6},{8,11},{9,8},{10,9... | collective-permute-start | bytes 1769480 | tf_op jit(solution)/shard_map/ppermute | solution.py:375
  107.8 47.0 %collective-permute-start.11 = (bf16[384,768]{1,0:T(8,128)(2,1)}, bf16[384,768]{1,0:T(8,128)(2,1)}, u32[]{:S(2)}, u32[]{:S(2)}) collective-permute-start(bf16[384,768]{1,0:T(8,128)(2,1)} %get-tuple-element.314), channel_id=1, source_target_pairs={{0,1},{1,2},{2,3},{3,0},{4,5},{5,6},{6,7},{7,4},{8,9},{9,10},{10,1... | collective-permute-start | bytes 1769480 | tf_op jit(solution)/shard_map/ppermute | solution.py:375
  107.8 47.0 %collective-permute-start.13 = (bf16[384,768]{1,0:T(8,128)(2,1)}, bf16[384,768]{1,0:T(8,128)(2,1)}, u32[]{:S(2)}, u32[]{:S(2)}) collective-permute-start(bf16[384,768]{1,0:T(8,128)(2,1)} %get-tuple-element.355), channel_id=1, source_target_pairs={{0,1},{1,2},{2,3},{3,0},{4,5},{5,6},{6,7},{7,4},{8,9},{9,10},{10,1... | collective-permute-start | bytes 1769480 | tf_op jit(solution)/shard_map/ppermute | solution.py:375
  161.2 40.5 %collective-permute-start.15 = (bf16[3,384,768]{2,1,0:T(8,128)(2,1)}, bf16[3,384,768]{2,1,0:T(8,128)(2,1)}, u32[]{:S(2)}, u32[]{:S(2)}) collective-permute-start(bf16[3,384,768]{2,1,0:T(8,128)(2,1)} %pad_maximum_fusion.8), channel_id=1, source_target_pairs={{0,4},{4,0},{1,5},{5,1},{2,6},{6,2},{3,7},{7,3},{8,12},{12,8},{9,1... | collective-permute-start | bytes 5308424 | tf_op jit(solution)/shard_map/ppermute | solution.py:375
  162.7 36.0 %collective-permute-start.14 = (bf16[512,1536]{1,0:T(8,128)(2,1)}, bf16[512,1536]{1,0:T(8,128)(2,1)}, u32[]{:S(2)}, u32[]{:S(2)}) collective-permute-start(bf16[512,1536]{1,0:T(8,128)(2,1)} %convolution_convert_fusion.3), channel_id=1, source_target_pairs={{0,1},{1,0},{2,3},{3,2},{4,5},{5,4},{6,7},{7,6},{8,9},{9,8},{10,11... | collective-permute-start | bytes 4718600 | tf_op jit(solution)/shard_map/ppermute | solution.py:362
  213.4 7.2 %collective-permute-start.16 = (bf16[4,384,768]{2,1,0:T(8,128)(2,1)S(1)}, bf16[4,384,768]{2,1,0:T(8,128)(2,1)S(1)}, u32[]{:S(2)}, u32[]{:S(2)}) collective-permute-start(bf16[4,384,768]{2,1,0:T(8,128)(2,1)S(1)} %pad_maximum_fusion.2.refs_0_), channel_id=1, source_target_pairs={{0,8},{8,0},{16,24},{24,16},{1,9},{9,1},{17,25},{25,17},{2,10},{10... | collective-permute-start | bytes 7077896 | tf_op jit(solution)/shard_map/ppermute | solution.py:362
  213.4 12.0 %collective-permute-start.17 = (bf16[4,384,768]{2,1,0:T(8,128)(2,1)S(1)}, bf16[4,384,768]{2,1,0:T(8,128)(2,1)}, u32[]{:S(2)}, u32[]{:S(2)}) collective-permute-start(bf16[4,384,768]{2,1,0:T(8,128)(2,1)S(1)} %pad_maximum_fusion.3.refs_1_), channel_id=1, source_target_pairs={{0,8},{8,0},{16,24},{24,16},{1,9},{9,1},{17,25},{25,17},{2,10},{10... | collective-permute-start | bytes 7077896 | tf_op jit(solution)/shard_map/ppermute | solution.py:362
  214.0 44.9 %collective-permute-start.21 = (bf16[512,1536]{1,0:T(8,128)(2,1)S(1)}, bf16[512,1536]{1,0:T(8,128)(2,1)}, u32[]{:S(2)}, u32[]{:S(2)}) collective-permute-start(bf16[512,1536]{1,0:T(8,128)(2,1)S(1)} %multiply_convert_fusion.n2_ref), channel_id=1, source_target_pairs={{0,16},{8,24},{16,0},{24,8},{1,17},{9,25},{17,1},{25,9},{2,18},{10... | collective-permute-start | bytes 4718600 | tf_op jit(solution)/shard_map/ppermute | solution.py:362
  215.5 37.0 %collective-permute-start.18 = (bf16[384,768]{1,0:T(8,128)(2,1)}, bf16[384,768]{1,0:T(8,128)(2,1)}, u32[]{:S(2)}, u32[]{:S(2)}) collective-permute-start(bf16[384,768]{1,0:T(8,128)(2,1)} %collective-permute-done.13), channel_id=1, source_target_pairs={{0,4},{4,0},{1,5},{5,1},{2,6},{6,2},{3,7},{7,3},{8,12},{12,8},{9,1... | collective-permute-start | bytes 1769480 | tf_op jit(solution)/shard_map/ppermute | solution.py:375
  217.0 35.5 %collective-permute-start.20 = (bf16[384,768]{1,0:T(8,128)(2,1)}, bf16[384,768]{1,0:T(8,128)(2,1)}, u32[]{:S(2)}, u32[]{:S(2)}) collective-permute-start(bf16[384,768]{1,0:T(8,128)(2,1)} %get-tuple-element.355), channel_id=1, source_target_pairs={{0,3},{1,0},{2,1},{3,2},{4,7},{5,4},{6,5},{7,6},{8,11},{9,8},{10,9... | collective-permute-start | bytes 1769480 | tf_op jit(solution)/shard_map/ppermute | solution.py:375
  222.1 36.8 %collective-permute-start.19 = (bf16[384,768]{1,0:T(8,128)(2,1)}, bf16[384,768]{1,0:T(8,128)(2,1)}, u32[]{:S(2)}, u32[]{:S(2)}) collective-permute-start(bf16[384,768]{1,0:T(8,128)(2,1)} %get-tuple-element.355), channel_id=1, source_target_pairs={{0,2},{1,3},{2,0},{3,1},{4,6},{5,7},{6,4},{7,5},{8,10},{9,11},{10,... | collective-permute-start | bytes 1769480 | tf_op jit(solution)/shard_map/ppermute | solution.py:375
  263.4 29.3 %collective-permute-start.23 = (bf16[4,384,768]{2,1,0:T(8,128)(2,1)}, bf16[4,384,768]{2,1,0:T(8,128)(2,1)}, u32[]{:S(2)}, u32[]{:S(2)}) collective-permute-start(bf16[4,384,768]{2,1,0:T(8,128)(2,1)} %pad_maximum_fusion.4.refs_0_), channel_id=1, source_target_pairs={{0,8},{8,0},{16,24},{24,16},{1,9},{9,1},{17,25},{25,17},{2,10},{10... | collective-permute-start | bytes 7077896 | tf_op jit(solution)/shard_map/ppermute | solution.py:362
  263.4 29.3 %collective-permute-start.22 = (bf16[2,384,768]{2,1,0:T(8,128)(2,1)S(1)}, bf16[2,384,768]{2,1,0:T(8,128)(2,1)}, u32[]{:S(2)}, u32[]{:S(2)}) collective-permute-start(bf16[2,384,768]{2,1,0:T(8,128)(2,1)S(1)} %pad_maximum_fusion.12), channel_id=1, source_target_pairs={{0,4},{4,0},{1,5},{5,1},{2,6},{6,2},{3,7},{7,3},{8,12},{12,8},{9,1... | collective-permute-start | bytes 3538952 | tf_op jit(solution)/shard_map/ppermute | solution.py:375
  296.0 4.5 collective-permute-start.25
  297.4 6.7 %collective-permute-start.24 = (bf16[4,384,768]{2,1,0:T(8,128)(2,1)S(1)}, bf16[4,384,768]{2,1,0:T(8,128)(2,1)}, u32[]{:S(2)}, u32[]{:S(2)}) collective-permute-start(bf16[4,384,768]{2,1,0:T(8,128)(2,1)S(1)} %pad_maximum_fusion.5.refs_1_), channel_id=1, source_target_pairs={{0,8},{8,0},{16,24},{24,16},{1,9},{9,1},{17,25},{25,17},{2,10},{10... | collective-permute-start | bytes 7077896 | tf_op jit(solution)/shard_map/ppermute | solution.py:362
  304.6 30.0 %collective-permute-start.27 = (bf16[4,384,768]{2,1,0:T(8,128)(2,1)}, bf16[4,384,768]{2,1,0:T(8,128)(2,1)}, u32[]{:S(2)}, u32[]{:S(2)}) collective-permute-start(bf16[4,384,768]{2,1,0:T(8,128)(2,1)} %get-tuple-element.410), channel_id=1, source_target_pairs={{0,8},{8,0},{16,24},{24,16},{1,9},{9,1},{17,25},{25,17},{2,10},{10... | collective-permute-start | bytes 7077896 | tf_op jit(solution)/shard_map/ppermute | solution.py:362
  306.1 28.5 %collective-permute-start.26 = (bf16[2,384,768]{2,1,0:T(8,128)(2,1)S(1)}, bf16[2,384,768]{2,1,0:T(8,128)(2,1)}, u32[]{:S(2)}, u32[]{:S(2)}) collective-permute-start(bf16[2,384,768]{2,1,0:T(8,128)(2,1)S(1)} %slice.304), channel_id=1, source_target_pairs={{0,4},{4,0},{1,5},{5,1},{2,6},{6,2},{3,7},{7,3},{8,12},{12,8},{9,1... | collective-permute-start | bytes 3538952 | tf_op jit(solution)/shard_map/ppermute | solution.py:375
  342.4 36.5 %collective-permute-start.30 = (bf16[512,1536]{1,0:T(8,128)(2,1)}, bf16[512,1536]{1,0:T(8,128)(2,1)S(1)}, u32[]{:S(2)}, u32[]{:S(2)}) collective-permute-start(bf16[512,1536]{1,0:T(8,128)(2,1)} %add_convert_fusion.4), channel_id=1, source_target_pairs={{0,16},{8,24},{16,0},{24,8},{1,17},{9,25},{17,1},{25,9},{2,18},{10... | collective-permute-start | bytes 4718600 | tf_op jit(solution)/shard_map/ppermute | solution.py:362
  344.0 33.2 %collective-permute-start.28 = (bf16[2,384,768]{2,1,0:T(8,128)(2,1)}, bf16[2,384,768]{2,1,0:T(8,128)(2,1)}, u32[]{:S(2)}, u32[]{:S(2)}) collective-permute-start(bf16[2,384,768]{2,1,0:T(8,128)(2,1)} %slice.311), channel_id=1, source_target_pairs={{0,4},{4,0},{1,5},{5,1},{2,6},{6,2},{3,7},{7,3},{8,12},{12,8},{9,1... | collective-permute-start | bytes 3538952 | tf_op jit(solution)/shard_map/ppermute | solution.py:375
  345.2 32.0 %collective-permute-start.29 = (bf16[384,768]{1,0:T(8,128)(2,1)}, bf16[384,768]{1,0:T(8,128)(2,1)}, u32[]{:S(2)}, u32[]{:S(2)}) collective-permute-start(bf16[384,768]{1,0:T(8,128)(2,1)} %get-tuple-element.440), channel_id=1, source_target_pairs={{0,3},{1,0},{2,1},{3,2},{4,7},{5,4},{6,5},{7,6},{8,11},{9,8},{10,9... | collective-permute-start | bytes 1769480 | tf_op jit(solution)/shard_map/ppermute | solution.py:375
  378.8 12.0 %collective-permute-start.31 = (bf16[4,384,768]{2,1,0:T(8,128)(2,1)}, bf16[4,384,768]{2,1,0:T(8,128)(2,1)}, u32[]{:S(2)}, u32[]{:S(2)}) collective-permute-start(bf16[4,384,768]{2,1,0:T(8,128)(2,1)} %get-tuple-element.442), channel_id=1, source_target_pairs={{0,8},{8,0},{16,24},{24,16},{1,9},{9,1},{17,25},{25,17},{2,10},{10... | collective-permute-start | bytes 7077896 | tf_op jit(solution)/shard_map/ppermute | solution.py:362
  390.8 36.9 %collective-permute-start.33 = (bf16[4,384,768]{2,1,0:T(8,128)(2,1)}, bf16[4,384,768]{2,1,0:T(8,128)(2,1)}, u32[]{:S(2)}, u32[]{:S(2)}) collective-permute-start(bf16[4,384,768]{2,1,0:T(8,128)(2,1)} %get-tuple-element.451), channel_id=1, source_target_pairs={{0,8},{8,0},{16,24},{24,16},{1,9},{9,1},{17,25},{25,17},{2,10},{10... | collective-permute-start | bytes 7077896 | tf_op jit(solution)/shard_map/ppermute | solution.py:362
  391.3 36.4 %collective-permute-start.32 = (bf16[512,1536]{1,0:T(8,128)(2,1)S(1)}, bf16[512,1536]{1,0:T(8,128)(2,1)}, u32[]{:S(2)}, u32[]{:S(2)}) collective-permute-start(bf16[512,1536]{1,0:T(8,128)(2,1)S(1)} %get-tuple-element.461), channel_id=1, source_target_pairs={{0,1},{1,0},{2,3},{3,2},{4,5},{5,4},{6,7},{7,6},{8,9},{9,8},{10,11... | collective-permute-start | bytes 4718600 | tf_op jit(solution)/shard_map/ppermute | solution.py:362
  401.9 57.2 %collective-permute-start.37 = (bf16[4,384,768]{2,1,0:T(8,128)(2,1)S(1)}, bf16[4,384,768]{2,1,0:T(8,128)(2,1)}, u32[]{:S(2)}, u32[]{:S(2)}) collective-permute-start(bf16[4,384,768]{2,1,0:T(8,128)(2,1)S(1)} %add_convert_fusion), channel_id=1, source_target_pairs={{0,4},{4,0},{1,5},{5,1},{2,6},{6,2},{3,7},{7,3},{8,12},{12,8},{9,1... | collective-permute-start | bytes 7077896 | tf_op jit(solution)/shard_map/ppermute | solution.py:375
  434.6 42.1 %collective-permute-start.36 = (bf16[4,96,1536]{2,1,0:T(8,128)(2,1)}, bf16[4,96,1536]{2,1,0:T(8,128)(2,1)}, u32[]{:S(2)}, u32[]{:S(2)}) collective-permute-start(bf16[4,96,1536]{2,1,0:T(8,128)(2,1)} %get-tuple-element.605), channel_id=1, source_target_pairs={{0,8},{8,0},{16,24},{24,16},{1,9},{9,1},{17,25},{25,17},{2,10},{10... | collective-permute-start | bytes 3538952 | tf_op jit(solution)/shard_map/ppermute | solution.py:362
  434.6 42.1 %collective-permute-start.34 = (bf16[384,768]{1,0:T(8,128)(2,1)}, bf16[384,768]{1,0:T(8,128)(2,1)S(1)}, u32[]{:S(2)}, u32[]{:S(2)}) collective-permute-start(bf16[384,768]{1,0:T(8,128)(2,1)} %get-tuple-element.466), channel_id=1, source_target_pairs={{0,2},{1,3},{2,0},{3,1},{4,6},{5,7},{6,4},{7,5},{8,10},{9,11},{10,... | collective-permute-start | bytes 1769480 | tf_op jit(solution)/shard_map/ppermute | solution.py:375
  436.7 40.0 %collective-permute-start.35 = (bf16[384,768]{1,0:T(8,128)(2,1)}, bf16[384,768]{1,0:T(8,128)(2,1)}, u32[]{:S(2)}, u32[]{:S(2)}) collective-permute-start(bf16[384,768]{1,0:T(8,128)(2,1)} %get-tuple-element.467), channel_id=1, source_target_pairs={{0,1},{1,2},{2,3},{3,0},{4,5},{5,6},{6,7},{7,4},{8,9},{9,10},{10,1... | collective-permute-start | bytes 1769480 | tf_op jit(solution)/shard_map/ppermute | solution.py:375
  476.7 25.0 %collective-permute-start.38 = (bf16[384,768]{1,0:T(8,128)(2,1)}, bf16[384,768]{1,0:T(8,128)(2,1)}, u32[]{:S(2)}, u32[]{:S(2)}) collective-permute-start(bf16[384,768]{1,0:T(8,128)(2,1)} %get-tuple-element.475), channel_id=1, source_target_pairs={{0,3},{1,0},{2,1},{3,2},{4,7},{5,4},{6,5},{7,6},{8,11},{9,8},{10,9... | collective-permute-start | bytes 1769480 | tf_op jit(solution)/shard_map/ppermute | solution.py:375
  476.8 29.8 %collective-permute-start.39 = (bf16[384,768]{1,0:T(8,128)(2,1)}, bf16[384,768]{1,0:T(8,128)(2,1)}, u32[]{:S(2)}, u32[]{:S(2)}) collective-permute-start(bf16[384,768]{1,0:T(8,128)(2,1)} %get-tuple-element.477), channel_id=1, source_target_pairs={{0,1},{1,2},{2,3},{3,0},{4,5},{5,6},{6,7},{7,4},{8,9},{9,10},{10,1... | collective-permute-start | bytes 1769480 | tf_op jit(solution)/shard_map/ppermute | solution.py:375
  483.5 23.1 %collective-permute-start.40 = (bf16[2,384,768]{2,1,0:T(8,128)(2,1)}, bf16[2,384,768]{2,1,0:T(8,128)(2,1)}, u32[]{:S(2)}, u32[]{:S(2)}) collective-permute-start(bf16[2,384,768]{2,1,0:T(8,128)(2,1)} %get-tuple-element.604), channel_id=1, source_target_pairs={{0,8},{8,0},{16,24},{24,16},{1,9},{9,1},{17,25},{25,17},{2,10},{10... | collective-permute-start | bytes 3538952 | tf_op jit(solution)/shard_map/ppermute | solution.py:362
  486.0 20.6 %collective-permute-start.41 = (bf16[4,96,768]{2,1,0:T(8,128)(2,1)S(1)}, bf16[4,96,768]{2,1,0:T(8,128)(2,1)S(1)}, u32[]{:S(2)}, u32[]{:S(2)}) collective-permute-start(bf16[4,96,768]{2,1,0:T(8,128)(2,1)S(1)} %get-tuple-element.626), channel_id=1, source_target_pairs={{0,4},{4,0},{1,5},{5,1},{2,6},{6,2},{3,7},{7,3},{8,12},{12,8},{9,1... | collective-permute-start | bytes 1769480 | tf_op jit(solution)/shard_map/ppermute | solution.py:375
  519.9 8.2 %collective-permute-start.42 = (bf16[2,384,768]{2,1,0:T(8,128)(2,1)}, bf16[2,384,768]{2,1,0:T(8,128)(2,1)}, u32[]{:S(2)}, u32[]{:S(2)}) collective-permute-start(bf16[2,384,768]{2,1,0:T(8,128)(2,1)} %get-tuple-element.495), channel_id=1, source_target_pairs={{0,8},{8,0},{16,24},{24,16},{1,9},{9,1},{17,25},{25,17},{2,10},{10... | collective-permute-start | bytes 3538952 | tf_op jit(solution)/shard_map/ppermute | solution.py:362
  519.9 27.5 %collective-permute-start.47 = (bf16[384,768]{1,0:T(8,128)(2,1)}, bf16[384,768]{1,0:T(8,128)(2,1)S(1)}, u32[]{:S(2)}, u32[]{:S(2)}) collective-permute-start(bf16[384,768]{1,0:T(8,128)(2,1)} %get-tuple-element.509), channel_id=1, source_target_pairs={{0,2},{1,3},{2,0},{3,1},{4,6},{5,7},{6,4},{7,5},{8,10},{9,11},{10,... | collective-permute-start | bytes 1769480 | tf_op jit(solution)/shard_map/ppermute | solution.py:375
  521.5 26.8 %collective-permute-start.44 = (bf16[384,768]{1,0:T(8,128)(2,1)S(1)}, bf16[384,768]{1,0:T(8,128)(2,1)S(1)}, u32[]{:S(2)}, u32[]{:S(2)}) collective-permute-start(bf16[384,768]{1,0:T(8,128)(2,1)S(1)} %get-tuple-element.622), channel_id=1, source_target_pairs={{0,4},{4,0},{1,5},{5,1},{2,6},{6,2},{3,7},{7,3},{8,12},{12,8},{9,1... | collective-permute-start | bytes 1769480 | tf_op jit(solution)/shard_map/ppermute | solution.py:375
  522.2 49.1 %collective-permute-start.45 = (bf16[512,1536]{1,0:T(8,128)(2,1)S(1)}, bf16[512,1536]{1,0:T(8,128)(2,1)S(1)}, u32[]{:S(2)}, u32[]{:S(2)}) collective-permute-start(bf16[512,1536]{1,0:T(8,128)(2,1)S(1)} %copy-done.55), channel_id=1, source_target_pairs={{0,1},{1,0},{2,3},{3,2},{4,5},{5,4},{6,7},{7,6},{8,9},{9,8},{10,11... | collective-permute-start | bytes 4718600 | tf_op jit(solution)/shard_map/ppermute | solution.py:362
  529.8 41.5 %collective-permute-start.43 = (bf16[384,768]{1,0:T(8,128)(2,1)S(1)}, bf16[384,768]{1,0:T(8,128)(2,1)S(1)}, u32[]{:S(2)}, u32[]{:S(2)}) collective-permute-start(bf16[384,768]{1,0:T(8,128)(2,1)S(1)} %get-tuple-element.624), channel_id=1, source_target_pairs={{0,4},{4,0},{1,5},{5,1},{2,6},{6,2},{3,7},{7,3},{8,12},{12,8},{9,1... | collective-permute-start | bytes 1769480 | tf_op jit(solution)/shard_map/ppermute | solution.py:375
  531.0 40.2 %collective-permute-start.46 = (bf16[384,768]{1,0:T(8,128)(2,1)S(1)}, bf16[384,768]{1,0:T(8,128)(2,1)S(1)}, u32[]{:S(2)}, u32[]{:S(2)}) collective-permute-start(bf16[384,768]{1,0:T(8,128)(2,1)S(1)} %add_convert_fusion.12), channel_id=1, source_target_pairs={{0,16},{8,24},{16,0},{24,8},{1,17},{9,25},{17,1},{25,9},{2,18},{10... | collective-permute-start | bytes 1769480 | tf_op jit(solution)/shard_map/ppermute | solution.py:362
  547.4 66.9 %collective-permute-start.58 = (bf16[512,1536]{1,0:T(8,128)(2,1)S(1)}, bf16[512,1536]{1,0:T(8,128)(2,1)S(1)}, u32[]{:S(2)}, u32[]{:S(2)}) collective-permute-start(bf16[512,1536]{1,0:T(8,128)(2,1)S(1)} %copy-done.43), channel_id=1, source_target_pairs={{0,16},{8,24},{16,0},{24,8},{1,17},{9,25},{17,1},{25,9},{2,18},{10... | collective-permute-start | bytes 4718600 | tf_op jit(solution)/shard_map/ppermute | solution.py:362
  575.1 14.0 %collective-permute-start.48 = (bf16[384,384]{1,0:T(8,128)(2,1)S(1)}, bf16[384,384]{1,0:T(8,128)(2,1)S(1)}, u32[]{:S(2)}, u32[]{:S(2)}) collective-permute-start(bf16[384,384]{1,0:T(8,128)(2,1)S(1)} %get-tuple-element.638), channel_id=1, source_target_pairs={{0,3},{1,0},{2,1},{3,2},{4,7},{5,4},{6,5},{7,6},{8,11},{9,8},{10,9... | collective-permute-start | bytes 884744 | tf_op jit(solution)/shard_map/ppermute | solution.py:375
  576.5 14.3 %collective-permute-start.50 = (bf16[384,384]{1,0:T(8,128)(2,1)S(1)}, bf16[384,384]{1,0:T(8,128)(2,1)S(1)}, u32[]{:S(2)}, u32[]{:S(2)}) collective-permute-start(bf16[384,384]{1,0:T(8,128)(2,1)S(1)} %get-tuple-element.636), channel_id=1, source_target_pairs={{0,1},{1,2},{2,3},{3,0},{4,5},{5,6},{6,7},{7,4},{8,9},{9,10},{10,1... | collective-permute-start | bytes 884744 | tf_op jit(solution)/shard_map/ppermute | solution.py:375
  577.3 27.8 %collective-permute-start.52 = (bf16[384,768]{1,0:T(8,128)(2,1)S(1)}, bf16[384,768]{1,0:T(8,128)(2,1)S(1)}, u32[]{:S(2)}, u32[]{:S(2)}) collective-permute-start(bf16[384,768]{1,0:T(8,128)(2,1)S(1)} %add_convert_fusion.9), channel_id=1, source_target_pairs={{0,16},{8,24},{16,0},{24,8},{1,17},{9,25},{17,1},{25,9},{2,18},{10... | collective-permute-start | bytes 1769480 | tf_op jit(solution)/shard_map/ppermute | solution.py:362
  578.0 27.9 %collective-permute-start.51 = (bf16[2,1,384,768]{3,2,1,0:T(8,128)(2,1)S(1)}, bf16[2,1,384,768]{3,2,1,0:T(8,128)(2,1)S(1)}, u32[]{:S(2)}, u32[]{:S(2)}) collective-permute-start(bf16[2,1,384,768]{3,2,1,0:T(8,128)(2,1)S(1)} %maximum_select_fusion.10), channel_id=1, source_target_pairs={{0,8},{8,0},{16,24},{24,16},{1,9},{9,1},{17,25},{25,17},{2,10},{10... | collective-permute-start | bytes 3538952 | tf_op jit(solution)/shard_map/ppermute | solution.py:362
  589.1 16.1 %collective-permute-start.49 = (bf16[384,384]{1,0:T(8,128)(2,1)S(1)}, bf16[384,384]{1,0:T(8,128)(2,1)S(1)}, u32[]{:S(2)}, u32[]{:S(2)}) collective-permute-start(bf16[384,384]{1,0:T(8,128)(2,1)S(1)} %get-tuple-element.637), channel_id=1, source_target_pairs={{0,2},{1,3},{2,0},{3,1},{4,6},{5,7},{6,4},{7,5},{8,10},{9,11},{10,... | collective-permute-start | bytes 884744 | tf_op jit(solution)/shard_map/ppermute | solution.py:375
  590.8 20.2 %collective-permute-start.57 = (bf16[96,768]{1,0:T(8,128)(2,1)S(1)}, bf16[96,768]{1,0:T(8,128)(2,1)S(1)}, u32[]{:S(2)}, u32[]{:S(2)}) collective-permute-start(bf16[96,768]{1,0:T(8,128)(2,1)S(1)} %get-tuple-element.632), channel_id=1, source_target_pairs={{0,1},{1,2},{2,3},{3,0},{4,5},{5,6},{6,7},{7,4},{8,9},{9,10},{10,1... | collective-permute-start | bytes 442376 | tf_op jit(solution)/shard_map/ppermute | solution.py:375
  605.1 7.7 %collective-permute-start.56 = (bf16[96,768]{1,0:T(8,128)(2,1)S(1)}, bf16[96,768]{1,0:T(8,128)(2,1)S(1)}, u32[]{:S(2)}, u32[]{:S(2)}) collective-permute-start(bf16[96,768]{1,0:T(8,128)(2,1)S(1)} %get-tuple-element.633), channel_id=1, source_target_pairs={{0,2},{1,3},{2,0},{3,1},{4,6},{5,7},{6,4},{7,5},{8,10},{9,11},{10,... | collective-permute-start | bytes 442376 | tf_op jit(solution)/shard_map/ppermute | solution.py:375
  605.2 9.2 %collective-permute-start.55 = (bf16[96,768]{1,0:T(8,128)(2,1)S(1)}, bf16[96,768]{1,0:T(8,128)(2,1)S(1)}, u32[]{:S(2)}, u32[]{:S(2)}) collective-permute-start(bf16[96,768]{1,0:T(8,128)(2,1)S(1)} %get-tuple-element.634), channel_id=1, source_target_pairs={{0,3},{1,0},{2,1},{3,2},{4,7},{5,4},{6,5},{7,6},{8,11},{9,8},{10,9... | collective-permute-start | bytes 442376 | tf_op jit(solution)/shard_map/ppermute | solution.py:375
  607.2 3.8 collective-permute-start.54
  614.7 5.9 collective-permute-start.61
  616.2 21.2 %collective-permute-start.59 = (bf16[2,576,384]{2,1,0:T(8,128)(2,1)S(1)}, bf16[2,576,384]{2,1,0:T(8,128)(2,1)S(1)}, u32[]{:S(2)}, u32[]{:S(2)}) collective-permute-start(bf16[2,576,384]{2,1,0:T(8,128)(2,1)S(1)} %maximum_maximum_fusion.1), channel_id=1, source_target_pairs={{0,16},{8,24},{16,0},{24,8},{1,17},{9,25},{17,1},{25,9},{2,18},{10... | collective-permute-start | bytes 2654216 | tf_op jit(solution)/shard_map/ppermute | solution.py:362
  618.5 6.6 %collective-permute-start.60 = (bf16[2,1,384,768]{3,2,1,0:T(8,128)(2,1)S(1)}, bf16[2,1,384,768]{3,2,1,0:T(8,128)(2,1)S(1)}, u32[]{:S(2)}, u32[]{:S(2)}) collective-permute-start(bf16[2,1,384,768]{3,2,1,0:T(8,128)(2,1)S(1)} %maximum_select_fusion.11), channel_id=1, source_target_pairs={{0,8},{8,0},{16,24},{24,16},{1,9},{9,1},{17,25},{25,17},{2,10},{10... | collective-permute-start | bytes 3538952 | tf_op jit(solution)/shard_map/ppermute | solution.py:362
  620.7 3.8 collective-permute-start.62
  624.4 4.7 collective-permute-start.63
  637.7 2.5 collective-permute-start.64
  (61 other events, 693.1 us)

commit v3 on v2

--- a/solution.py
+++ b/solution.py
@@ -252,22 +252,23 @@
 
 
 def place_kernel(*refs):
-    parts, (gate_up_ref, down_ref) = refs[:-2], refs[-2:]
-    sub, block = parts[0].shape[2] // 3, parts[0].shape[3]
-    tiles = 4 * len(parts)
-    for y in range(2):
-        for core in range(2):
-            for k, part in enumerate(parts):
-                tile = (2 * y + core) * len(parts) + k
+    cores, (gate_up_ref, down_ref) = refs[:2], refs[2:]
+    parts, _, rows, block = cores[0].shape
+    sub = rows // 3
+    for core, ref in enumerate(cores):
+        for y in range(2):
+            for k in range(parts):
+                tile = (2 * y + core) * parts + k
                 for half in range(2):
-                    piece = part[y, core, half * sub : (half + 1) * sub].astype(F32)
-                    gate_up_ref[pl.ds(2 * tile + half, block, stride=2 * tiles), :] = piece.T
-                down_ref[tile * sub : (tile + 1) * sub] = part[y, core, 2 * sub :].astype(F32)
-
-
-def place(parts):
-    sub, block = parts[0].shape[2] // 3, parts[0].shape[3]
-    tiles = 4 * len(parts)
+                    piece = ref[k, y, half * sub : (half + 1) * sub].astype(F32)
+                    gate_up_ref[pl.ds(2 * tile + half, block, stride=8 * parts), :] = piece.T
+                down_ref[tile * sub : (tile + 1) * sub] = ref[k, y, 2 * sub :].astype(F32)
+
+
+def place(first, second):
+    parts, _, rows, block = first.shape
+    sub = rows // 3
+    tiles = 4 * parts
     gate_up, down = pl.pallas_call(
         place_kernel,
         out_shape=[
@@ -277,8 +278,37 @@
         compiler_params=pltpu.CompilerParams(vmem_limit_bytes=48 * 1024 * 1024),
         cost_estimate=QUICK,
         name="place",
-    )(*parts)
+    )(first, second)
     return gate_up.reshape(block, tiles, 2, sub).transpose(0, 2, 1, 3).reshape(block, 2, -1), down
+
+
+def combine_kernel(*refs):
+    out_ref = refs[-1]
+    *rows, mine, other = refs[:-1]
+    qkv = sum(r[...].astype(F32) for r in rows).astype(BF)
+    heads = (mine[...].astype(F32) + other[...].astype(F32)).astype(BF)
+    split = qkv.shape[0]
+    for p in range(2):
+        out_ref[p, :split] = qkv[:, p * GROUP : (p + 1) * GROUP]
+        for n in range(2 * split // GROUP):
+            here = slice(split + n * HEAD_DIM, split + (n + 1) * HEAD_DIM)
+            out_ref[p, here] = heads[p, :, n * GROUP : (n + 1) * GROUP]
+
+
+def combine(rows, arrived, heads, heads_arrived):
+    split, block = rows[0].shape[0], heads.shape[2]
+    if block % GROUP:
+        qkv = sum(r.astype(F32) for r in rows + [arrived])
+        heads = heads.astype(F32) + heads_arrived.astype(F32)
+        parts = [jnp.concatenate([qkv[:, p * GROUP : (p + 1) * GROUP], heads[p].reshape(-1, GROUP)]) for p in range(2)]
+        return jnp.stack(parts).astype(BF)
+    return pl.pallas_call(
+        combine_kernel,
+        out_shape=jax.ShapeDtypeStruct((2, split + HEAD_DIM * block // GROUP, GROUP), BF),
+        compiler_params=pltpu.CompilerParams(vmem_limit_bytes=32 * 1024 * 1024),
+        cost_estimate=QUICK,
+        name="combine",
+    )(*rows, arrived, heads, heads_arrived)
 
 
 def place_attention_kernel(*refs):
@@ -316,6 +346,77 @@
         both = jnp.stack([a[:, block // 2 :].reshape(2, HEAD_DIM, block) for a in (first, second)], axis=1)
         projection = both.astype(F32).reshape(-1, block)
     return query, pair.transpose(2, 0, 1), projection
+
+
+def assemble_kernel(groups, core_ref, *refs):
+    pieces, (qkv_ref, projection_ref) = refs[:-2], refs[-2:]
+    first = core_ref[0] == 0
+    blocks = len(pieces) // groups
+    rows = qkv_ref.shape[0] // (2 * blocks)
+    projection_ref[...] = jnp.zeros_like(projection_ref)
+    for i in range(blocks):
+        for k in range(groups // 2):
+            mine, other = pieces[i * groups + 2 * k], pieces[i * groups + 2 * k + 1]
+            for p in range(2):
+                a, b = mine[p], other[p]
+                group = 2 * k + p
+                for core, piece in enumerate((jnp.where(first, a, b), jnp.where(first, b, a))):
+                    start = (2 * i + core) * rows
+                    qkv_ref[start : start + rows, group * GROUP : (group + 1) * GROUP] = piece[:rows]
+                    place = group * 2 * LANES + core * LANES
+                    for n in range(2 * rows // GROUP):
+                        lanes = slice(2 * i * rows + n * GROUP, 2 * i * rows + (n + 1) * GROUP)
+                        head = piece[rows + n * HEAD_DIM : rows + (n + 1) * HEAD_DIM]
+                        projection_ref[place : place + HALF, lanes] = head[:HALF]
+                        projection_ref[place + LANES // 2 : place + LANES // 2 + HALF, lanes] = head[HALF:]
+
+
+def assemble(core, pieces, model):
+    groups = len(pieces[0])
+    flat = [a for row in pieces for a in row]
+    return pl.pallas_call(
+        functools.partial(assemble_kernel, groups),
+        in_specs=[pl.BlockSpec(memory_space=pltpu.SMEM)] + [pl.BlockSpec(memory_space=pltpu.VMEM)] * len(flat),
+        out_shape=[
+            jax.ShapeDtypeStruct((model, groups * GROUP), BF),
+            jax.ShapeDtypeStruct((groups * 2 * LANES, model), BF),
+        ],
+        compiler_params=pltpu.CompilerParams(vmem_limit_bytes=48 * 1024 * 1024),
+        cost_estimate=QUICK,
+        name="assemble",
+    )(core.astype(jnp.int32)[None], *flat)
+
+
+def halves_kernel(gap, core_ref, a_ref, b_ref, out_ref):
+    g = dot_tn(a_ref[...], b_ref[...]).astype(BF)
+    if gap:
+        out_ref[0, 0, :HALF] = g[:HALF]
+        out_ref[0, 0, HALF:] = g[LANES // 2 : LANES // 2 + HALF]
+    else:
+        out_ref[0, 0] = g
+
+
+def gradient_halves(core, a, b, rows, gap=False):
+    tokens, width = a.shape
+    blocks = width // (2 * rows)
+    kept = HEAD_DIM if gap else rows
+    columns = b.shape[1]
+    return pl.pallas_call(
+        functools.partial(halves_kernel, gap),
+        grid_spec=pltpu.PrefetchScalarGridSpec(
+            num_scalar_prefetch=1,
+            grid=(2, blocks),
+            in_specs=[
+                pl.BlockSpec((tokens, rows), lambda h, i, core: (0, 2 * i + (core[0] + h) % 2)),
+                pl.BlockSpec(b.shape, lambda h, i, core: (0, 0)),
+            ],
+            out_specs=pl.BlockSpec((1, 1, kept, columns), lambda h, i, core: (h, i, 0, 0)),
+        ),
+        out_shape=jax.ShapeDtypeStruct((2, blocks, kept, columns), BF),
+        compiler_params=pltpu.CompilerParams(vmem_limit_bytes=48 * 1024 * 1024),
+        cost_estimate=QUICK,
+        name="gradient_halves",
+    )(core.astype(jnp.int32)[None], a, b)
 
 
 def inverse_rms(field):
@@ -389,9 +490,6 @@
     def gather_rows(piece):
         return [piece] + [shift(piece, "row", -i) for i in range(1, row_size)]
 
-    def gather_columns(piece_of):
-        return [piece_of(0)] + [shift(piece_of(j & 1), "col", j) for j in range(1, col_size)]
-
     def pick(a, index, axis):
         return lax.dynamic_index_in_dim(a, index, axis, keepdims=False)
 
@@ -400,16 +498,6 @@
 
     def by_rows(blocks):
         return list(blocks) if len(blocks) == row_size else jnp.split(blocks[0], row_size, axis=2)
-
-    def reduce_columns(parts, first=0):
-        return [shift(part, "col", -j) if j else part for j, part in enumerate(parts, first)]
-
-    def by_core(a, axis):
-        mine, other = pick(a, core, axis), pick(a, 1 - core, axis)
-        return small(mine, to_core(other))
-
-    def by_parity(arrived):
-        return halves(parity == 0, small(*arrived[0::2])[None], small(*arrived[1::2])[None], 0)
 
     fence = lax.optimization_barrier
 
@@ -423,7 +511,6 @@
             return a.reshape(a.shape[:-2] + (HEAD_DIM, block))
         return jnp.concatenate([a[..., k : k + HEAD_DIM, :] for k in range(0, a.shape[-2], HEAD_DIM)], axis=-1)
 
-    near, far = slice(1, None, 2), slice(2, None, 2)
 
     def total(*parts):
         return sum(part.astype(F32) for part in parts)
@@ -442,11 +529,12 @@
     packed = jnp.concatenate([query_blocks, pair_blocks[:, 0], pair_blocks[:, 1]], axis=-1)
     packed = lax.dynamic_slice_in_dim(packed, core * (block // 2), block // 2, 0)
     head_rows = pick(projection_weight.reshape(2, 2, HEAD_DIM, block), core, 1)
-    packed = fence(
-        [jnp.concatenate([pick(packed, p, 1), fold(pick(head_rows, p, 0))]) for p in (parity, 1 - parity)]
-    )
-    along = gather_columns(lambda which: packed[which])
-    own_packed = gather_rows(packed[0])
+    packed = jnp.stack([jnp.concatenate([packed[:, p], fold(head_rows[p])]) for p in range(2)])
+    packed, tokens, cotangent, gate_up_weight, down_weight = fence(
+        (packed, tokens, cotangent, gate_up_weight, down_weight)
+    )
+    far_packed = shift(packed, "col", 2)
+    own_packed = gather_rows(packed)
 
     pieces = []
     for part in range(PARTS):
@@ -454,47 +542,48 @@
         gate_up = lax.dynamic_slice_in_dim(gate_up_weight, start, sub, 2).transpose(1, 2, 0).reshape(2 * sub, block)
         pieces.append(jnp.concatenate([gate_up, lax.dynamic_slice_in_dim(down_weight, start, sub, 0)]))
     own_rows = gather_rows(jnp.stack(pieces))
-
+    grad_out = rel(cotangent)
+    grad_out_other = to_y(grad_out)
     gain_one, gain_two = rel(attention_gain), rel(feedforward_gain)
     inputs = rel(tokens)
-    grad_out = rel(cotangent)
     wide_inputs = inputs.astype(F32)
     normed = (wide_inputs * inverse_rms(wide_inputs) * gain_one).astype(BF)
+    normed_other = to_pair(normed)
     tables = rotary_tables()
     spread = spread_matrix()
     spread_back = spread.T
-    along, own_packed, own_rows, pieces, normed, inputs, grad_out, tables, spread, spread_back = fence(
-        (along, own_packed, own_rows, pieces, normed, inputs, grad_out, tables, spread, spread_back)
-    )
-
-    normed_other = to_pair(normed)
-    got = gather_rows(jnp.stack(along[1:]))
-    grad_out_other = to_y(grad_out)
-    others = [None, shift(pieces[0], "col", 2), None]
-    mine = [jnp.concatenate([own_packed[0][None], got[0]])]
-    mine_other = [to_core(mine[0])]
-    got, own_packed, normed, normed_other, own_rows, pieces, grad_out, grad_out_other, others, mine, mine_other = fence(
-        (got, own_packed, normed, normed_other, own_rows, pieces, grad_out, grad_out_other, others, mine, mine_other)
-    )
-
-    mine += [jnp.concatenate([a[None], b]) for a, b in zip(own_packed[1:], got[1:])]
-    mine[1:] = fence(mine[1:])
-    mine_other += [to_core(a) for a in mine[1:]]
+    far_packed, own_packed, own_rows, pieces, grad_out, grad_out_other, inputs, normed, normed_other, tables = fence(
+        (far_packed, own_packed, own_rows, pieces, grad_out, grad_out_other, inputs, normed, normed_other, tables)
+    )
+
+    far_rows = gather_rows(far_packed)
+    own_cores = [to_core(a) for a in own_packed]
+    others = [shift(pieces[0], "col", 1)]
+    late_others = [shift(pieces[1], "col", 1)]
     normed_all = in_sequence(normed, normed_other)
-    others = [shift(pieces[0], "col", 1), others[1], shift(pieces[0], "col", 3)]
-    late_others = [shift(pieces[1], "col", 1)]
-    pairs = [halves(core == 0, a[:, None], b[:, None], 1) for a, b in zip(mine, mine_other)]
+    far_rows, own_cores, own_packed, others, late_others, normed_all, spread, spread_back = fence(
+        (far_rows, own_cores, own_packed, others, late_others, normed_all, spread, spread_back)
+    )
+    far_cores = [to_core(a) for a in far_rows]
+    others += [shift(pieces[0], "col", j) for j in range(2, col_size)]
     split = block // 2
-    weight_qkv = jnp.concatenate([jnp.concatenate([p[j, :, :split] for j in range(col_size)], axis=-1) for p in pairs])
-    weight_qkv = weight_qkv.reshape(model, -1)
-    heads = jnp.concatenate([unfold(p[:, :, split:]) for p in pairs], axis=-1)
-    gap = jnp.zeros(heads.shape[:2] + (LANES // 2 - HALF, model), BF)
-    weight_projection = jnp.concatenate(
-        [heads[:, :, :HALF], gap, heads[:, :, HALF:], gap], axis=2
-    ).reshape(-1, model)
-    weight_qkv, weight_projection, normed_all, grad_out, grad_out_other = fence(
-        (weight_qkv, weight_projection, normed_all, grad_out, grad_out_other)
-    )
+    if split % LANES == 0:
+        rows = [list(parts) for parts in zip(far_rows, far_cores, own_packed, own_cores)]
+        weight_qkv, weight_projection = assemble(core, rows, model)
+    else:
+        pick_core = lambda a, b: halves(core == 0, a[:, None], b[:, None], 1)
+        pairs = [
+            jnp.concatenate([pick_core(*far), pick_core(*mine)])
+            for far, mine in zip(zip(far_rows, far_cores), zip(own_packed, own_cores))
+        ]
+        weight_qkv = jnp.concatenate([jnp.concatenate([p[j, :, :split] for j in range(col_size)], axis=-1) for p in pairs])
+        weight_qkv = weight_qkv.reshape(model, -1)
+        heads = jnp.concatenate([unfold(p[:, :, split:]) for p in pairs], axis=-1)
+        gap = jnp.zeros(heads.shape[:2] + (LANES // 2 - HALF, model), BF)
+        weight_projection = jnp.concatenate(
+            [heads[:, :, :HALF], gap, heads[:, :, HALF:], gap], axis=2
+        ).reshape(-1, model)
+    weight_qkv, weight_projection = fence((weight_qkv, weight_projection))
 
     qkv, attended = attention_forward(normed_all, weight_qkv, spread, *tables)
     qkv, attended, others, late_others, grad_out, grad_out_other, weight_projection = fence(
@@ -506,16 +595,24 @@
     sent, stacked, attended, weight_projection = fence((sent, stacked, attended, weight_projection))
     arrived = to_pair(sent)
     rest = gather_rows(stacked)
+    fine = row_size * SPLIT_MODEL <= model
+    own_first = [a[0] for a in own_rows]
     kept = dot(rows_of(attended, parity * own), weight_projection)
-    kept, arrived, rest, pieces, own_rows = fence((kept, arrived, rest, pieces, own_rows))
+    kept, stacked = fence((kept, stacked))
+    mine = [jnp.concatenate([own_first[0][None], stacked])] if fine else []
+    mine_other = [to_core(a) for a in mine]
+    kept, arrived, rest, mine, mine_other, pieces, own_rows = fence(
+        (kept, arrived, rest, mine, mine_other, pieces, own_rows)
+    )
 
     middle = inputs.astype(F32) + kept + arrived.astype(F32)
     normed_two = (middle * inverse_rms(middle) * gain_two).astype(BF)
-    mine = merge([jnp.concatenate([a[None], b]) for a, b in zip([a[0] for a in own_rows], rest)])
-    normed_two, middle, mine = fence((normed_two, middle, mine))
+    n = len(mine)
+    late = merge([jnp.concatenate([a[None], b]) for a, b in zip(own_first[n:], rest[n:])])
+    normed_two, middle, late = fence((normed_two, middle, late))
     normed_two_other = to_y(normed_two)
+    weights = [mine + late, mine_other + [to_core(a) for a in late]]
     others = [shift(pieces[1], "col", j) for j in (2, 3)]
-    weights = [mine, [to_core(a) for a in mine]]
     weights, normed_two = fence((weights, normed_two))
 
     rest = [gather_rows(late_others[0])]
@@ -542,25 +639,27 @@
     arrived = [to_core(a) for a in other[1:]]
     mine, other[0], late, late_other, arrived = fence((mine, other[0], late, late_other, arrived))
     weights = [early + late, early_other + late_other]
-    cut = col_size // 2
-    sent = [small(*pair) for pair in zip(mine[1:], arrived)]
+    middle_columns = lambda a: a[1:3]
+    outer_columns = lambda a: jnp.stack([a[0], a[3]])
+    sent = [[small(cut(a), cut(b)) for a, b in zip(mine[1:], arrived)] for cut in (middle_columns, outer_columns)]
     weights, mine[0], other[0], sent, normed_two_other = fence((weights, mine[0], other[0], sent, normed_two_other))
-    rows = [shift(a[:cut], "row", i) for i, a in enumerate(sent, 1)]
+    rows = [shift(a, "row", i) for i, a in enumerate(sent[0], 1)]
     arrived = to_core(other[0])
     grads, *sums = feedforward(normed_two_other, grad_out_other, weights, PARTS)
     grads, sums, rows, mine[0], arrived, sent, weights = fence((grads, sums, rows, mine[0], arrived, sent, weights))
     other_sums.append(sums)
 
-    blocks = [small(mine[0][j], arrived[j], *[r[j] for r in rows]) for j in range(cut)]
+    blocks = [small(mine[0][j], arrived[j], *[r[j - 1] for r in rows]) for j in (1, 2)]
     sums = small(*[p[1] for p in other_sums])
     sums, blocks, grads, other_sums, own_sums = fence((sums, blocks, grads, other_sums, own_sums))
     grad_two_other = to_y(sums)
-    rows = [shift(a[cut:], "row", i) for i, a in enumerate(sent, 1)]
-    along = [blocks[0]] + [shift(blocks[j], "col", -j) for j in range(1, cut)]
+    rows = [shift(a, "row", i) for i, a in enumerate(sent[1], 1)]
+    along = [shift(blocks[1], "col", -2)]
     grads, *sums = feedforward(normed_two, grad_out, weights, PARTS, grads)
-    grads, sums, rows, along, mine[0], arrived, grad_two_other = fence(
-        (grads, sums, rows, along, mine[0], arrived, grad_two_other)
-    )
+    grads, sums, rows, along, blocks, mine[0], arrived, grad_two_other = fence(
+        (grads, sums, rows, along, blocks, mine[0], arrived, grad_two_other)
+    )
+    along.append(shift(blocks[0], "col", -1))
     own_sums.append(sums)
     last, other = by_rows(grads[0]), by_rows(grads[1])
     last_rows = [to_core(a) for a in other[1:]]
@@ -568,117 +667,113 @@
     grad_middle, gain_two_term = norm_back(middle, gain_two, kept)
     grad_middle = grad_middle + grad_out.astype(F32)
     branch = grad_middle.astype(BF)
-    last_rows, branch, grad_middle, gain_two_term, last, other[0] = fence(
-        (last_rows, branch, grad_middle, gain_two_term, last, other[0])
+    last_rows, branch, grad_middle, gain_two_term, last, other[0], along = fence(
+        (last_rows, branch, grad_middle, gain_two_term, last, other[0], along)
     )
     branch_other = to_pair(branch)
-    sent = [small(*pair) for pair in zip(last[1:], last_rows)]
-    last_rows = [shift(a, "row", i) for i, a in enumerate(sent, 1)]
+    sent = [[small(cut(a), cut(b)) for a, b in zip(last[1:], last_rows)] for cut in (middle_columns, outer_columns)]
+    last_rows = [shift(a, "row", i) for i, a in enumerate(sent[0], 1)]
     last_core = to_core(other[0])
     out_kept = middle + total(*[p[0] for p in own_sums])
     out_sent = small(*[p[0] for p in other_sums])
-    blocks = [small(mine[0][j], arrived[j], *[r[j - cut] for r in rows]) for j in range(cut, col_size)]
-    branch, branch_other, last_core, out_kept, out_sent, blocks, grad_middle, gain_two_term = fence(
-        (branch, branch_other, last_core, out_kept, out_sent, blocks, grad_middle, gain_two_term)
-    )
-
-    along += [shift(blocks[j - cut], "col", -j) for j in range(cut, col_size)]
+    blocks = [small(mine[0][j], arrived[j], *[r[j // 3] for r in rows]) for j in (0, 3)]
+    branch, branch_other, last_core, last_rows, sent, out_kept, out_sent, blocks, grad_middle, gain_two_term = fence(
+        (branch, branch_other, last_core, last_rows, sent, out_kept, out_sent, blocks, grad_middle, gain_two_term)
+    )
+
+    along += [blocks[0], shift(blocks[1], "col", -3)]
+    out_other = to_y(out_sent)
+    outer_rows = [shift(a, "row", i) for i, a in enumerate(sent[1], 1)]
     branch_all = in_sequence(branch, branch_other)
     grad_attended = dot_nt(branch_all, weight_projection).astype(BF)
-    g = dot_tn(attended, branch_all).astype(BF).reshape(col_size, 2, LANES, model)
-    projection_halves = jnp.concatenate([g[:, :, :HALF], g[:, :, LANES // 2 : LANES // 2 + HALF]], axis=2)
-    projection_halves = [pick(projection_halves, which, 1) for which in (core, 1 - core)]
-    projection_other = to_core(projection_halves[1])
-    blocks = [small(last[0][j], last_core[j], *[r[j] for r in last_rows]) for j in range(col_size)]
-
     count = col_size // 2
     wide = count * GROUP
     to_rows = lambda g: [shift(g[i], "row", i) for i in range(1, row_size)]
-    qkv_halves = lambda part: dot_tn(normed_all, part).astype(BF).reshape(row_size, 2, block // 2, wide)
-    by_halves = lambda g: [pick(g, which, 1) for which in (core, 1 - core)]
+
+    def qkv_halves(part):
+        if split % LANES == 0:
+            return gradient_halves(core, normed_all, part, split)
+        g = dot_tn(normed_all, part).astype(BF).reshape(row_size, 2, split, wide)
+        return jnp.stack([pick(g, core, 1), pick(g, 1 - core, 1)])
 
     first = attention_backward(qkv, grad_attended, spread_back, *tables, 0, count)
-    first, along, projection_halves, projection_other, blocks, grad_attended = fence(
-        (first, along, projection_halves, projection_other, blocks, grad_attended)
-    )
+    first, along, outer_rows, grad_attended, branch_all = fence((first, along, outer_rows, grad_attended, branch_all))
+    rows = [[m[0] for m in outer_rows], [m[0] for m in last_rows], [m[1] for m in last_rows], [m[1] for m in outer_rows]]
+    blocks = [small(last[0][j], last_core[j], *rows[j]) for j in range(col_size)]
+    blocks, grad_attended, first, branch_all = fence((blocks, grad_attended, first, branch_all))
     last_along = [blocks[0]] + [shift(blocks[j], "col", -j) if j & 1 else blocks[j] for j in range(1, col_size)]
-    first_halves = by_halves(qkv_halves(first))
-    first_other = to_core(first_halves[1])
+    projection_halves = gradient_halves(core, attended, branch_all, LANES, True)
+    first_halves = qkv_halves(first)
+    second = attention_backward(qkv, grad_attended, spread_back, *tables, count, count)
+    second, last_along, along, first_halves, projection_halves, out_other = fence(
+        (second, last_along, along, first_halves, projection_halves, out_other)
+    )
+
+    product = lambda rows: sum(
+        dot_nt(rows(part), weight_qkv[:, k * wide : (k + 1) * wide]) for k, part in enumerate((first, second))
+    )
+    first_other, projection_other = to_core(first_halves[1]), to_core(projection_halves[1])
+    sent = product(lambda a: rows_of(a, (1 - parity) * own)).astype(BF)
+    second_halves = qkv_halves(second)
+    first_part = small(*along)
+    sent, second_halves, first_part, last_along, first_other, projection_other, first_halves, projection_halves = fence(
+        (sent, second_halves, first_part, last_along, first_other, projection_other, first_halves, projection_halves)
+    )
+    half = own // 2
+    grad_one_other = [to_pair(sent[:half])]
+    last_along[2] = shift(last_along[2], "col", -2)
+    first_rows = small(first_halves[0], first_other)
     g = small(projection_halves[0], projection_other)
+    sent, first_rows, g, second_halves = fence((sent, first_rows, g, second_halves))
+    first_rows = [first_rows[0]] + to_rows(first_rows)
     projection_rows = [g[:, :, i * block : (i + 1) * block] for i in range(row_size)]
     projection_rows[1:] = to_rows(projection_rows)
-    second = attention_backward(qkv, grad_attended, spread_back, *tables, count, count)
-    second, last_along, first_other, projection_rows, along, first_halves = fence(
-        (second, last_along, first_other, projection_rows, along, first_halves)
-    )
-
-    product = lambda rows: sum(
-        dot_nt(rows(part), weight_qkv[:, k * wide : (k + 1) * wide]) for k, part in enumerate((first, second))
-    )
-    sent = product(lambda a: rows_of(a, (1 - parity) * own)).astype(BF)
-    second_halves = by_halves(qkv_halves(second))
-    first_rows = small(first_halves[0], first_other)
+    second_other = to_core(second_halves[1])
+    kept = product(lambda a: rows_of(a, parity * own))
+    sent, grad_one_other, last_along, first_rows, projection_rows, second_halves, second_other, first_part, kept = fence(
+        (sent, grad_one_other, last_along, first_rows, projection_rows, second_halves, second_other, first_part, kept)
+    )
+
+    second_rows = small(second_halves[0], second_other)
+    first_rows = small(*first_rows)
     g = small(*projection_rows)
-    sent, second, second_halves, first_rows, g, along, out_sent = fence(
-        (sent, second, second_halves, first_rows, g, along, out_sent)
-    )
-    grad_one_other = to_pair(sent)
-    first_rows = [first_rows[0]] + to_rows(first_rows)
-    second_other = to_core(second_halves[1])
-    first_part = small(*along)
-    second_halves, second_other, g, first_part = fence((second_halves, second_other, g, first_part))
-    second_rows = small(second_halves[0], second_other)
+    both_parts = jnp.stack([first_part, small(*last_along)])
+    second_rows, first_rows, both_parts, g = fence((second_rows, first_rows, both_parts, g))
     second_rows = [second_rows[0]] + to_rows(second_rows)
-    last_along[far] = [shift(last_along[j], "col", -j) for j in range(2, col_size, 2)]
-    first_part_other = to_y(first_part)
-    kept = product(lambda a: rows_of(a, parity * own))
-    second_rows, first_rows, grad_one_other, kept, first_part, first_part_other, last_along = fence(
-        (second_rows, first_rows, grad_one_other, kept, first_part, first_part_other, last_along)
-    )
-
-    columns = lambda g, first: reduce_columns([g[:, j * GROUP : (j + 1) * GROUP] for j in range(count)], first)
-    blocks = [small(*first_rows), small(*second_rows)]
-    last_part = small(*last_along)
-    blocks, last_part = fence((blocks, last_part))
-    arrived = columns(blocks[1], count) + columns(blocks[0], 0)
-    arrived = arrived[count:] + arrived[:count]
-    last_part_other = to_y(last_part)
-    grad_inputs, gain_one_term = norm_back(inputs.astype(F32), gain_one, kept + grad_one_other.astype(F32))
+    first_rows = shift(first_rows, "col", 2)
+    projection_far = shift(g[:2], "col", 2)
+    grad_one_other.append(to_pair(sent[half:]))
+    both_parts_other = to_y(both_parts)
+    second_rows, first_rows, projection_far, grad_one_other, both_parts, both_parts_other, g = fence(
+        (second_rows, first_rows, projection_far, grad_one_other, both_parts, both_parts_other, g)
+    )
+
+    both = combine(second_rows, first_rows, g[2:], projection_far)
+    both, both_parts, both_parts_other, grad_one_other = fence((both, both_parts, both_parts_other, grad_one_other))
+    both_other = to_y(both)
+    both_parts = halves(y == 0, both_parts[:, None], both_parts_other[:, None], 1)
+    both_parts_core = to_core(both_parts)
+    arrived = jnp.concatenate(grad_one_other).astype(F32)
+    grad_inputs, gain_one_term = norm_back(inputs.astype(F32), gain_one, kept + arrived)
     grad_inputs = unrel((grad_inputs + grad_middle).astype(BF))
     gains = unrel(jnp.stack([gain_one_term, gain_two_term]))
-    first_part = halves(y == 0, first_part[None], first_part_other[None], 0)[:, None]
-    first_part_other = to_core(first_part)
-    arrived, gains, grad_inputs, first_part, first_part_other, last_part, last_part_other = fence(
-        (arrived, gains, grad_inputs, first_part, first_part_other, last_part, last_part_other)
-    )
-    projection_along = reduce_columns([g[j] for j in range(col_size)])
-    out_other = to_y(out_sent)
-    gains = gains + swap(gains, "dp", 1)
-    gains = gains + swap(gains, "dp", 2)
-    last_part = halves(y == 0, last_part[None], last_part_other[None], 0)[:, None]
-    arrived = by_parity(arrived)
-    gains, last_part, projection_along, arrived, out_other, first_part = fence(
-        (gains, last_part, projection_along, arrived, out_other, first_part)
-    )
-
-    both = jnp.concatenate([arrived, jnp.stack([fold(p) for p in by_parity(projection_along)])], axis=1)
-    both, gains, last_part = fence((both, gains, last_part))
-    both_other = to_y(both)
-    last_part_other = to_core(last_part)
     for axis, n in (("row", row_size), ("col", col_size)):
         bit = 1
         while bit < n:
             gains = gains + lax.ppermute(gains, axis, [(i, i ^ bit) for i in range(n)])
             bit *= 2
-    attention_gain_grad, feedforward_gain_grad = gains[0], gains[1]
+    gains = gains + swap(gains, "dp", 1)
+    gate_up_grad, down_grad = place(
+        jnp.where(core == 0, both_parts, both_parts_core), jnp.where(core == 0, both_parts_core, both_parts)
+    )
     output = unrel((out_kept + out_other.astype(F32)).astype(BF))
-    sides = [halves(core == 0, a, b, 1) for a, b in ((first_part, first_part_other), (last_part, last_part_other))]
-    gate_up_grad, down_grad = place(sides)
-    both, both_other, gate_up_grad, down_grad, gains, output = fence(
-        (both, both_other, gate_up_grad, down_grad, gains, output)
+    both, both_other, gate_up_grad, down_grad, gains, output, grad_inputs = fence(
+        (both, both_other, gate_up_grad, down_grad, gains, output, grad_inputs)
     )
     both = small(both, both_other)
     both_other = to_core(both)
+    gains = gains + swap(gains, "dp", 2)
+    attention_gain_grad, feedforward_gain_grad = gains[0], gains[1]
     query_grad, key_value_grad, projection_grad = place_attention(
         jnp.where(core == 0, both, both_other), jnp.where(core == 0, both_other, both), block
     )

time: 651 us -> 614 us (0.943)
  Pallas kernels: 180 us -> 205 us
  other arithmetic: 97.8 us -> 73.3 us
  matrix products: 33.1 us -> 13 us
  waiting for transfers between devices: 231 us -> 216 us
  local copies, waits for them, and re-layouts: 34 us -> 26.6 us
    ppermute x29 -> x30, waiting for transfers between devices: 96.2 us -> 55.3 us  [swap(): return lax.ppermute(a, axis, [(i, i ^ bit) for i in range(n)])]
    pallas_call x0 -> x5, Pallas kernels: none -> 24.5 us  [the longest x3 17.7 us: gradient_halves(): pl.pallas_call(functools.partial(halves_kernel, gap), grid_spec=pltpu.Pre...]
    ppermute x33 -> x28, waiting for transfers between devices: 129 us -> 151 us  [shift(): return lax.ppermute(a, axis, [(i, (i + by) % n) for i in range(n)])]
    dot_general x3 -> x0, matrix products: 11.8 us -> none  [dot_tn(): lax.dot_general(a, b, (((0,), (0,)), ((), ())), preferred_element_type=F32)]
    convert_element_type x16, other arithmetic: 33.4 us -> 24.4 us  [small(): return total(*parts).astype(BF)]
    concatenate x7 -> x1, other arithmetic: 7.13 us -> 0.21 us  [per_device(): mine = [jnp.concatenate([own_first[0][None], stacked])] if fine else []]
    ppermute x29 -> x30, starting transfers between devices: 14.1 us -> 19.3 us  [swap(): return lax.ppermute(a, axis, [(i, i ^ bit) for i in range(n)])]
    ppermute x33 -> x28, starting transfers between devices: 46.3 us -> 49.2 us  [shift(): return lax.ppermute(a, axis, [(i, (i + by) % n) for i in range(n)])]
  transfers between devices with their start and end apart: 65 -> 61, of which waited for: 27 -> 21; matrix products, arithmetic and copies ran while one was open for 15% -> 11% of each run, Pallas kernels for 28% -> 33%
where the time goes in v3:
time: 614 us; the launch traced here: 607 us
  waiting for transfers between devices  216 us (35%)
  Pallas kernels  205 us (33%)
  other arithmetic  73.3 us (12%)
  starting transfers between devices  70.2 us (11%)
  local copies, waits for them, and re-layouts  26.6 us (4%)
  matrix products  13 us (2%)
    ppermute x28, waiting for transfers between devices, shift(): return lax.ppermute(a, axis, [(i, (i + by) % n) for i in range(n)])  151 us
    pallas_call x4, Pallas kernels, feedforward(): pl.pallas_call(functools.partial(feedforward_kernel, col_step, sub, rows_...  111 us
    ppermute x30, waiting for transfers between devices, swap(): return lax.ppermute(a, axis, [(i, i ^ bit) for i in range(n)])  55.3 us
    ppermute x28, starting transfers between devices, shift(): return lax.ppermute(a, axis, [(i, (i + by) % n) for i in range(n)])  49.2 us
    pallas_call x2, Pallas kernels, attention_backward(): pl.pallas_call(attention_backward_kernel, grid=(groups,), in_specs=[pl.Bl...  30.9 us
    pallas_call x1, Pallas kernels, attention_forward(): pl.pallas_call(attention_forward_kernel, grid=(groups,), in_specs=[whole(...  29.7 us
    convert_element_type x16, other arithmetic, small(): return total(*parts).astype(BF)  24.4 us
    ppermute x30, starting transfers between devices, swap(): return lax.ppermute(a, axis, [(i, i ^ bit) for i in range(n)])  19.3 us
  transfers between devices with their start and end apart: 61, of which 21 were waited for; matrix products, arithmetic and copies ran while one was open for 11% of the time, Pallas kernels for 33%

profile of v3, /device:TPU:0, one launch (start us, length us, event | category | flops | bytes accessed | tf_op | source)
XLA Modules:
  0.0 606.8 jit_solution(16652897124810355233)
XLA Ops:
  5.0 3.0 maximum_select_fusion.3.cot_ref
  8.0 3.0 collective-permute-start.3
  17.1 1.7 dynamic-slice_bitcast_fusion.1
  21.7 2.7 collective-permute-start
  24.3 1.9 collective-permute-start.1
  26.3 1.9 multiply_sine_fusion
  28.7 39.9 %collective-permute-done.refs_0_ = bf16[2,576,384]{2,1,0:T(8,128)(2,1)} collective-permute-done((bf16[2,576,384]{2,1,0:T(8,128)(2,1)S(1)}, bf16[2,576,384]{2,1,0:T(8,128)(2,1)}, u32[]{:S(2)}, u32[]{:S(2)}) %collective-permute-start) | collective-permute-done | bytes 884768 | tf_op jit(solution)/shard_map/ppermute | solution.py:476
  70.6 2.8 collective-permute-start.8
  74.0 4.5 maximum_select_fusion.n1_ref.a_ref
  78.5 10.4 %collective-permute-done.8 = bf16[384,768]{1,0:T(8,128)(2,1)S(1)} collective-permute-done((bf16[384,768]{1,0:T(8,128)(2,1)}, bf16[384,768]{1,0:T(8,128)(2,1)S(1)}, u32[]{:S(2)}, u32[]{:S(2)}) %collective-permute-start.8) | collective-permute-done | bytes 589856 | tf_op jit(solution)/shard_map/ppermute | solution.py:476
  88.9 11.9 %collective-permute-done.9 = bf16[384,768]{1,0:T(8,128)(2,1)} collective-permute-done((bf16[384,768]{1,0:T(8,128)(2,1)}, bf16[384,768]{1,0:T(8,128)(2,1)}, u32[]{:S(2)}, u32[]{:S(2)}) %collective-permute-start.9) | collective-permute-done | bytes 589856 | tf_op jit(solution)/shard_map/ppermute | solution.py:476
  103.0 2.7 collective-permute-start.13
  108.0 6.5 %assemble.1 = (bf16[1536,1536]{1,0:T(8,128)(2,1)}, bf16[1024,1536]{1,0:T(8,128)(2,1)}) custom-call(s32[1]{0:T(128)} %bitcast.17.core_ref, bf16[2,576,384]{2,1,0:T(8,128)(2,1)} %collective-permute-done.refs_0_, bf16[2,576,384]{2,1,0:T(8,128)(2,1)} %collective-permute-done.10.refs_1_, bf16[2,576,384]{2,1,0:T(8,128)(2,1)S(1)} %pad_maximum_fusion.8.refs_2_, ...), custom_call_target="tpu_custom_call" | custom-call | flops 1 | bytes 1 | tf_op jit(solution)/shard_map/assemble/pallas_call | solution.py:377
  114.4 29.7 %attention_forward.1 = (bf16[1024,2048]{1,0:T(8,128)(2,1)}, bf16[1024,1024]{1,0:T(8,128)(2,1)S(1)}) custom-call(bf16[1024,1536]{1,0:T(8,128)(2,1)} %maximum_select_fusion.n1_ref.a_ref, bf16[1536,1536]{1,0:T(8,128)(2,1)} %get-tuple-element.307.w_ref, bf16[384,512]{1,0:T(8,128)(2,1)S(1)} %fusion.33.spread_ref, f32[1024,128]{1,0:T(8,128)S(1)} %get-tuple-element.309.cos_ref, ...), custom_call_target="tpu_custom_call" | custom-call | flops 1 | bytes 1 | tf_op jit(solution)/shard_map/attention_forward/pallas_call | solution.py:126
  144.2 1.8 convolution_convert_fusion
  147.5 1.8 fusion.21
  149.6 1.9 collective-permute-start.15
  153.1 35.0 %collective-permute-done.14 = bf16[512,1536]{1,0:T(8,128)(2,1)S(1)} collective-permute-done((bf16[512,1536]{1,0:T(8,128)(2,1)S(1)}, bf16[512,1536]{1,0:T(8,128)(2,1)S(1)}, u32[]{:S(2)}, u32[]{:S(2)}) %collective-permute-start.14) | collective-permute-done | bytes 1572896 | tf_op jit(solution)/shard_map/ppermute | solution.py:463
  188.0 2.7 collective-permute-done.15
  195.1 1.8 collective-permute-start.18
  197.5 2.6 collective-permute-start.20
  200.9 26.7 %feedforward.4 = (bf16[4,384,768]{2,1,0:T(8,128)(2,1)}, bf16[4,384,768]{2,1,0:T(8,128)(2,1)}, bf16[4,384,768]{2,1,0:T(8,128)(2,1)}, bf16[4,384,768]{2,1,0:T(8,12...) custom-call(bf16[512,1536]{1,0:T(8,128)(2,1)} %copy-done.14, bf16[512,1536]{1,0:T(8,128)(2,1)} %maximum_select_fusion.3.cot_ref, ...), custom_call_target="tpu_custom_call" | custom-call | flops 1 | bytes 1 | tf_op jit(solution)/shard_map/feedforward/pallas_call | solution.py:237
  227.6 3.6 collective-permute-done.21.n2_ref
  232.6 3.1 pad_maximum_fusion.2.refs_0_
  235.7 1.8 collective-permute-start.22
  237.4 28.8 %feedforward.5 = (bf16[4,384,768]{2,1,0:T(8,128)(2,1)}, bf16[4,384,768]{2,1,0:T(8,128)(2,1)}, bf16[4,384,768]{2,1,0:T(8,128)(2,1)}, bf16[4,384,768]{2,1,0:T(8,12...) custom-call(bf16[512,1536]{1,0:T(8,128)(2,1)} %collective-permute-done.21.n2_ref, ...), custom_call_target="tpu_custom_call" | custom-call | flops 1 | bytes 1 | tf_op jit(solution)/shard_map/feedforward/pallas_call | solution.py:237
  267.4 1.8 pad_maximum_fusion.3.refs_1_
  269.8 4.0 collective-permute-done.24.refs_3_
  275.3 1.9 collective-permute-done.25
  279.5 27.1 %feedforward.6 = (bf16[4,384,768]{2,1,0:T(8,128)(2,1)}, bf16[4,384,768]{2,1,0:T(8,128)(2,1)}, bf16[4,384,768]{2,1,0:T(8,128)(2,1)}, bf16[4,384,768]{2,1,0:T(8,12...) custom-call(bf16[512,1536]{1,0:T(8,128)(2,1)} %collective-permute-done.21.n2_ref, ...), custom_call_target="tpu_custom_call" | custom-call | flops 1 | bytes 1 | tf_op jit(solution)/shard_map/feedforward/pallas_call | solution.py:237
  307.5 4.6 add_convert_fusion.2
  312.2 3.0 fusion.35
  316.9 6.5 %collective-permute-start.29 = (bf16[384,768]{1,0:T(8,128)(2,1)}, bf16[384,768]{1,0:T(8,128)(2,1)}, u32[]{:S(2)}, u32[]{:S(2)}) collective-permute-start(bf16[384,768]{1,0:T(8,128)(2,1)} %get-tuple-element.439), channel_id=1, source_target_pairs={{0,2},{1,3},{2,0},{3,1},{4,6},{5,7},{6,4},{7,5},{8,10},{9,11},{10,... | collective-permute-start | bytes 1769480 | tf_op jit(solution)/shard_map/ppermute | solution.py:476
  323.4 28.9 %feedforward.7 = (bf16[4,384,768]{2,1,0:T(8,128)(2,1)}, bf16[4,384,768]{2,1,0:T(8,128)(2,1)}, bf16[4,384,768]{2,1,0:T(8,128)(2,1)}, bf16[4,384,768]{2,1,0:T(8,12...) custom-call(bf16[512,1536]{1,0:T(8,128)(2,1)} %copy-done.14, bf16[512,1536]{1,0:T(8,128)(2,1)} %maximum_select_fusion.3.cot_ref, ...), custom_call_target="tpu_custom_call" | custom-call | flops 1 | bytes 1 | tf_op jit(solution)/shard_map/feedforward/pallas_call | solution.py:237
  352.4 2.3 multiply_reduce_fusion.2
  354.7 7.1 %collective-permute-start.32 = (bf16[384,768]{1,0:T(8,128)(2,1)}, bf16[384,768]{1,0:T(8,128)(2,1)S(1)}, u32[]{:S(2)}, u32[]{:S(2)}) collective-permute-start(bf16[384,768]{1,0:T(8,128)(2,1)} %get-tuple-element.451), channel_id=1, source_target_pairs={{0,3},{1,0},{2,1},{3,2},{4,7},{5,4},{6,5},{7,6},{8,11},{9,8},{10,9... | collective-permute-start | bytes 1769480 | tf_op jit(solution)/shard_map/ppermute | solution.py:476
  361.8 6.7 %multiply_reduce_fusion = (f32[1536]{0:T(1024)S(1)}, f32[512]{0:T(512)S(1)}, f32[512,1536]{1,0:T(8,128)S(1)}, f32[512,1536]{1,0:T(8,128)}) fusion(f32[512,1536]{1,0:T(8,128)S(1)} %copy-done.7, f32[512]{0:T(512)S(1)} %add_rsqrt_fusion.1, f32[1536]{0:T(1024)S(1)} %maximum_select_fusion.8, f32[512,1536]{1,0:T(8,128)} %get-tuple-element.446, ...), kind=kLoop, calls=%fused_computation.26 | loop fusion | flops 8648704 | bytes 23609344 | tf_op jit(solution)/shard_map/reduce_sum | solution.py:430
  368.6 4.0 fusion.64
  372.6 2.8 collective-permute-done.32
  380.2 3.1 fusion.37
  384.8 20.5 %collective-permute-done.35 = bf16[2,384,768]{2,1,0:T(8,128)(2,1)S(1)} collective-permute-done((bf16[2,384,768]{2,1,0:T(8,128)(2,1)S(1)}, bf16[2,384,768]{2,1,0:T(8,128)(2,1)S(1)}, u32[]{:S(2)}, u32[]{:S(2)}) %collective-permute-start.35) | collective-permute-done | bytes 1179680 | tf_op jit(solution)/shard_map/ppermute | solution.py:476
  405.3 7.0 %collective-permute-done.33 = bf16[512,1536]{1,0:T(8,128)(2,1)S(1)} collective-permute-done((bf16[512,1536]{1,0:T(8,128)(2,1)S(1)}, bf16[512,1536]{1,0:T(8,128)(2,1)S(1)}, u32[]{:S(2)}, u32[]{:S(2)}) %collective-permute-start.33) | collective-permute-done | bytes 1572896 | tf_op jit(solution)/shard_map/ppermute | solution.py:463
  416.6 3.7 convolution_convert_fusion.1.do_ref
  420.3 15.7 %attention_backward.2.b_ref = bf16[1024,768]{1,0:T(8,128)(2,1)S(1)} custom-call(bf16[1024,2048]{1,0:T(8,128)(2,1)} %get-tuple-element.467.qkv_ref, bf16[1024,1024]{1,0:T(8,128)(2,1)S(1)} %convolution_convert_fusion.1.do_ref, bf16[512,384]{1,0:T(8,128)(2,1)S(1)} %fusion.32.gather_ref, f32[1024,128]{1,0:T(8,128)S(1)} %get-tuple-element.309.cos_ref, ...), custom_call_target="tpu_custom_call" | custom-call | flops 1 | bytes 1 | tf_op jit(solution)/shard_map/attention_backward/pallas_call | solution.py:153
  436.1 4.3 collective-permute-done.37
  440.4 3.3 fusion.41
  443.7 3.2 collective-permute-start.38
  448.5 15.1 %attention_backward.3.b_ref = bf16[1024,768]{1,0:T(8,128)(2,1)S(1)} custom-call(bf16[1024,2048]{1,0:T(8,128)(2,1)} %get-tuple-element.467.qkv_ref, bf16[1024,1024]{1,0:T(8,128)(2,1)S(1)} %copy-done.1, bf16[512,384]{1,0:T(8,128)(2,1)S(1)} %fusion.32.gather_ref, f32[1024,128]{1,0:T(8,128)S(1)} %get-tuple-element.309.cos_ref, ...), custom_call_target="tpu_custom_call" | custom-call | flops 1 | bytes 1 | tf_op jit(solution)/shard_map/attention_backward/pallas_call | solution.py:153
  463.6 5.0 gradient_halves.3
  468.7 7.5 %gradient_halves.4 = bf16[2,4,96,1536]{3,2,1,0:T(8,128)(2,1)S(1)} custom-call(s32[1]{0:T(128)} %bitcast.17.core_ref, bf16[1024,1024]{1,0:T(8,128)(2,1)S(1)} %copy-done.3, bf16[1024,1536]{1,0:T(8,128)(2,1)} %copy-done.15), custom_call_target="tpu_custom_call" | custom-call | flops 1 | bytes 1 | tf_op jit(solution)/shard_map/gradient_halves/pallas_call | solution.py:404
  478.9 5.3 gradient_halves.5
  490.3 1.6 fusion.13
  493.4 3.0 collective-permute-start.44
  501.7 21.3 %collective-permute-done.44 = bf16[384,768]{1,0:T(8,128)(2,1)S(1)} collective-permute-done((bf16[384,768]{1,0:T(8,128)(2,1)S(1)}, bf16[384,768]{1,0:T(8,128)(2,1)S(1)}, u32[]{:S(2)}, u32[]{:S(2)}) %collective-permute-start.44) | collective-permute-done | bytes 589856 | tf_op jit(solution)/shard_map/ppermute | solution.py:476
  523.0 2.1 collective-permute-done.46
  529.6 2.0 add_convert_fusion
  533.7 2.2 collective-permute-start.51
  538.8 34.5 %collective-permute-done.50.refs_4_ = bf16[2,96,768]{2,1,0:T(8,128)(2,1)S(1)} collective-permute-done((bf16[2,96,768]{2,1,0:T(8,128)(2,1)S(1)}, bf16[2,96,768]{2,1,0:T(8,128)(2,1)S(1)}, u32[]{:S(2)}, u32[]{:S(2)}) %collective-permute-start.50) | collective-permute-done | bytes 294944 | tf_op jit(solution)/shard_map/ppermute | solution.py:476
  579.0 2.3 collective-permute-done.55
  582.3 2.7 collective-permute-done.56
  585.4 4.3 collective-permute-done.57
  592.2 6.8 %place.1 = (f32[12288,128]{1,0:T(8,128)}, f32[1024,768]{1,0:T(8,128)}) custom-call(bf16[2,2,384,768]{3,2,1,0:T(8,128)(2,1)S(1)} %get-tuple-element.589.refs_0_, bf16[2,2,384,768]{3,2,1,0:T(8,128)(2,1)S(1)} %get-tuple-element.588.refs_1_), custom_call_target="tpu_custom_call" | custom-call | flops 1 | bytes 1 | tf_op jit(solution)/shard_map/place/pallas_call | solution.py:272
  600.6 2.8 collective-permute-done.59
  604.3 2.0 place_attention.1
  (286 shorter events, 88.5 us)
Async XLA Ops:
  8.0 60.6 %collective-permute-start.3 = (bf16[512,1536]{1,0:T(8,128)(2,1)}, bf16[512,1536]{1,0:T(8,128)(2,1)}, u32[]{:S(2)}, u32[]{:S(2)}) collective-permute-start(bf16[512,1536]{1,0:T(8,128)(2,1)} %maximum_select_fusion.3.cot_ref), channel_id=1, source_target_pairs={{0,16},{8,24},{16,0},{24,8},{1,17},{9,25},{17,1},{25,9},{2,18},{10... | collective-permute-start | bytes 4718600 | tf_op jit(solution)/shard_map/ppermute | solution.py:463
  14.5 55.1 %collective-permute-start.4 = (bf16[512,1536]{1,0:T(8,128)(2,1)}, bf16[512,1536]{1,0:T(8,128)(2,1)}, u32[]{:S(2)}, u32[]{:S(2)}) collective-permute-start(bf16[512,1536]{1,0:T(8,128)(2,1)} %fusion.2), channel_id=1, source_target_pairs={{0,1},{1,0},{2,3},{3,2},{4,5},{5,4},{6,7},{7,6},{8,9},{9,8},{10,11... | collective-permute-start | bytes 4718600 | tf_op jit(solution)/shard_map/ppermute | solution.py:463
  21.6 47.0 %collective-permute-start.2 = (bf16[2,384,768]{2,1,0:T(8,128)(2,1)S(1)}, bf16[2,384,768]{2,1,0:T(8,128)(2,1)}, u32[]{:S(2)}, u32[]{:S(2)}) collective-permute-start(bf16[2,384,768]{2,1,0:T(8,128)(2,1)S(1)} %pad_maximum_fusion.5), channel_id=1, source_target_pairs={{0,4},{4,0},{1,5},{5,1},{2,6},{6,2},{3,7},{7,3},{8,12},{12,8},{9,1... | collective-permute-start | bytes 3538952 | tf_op jit(solution)/shard_map/ppermute | solution.py:476
  21.7 46.9 %collective-permute-start = (bf16[2,576,384]{2,1,0:T(8,128)(2,1)S(1)}, bf16[2,576,384]{2,1,0:T(8,128)(2,1)}, u32[]{:S(2)}, u32[]{:S(2)}) collective-permute-start(bf16[2,576,384]{2,1,0:T(8,128)(2,1)S(1)} %pad_maximum_fusion.8.refs_2_), channel_id=1, source_target_pairs={{0,2},{1,3},{2,0},{3,1},{4,6},{5,7},{6,4},{7,5},{8,10},{9,11},{10,... | collective-permute-start | bytes 2654216 | tf_op jit(solution)/shard_map/ppermute | solution.py:476
  24.3 44.3 %collective-permute-start.1 = (bf16[2,576,384]{2,1,0:T(8,128)(2,1)S(1)}, bf16[2,576,384]{2,1,0:T(8,128)(2,1)}, u32[]{:S(2)}, u32[]{:S(2)}) collective-permute-start(bf16[2,576,384]{2,1,0:T(8,128)(2,1)S(1)} %pad_maximum_fusion.8.refs_2_), channel_id=1, source_target_pairs={{0,4},{4,0},{1,5},{5,1},{2,6},{6,2},{3,7},{7,3},{8,12},{12,8},{9,1... | collective-permute-start | bytes 2654216 | tf_op jit(solution)/shard_map/ppermute | solution.py:476
  69.6 31.1 %collective-permute-start.5 = (bf16[2,576,384]{2,1,0:T(8,128)(2,1)}, bf16[2,576,384]{2,1,0:T(8,128)(2,1)}, u32[]{:S(2)}, u32[]{:S(2)}) collective-permute-start(bf16[2,576,384]{2,1,0:T(8,128)(2,1)} %collective-permute-done.refs_0_), channel_id=1, source_target_pairs={{0,4},{4,0},{1,5},{5,1},{2,6},{6,2},{3,7},{7,3},{8,12},{12,8},{9,1... | collective-permute-start | bytes 2654216 | tf_op jit(solution)/shard_map/ppermute | solution.py:476
  69.6 31.1 %collective-permute-start.6 = (bf16[2,576,384]{2,1,0:T(8,128)(2,1)S(1)}, bf16[2,576,384]{2,1,0:T(8,128)(2,1)S(1)}, u32[]{:S(2)}, u32[]{:S(2)}) collective-permute-start(bf16[2,576,384]{2,1,0:T(8,128)(2,1)S(1)} %pad_maximum_fusion.8.refs_2_), channel_id=1, source_target_pairs={{0,8},{8,0},{16,24},{24,16},{1,9},{9,1},{17,25},{25,17},{2,10},{10... | collective-permute-start | bytes 2654216 | tf_op jit(solution)/shard_map/ppermute | solution.py:463
  69.6 32.1 %collective-permute-start.7 = (bf16[2,576,384]{2,1,0:T(8,128)(2,1)}, bf16[2,576,384]{2,1,0:T(8,128)(2,1)}, u32[]{:S(2)}, u32[]{:S(2)}) collective-permute-start(bf16[2,576,384]{2,1,0:T(8,128)(2,1)} %collective-permute-done.1.refs_6_), channel_id=1, source_target_pairs={{0,8},{8,0},{16,24},{24,16},{1,9},{9,1},{17,25},{25,17},{2,10},{10... | collective-permute-start | bytes 2654216 | tf_op jit(solution)/shard_map/ppermute | solution.py:463
  70.6 18.2 %collective-permute-start.8 = (bf16[384,768]{1,0:T(8,128)(2,1)}, bf16[384,768]{1,0:T(8,128)(2,1)S(1)}, u32[]{:S(2)}, u32[]{:S(2)}) collective-permute-start(bf16[384,768]{1,0:T(8,128)(2,1)} %get-tuple-element.296), channel_id=1, source_target_pairs={{0,1},{1,2},{2,3},{3,0},{4,5},{5,6},{6,7},{7,4},{8,9},{9,10},{10,1... | collective-permute-start | bytes 1769480 | tf_op jit(solution)/shard_map/ppermute | solution.py:476
  73.4 27.3 %collective-permute-start.9 = (bf16[384,768]{1,0:T(8,128)(2,1)}, bf16[384,768]{1,0:T(8,128)(2,1)}, u32[]{:S(2)}, u32[]{:S(2)}) collective-permute-start(bf16[384,768]{1,0:T(8,128)(2,1)} %get-tuple-element.352), channel_id=1, source_target_pairs={{0,1},{1,2},{2,3},{3,0},{4,5},{5,6},{6,7},{7,4},{8,9},{9,10},{10,1... | collective-permute-start | bytes 1769480 | tf_op jit(solution)/shard_map/ppermute | solution.py:476
  101.7 5.1 collective-permute-start.10
  101.7 5.1 collective-permute-start.11
  102.2 42.0 %collective-permute-start.12 = (bf16[384,768]{1,0:T(8,128)(2,1)}, bf16[384,768]{1,0:T(8,128)(2,1)}, u32[]{:S(2)}, u32[]{:S(2)}) collective-permute-start(bf16[384,768]{1,0:T(8,128)(2,1)} %get-tuple-element.296), channel_id=1, source_target_pairs={{0,2},{1,3},{2,0},{3,1},{4,6},{5,7},{6,4},{7,5},{8,10},{9,11},{10,... | collective-permute-start | bytes 1769480 | tf_op jit(solution)/shard_map/ppermute | solution.py:476
  103.0 41.2 %collective-permute-start.13 = (bf16[384,768]{1,0:T(8,128)(2,1)}, bf16[384,768]{1,0:T(8,128)(2,1)}, u32[]{:S(2)}, u32[]{:S(2)}) collective-permute-start(bf16[384,768]{1,0:T(8,128)(2,1)} %get-tuple-element.296), channel_id=1, source_target_pairs={{0,3},{1,0},{2,1},{3,2},{4,7},{5,4},{6,5},{7,6},{8,11},{9,8},{10,9... | collective-permute-start | bytes 1769480 | tf_op jit(solution)/shard_map/ppermute | solution.py:476
  114.4 29.8 %copy-start.40 = (bf16[1024,1536]{1,0:T(8,128)(2,1)S(1)}, bf16[1024,1536]{1,0:T(8,128)(2,1)}, u32[]{:S(2)}) copy-start(bf16[1024,1536]{1,0:T(8,128)(2,1)} %get-tuple-element.324) | copy-start | bytes 9437188
  149.3 41.5 %copy-start.9 = (bf16[512,1536]{1,0:T(8,128)(2,1)S(1)}, bf16[512,1536]{1,0:T(8,128)(2,1)}, u32[]{:S(2)}) copy-start(bf16[512,1536]{1,0:T(8,128)(2,1)} %copy-done.8) | copy-start | bytes 4718596
  149.5 41.2 %copy-start.11 = (bf16[4,384,768]{2,1,0:T(8,128)(2,1)}, bf16[4,384,768]{2,1,0:T(8,128)(2,1)S(1)}, u32[]{:S(2)}) copy-start(bf16[4,384,768]{2,1,0:T(8,128)(2,1)S(1)} %pad_maximum_fusion.refs_0_) | copy-start | bytes 7077892
  149.6 41.2 %collective-permute-start.16 = (bf16[4,384,768]{2,1,0:T(8,128)(2,1)S(1)}, bf16[4,384,768]{2,1,0:T(8,128)(2,1)}, u32[]{:S(2)}, u32[]{:S(2)}) collective-permute-start(bf16[4,384,768]{2,1,0:T(8,128)(2,1)S(1)} %pad_maximum_fusion.refs_0_), channel_id=1, source_target_pairs={{0,8},{8,0},{16,24},{24,16},{1,9},{9,1},{17,25},{25,17},{2,10},{10... | collective-permute-start | bytes 7077896 | tf_op jit(solution)/shard_map/ppermute | solution.py:463
  149.6 41.1 %collective-permute-start.15 = (bf16[3,384,768]{2,1,0:T(8,128)(2,1)S(1)}, bf16[3,384,768]{2,1,0:T(8,128)(2,1)S(1)}, u32[]{:S(2)}, u32[]{:S(2)}) collective-permute-start(bf16[3,384,768]{2,1,0:T(8,128)(2,1)S(1)} %pad_maximum_fusion.4), channel_id=1, source_target_pairs={{0,4},{4,0},{1,5},{5,1},{2,6},{6,2},{3,7},{7,3},{8,12},{12,8},{9,1... | collective-permute-start | bytes 5308424 | tf_op jit(solution)/shard_map/ppermute | solution.py:476
  151.6 36.5 %collective-permute-start.14 = (bf16[512,1536]{1,0:T(8,128)(2,1)S(1)}, bf16[512,1536]{1,0:T(8,128)(2,1)S(1)}, u32[]{:S(2)}, u32[]{:S(2)}) collective-permute-start(bf16[512,1536]{1,0:T(8,128)(2,1)S(1)} %convolution_convert_fusion), channel_id=1, source_target_pairs={{0,1},{1,0},{2,3},{3,2},{4,5},{5,4},{6,7},{7,6},{8,9},{9,8},{10,11... | collective-permute-start | bytes 4718600 | tf_op jit(solution)/shard_map/ppermute | solution.py:463
  194.3 6.6 %collective-permute-start.17 = (bf16[4,384,768]{2,1,0:T(8,128)(2,1)S(1)}, bf16[4,384,768]{2,1,0:T(8,128)(2,1)}, u32[]{:S(2)}, u32[]{:S(2)}) collective-permute-start(bf16[4,384,768]{2,1,0:T(8,128)(2,1)S(1)} %pad_maximum_fusion.1.refs_1_), channel_id=1, source_target_pairs={{0,8},{8,0},{16,24},{24,16},{1,9},{9,1},{17,25},{25,17},{2,10},{10... | collective-permute-start | bytes 7077896 | tf_op jit(solution)/shard_map/ppermute | solution.py:463
  194.3 36.9 %collective-permute-start.21 = (bf16[512,1536]{1,0:T(8,128)(2,1)S(1)}, bf16[512,1536]{1,0:T(8,128)(2,1)}, u32[]{:S(2)}, u32[]{:S(2)}) collective-permute-start(bf16[512,1536]{1,0:T(8,128)(2,1)S(1)} %multiply_convert_fusion.n2_ref), channel_id=1, source_target_pairs={{0,16},{8,24},{16,0},{24,8},{1,17},{9,25},{17,1},{25,9},{2,18},{10... | collective-permute-start | bytes 4718600 | tf_op jit(solution)/shard_map/ppermute | solution.py:463
  195.1 32.5 %collective-permute-start.18 = (bf16[384,768]{1,0:T(8,128)(2,1)}, bf16[384,768]{1,0:T(8,128)(2,1)}, u32[]{:S(2)}, u32[]{:S(2)}) collective-permute-start(bf16[384,768]{1,0:T(8,128)(2,1)} %collective-permute-done.9), channel_id=1, source_target_pairs={{0,4},{4,0},{1,5},{5,1},{2,6},{6,2},{3,7},{7,3},{8,12},{12,8},{9,1... | collective-permute-start | bytes 1769480 | tf_op jit(solution)/shard_map/ppermute | solution.py:476
  196.9 30.7 %collective-permute-start.19 = (bf16[384,768]{1,0:T(8,128)(2,1)}, bf16[384,768]{1,0:T(8,128)(2,1)}, u32[]{:S(2)}, u32[]{:S(2)}) collective-permute-start(bf16[384,768]{1,0:T(8,128)(2,1)} %get-tuple-element.352), channel_id=1, source_target_pairs={{0,2},{1,3},{2,0},{3,1},{4,6},{5,7},{6,4},{7,5},{8,10},{9,11},{10,... | collective-permute-start | bytes 1769480 | tf_op jit(solution)/shard_map/ppermute | solution.py:476
  197.5 30.1 %collective-permute-start.20 = (bf16[384,768]{1,0:T(8,128)(2,1)}, bf16[384,768]{1,0:T(8,128)(2,1)}, u32[]{:S(2)}, u32[]{:S(2)}) collective-permute-start(bf16[384,768]{1,0:T(8,128)(2,1)} %get-tuple-element.352), channel_id=1, source_target_pairs={{0,3},{1,0},{2,1},{3,2},{4,7},{5,4},{6,5},{7,6},{8,11},{9,8},{10,9... | collective-permute-start | bytes 1769480 | tf_op jit(solution)/shard_map/ppermute | solution.py:476
  235.7 30.6 %collective-permute-start.23 = (bf16[4,384,768]{2,1,0:T(8,128)(2,1)}, bf16[4,384,768]{2,1,0:T(8,128)(2,1)}, u32[]{:S(2)}, u32[]{:S(2)}) collective-permute-start(bf16[4,384,768]{2,1,0:T(8,128)(2,1)} %pad_maximum_fusion.2.refs_0_), channel_id=1, source_target_pairs={{0,8},{8,0},{16,24},{24,16},{1,9},{9,1},{17,25},{25,17},{2,10},{10... | collective-permute-start | bytes 7077896 | tf_op jit(solution)/shard_map/ppermute | solution.py:463
  235.7 30.6 %collective-permute-start.22 = (bf16[2,384,768]{2,1,0:T(8,128)(2,1)S(1)}, bf16[2,384,768]{2,1,0:T(8,128)(2,1)}, u32[]{:S(2)}, u32[]{:S(2)}) collective-permute-start(bf16[2,384,768]{2,1,0:T(8,128)(2,1)S(1)} %pad_maximum_fusion.6), channel_id=1, source_target_pairs={{0,4},{4,0},{1,5},{5,1},{2,6},{6,2},{3,7},{7,3},{8,12},{12,8},{9,1... | collective-permute-start | bytes 3538952 | tf_op jit(solution)/shard_map/ppermute | solution.py:476
  269.2 4.6 collective-permute-start.24
  269.6 7.6 %collective-permute-start.25 = (bf16[4,384,768]{2,1,0:T(8,128)(2,1)S(1)}, bf16[4,384,768]{2,1,0:T(8,128)(2,1)S(1)}, u32[]{:S(2)}, u32[]{:S(2)}) collective-permute-start(bf16[4,384,768]{2,1,0:T(8,128)(2,1)S(1)} %copy-done.43), channel_id=1, source_target_pairs={{0,8},{8,0},{16,24},{24,16},{1,9},{9,1},{17,25},{25,17},{2,10},{10... | collective-permute-start | bytes 7077896 | tf_op jit(solution)/shard_map/ppermute | solution.py:463
  279.0 28.5 %collective-permute-start.27 = (bf16[4,384,768]{2,1,0:T(8,128)(2,1)}, bf16[4,384,768]{2,1,0:T(8,128)(2,1)}, u32[]{:S(2)}, u32[]{:S(2)}) collective-permute-start(bf16[4,384,768]{2,1,0:T(8,128)(2,1)} %get-tuple-element.409), channel_id=1, source_target_pairs={{0,8},{8,0},{16,24},{24,16},{1,9},{9,1},{17,25},{25,17},{2,10},{10... | collective-permute-start | bytes 7077896 | tf_op jit(solution)/shard_map/ppermute | solution.py:463
  279.3 28.3 %collective-permute-start.26 = (bf16[2,384,768]{2,1,0:T(8,128)(2,1)S(1)}, bf16[2,384,768]{2,1,0:T(8,128)(2,1)}, u32[]{:S(2)}, u32[]{:S(2)}) collective-permute-start(bf16[2,384,768]{2,1,0:T(8,128)(2,1)S(1)} %add_convert_fusion.6), channel_id=1, source_target_pairs={{0,4},{4,0},{1,5},{5,1},{2,6},{6,2},{3,7},{7,3},{8,12},{12,8},{9,1... | collective-permute-start | bytes 3538952 | tf_op jit(solution)/shard_map/ppermute | solution.py:476
  315.2 37.1 %collective-permute-start.30 = (bf16[512,1536]{1,0:T(8,128)(2,1)}, bf16[512,1536]{1,0:T(8,128)(2,1)S(1)}, u32[]{:S(2)}, u32[]{:S(2)}) collective-permute-start(bf16[512,1536]{1,0:T(8,128)(2,1)} %add_convert_fusion.2), channel_id=1, source_target_pairs={{0,16},{8,24},{16,0},{24,8},{1,17},{9,25},{17,1},{25,9},{2,18},{10... | collective-permute-start | bytes 4718600 | tf_op jit(solution)/shard_map/ppermute | solution.py:463
  316.0 36.3 %collective-permute-start.28 = (bf16[2,384,768]{2,1,0:T(8,128)(2,1)}, bf16[2,384,768]{2,1,0:T(8,128)(2,1)}, u32[]{:S(2)}, u32[]{:S(2)}) collective-permute-start(bf16[2,384,768]{2,1,0:T(8,128)(2,1)} %add_convert_fusion.5), channel_id=1, source_target_pairs={{0,4},{4,0},{1,5},{5,1},{2,6},{6,2},{3,7},{7,3},{8,12},{12,8},{9,1... | collective-permute-start | bytes 3538952 | tf_op jit(solution)/shard_map/ppermute | solution.py:476
  316.9 35.4 %collective-permute-start.29 = (bf16[384,768]{1,0:T(8,128)(2,1)}, bf16[384,768]{1,0:T(8,128)(2,1)}, u32[]{:S(2)}, u32[]{:S(2)}) collective-permute-start(bf16[384,768]{1,0:T(8,128)(2,1)} %get-tuple-element.439), channel_id=1, source_target_pairs={{0,2},{1,3},{2,0},{3,1},{4,6},{5,7},{6,4},{7,5},{8,10},{9,11},{10,... | collective-permute-start | bytes 1769480 | tf_op jit(solution)/shard_map/ppermute | solution.py:476
  352.3 23.1 %collective-permute-start.31 = (bf16[4,384,768]{2,1,0:T(8,128)(2,1)}, bf16[4,384,768]{2,1,0:T(8,128)(2,1)S(1)}, u32[]{:S(2)}, u32[]{:S(2)}) collective-permute-start(bf16[4,384,768]{2,1,0:T(8,128)(2,1)} %get-tuple-element.442), channel_id=1, source_target_pairs={{0,8},{8,0},{16,24},{24,16},{1,9},{9,1},{17,25},{25,17},{2,10},{10... | collective-permute-start | bytes 7077896 | tf_op jit(solution)/shard_map/ppermute | solution.py:463
  354.7 20.7 %collective-permute-start.32 = (bf16[384,768]{1,0:T(8,128)(2,1)}, bf16[384,768]{1,0:T(8,128)(2,1)S(1)}, u32[]{:S(2)}, u32[]{:S(2)}) collective-permute-start(bf16[384,768]{1,0:T(8,128)(2,1)} %get-tuple-element.451), channel_id=1, source_target_pairs={{0,3},{1,0},{2,1},{3,2},{4,7},{5,4},{6,5},{7,6},{8,11},{9,8},{10,9... | collective-permute-start | bytes 1769480 | tf_op jit(solution)/shard_map/ppermute | solution.py:476
  375.4 36.9 %collective-permute-start.34 = (bf16[4,384,768]{2,1,0:T(8,128)(2,1)S(1)}, bf16[4,384,768]{2,1,0:T(8,128)(2,1)S(1)}, u32[]{:S(2)}, u32[]{:S(2)}) collective-permute-start(bf16[4,384,768]{2,1,0:T(8,128)(2,1)S(1)} %copy-done.42), channel_id=1, source_target_pairs={{0,8},{8,0},{16,24},{24,16},{1,9},{9,1},{17,25},{25,17},{2,10},{10... | collective-permute-start | bytes 7077896 | tf_op jit(solution)/shard_map/ppermute | solution.py:463
  376.2 36.0 %collective-permute-start.33 = (bf16[512,1536]{1,0:T(8,128)(2,1)S(1)}, bf16[512,1536]{1,0:T(8,128)(2,1)S(1)}, u32[]{:S(2)}, u32[]{:S(2)}) collective-permute-start(bf16[512,1536]{1,0:T(8,128)(2,1)S(1)} %get-tuple-element.468), channel_id=1, source_target_pairs={{0,1},{1,0},{2,3},{3,2},{4,5},{5,4},{6,7},{7,6},{8,9},{9,8},{10,11... | collective-permute-start | bytes 4718600 | tf_op jit(solution)/shard_map/ppermute | solution.py:463
  377.9 27.4 %collective-permute-start.35 = (bf16[2,384,768]{2,1,0:T(8,128)(2,1)S(1)}, bf16[2,384,768]{2,1,0:T(8,128)(2,1)S(1)}, u32[]{:S(2)}, u32[]{:S(2)}) collective-permute-start(bf16[2,384,768]{2,1,0:T(8,128)(2,1)S(1)} %add_convert_fusion.4), channel_id=1, source_target_pairs={{0,4},{4,0},{1,5},{5,1},{2,6},{6,2},{3,7},{7,3},{8,12},{12,8},{9,1... | collective-permute-start | bytes 3538952 | tf_op jit(solution)/shard_map/ppermute | solution.py:476
  412.3 23.8 %collective-permute-start.36 = (bf16[384,768]{1,0:T(8,128)(2,1)}, bf16[384,768]{1,0:T(8,128)(2,1)}, u32[]{:S(2)}, u32[]{:S(2)}) collective-permute-start(bf16[384,768]{1,0:T(8,128)(2,1)} %get-tuple-element.474), channel_id=1, source_target_pairs={{0,1},{1,2},{2,3},{3,0},{4,5},{5,6},{6,7},{7,4},{8,9},{9,10},{10,1... | collective-permute-start | bytes 1769480 | tf_op jit(solution)/shard_map/ppermute | solution.py:476
  413.6 26.8 %collective-permute-start.37 = (bf16[2,384,768]{2,1,0:T(8,128)(2,1)}, bf16[2,384,768]{2,1,0:T(8,128)(2,1)}, u32[]{:S(2)}, u32[]{:S(2)}) collective-permute-start(bf16[2,384,768]{2,1,0:T(8,128)(2,1)} %add_convert_fusion.3), channel_id=1, source_target_pairs={{0,4},{4,0},{1,5},{5,1},{2,6},{6,2},{3,7},{7,3},{8,12},{12,8},{9,1... | collective-permute-start | bytes 3538952 | tf_op jit(solution)/shard_map/ppermute | solution.py:476
  414.3 61.8 %collective-permute-start.40 = (bf16[512,1536]{1,0:T(8,128)(2,1)}, bf16[512,1536]{1,0:T(8,128)(2,1)}, u32[]{:S(2)}, u32[]{:S(2)}) collective-permute-start(bf16[512,1536]{1,0:T(8,128)(2,1)} %add_convert_fusion.1), channel_id=1, source_target_pairs={{0,16},{8,24},{16,0},{24,8},{1,17},{9,25},{17,1},{25,9},{2,18},{10... | collective-permute-start | bytes 4718600 | tf_op jit(solution)/shard_map/ppermute | solution.py:463
  443.7 32.4 %collective-permute-start.38 = (bf16[384,768]{1,0:T(8,128)(2,1)}, bf16[384,768]{1,0:T(8,128)(2,1)}, u32[]{:S(2)}, u32[]{:S(2)}) collective-permute-start(bf16[384,768]{1,0:T(8,128)(2,1)} %get-tuple-element.484), channel_id=1, source_target_pairs={{0,3},{1,0},{2,1},{3,2},{4,7},{5,4},{6,5},{7,6},{8,11},{9,8},{10,9... | collective-permute-start | bytes 1769480 | tf_op jit(solution)/shard_map/ppermute | solution.py:476
  446.9 29.3 %collective-permute-start.39 = (bf16[384,768]{1,0:T(8,128)(2,1)}, bf16[384,768]{1,0:T(8,128)(2,1)}, u32[]{:S(2)}, u32[]{:S(2)}) collective-permute-start(bf16[384,768]{1,0:T(8,128)(2,1)} %get-tuple-element.486), channel_id=1, source_target_pairs={{0,1},{1,2},{2,3},{3,0},{4,5},{5,6},{6,7},{7,4},{8,9},{9,10},{10,1... | collective-permute-start | bytes 1769480 | tf_op jit(solution)/shard_map/ppermute | solution.py:476
  477.3 11.4 %collective-permute-start.41 = (bf16[2,384,768]{2,1,0:T(8,128)(2,1)}, bf16[2,384,768]{2,1,0:T(8,128)(2,1)}, u32[]{:S(2)}, u32[]{:S(2)}) collective-permute-start(bf16[2,384,768]{2,1,0:T(8,128)(2,1)} %slice_bitcast_fusion.2), channel_id=1, source_target_pairs={{0,8},{8,0},{16,24},{24,16},{1,9},{9,1},{17,25},{25,17},{2,10},{10... | collective-permute-start | bytes 3538952 | tf_op jit(solution)/shard_map/ppermute | solution.py:463
  478.4 10.3 %collective-permute-start.42 = (bf16[4,96,1536]{2,1,0:T(8,128)(2,1)}, bf16[4,96,1536]{2,1,0:T(8,128)(2,1)}, u32[]{:S(2)}, u32[]{:S(2)}) collective-permute-start(bf16[4,96,1536]{2,1,0:T(8,128)(2,1)} %slice_bitcast_fusion.1), channel_id=1, source_target_pairs={{0,8},{8,0},{16,24},{24,16},{1,9},{9,1},{17,25},{25,17},{2,10},{10... | collective-permute-start | bytes 3538952 | tf_op jit(solution)/shard_map/ppermute | solution.py:463
  492.0 33.1 %collective-permute-start.43 = (bf16[256,1536]{1,0:T(8,128)(2,1)S(1)}, bf16[256,1536]{1,0:T(8,128)(2,1)S(1)}, u32[]{:S(2)}, u32[]{:S(2)}) collective-permute-start(bf16[256,1536]{1,0:T(8,128)(2,1)S(1)} %slice.320), channel_id=1, source_target_pairs={{0,1},{1,0},{2,3},{3,2},{4,5},{5,4},{6,7},{7,6},{8,9},{9,8},{10,11... | collective-permute-start | bytes 2359304 | tf_op jit(solution)/shard_map/ppermute | solution.py:463
  493.4 29.6 %collective-permute-start.44 = (bf16[384,768]{1,0:T(8,128)(2,1)S(1)}, bf16[384,768]{1,0:T(8,128)(2,1)S(1)}, u32[]{:S(2)}, u32[]{:S(2)}) collective-permute-start(bf16[384,768]{1,0:T(8,128)(2,1)S(1)} %copy-done.33), channel_id=1, source_target_pairs={{0,2},{1,3},{2,0},{3,1},{4,6},{5,7},{6,4},{7,5},{8,10},{9,11},{10,... | collective-permute-start | bytes 1769480 | tf_op jit(solution)/shard_map/ppermute | solution.py:476
  496.5 28.6 %collective-permute-start.47 = (bf16[2,384,768]{2,1,0:T(8,128)(2,1)S(1)}, bf16[2,384,768]{2,1,0:T(8,128)(2,1)S(1)}, u32[]{:S(2)}, u32[]{:S(2)}) collective-permute-start(bf16[2,384,768]{2,1,0:T(8,128)(2,1)S(1)} %slice_bitcast_fusion), channel_id=1, source_target_pairs={{0,8},{8,0},{16,24},{24,16},{1,9},{9,1},{17,25},{25,17},{2,10},{10... | collective-permute-start | bytes 3538952 | tf_op jit(solution)/shard_map/ppermute | solution.py:463
  496.7 26.3 %collective-permute-start.45 = (bf16[384,768]{1,0:T(8,128)(2,1)S(1)}, bf16[384,768]{1,0:T(8,128)(2,1)S(1)}, u32[]{:S(2)}, u32[]{:S(2)}) collective-permute-start(bf16[384,768]{1,0:T(8,128)(2,1)S(1)} %get-tuple-element.620), channel_id=1, source_target_pairs={{0,4},{4,0},{1,5},{5,1},{2,6},{6,2},{3,7},{7,3},{8,12},{12,8},{9,1... | collective-permute-start | bytes 1769480 | tf_op jit(solution)/shard_map/ppermute | solution.py:476
  497.4 27.6 %collective-permute-start.46 = (bf16[4,96,768]{2,1,0:T(8,128)(2,1)S(1)}, bf16[4,96,768]{2,1,0:T(8,128)(2,1)S(1)}, u32[]{:S(2)}, u32[]{:S(2)}) collective-permute-start(bf16[4,96,768]{2,1,0:T(8,128)(2,1)S(1)} %get-tuple-element.618), channel_id=1, source_target_pairs={{0,4},{4,0},{1,5},{5,1},{2,6},{6,2},{3,7},{7,3},{8,12},{12,8},{9,1... | collective-permute-start | bytes 1769480 | tf_op jit(solution)/shard_map/ppermute | solution.py:476
  528.0 45.3 %collective-permute-start.52 = (bf16[2,384,768]{2,1,0:T(8,128)(2,1)S(1)}, bf16[2,384,768]{2,1,0:T(8,128)(2,1)S(1)}, u32[]{:S(2)}, u32[]{:S(2)}) collective-permute-start(bf16[2,384,768]{2,1,0:T(8,128)(2,1)S(1)} %pad_maximum_fusion.7), channel_id=1, source_target_pairs={{0,16},{8,24},{16,0},{24,8},{1,17},{9,25},{17,1},{25,9},{2,18},{10... | collective-permute-start | bytes 3538952 | tf_op jit(solution)/shard_map/ppermute | solution.py:463
  531.7 41.6 %collective-permute-start.48 = (bf16[384,768]{1,0:T(8,128)(2,1)S(1)}, bf16[384,768]{1,0:T(8,128)(2,1)S(1)}, u32[]{:S(2)}, u32[]{:S(2)}) collective-permute-start(bf16[384,768]{1,0:T(8,128)(2,1)S(1)} %get-tuple-element.616), channel_id=1, source_target_pairs={{0,4},{4,0},{1,5},{5,1},{2,6},{6,2},{3,7},{7,3},{8,12},{12,8},{9,1... | collective-permute-start | bytes 1769480 | tf_op jit(solution)/shard_map/ppermute | solution.py:476
  532.4 40.9 %collective-permute-start.49 = (bf16[384,768]{1,0:T(8,128)(2,1)S(1)}, bf16[384,768]{1,0:T(8,128)(2,1)S(1)}, u32[]{:S(2)}, u32[]{:S(2)}) collective-permute-start(bf16[384,768]{1,0:T(8,128)(2,1)S(1)} %add_convert_fusion.10), channel_id=1, source_target_pairs={{0,2},{1,3},{2,0},{3,1},{4,6},{5,7},{6,4},{7,5},{8,10},{9,11},{10,... | collective-permute-start | bytes 1769480 | tf_op jit(solution)/shard_map/ppermute | solution.py:476
  533.7 39.5 %collective-permute-start.51 = (bf16[256,1536]{1,0:T(8,128)(2,1)S(1)}, bf16[256,1536]{1,0:T(8,128)(2,1)S(1)}, u32[]{:S(2)}, u32[]{:S(2)}) collective-permute-start(bf16[256,1536]{1,0:T(8,128)(2,1)S(1)} %slice.330), channel_id=1, source_target_pairs={{0,1},{1,0},{2,3},{3,2},{4,5},{5,4},{6,7},{7,6},{8,9},{9,8},{10,11... | collective-permute-start | bytes 2359304 | tf_op jit(solution)/shard_map/ppermute | solution.py:463
  536.0 37.2 %collective-permute-start.50 = (bf16[2,96,768]{2,1,0:T(8,128)(2,1)S(1)}, bf16[2,96,768]{2,1,0:T(8,128)(2,1)S(1)}, u32[]{:S(2)}, u32[]{:S(2)}) collective-permute-start(bf16[2,96,768]{2,1,0:T(8,128)(2,1)S(1)} %slice.329), channel_id=1, source_target_pairs={{0,2},{1,3},{2,0},{3,1},{4,6},{5,7},{6,4},{7,5},{8,10},{9,11},{10,... | collective-permute-start | bytes 884744 | tf_op jit(solution)/shard_map/ppermute | solution.py:476
  573.6 25.4 %collective-permute-start.53 = (bf16[2,576,384]{2,1,0:T(8,128)(2,1)S(1)}, bf16[2,576,384]{2,1,0:T(8,128)(2,1)S(1)}, u32[]{:S(2)}, u32[]{:S(2)}) collective-permute-start(bf16[2,576,384]{2,1,0:T(8,128)(2,1)S(1)} %combine.1), channel_id=1, source_target_pairs={{0,16},{8,24},{16,0},{24,8},{1,17},{9,25},{17,1},{25,9},{2,18},{10... | collective-permute-start | bytes 2654216 | tf_op jit(solution)/shard_map/ppermute | solution.py:463
  575.2 16.1 %collective-permute-start.54 = (bf16[2,2,384,768]{3,2,1,0:T(8,128)(2,1)S(1)}, bf16[2,2,384,768]{3,2,1,0:T(8,128)(2,1)S(1)}, u32[]{:S(2)}, u32[]{:S(2)}) collective-permute-start(bf16[2,2,384,768]{3,2,1,0:T(8,128)(2,1)S(1)} %maximum_select_fusion.2), channel_id=1, source_target_pairs={{0,8},{8,0},{16,24},{24,16},{1,9},{9,1},{17,25},{25,17},{2,10},{10... | collective-permute-start | bytes 7077896 | tf_op jit(solution)/shard_map/ppermute | solution.py:463
  577.5 3.8 collective-permute-start.55
  581.3 3.8 collective-permute-start.56
  585.0 4.7 collective-permute-start.57
  589.7 1.6 collective-permute-start.58
  599.2 4.9 collective-permute-start.60
  599.8 3.7 collective-permute-start.59
  (43 other events, 214.0 us)

commit v4 on v3

--- a/solution.py
+++ b/solution.py
@@ -42,15 +42,15 @@
     return lax.dot_general(a, b, (((0,), (0,)), ((), ())), preferred_element_type=F32)
 
 
-def scores_t(keys, queries, block):
+def exponentials_t(keys, queries, block):
     s = dot_nt(keys, queries)
-    length = s.shape[0]
-    key_pos = lax.broadcasted_iota(jnp.int32, s.shape, 0)
-    query_pos = lax.broadcasted_iota(jnp.int32, s.shape, 1) + block * BLOCK
-    s = jnp.where(key_pos <= query_pos, s, -1e30)
+    here = s[block * BLOCK :]
+    later = lax.broadcasted_iota(jnp.int32, here.shape, 0) > lax.broadcasted_iota(jnp.int32, here.shape, 1)
+    here = jnp.where(later, -1e30, here)
+    s = jnp.concatenate([s[: block * BLOCK], here], axis=0) if block else here
     top = jnp.max(s, axis=0, keepdims=True)
     e = jnp.exp2((s - top) * (SCALE * math.log2(math.e)))
-    return e * (1.0 / jnp.sum(e, axis=0, keepdims=True))
+    return e, 1.0 / jnp.sum(e, axis=0, keepdims=True)
 
 
 def attention_forward_kernel(n1_ref, w_ref, spread_ref, cos_ref, sin_ref, qkv_ref, o_ref):
@@ -68,8 +68,8 @@
         for block in range(SEQUENCE_TOKENS // BLOCK):
             rows = slice(block * BLOCK, (block + 1) * BLOCK)
             length = (block + 1) * BLOCK
-            p = scores_t(qkv_ref[:length, 2 * LANES : 3 * LANES], qkv_ref[rows, lanes], block)
-            o_t = dot(v_t[:, :length], p.astype(BF))
+            e, inverse = exponentials_t(qkv_ref[:length, 2 * LANES : 3 * LANES], qkv_ref[rows, lanes], block)
+            o_t = dot(v_t[:, :length], e.astype(BF)) * inverse
             o_ref[rows, lanes] = o_t.T.astype(BF)
 
 
@@ -90,7 +90,8 @@
             length = (block + 1) * BLOCK
             q = qkv_ref[rows, lanes]
             do = do_ref[rows, lanes]
-            p = scores_t(qkv_ref[:length, 2 * LANES : 3 * LANES], q, block)
+            e, inverse = exponentials_t(qkv_ref[:length, 2 * LANES : 3 * LANES], q, block)
+            p = e * inverse
             dp = dot_nt(qkv_ref[:length, 3 * LANES :], do)
             ds = (p * (dp - jnp.sum(p * dp, axis=0, keepdims=True))).astype(BF)
             dv_ref[:length, :] += dot(p.astype(BF), do)
@@ -175,7 +176,7 @@
 
 
 def feedforward_kernel(col_step, sub, rows_of, n2_ref, cot_ref, *refs):
-    *blocks, out_ref, dn2_ref, h_ref, dgu_ref = refs
+    *blocks, out_bf_ref, dn2_bf_ref, out_ref, dn2_ref, h_ref, dgu_ref = refs
     sides = [blocks[k : k + rows_of] for k in range(0, len(blocks), rows_of)]
     weights, earlier, grads = sides[:2], sides[2:-2], sides[-2:]
     step, half = pl.program_id(0), pl.num_programs(0) // 2
@@ -221,6 +222,11 @@
     pl.when(step < half)(lambda: work(1))
     pl.when(step >= half)(lambda: work(0))
 
+    @pl.when(step == 2 * half - 1)
+    def _():
+        out_bf_ref[...] = out_ref[...].astype(BF)
+        dn2_bf_ref[...] = dn2_ref[...].astype(BF)
+
 
 def feedforward(n2, cot, weights, col_step, earlier=()):
     tokens, model = n2.shape
@@ -233,7 +239,7 @@
     flat = [a for side in weights for a in side]
     specs = [pl.BlockSpec((col_step, rows, width), place[whose]) for whose in range(2) for _ in range(rows_of)]
     earlier = [a for side in earlier for a in side]
-    total = jax.ShapeDtypeStruct((tokens, model), F32)
+    total = jax.ShapeDtypeStruct((tokens, model), BF)
     outs = pl.pallas_call(
         functools.partial(feedforward_kernel, col_step, sub, rows_of),
         grid=(2 * half,),
@@ -241,6 +247,8 @@
         out_specs=specs + [once(total), once(total)],
         out_shape=[jax.ShapeDtypeStruct(a.shape, BF) for a in flat] + [total, total],
         scratch_shapes=[
+            pltpu.VMEM((tokens, model), F32),
+            pltpu.VMEM((tokens, model), F32),
             pltpu.VMEM((tokens, col_step * sub), BF),
             pltpu.VMEM((tokens, 2 * col_step * sub), BF),
         ],
@@ -430,6 +438,46 @@
     return r * scaled - field * (r * r * r * inner), jnp.sum(grad * field * r, axis=0)
 
 
+def norm_back_kernel(field_ref, gain_ref, skip_ref, *refs):
+    *terms, out_ref, rounded_ref, gain_grad_ref = refs
+    field = field_ref[...]
+    grad = sum(t[...].astype(F32) for t in terms)
+    r = inverse_rms(field)
+    scaled = gain_ref[...] * grad
+    inner = jnp.mean(field * scaled, axis=-1, keepdims=True)
+    out = skip_ref[...].astype(F32) + r * scaled - field * (r * r * r * inner)
+    out_ref[...] = out
+    rounded_ref[...] = out.astype(BF)
+
+    @pl.when(pl.program_id(0) == 0)
+    def _():
+        gain_grad_ref[...] = jnp.zeros_like(gain_grad_ref)
+
+    gain_grad_ref[...] += jnp.sum(grad * (field * r), axis=0, keepdims=True)
+
+
+def norm_back_rows(field, gain, skip, terms):
+    tokens, model = field.shape
+    rows = 128
+    block = pl.BlockSpec((rows, model), lambda i: (i, 0))
+    line = pl.BlockSpec((1, model), lambda i: (0, 0))
+    out, rounded, gain_grad = pl.pallas_call(
+        norm_back_kernel,
+        grid=(tokens // rows,),
+        in_specs=[block, line, block] + [block] * len(terms),
+        out_specs=[block, block, line],
+        out_shape=[
+            jax.ShapeDtypeStruct(field.shape, F32),
+            jax.ShapeDtypeStruct(field.shape, BF),
+            jax.ShapeDtypeStruct((1, model), F32),
+        ],
+        compiler_params=pltpu.CompilerParams(vmem_limit_bytes=60 * 1024 * 1024),
+        cost_estimate=QUICK,
+        name="norm_back",
+    )(field, gain[None], skip, *terms)
+    return out, rounded, gain_grad[0]
+
+
 def halves(first_is_mine, mine, other, axis):
     return jnp.where(
         first_is_mine, jnp.concatenate([mine, other], axis), jnp.concatenate([other, mine], axis)
@@ -541,9 +589,6 @@
         start = ((2 * y + core) * PARTS + part) * sub
         gate_up = lax.dynamic_slice_in_dim(gate_up_weight, start, sub, 2).transpose(1, 2, 0).reshape(2 * sub, block)
         pieces.append(jnp.concatenate([gate_up, lax.dynamic_slice_in_dim(down_weight, start, sub, 0)]))
-    own_rows = gather_rows(jnp.stack(pieces))
-    grad_out = rel(cotangent)
-    grad_out_other = to_y(grad_out)
     gain_one, gain_two = rel(attention_gain), rel(feedforward_gain)
     inputs = rel(tokens)
     wide_inputs = inputs.astype(F32)
@@ -552,8 +597,8 @@
     tables = rotary_tables()
     spread = spread_matrix()
     spread_back = spread.T
-    far_packed, own_packed, own_rows, pieces, grad_out, grad_out_other, inputs, normed, normed_other, tables = fence(
-        (far_packed, own_packed, own_rows, pieces, grad_out, grad_out_other, inputs, normed, normed_other, tables)
+    far_packed, own_packed, pieces, inputs, normed, normed_other, tables = fence(
+        (far_packed, own_packed, pieces, inputs, normed, normed_other, tables)
     )
 
     far_rows = gather_rows(far_packed)
@@ -561,9 +606,12 @@
     others = [shift(pieces[0], "col", 1)]
     late_others = [shift(pieces[1], "col", 1)]
     normed_all = in_sequence(normed, normed_other)
-    far_rows, own_cores, own_packed, others, late_others, normed_all, spread, spread_back = fence(
-        (far_rows, own_cores, own_packed, others, late_others, normed_all, spread, spread_back)
-    )
+    grad_out = rel(cotangent)
+    far_rows, own_cores, own_packed, others, late_others, normed_all, spread, spread_back, grad_out, pieces = fence(
+        (far_rows, own_cores, own_packed, others, late_others, normed_all, spread, spread_back, grad_out, pieces)
+    )
+    own_rows = gather_rows(jnp.stack(pieces))
+    rest_near = gather_rows(others[0])
     far_cores = [to_core(a) for a in far_rows]
     others += [shift(pieces[0], "col", j) for j in range(2, col_size)]
     split = block // 2
@@ -586,29 +634,30 @@
     weight_qkv, weight_projection = fence((weight_qkv, weight_projection))
 
     qkv, attended = attention_forward(normed_all, weight_qkv, spread, *tables)
-    qkv, attended, others, late_others, grad_out, grad_out_other, weight_projection = fence(
-        (qkv, attended, others, late_others, grad_out, grad_out_other, weight_projection)
+    qkv, attended, others, late_others, own_rows, grad_out, weight_projection, rest_near = fence(
+        (qkv, attended, others, late_others, own_rows, grad_out, weight_projection, rest_near)
     )
 
     sent = dot(rows_of(attended, (1 - parity) * own), weight_projection).astype(BF)
-    stacked = jnp.stack(others)
+    stacked = jnp.stack(others[1:])
     sent, stacked, attended, weight_projection = fence((sent, stacked, attended, weight_projection))
     arrived = to_pair(sent)
     rest = gather_rows(stacked)
+    grad_out_other = to_y(grad_out)
     fine = row_size * SPLIT_MODEL <= model
     own_first = [a[0] for a in own_rows]
     kept = dot(rows_of(attended, parity * own), weight_projection)
     kept, stacked = fence((kept, stacked))
-    mine = [jnp.concatenate([own_first[0][None], stacked])] if fine else []
+    mine = [jnp.concatenate([own_first[0][None], rest_near[0][None], stacked])] if fine else []
     mine_other = [to_core(a) for a in mine]
-    kept, arrived, rest, mine, mine_other, pieces, own_rows = fence(
-        (kept, arrived, rest, mine, mine_other, pieces, own_rows)
+    kept, arrived, rest, mine, mine_other, pieces, own_rows, grad_out, grad_out_other = fence(
+        (kept, arrived, rest, mine, mine_other, pieces, own_rows, grad_out, grad_out_other)
     )
 
     middle = inputs.astype(F32) + kept + arrived.astype(F32)
     normed_two = (middle * inverse_rms(middle) * gain_two).astype(BF)
     n = len(mine)
-    late = merge([jnp.concatenate([a[None], b]) for a, b in zip(own_first[n:], rest[n:])])
+    late = merge([jnp.concatenate([a[None], b[None], c]) for a, b, c in zip(own_first[n:], rest_near[n:], rest[n:])])
     normed_two, middle, late = fence((normed_two, middle, late))
     normed_two_other = to_y(normed_two)
     weights = [mine + late, mine_other + [to_core(a) for a in late]]
@@ -659,30 +708,27 @@
     grads, sums, rows, along, blocks, mine[0], arrived, grad_two_other = fence(
         (grads, sums, rows, along, blocks, mine[0], arrived, grad_two_other)
     )
-    along.append(shift(blocks[0], "col", -1))
+    near_block = blocks[0]
     own_sums.append(sums)
     last, other = by_rows(grads[0]), by_rows(grads[1])
     last_rows = [to_core(a) for a in other[1:]]
-    kept = total(grad_two_other, *[p[1] for p in own_sums])
-    grad_middle, gain_two_term = norm_back(middle, gain_two, kept)
-    grad_middle = grad_middle + grad_out.astype(F32)
-    branch = grad_middle.astype(BF)
-    last_rows, branch, grad_middle, gain_two_term, last, other[0], along = fence(
-        (last_rows, branch, grad_middle, gain_two_term, last, other[0], along)
+    terms = [grad_two_other] + [p[1] for p in own_sums]
+    grad_middle, branch, gain_two_term = norm_back_rows(middle, gain_two, grad_out, terms)
+    last_rows, branch, grad_middle, gain_two_term, last, other[0] = fence(
+        (last_rows, branch, grad_middle, gain_two_term, last, other[0])
     )
     branch_other = to_pair(branch)
     sent = [[small(cut(a), cut(b)) for a, b in zip(last[1:], last_rows)] for cut in (middle_columns, outer_columns)]
     last_rows = [shift(a, "row", i) for i, a in enumerate(sent[0], 1)]
     last_core = to_core(other[0])
-    out_kept = middle + total(*[p[0] for p in own_sums])
-    out_sent = small(*[p[0] for p in other_sums])
     blocks = [small(mine[0][j], arrived[j], *[r[j // 3] for r in rows]) for j in (0, 3)]
-    branch, branch_other, last_core, last_rows, sent, out_kept, out_sent, blocks, grad_middle, gain_two_term = fence(
-        (branch, branch_other, last_core, last_rows, sent, out_kept, out_sent, blocks, grad_middle, gain_two_term)
-    )
-
-    along += [blocks[0], shift(blocks[1], "col", -3)]
-    out_other = to_y(out_sent)
+    blocks.append(near_block)
+    branch, branch_other, last_core, last_rows, sent, own_sums, other_sums, blocks, grad_middle, gain_two_term = fence(
+        (branch, branch_other, last_core, last_rows, sent, own_sums, other_sums, blocks, grad_middle, gain_two_term)
+    )
+
+    along += [blocks[0], shift(blocks[1], "col", -3), shift(blocks[2], "col", -1)]
+    out_other = to_y(small(*[p[0] for p in other_sums]))
     outer_rows = [shift(a, "row", i) for i, a in enumerate(sent[1], 1)]
     branch_all = in_sequence(branch, branch_other)
     grad_attended = dot_nt(branch_all, weight_projection).astype(BF)
@@ -724,14 +770,15 @@
     last_along[2] = shift(last_along[2], "col", -2)
     first_rows = small(first_halves[0], first_other)
     g = small(projection_halves[0], projection_other)
-    sent, first_rows, g, second_halves = fence((sent, first_rows, g, second_halves))
+    sent, first_rows, g, second_halves, own_sums = fence((sent, first_rows, g, second_halves, own_sums))
+    out_kept = middle + total(*[p[0] for p in own_sums])
     first_rows = [first_rows[0]] + to_rows(first_rows)
     projection_rows = [g[:, :, i * block : (i + 1) * block] for i in range(row_size)]
     projection_rows[1:] = to_rows(projection_rows)
     second_other = to_core(second_halves[1])
     kept = product(lambda a: rows_of(a, parity * own))
-    sent, grad_one_other, last_along, first_rows, projection_rows, second_halves, second_other, first_part, kept = fence(
-        (sent, grad_one_other, last_along, first_rows, projection_rows, second_halves, second_other, first_part, kept)
+    sent, grad_one_other, last_along, first_rows, projection_rows, second_halves, second_other, first_part, kept, out_kept = fence(
+        (sent, grad_one_other, last_along, first_rows, projection_rows, second_halves, second_other, first_part, kept, out_kept)
     )
 
     second_rows = small(second_halves[0], second_other)

time: 614 us -> 604 us (0.984)
  waiting for transfers between devices: 216 us -> 207 us
  other arithmetic: 73.3 us -> 66.2 us
    ppermute x30, waiting for transfers between devices: 55.3 us -> 44.6 us  [swap(): return lax.ppermute(a, axis, [(i, i ^ bit) for i in range(n)])]
    pallas_call x0 -> x1, Pallas kernels: none -> 6.8 us  [norm_back_rows(): pl.pallas_call(norm_back_kernel, grid=(tokens // rows,), in_specs=[block,...]
    reduce_sum x1 -> x0, other arithmetic: 6.72 us -> none  [norm_back(): jnp.sum(grad * field * r, axis=0)]
    ppermute x28 -> x29, starting transfers between devices: 49.2 us -> 44.3 us  [shift(): return lax.ppermute(a, axis, [(i, (i + by) % n) for i in range(n)])]
    unnamed x95 -> x107, local copies, waits for them, and re-layouts: 14.3 us -> 17.8 us
    ppermute x28 -> x29, waiting for transfers between devices: 151 us -> 152 us  [shift(): return lax.ppermute(a, axis, [(i, (i + by) % n) for i in range(n)])]
  transfers between devices with their start and end apart: 61 -> 62, of which waited for: 21 -> 24; matrix products, arithmetic and copies ran while one was open for 11% -> 10% of each run, Pallas kernels for 33% -> 33%
where the time goes in v4:
time: 604 us; the launch traced here: 596 us
  waiting for transfers between devices  207 us (34%)
  Pallas kernels  207 us (34%)
  starting transfers between devices  66.9 us (11%)
  other arithmetic  66.2 us (11%)
  local copies, waits for them, and re-layouts  32.4 us (5%)
  matrix products  14.6 us (2%)
    ppermute x29, waiting for transfers between devices, shift(): return lax.ppermute(a, axis, [(i, (i + by) % n) for i in range(n)])  152 us
    pallas_call x4, Pallas kernels, feedforward(): pl.pallas_call(functools.partial(feedforward_kernel, col_step, sub, rows_...  109 us
    ppermute x30, waiting for transfers between devices, swap(): return lax.ppermute(a, axis, [(i, i ^ bit) for i in range(n)])  44.6 us
    ppermute x29, starting transfers between devices, shift(): return lax.ppermute(a, axis, [(i, (i + by) % n) for i in range(n)])  44.3 us
    pallas_call x2, Pallas kernels, attention_backward(): pl.pallas_call(attention_backward_kernel, grid=(groups,), in_specs=[pl.Bl...  30.8 us
    pallas_call x1, Pallas kernels, attention_forward(): pl.pallas_call(attention_forward_kernel, grid=(groups,), in_specs=[whole(...  27.5 us
    convert_element_type x16, other arithmetic, small(): return total(*parts).astype(BF)  23.2 us
    ppermute x30, starting transfers between devices, swap(): return lax.ppermute(a, axis, [(i, i ^ bit) for i in range(n)])  21.7 us
  transfers between devices with their start and end apart: 62, of which 24 were waited for; matrix products, arithmetic and copies ran while one was open for 10% of the time, Pallas kernels for 33%

profile of v4, /device:TPU:0, one launch (start us, length us, event | category | flops | bytes accessed | tf_op | source)
XLA Modules:
  0.0 596.2 jit_solution(14060294221256959132)
XLA Ops:
  3.7 4.1 collective-permute-start
  9.5 2.1 fusion
  16.9 1.7 dynamic-slice_bitcast_fusion
  19.5 1.9 multiply_sine_fusion
  24.2 2.9 maximum_select_fusion.4.cot_ref.skip_ref
  27.2 19.5 %collective-permute-done.refs_0_ = bf16[2,576,384]{2,1,0:T(8,128)(2,1)} collective-permute-done((bf16[2,576,384]{2,1,0:T(8,128)(2,1)S(1)}, bf16[2,576,384]{2,1,0:T(8,128)(2,1)}, u32[]{:S(2)}, u32[]{:S(2)}) %collective-permute-start) | collective-permute-done | bytes 884768 | tf_op jit(solution)/shard_map/ppermute | solution.py:524
  46.7 21.3 %collective-permute-done.2 = bf16[512,1536]{1,0:T(8,128)(2,1)} collective-permute-done((bf16[512,1536]{1,0:T(8,128)(2,1)}, bf16[512,1536]{1,0:T(8,128)(2,1)}, u32[]{:S(2)}, u32[]{:S(2)}) %collective-permute-start.2) | collective-permute-done | bytes 1572896 | tf_op jit(solution)/shard_map/ppermute | solution.py:511
  70.2 4.4 maximum_select_fusion.n1_ref.a_ref
  74.6 12.5 %collective-permute-done.6 = bf16[384,768]{1,0:T(8,128)(2,1)} collective-permute-done((bf16[384,768]{1,0:T(8,128)(2,1)S(1)}, bf16[384,768]{1,0:T(8,128)(2,1)}, u32[]{:S(2)}, u32[]{:S(2)}) %collective-permute-start.6) | collective-permute-done | bytes 589856 | tf_op jit(solution)/shard_map/ppermute | solution.py:524
  87.1 11.7 %collective-permute-done.7 = bf16[384,768]{1,0:T(8,128)(2,1)} collective-permute-done((bf16[384,768]{1,0:T(8,128)(2,1)}, bf16[384,768]{1,0:T(8,128)(2,1)}, u32[]{:S(2)}, u32[]{:S(2)}) %collective-permute-start.7) | collective-permute-done | bytes 589856 | tf_op jit(solution)/shard_map/ppermute | solution.py:524
  99.7 2.5 pad_maximum_fusion.4
  102.2 2.0 collective-permute-start.12
  109.4 6.2 %assemble.1 = (bf16[1536,1536]{1,0:T(8,128)(2,1)}, bf16[1024,1536]{1,0:T(8,128)(2,1)}) custom-call(s32[1]{0:T(128)} %bitcast.15.core_ref, bf16[2,576,384]{2,1,0:T(8,128)(2,1)} %collective-permute-done.refs_0_, bf16[2,576,384]{2,1,0:T(8,128)(2,1)S(1)} %copy-done.7, bf16[2,576,384]{2,1,0:T(8,128)(2,1)S(1)} %pad_maximum_fusion.8.refs_2_, ...), custom_call_target="tpu_custom_call" | custom-call | flops 1 | bytes 1 | tf_op jit(solution)/shard_map/assemble/pallas_call | solution.py:385
  115.5 27.5 %attention_forward.1 = (bf16[1024,2048]{1,0:T(8,128)(2,1)}, bf16[1024,1024]{1,0:T(8,128)(2,1)S(1)}) custom-call(bf16[1024,1536]{1,0:T(8,128)(2,1)} %maximum_select_fusion.n1_ref.a_ref, bf16[1536,1536]{1,0:T(8,128)(2,1)} %get-tuple-element.317.w_ref, bf16[384,512]{1,0:T(8,128)(2,1)S(1)} %fusion.33.spread_ref, f32[1024,128]{1,0:T(8,128)S(1)} %get-tuple-element.319.cos_ref, ...), custom_call_target="tpu_custom_call" | custom-call | flops 1 | bytes 1 | tf_op jit(solution)/shard_map/attention_forward/pallas_call | solution.py:127
  145.1 1.8 convolution_convert_fusion
  146.9 1.8 fusion.21
  156.6 25.3 %collective-permute-done.15 = bf16[2,384,768]{2,1,0:T(8,128)(2,1)S(1)} collective-permute-done((bf16[2,384,768]{2,1,0:T(8,128)(2,1)S(1)}, bf16[2,384,768]{2,1,0:T(8,128)(2,1)S(1)}, u32[]{:S(2)}, u32[]{:S(2)}) %collective-permute-start.15) | collective-permute-done | bytes 1179680 | tf_op jit(solution)/shard_map/ppermute | solution.py:524
  181.9 6.3 %collective-permute-done.14 = bf16[512,1536]{1,0:T(8,128)(2,1)S(1)} collective-permute-done((bf16[512,1536]{1,0:T(8,128)(2,1)S(1)}, bf16[512,1536]{1,0:T(8,128)(2,1)S(1)}, u32[]{:S(2)}, u32[]{:S(2)}) %collective-permute-start.14) | collective-permute-done | bytes 1572896 | tf_op jit(solution)/shard_map/ppermute | solution.py:511
  192.8 1.7 pad_maximum_fusion.1.refs_1_
  198.9 2.9 collective-permute-start.20
  202.7 1.9 slice.276
  204.6 26.1 %feedforward.4 = (bf16[4,384,768]{2,1,0:T(8,128)(2,1)}, bf16[4,384,768]{2,1,0:T(8,128)(2,1)}, bf16[4,384,768]{2,1,0:T(8,128)(2,1)}, bf16[4,384,768]{2,1,0:T(8,12...) custom-call(bf16[512,1536]{1,0:T(8,128)(2,1)} %copy-done.17, ...), custom_call_target="tpu_custom_call" | custom-call | flops 1 | bytes 1 | tf_op jit(solution)/shard_map/feedforward/pallas_call | solution.py:243
  230.7 2.2 collective-permute-done.22.n2_ref
  234.3 3.1 pad_maximum_fusion.2.refs_0_
  238.7 28.0 %feedforward.5 = (bf16[4,384,768]{2,1,0:T(8,128)(2,1)}, bf16[4,384,768]{2,1,0:T(8,128)(2,1)}, bf16[4,384,768]{2,1,0:T(8,128)(2,1)}, bf16[4,384,768]{2,1,0:T(8,12...) custom-call(bf16[512,1536]{1,0:T(8,128)(2,1)} %collective-permute-done.22.n2_ref, ...), custom_call_target="tpu_custom_call" | custom-call | flops 1 | bytes 1 | tf_op jit(solution)/shard_map/feedforward/pallas_call | solution.py:243
  267.8 1.8 pad_maximum_fusion.3.refs_1_
  270.2 4.0 collective-permute-done.25.refs_3_
  275.6 2.0 collective-permute-done.26
  281.4 26.3 %feedforward.6 = (bf16[4,384,768]{2,1,0:T(8,128)(2,1)}, bf16[4,384,768]{2,1,0:T(8,128)(2,1)}, bf16[4,384,768]{2,1,0:T(8,128)(2,1)}, bf16[4,384,768]{2,1,0:T(8,12...) custom-call(bf16[512,1536]{1,0:T(8,128)(2,1)} %collective-permute-done.22.n2_ref, ...), custom_call_target="tpu_custom_call" | custom-call | flops 1 | bytes 1 | tf_op jit(solution)/shard_map/feedforward/pallas_call | solution.py:243
  309.2 3.2 add_convert_fusion.2
  312.3 3.1 fusion.35
  317.6 6.4 %collective-permute-start.30 = (bf16[384,768]{1,0:T(8,128)(2,1)}, bf16[384,768]{1,0:T(8,128)(2,1)}, u32[]{:S(2)}, u32[]{:S(2)}) collective-permute-start(bf16[384,768]{1,0:T(8,128)(2,1)} %get-tuple-element.452), channel_id=1, source_target_pairs={{0,2},{1,3},{2,0},{3,1},{4,6},{5,7},{6,4},{7,5},{8,10},{9,11},{10,... | collective-permute-start | bytes 1769480 | tf_op jit(solution)/shard_map/ppermute | solution.py:524
  324.1 28.2 %feedforward.7 = (bf16[4,384,768]{2,1,0:T(8,128)(2,1)}, bf16[4,384,768]{2,1,0:T(8,128)(2,1)}, bf16[4,384,768]{2,1,0:T(8,128)(2,1)}, bf16[4,384,768]{2,1,0:T(8,12...) custom-call(bf16[512,1536]{1,0:T(8,128)(2,1)} %copy-done.17, ...), custom_call_target="tpu_custom_call" | custom-call | flops 1 | bytes 1 | tf_op jit(solution)/shard_map/feedforward/pallas_call | solution.py:243
  353.5 6.8 %norm_back.1 = (f32[512,1536]{1,0:T(8,128)}, bf16[512,1536]{1,0:T(8,128)(2,1)}, f32[1,1536]{1,0:T(1,128)}) custom-call(f32[512,1536]{1,0:T(8,128)} %copy-done.8, f32[1,1536]{1,0:T(1,128)} %broadcast_in_dim.41.gain_ref, bf16[512,1536]{1,0:T(8,128)(2,1)} %maximum_select_fusion.4.cot_ref.skip_ref, bf16[512,1536]{1,0:T(8,128)(2,1)} %copy-done.33, ...), custom_call_target="tpu_custom_call" | custom-call | flops 1 | bytes 1 | tf_op jit(solution)/shard_map/norm_back/pallas_call | solution.py:464
  361.1 6.9 %collective-permute-start.33 = (bf16[512,1536]{1,0:T(8,128)(2,1)}, bf16[512,1536]{1,0:T(8,128)(2,1)S(1)}, u32[]{:S(2)}, u32[]{:S(2)}) collective-permute-start(bf16[512,1536]{1,0:T(8,128)(2,1)} %get-tuple-element.483), channel_id=1, source_target_pairs={{0,1},{1,0},{2,3},{3,2},{4,5},{5,4},{6,7},{7,6},{8,9},{9,8},{10,11... | collective-permute-start | bytes 4718600 | tf_op jit(solution)/shard_map/ppermute | solution.py:511
  368.0 1.9 add_convert_fusion.4
  371.4 3.1 fusion.37
  377.3 20.8 %collective-permute-done.35 = bf16[2,384,768]{2,1,0:T(8,128)(2,1)S(1)} collective-permute-done((bf16[2,384,768]{2,1,0:T(8,128)(2,1)S(1)}, bf16[2,384,768]{2,1,0:T(8,128)(2,1)S(1)}, u32[]{:S(2)}, u32[]{:S(2)}) %collective-permute-start.35) | collective-permute-done | bytes 1179680 | tf_op jit(solution)/shard_map/ppermute | solution.py:524
  398.0 5.2 collective-permute-done.33
  403.2 1.8 collective-permute-start.36
  405.0 2.1 collective-permute-start.37
  411.9 3.7 convolution_convert_fusion.1.do_ref
  415.6 15.7 %attention_backward.2.b_ref = bf16[1024,768]{1,0:T(8,128)(2,1)S(1)} custom-call(bf16[1024,2048]{1,0:T(8,128)(2,1)} %get-tuple-element.482.qkv_ref, bf16[1024,1024]{1,0:T(8,128)(2,1)S(1)} %convolution_convert_fusion.1.do_ref, bf16[512,384]{1,0:T(8,128)(2,1)S(1)} %fusion.32.gather_ref, f32[1024,128]{1,0:T(8,128)S(1)} %get-tuple-element.319.cos_ref, ...), custom_call_target="tpu_custom_call" | custom-call | flops 1 | bytes 1 | tf_op jit(solution)/shard_map/attention_backward/pallas_call | solution.py:154
  432.5 2.0 collective-permute-done.38
  434.5 3.3 fusion.41
  441.5 15.1 %attention_backward.3.b_ref = bf16[1024,768]{1,0:T(8,128)(2,1)S(1)} custom-call(bf16[1024,2048]{1,0:T(8,128)(2,1)} %get-tuple-element.482.qkv_ref, bf16[1024,1024]{1,0:T(8,128)(2,1)S(1)} %copy-done.1, bf16[512,384]{1,0:T(8,128)(2,1)S(1)} %fusion.32.gather_ref, f32[1024,128]{1,0:T(8,128)S(1)} %get-tuple-element.319.cos_ref, ...), custom_call_target="tpu_custom_call" | custom-call | flops 1 | bytes 1 | tf_op jit(solution)/shard_map/attention_backward/pallas_call | solution.py:154
  456.6 5.1 gradient_halves.3
  461.7 7.5 %gradient_halves.4 = bf16[2,4,96,1536]{3,2,1,0:T(8,128)(2,1)S(1)} custom-call(s32[1]{0:T(128)} %bitcast.15.core_ref, bf16[1024,1024]{1,0:T(8,128)(2,1)S(1)} %copy-done.3, bf16[1024,1536]{1,0:T(8,128)(2,1)} %copy-done.18), custom_call_target="tpu_custom_call" | custom-call | flops 1 | bytes 1 | tf_op jit(solution)/shard_map/gradient_halves/pallas_call | solution.py:412
  469.3 3.1 fusion.17
  472.4 5.1 gradient_halves.5
  480.0 1.8 add_convert_fusion.11
  486.1 3.2 collective-permute-start.45
  493.0 22.1 %collective-permute-done.45 = bf16[384,768]{1,0:T(8,128)(2,1)S(1)} collective-permute-done((bf16[384,768]{1,0:T(8,128)(2,1)S(1)}, bf16[384,768]{1,0:T(8,128)(2,1)S(1)}, u32[]{:S(2)}, u32[]{:S(2)}) %collective-permute-start.45) | collective-permute-done | bytes 589856 | tf_op jit(solution)/shard_map/ppermute | solution.py:524
  515.1 2.9 collective-permute-done.47
  523.2 2.4 collective-permute-start.51
  527.5 2.0 add_convert_fusion
  531.1 32.3 %collective-permute-done.51.refs_4_ = bf16[2,96,768]{2,1,0:T(8,128)(2,1)S(1)} collective-permute-done((bf16[2,96,768]{2,1,0:T(8,128)(2,1)S(1)}, bf16[2,96,768]{2,1,0:T(8,128)(2,1)S(1)}, u32[]{:S(2)}, u32[]{:S(2)}) %collective-permute-start.51) | collective-permute-done | bytes 294944 | tf_op jit(solution)/shard_map/ppermute | solution.py:524
  567.5 3.1 collective-permute-done.56
  571.7 2.7 collective-permute-done.57
  574.6 4.5 collective-permute-done.58
  581.6 6.8 %place.1 = (f32[12288,128]{1,0:T(8,128)}, f32[1024,768]{1,0:T(8,128)}) custom-call(bf16[2,2,384,768]{3,2,1,0:T(8,128)(2,1)S(1)} %get-tuple-element.604.refs_0_, bf16[2,2,384,768]{3,2,1,0:T(8,128)(2,1)S(1)} %get-tuple-element.603.refs_1_), custom_call_target="tpu_custom_call" | custom-call | flops 1 | bytes 1 | tf_op jit(solution)/shard_map/place/pallas_call | solution.py:280
  589.2 1.6 collective-permute-start.60
  590.8 2.1 collective-permute-done.60
  593.7 2.0 place_attention.1
  (299 shorter events, 99.2 us)
Async XLA Ops:
  3.7 42.9 %collective-permute-start = (bf16[2,576,384]{2,1,0:T(8,128)(2,1)S(1)}, bf16[2,576,384]{2,1,0:T(8,128)(2,1)}, u32[]{:S(2)}, u32[]{:S(2)}) collective-permute-start(bf16[2,576,384]{2,1,0:T(8,128)(2,1)S(1)} %pad_maximum_fusion.8.refs_2_), channel_id=1, source_target_pairs={{0,2},{1,3},{2,0},{3,1},{4,6},{5,7},{6,4},{7,5},{8,10},{9,11},{10,... | collective-permute-start | bytes 2654216 | tf_op jit(solution)/shard_map/ppermute | solution.py:524
  7.8 38.8 %collective-permute-start.1 = (bf16[2,576,384]{2,1,0:T(8,128)(2,1)S(1)}, bf16[2,576,384]{2,1,0:T(8,128)(2,1)}, u32[]{:S(2)}, u32[]{:S(2)}) collective-permute-start(bf16[2,576,384]{2,1,0:T(8,128)(2,1)S(1)} %pad_maximum_fusion.8.refs_2_), channel_id=1, source_target_pairs={{0,4},{4,0},{1,5},{5,1},{2,6},{6,2},{3,7},{7,3},{8,12},{12,8},{9,1... | collective-permute-start | bytes 2654216 | tf_op jit(solution)/shard_map/ppermute | solution.py:524
  14.2 53.7 %collective-permute-start.2 = (bf16[512,1536]{1,0:T(8,128)(2,1)}, bf16[512,1536]{1,0:T(8,128)(2,1)}, u32[]{:S(2)}, u32[]{:S(2)}) collective-permute-start(bf16[512,1536]{1,0:T(8,128)(2,1)} %fusion.2), channel_id=1, source_target_pairs={{0,1},{1,0},{2,3},{3,2},{4,5},{5,4},{6,7},{7,6},{8,9},{9,8},{10,11... | collective-permute-start | bytes 4718600 | tf_op jit(solution)/shard_map/ppermute | solution.py:511
  67.9 30.9 %collective-permute-start.3 = (bf16[2,576,384]{2,1,0:T(8,128)(2,1)}, bf16[2,576,384]{2,1,0:T(8,128)(2,1)}, u32[]{:S(2)}, u32[]{:S(2)}) collective-permute-start(bf16[2,576,384]{2,1,0:T(8,128)(2,1)} %collective-permute-done.refs_0_), channel_id=1, source_target_pairs={{0,4},{4,0},{1,5},{5,1},{2,6},{6,2},{3,7},{7,3},{8,12},{12,8},{9,1... | collective-permute-start | bytes 2654216 | tf_op jit(solution)/shard_map/ppermute | solution.py:524
  67.9 30.9 %collective-permute-start.4 = (bf16[2,576,384]{2,1,0:T(8,128)(2,1)S(1)}, bf16[2,576,384]{2,1,0:T(8,128)(2,1)S(1)}, u32[]{:S(2)}, u32[]{:S(2)}) collective-permute-start(bf16[2,576,384]{2,1,0:T(8,128)(2,1)S(1)} %pad_maximum_fusion.8.refs_2_), channel_id=1, source_target_pairs={{0,8},{8,0},{16,24},{24,16},{1,9},{9,1},{17,25},{25,17},{2,10},{10... | collective-permute-start | bytes 2654216 | tf_op jit(solution)/shard_map/ppermute | solution.py:511
  67.9 31.8 %collective-permute-start.5 = (bf16[2,576,384]{2,1,0:T(8,128)(2,1)}, bf16[2,576,384]{2,1,0:T(8,128)(2,1)S(1)}, u32[]{:S(2)}, u32[]{:S(2)}) collective-permute-start(bf16[2,576,384]{2,1,0:T(8,128)(2,1)} %collective-permute-done.1.refs_6_), channel_id=1, source_target_pairs={{0,8},{8,0},{16,24},{24,16},{1,9},{9,1},{17,25},{25,17},{2,10},{10... | collective-permute-start | bytes 2654216 | tf_op jit(solution)/shard_map/ppermute | solution.py:511
  69.0 18.2 %collective-permute-start.6 = (bf16[384,768]{1,0:T(8,128)(2,1)S(1)}, bf16[384,768]{1,0:T(8,128)(2,1)}, u32[]{:S(2)}, u32[]{:S(2)}) collective-permute-start(bf16[384,768]{1,0:T(8,128)(2,1)S(1)} %pad_maximum_fusion.9), channel_id=1, source_target_pairs={{0,1},{1,2},{2,3},{3,0},{4,5},{5,6},{6,7},{7,4},{8,9},{9,10},{10,1... | collective-permute-start | bytes 1769480 | tf_op jit(solution)/shard_map/ppermute | solution.py:524
  69.0 29.8 %collective-permute-start.7 = (bf16[384,768]{1,0:T(8,128)(2,1)}, bf16[384,768]{1,0:T(8,128)(2,1)}, u32[]{:S(2)}, u32[]{:S(2)}) collective-permute-start(bf16[384,768]{1,0:T(8,128)(2,1)} %pad_maximum_fusion.10), channel_id=1, source_target_pairs={{0,1},{1,2},{2,3},{3,0},{4,5},{5,6},{6,7},{7,4},{8,9},{9,10},{10,1... | collective-permute-start | bytes 1769480 | tf_op jit(solution)/shard_map/ppermute | solution.py:524
  99.7 5.6 collective-permute-start.8
  102.2 41.3 %collective-permute-start.12 = (bf16[2,384,768]{2,1,0:T(8,128)(2,1)}, bf16[2,384,768]{2,1,0:T(8,128)(2,1)}, u32[]{:S(2)}, u32[]{:S(2)}) collective-permute-start(bf16[2,384,768]{2,1,0:T(8,128)(2,1)} %pad_maximum_fusion.4), channel_id=1, source_target_pairs={{0,4},{4,0},{1,5},{5,1},{2,6},{6,2},{3,7},{7,3},{8,12},{12,8},{9,1... | collective-permute-start | bytes 3538952 | tf_op jit(solution)/shard_map/ppermute | solution.py:524
  104.3 2.8 collective-permute-start.9
  104.3 38.8 %collective-permute-start.10 = (bf16[384,768]{1,0:T(8,128)(2,1)S(1)}, bf16[384,768]{1,0:T(8,128)(2,1)}, u32[]{:S(2)}, u32[]{:S(2)}) collective-permute-start(bf16[384,768]{1,0:T(8,128)(2,1)S(1)} %pad_maximum_fusion.9), channel_id=1, source_target_pairs={{0,2},{1,3},{2,0},{3,1},{4,6},{5,7},{6,4},{7,5},{8,10},{9,11},{10,... | collective-permute-start | bytes 1769480 | tf_op jit(solution)/shard_map/ppermute | solution.py:524
  104.3 38.8 %collective-permute-start.11 = (bf16[384,768]{1,0:T(8,128)(2,1)S(1)}, bf16[384,768]{1,0:T(8,128)(2,1)}, u32[]{:S(2)}, u32[]{:S(2)}) collective-permute-start(bf16[384,768]{1,0:T(8,128)(2,1)S(1)} %pad_maximum_fusion.9), channel_id=1, source_target_pairs={{0,3},{1,0},{2,1},{3,2},{4,7},{5,4},{6,5},{7,6},{8,11},{9,8},{10,9... | collective-permute-start | bytes 1769480 | tf_op jit(solution)/shard_map/ppermute | solution.py:524
  106.2 37.3 %collective-permute-start.13 = (bf16[384,768]{1,0:T(8,128)(2,1)}, bf16[384,768]{1,0:T(8,128)(2,1)}, u32[]{:S(2)}, u32[]{:S(2)}) collective-permute-start(bf16[384,768]{1,0:T(8,128)(2,1)} %collective-permute-done.6), channel_id=1, source_target_pairs={{0,4},{4,0},{1,5},{5,1},{2,6},{6,2},{3,7},{7,3},{8,12},{12,8},{9,1... | collective-permute-start | bytes 1769480 | tf_op jit(solution)/shard_map/ppermute | solution.py:524
  149.8 40.4 %copy-start.11 = (bf16[512,1536]{1,0:T(8,128)(2,1)S(1)}, bf16[512,1536]{1,0:T(8,128)(2,1)}, u32[]{:S(2)}) copy-start(bf16[512,1536]{1,0:T(8,128)(2,1)} %copy-done.10) | copy-start | bytes 4718596
  151.3 37.8 %copy-start.14 = (bf16[4,384,768]{2,1,0:T(8,128)(2,1)}, bf16[4,384,768]{2,1,0:T(8,128)(2,1)S(1)}, u32[]{:S(2)}) copy-start(bf16[4,384,768]{2,1,0:T(8,128)(2,1)S(1)} %pad_maximum_fusion.refs_0_) | copy-start | bytes 7077892
  151.3 38.9 %collective-permute-start.16 = (bf16[4,384,768]{2,1,0:T(8,128)(2,1)S(1)}, bf16[4,384,768]{2,1,0:T(8,128)(2,1)}, u32[]{:S(2)}, u32[]{:S(2)}) collective-permute-start(bf16[4,384,768]{2,1,0:T(8,128)(2,1)S(1)} %pad_maximum_fusion.refs_0_), channel_id=1, source_target_pairs={{0,8},{8,0},{16,24},{24,16},{1,9},{9,1},{17,25},{25,17},{2,10},{10... | collective-permute-start | bytes 7077896 | tf_op jit(solution)/shard_map/ppermute | solution.py:511
  151.6 36.6 %collective-permute-start.14 = (bf16[512,1536]{1,0:T(8,128)(2,1)S(1)}, bf16[512,1536]{1,0:T(8,128)(2,1)S(1)}, u32[]{:S(2)}, u32[]{:S(2)}) collective-permute-start(bf16[512,1536]{1,0:T(8,128)(2,1)S(1)} %convolution_convert_fusion), channel_id=1, source_target_pairs={{0,1},{1,0},{2,3},{3,2},{4,5},{5,4},{6,7},{7,6},{8,9},{9,8},{10,11... | collective-permute-start | bytes 4718600 | tf_op jit(solution)/shard_map/ppermute | solution.py:511
  152.6 36.5 %collective-permute-start.17 = (bf16[512,1536]{1,0:T(8,128)(2,1)S(1)}, bf16[512,1536]{1,0:T(8,128)(2,1)S(1)}, u32[]{:S(2)}, u32[]{:S(2)}) collective-permute-start(bf16[512,1536]{1,0:T(8,128)(2,1)S(1)} %copy-done.13), channel_id=1, source_target_pairs={{0,16},{8,24},{16,0},{24,8},{1,17},{9,25},{17,1},{25,9},{2,18},{10... | collective-permute-start | bytes 4718600 | tf_op jit(solution)/shard_map/ppermute | solution.py:511
  154.1 27.8 %collective-permute-start.15 = (bf16[2,384,768]{2,1,0:T(8,128)(2,1)S(1)}, bf16[2,384,768]{2,1,0:T(8,128)(2,1)S(1)}, u32[]{:S(2)}, u32[]{:S(2)}) collective-permute-start(bf16[2,384,768]{2,1,0:T(8,128)(2,1)S(1)} %pad_maximum_fusion.5), channel_id=1, source_target_pairs={{0,4},{4,0},{1,5},{5,1},{2,6},{6,2},{3,7},{7,3},{8,12},{12,8},{9,1... | collective-permute-start | bytes 3538952 | tf_op jit(solution)/shard_map/ppermute | solution.py:524
  196.0 8.6 %collective-permute-start.18 = (bf16[4,384,768]{2,1,0:T(8,128)(2,1)S(1)}, bf16[4,384,768]{2,1,0:T(8,128)(2,1)}, u32[]{:S(2)}, u32[]{:S(2)}) collective-permute-start(bf16[4,384,768]{2,1,0:T(8,128)(2,1)S(1)} %pad_maximum_fusion.1.refs_1_), channel_id=1, source_target_pairs={{0,8},{8,0},{16,24},{24,16},{1,9},{9,1},{17,25},{25,17},{2,10},{10... | collective-permute-start | bytes 7077896 | tf_op jit(solution)/shard_map/ppermute | solution.py:511
  196.0 36.9 %collective-permute-start.22 = (bf16[512,1536]{1,0:T(8,128)(2,1)S(1)}, bf16[512,1536]{1,0:T(8,128)(2,1)}, u32[]{:S(2)}, u32[]{:S(2)}) collective-permute-start(bf16[512,1536]{1,0:T(8,128)(2,1)S(1)} %multiply_convert_fusion.n2_ref), channel_id=1, source_target_pairs={{0,16},{8,24},{16,0},{24,8},{1,17},{9,25},{17,1},{25,9},{2,18},{10... | collective-permute-start | bytes 4718600 | tf_op jit(solution)/shard_map/ppermute | solution.py:511
  197.5 33.2 %collective-permute-start.19 = (bf16[384,768]{1,0:T(8,128)(2,1)}, bf16[384,768]{1,0:T(8,128)(2,1)}, u32[]{:S(2)}, u32[]{:S(2)}) collective-permute-start(bf16[384,768]{1,0:T(8,128)(2,1)} %collective-permute-done.7), channel_id=1, source_target_pairs={{0,4},{4,0},{1,5},{5,1},{2,6},{6,2},{3,7},{7,3},{8,12},{12,8},{9,1... | collective-permute-start | bytes 1769480 | tf_op jit(solution)/shard_map/ppermute | solution.py:524
  198.9 31.8 %collective-permute-start.20 = (bf16[384,768]{1,0:T(8,128)(2,1)}, bf16[384,768]{1,0:T(8,128)(2,1)}, u32[]{:S(2)}, u32[]{:S(2)}) collective-permute-start(bf16[384,768]{1,0:T(8,128)(2,1)} %pad_maximum_fusion.10), channel_id=1, source_target_pairs={{0,2},{1,3},{2,0},{3,1},{4,6},{5,7},{6,4},{7,5},{8,10},{9,11},{10,... | collective-permute-start | bytes 1769480 | tf_op jit(solution)/shard_map/ppermute | solution.py:524
  201.8 28.9 %collective-permute-start.21 = (bf16[384,768]{1,0:T(8,128)(2,1)}, bf16[384,768]{1,0:T(8,128)(2,1)}, u32[]{:S(2)}, u32[]{:S(2)}) collective-permute-start(bf16[384,768]{1,0:T(8,128)(2,1)} %pad_maximum_fusion.10), channel_id=1, source_target_pairs={{0,3},{1,0},{2,1},{3,2},{4,7},{5,4},{6,5},{7,6},{8,11},{9,8},{10,9... | collective-permute-start | bytes 1769480 | tf_op jit(solution)/shard_map/ppermute | solution.py:524
  237.4 29.3 %collective-permute-start.24 = (bf16[4,384,768]{2,1,0:T(8,128)(2,1)}, bf16[4,384,768]{2,1,0:T(8,128)(2,1)}, u32[]{:S(2)}, u32[]{:S(2)}) collective-permute-start(bf16[4,384,768]{2,1,0:T(8,128)(2,1)} %pad_maximum_fusion.2.refs_0_), channel_id=1, source_target_pairs={{0,8},{8,0},{16,24},{24,16},{1,9},{9,1},{17,25},{25,17},{2,10},{10... | collective-permute-start | bytes 7077896 | tf_op jit(solution)/shard_map/ppermute | solution.py:511
  237.4 29.3 %collective-permute-start.23 = (bf16[2,384,768]{2,1,0:T(8,128)(2,1)S(1)}, bf16[2,384,768]{2,1,0:T(8,128)(2,1)}, u32[]{:S(2)}, u32[]{:S(2)}) collective-permute-start(bf16[2,384,768]{2,1,0:T(8,128)(2,1)S(1)} %pad_maximum_fusion.6), channel_id=1, source_target_pairs={{0,4},{4,0},{1,5},{5,1},{2,6},{6,2},{3,7},{7,3},{8,12},{12,8},{9,1... | collective-permute-start | bytes 3538952 | tf_op jit(solution)/shard_map/ppermute | solution.py:524
  269.6 4.6 collective-permute-start.25
  270.0 7.6 %collective-permute-start.26 = (bf16[4,384,768]{2,1,0:T(8,128)(2,1)S(1)}, bf16[4,384,768]{2,1,0:T(8,128)(2,1)S(1)}, u32[]{:S(2)}, u32[]{:S(2)}) collective-permute-start(bf16[4,384,768]{2,1,0:T(8,128)(2,1)S(1)} %copy-done.48), channel_id=1, source_target_pairs={{0,8},{8,0},{16,24},{24,16},{1,9},{9,1},{17,25},{25,17},{2,10},{10... | collective-permute-start | bytes 7077896 | tf_op jit(solution)/shard_map/ppermute | solution.py:511
  280.5 28.7 %collective-permute-start.28 = (bf16[4,384,768]{2,1,0:T(8,128)(2,1)}, bf16[4,384,768]{2,1,0:T(8,128)(2,1)}, u32[]{:S(2)}, u32[]{:S(2)}) collective-permute-start(bf16[4,384,768]{2,1,0:T(8,128)(2,1)} %get-tuple-element.422), channel_id=1, source_target_pairs={{0,8},{8,0},{16,24},{24,16},{1,9},{9,1},{17,25},{25,17},{2,10},{10... | collective-permute-start | bytes 7077896 | tf_op jit(solution)/shard_map/ppermute | solution.py:511
  280.7 28.5 %collective-permute-start.27 = (bf16[2,384,768]{2,1,0:T(8,128)(2,1)}, bf16[2,384,768]{2,1,0:T(8,128)(2,1)}, u32[]{:S(2)}, u32[]{:S(2)}) collective-permute-start(bf16[2,384,768]{2,1,0:T(8,128)(2,1)} %add_convert_fusion.6), channel_id=1, source_target_pairs={{0,4},{4,0},{1,5},{5,1},{2,6},{6,2},{3,7},{7,3},{8,12},{12,8},{9,1... | collective-permute-start | bytes 3538952 | tf_op jit(solution)/shard_map/ppermute | solution.py:524
  315.4 37.0 %collective-permute-start.31 = (bf16[512,1536]{1,0:T(8,128)(2,1)}, bf16[512,1536]{1,0:T(8,128)(2,1)S(1)}, u32[]{:S(2)}, u32[]{:S(2)}) collective-permute-start(bf16[512,1536]{1,0:T(8,128)(2,1)} %add_convert_fusion.2), channel_id=1, source_target_pairs={{0,16},{8,24},{16,0},{24,8},{1,17},{9,25},{17,1},{25,9},{2,18},{10... | collective-permute-start | bytes 4718600 | tf_op jit(solution)/shard_map/ppermute | solution.py:511
  317.0 35.4 %collective-permute-start.29 = (bf16[2,384,768]{2,1,0:T(8,128)(2,1)}, bf16[2,384,768]{2,1,0:T(8,128)(2,1)}, u32[]{:S(2)}, u32[]{:S(2)}) collective-permute-start(bf16[2,384,768]{2,1,0:T(8,128)(2,1)} %add_convert_fusion.5), channel_id=1, source_target_pairs={{0,4},{4,0},{1,5},{5,1},{2,6},{6,2},{3,7},{7,3},{8,12},{12,8},{9,1... | collective-permute-start | bytes 3538952 | tf_op jit(solution)/shard_map/ppermute | solution.py:524
  317.6 34.7 %collective-permute-start.30 = (bf16[384,768]{1,0:T(8,128)(2,1)}, bf16[384,768]{1,0:T(8,128)(2,1)}, u32[]{:S(2)}, u32[]{:S(2)}) collective-permute-start(bf16[384,768]{1,0:T(8,128)(2,1)} %get-tuple-element.452), channel_id=1, source_target_pairs={{0,2},{1,3},{2,0},{3,1},{4,6},{5,7},{6,4},{7,5},{8,10},{9,11},{10,... | collective-permute-start | bytes 1769480 | tf_op jit(solution)/shard_map/ppermute | solution.py:524
  352.4 8.7 %collective-permute-start.32 = (bf16[4,384,768]{2,1,0:T(8,128)(2,1)}, bf16[4,384,768]{2,1,0:T(8,128)(2,1)}, u32[]{:S(2)}, u32[]{:S(2)}) collective-permute-start(bf16[4,384,768]{2,1,0:T(8,128)(2,1)} %get-tuple-element.455), channel_id=1, source_target_pairs={{0,8},{8,0},{16,24},{24,16},{1,9},{9,1},{17,25},{25,17},{2,10},{10... | collective-permute-start | bytes 7077896 | tf_op jit(solution)/shard_map/ppermute | solution.py:511
  361.0 42.2 %collective-permute-start.34 = (bf16[4,384,768]{2,1,0:T(8,128)(2,1)}, bf16[4,384,768]{2,1,0:T(8,128)(2,1)S(1)}, u32[]{:S(2)}, u32[]{:S(2)}) collective-permute-start(bf16[4,384,768]{2,1,0:T(8,128)(2,1)} %get-tuple-element.468), channel_id=1, source_target_pairs={{0,8},{8,0},{16,24},{24,16},{1,9},{9,1},{17,25},{25,17},{2,10},{10... | collective-permute-start | bytes 7077896 | tf_op jit(solution)/shard_map/ppermute | solution.py:511
  361.1 42.1 %collective-permute-start.33 = (bf16[512,1536]{1,0:T(8,128)(2,1)}, bf16[512,1536]{1,0:T(8,128)(2,1)S(1)}, u32[]{:S(2)}, u32[]{:S(2)}) collective-permute-start(bf16[512,1536]{1,0:T(8,128)(2,1)} %get-tuple-element.483), channel_id=1, source_target_pairs={{0,1},{1,0},{2,3},{3,2},{4,5},{5,4},{6,7},{7,6},{8,9},{9,8},{10,11... | collective-permute-start | bytes 4718600 | tf_op jit(solution)/shard_map/ppermute | solution.py:511
  369.9 28.1 %collective-permute-start.35 = (bf16[2,384,768]{2,1,0:T(8,128)(2,1)S(1)}, bf16[2,384,768]{2,1,0:T(8,128)(2,1)S(1)}, u32[]{:S(2)}, u32[]{:S(2)}) collective-permute-start(bf16[2,384,768]{2,1,0:T(8,128)(2,1)S(1)} %add_convert_fusion.4), channel_id=1, source_target_pairs={{0,4},{4,0},{1,5},{5,1},{2,6},{6,2},{3,7},{7,3},{8,12},{12,8},{9,1... | collective-permute-start | bytes 3538952 | tf_op jit(solution)/shard_map/ppermute | solution.py:524
  403.2 28.1 %collective-permute-start.36 = (bf16[384,768]{1,0:T(8,128)(2,1)}, bf16[384,768]{1,0:T(8,128)(2,1)}, u32[]{:S(2)}, u32[]{:S(2)}) collective-permute-start(bf16[384,768]{1,0:T(8,128)(2,1)} %get-tuple-element.488), channel_id=1, source_target_pairs={{0,1},{1,2},{2,3},{3,0},{4,5},{5,6},{6,7},{7,4},{8,9},{9,10},{10,1... | collective-permute-start | bytes 1769480 | tf_op jit(solution)/shard_map/ppermute | solution.py:524
  405.0 27.6 %collective-permute-start.37 = (bf16[384,768]{1,0:T(8,128)(2,1)}, bf16[384,768]{1,0:T(8,128)(2,1)}, u32[]{:S(2)}, u32[]{:S(2)}) collective-permute-start(bf16[384,768]{1,0:T(8,128)(2,1)} %get-tuple-element.489), channel_id=1, source_target_pairs={{0,3},{1,0},{2,1},{3,2},{4,7},{5,4},{6,5},{7,6},{8,11},{9,8},{10,9... | collective-permute-start | bytes 1769480 | tf_op jit(solution)/shard_map/ppermute | solution.py:524
  407.0 27.5 %collective-permute-start.38 = (bf16[2,384,768]{2,1,0:T(8,128)(2,1)}, bf16[2,384,768]{2,1,0:T(8,128)(2,1)}, u32[]{:S(2)}, u32[]{:S(2)}) collective-permute-start(bf16[2,384,768]{2,1,0:T(8,128)(2,1)} %add_convert_fusion.3), channel_id=1, source_target_pairs={{0,4},{4,0},{1,5},{5,1},{2,6},{6,2},{3,7},{7,3},{8,12},{12,8},{9,1... | collective-permute-start | bytes 3538952 | tf_op jit(solution)/shard_map/ppermute | solution.py:524
  410.0 59.2 %collective-permute-start.41 = (bf16[512,1536]{1,0:T(8,128)(2,1)}, bf16[512,1536]{1,0:T(8,128)(2,1)}, u32[]{:S(2)}, u32[]{:S(2)}) collective-permute-start(bf16[512,1536]{1,0:T(8,128)(2,1)} %add_convert_fusion.1), channel_id=1, source_target_pairs={{0,16},{8,24},{16,0},{24,8},{1,17},{9,25},{17,1},{25,9},{2,18},{10... | collective-permute-start | bytes 4718600 | tf_op jit(solution)/shard_map/ppermute | solution.py:511
  437.8 31.4 %collective-permute-start.39 = (bf16[384,768]{1,0:T(8,128)(2,1)}, bf16[384,768]{1,0:T(8,128)(2,1)}, u32[]{:S(2)}, u32[]{:S(2)}) collective-permute-start(bf16[384,768]{1,0:T(8,128)(2,1)} %get-tuple-element.499), channel_id=1, source_target_pairs={{0,3},{1,0},{2,1},{3,2},{4,7},{5,4},{6,5},{7,6},{8,11},{9,8},{10,9... | collective-permute-start | bytes 1769480 | tf_op jit(solution)/shard_map/ppermute | solution.py:524
  439.3 29.9 %collective-permute-start.40 = (bf16[384,768]{1,0:T(8,128)(2,1)}, bf16[384,768]{1,0:T(8,128)(2,1)}, u32[]{:S(2)}, u32[]{:S(2)}) collective-permute-start(bf16[384,768]{1,0:T(8,128)(2,1)} %get-tuple-element.501), channel_id=1, source_target_pairs={{0,1},{1,2},{2,3},{3,0},{4,5},{5,6},{6,7},{7,4},{8,9},{9,10},{10,1... | collective-permute-start | bytes 1769480 | tf_op jit(solution)/shard_map/ppermute | solution.py:524
  479.0 5.6 collective-permute-start.42
  479.2 5.5 collective-permute-start.43
  485.4 32.7 %collective-permute-start.44 = (bf16[256,1536]{1,0:T(8,128)(2,1)S(1)}, bf16[256,1536]{1,0:T(8,128)(2,1)S(1)}, u32[]{:S(2)}, u32[]{:S(2)}) collective-permute-start(bf16[256,1536]{1,0:T(8,128)(2,1)S(1)} %slice.320), channel_id=1, source_target_pairs={{0,1},{1,0},{2,3},{3,2},{4,5},{5,4},{6,7},{7,6},{8,9},{9,8},{10,11... | collective-permute-start | bytes 2359304 | tf_op jit(solution)/shard_map/ppermute | solution.py:511
  486.1 28.9 %collective-permute-start.45 = (bf16[384,768]{1,0:T(8,128)(2,1)S(1)}, bf16[384,768]{1,0:T(8,128)(2,1)S(1)}, u32[]{:S(2)}, u32[]{:S(2)}) collective-permute-start(bf16[384,768]{1,0:T(8,128)(2,1)S(1)} %copy-done.41), channel_id=1, source_target_pairs={{0,2},{1,3},{2,0},{3,1},{4,6},{5,7},{6,4},{7,5},{8,10},{9,11},{10,... | collective-permute-start | bytes 1769480 | tf_op jit(solution)/shard_map/ppermute | solution.py:524
  489.4 28.6 %collective-permute-start.48 = (bf16[2,384,768]{2,1,0:T(8,128)(2,1)S(1)}, bf16[2,384,768]{2,1,0:T(8,128)(2,1)S(1)}, u32[]{:S(2)}, u32[]{:S(2)}) collective-permute-start(bf16[2,384,768]{2,1,0:T(8,128)(2,1)S(1)} %slice_bitcast_fusion), channel_id=1, source_target_pairs={{0,8},{8,0},{16,24},{24,16},{1,9},{9,1},{17,25},{25,17},{2,10},{10... | collective-permute-start | bytes 3538952 | tf_op jit(solution)/shard_map/ppermute | solution.py:511
  489.6 25.5 %collective-permute-start.46 = (bf16[384,768]{1,0:T(8,128)(2,1)S(1)}, bf16[384,768]{1,0:T(8,128)(2,1)S(1)}, u32[]{:S(2)}, u32[]{:S(2)}) collective-permute-start(bf16[384,768]{1,0:T(8,128)(2,1)S(1)} %get-tuple-element.634), channel_id=1, source_target_pairs={{0,4},{4,0},{1,5},{5,1},{2,6},{6,2},{3,7},{7,3},{8,12},{12,8},{9,1... | collective-permute-start | bytes 1769480 | tf_op jit(solution)/shard_map/ppermute | solution.py:524
  491.2 26.8 %collective-permute-start.47 = (bf16[4,96,768]{2,1,0:T(8,128)(2,1)S(1)}, bf16[4,96,768]{2,1,0:T(8,128)(2,1)S(1)}, u32[]{:S(2)}, u32[]{:S(2)}) collective-permute-start(bf16[4,96,768]{2,1,0:T(8,128)(2,1)S(1)} %get-tuple-element.632), channel_id=1, source_target_pairs={{0,4},{4,0},{1,5},{5,1},{2,6},{6,2},{3,7},{7,3},{8,12},{12,8},{9,1... | collective-permute-start | bytes 1769480 | tf_op jit(solution)/shard_map/ppermute | solution.py:524
  521.0 42.4 %collective-permute-start.49 = (bf16[384,768]{1,0:T(8,128)(2,1)S(1)}, bf16[384,768]{1,0:T(8,128)(2,1)S(1)}, u32[]{:S(2)}, u32[]{:S(2)}) collective-permute-start(bf16[384,768]{1,0:T(8,128)(2,1)S(1)} %get-tuple-element.630), channel_id=1, source_target_pairs={{0,4},{4,0},{1,5},{5,1},{2,6},{6,2},{3,7},{7,3},{8,12},{12,8},{9,1... | collective-permute-start | bytes 1769480 | tf_op jit(solution)/shard_map/ppermute | solution.py:524
  522.5 40.8 %collective-permute-start.50 = (bf16[384,768]{1,0:T(8,128)(2,1)S(1)}, bf16[384,768]{1,0:T(8,128)(2,1)S(1)}, u32[]{:S(2)}, u32[]{:S(2)}) collective-permute-start(bf16[384,768]{1,0:T(8,128)(2,1)S(1)} %add_convert_fusion.10), channel_id=1, source_target_pairs={{0,2},{1,3},{2,0},{3,1},{4,6},{5,7},{6,4},{7,5},{8,10},{9,11},{10,... | collective-permute-start | bytes 1769480 | tf_op jit(solution)/shard_map/ppermute | solution.py:524
  523.2 40.2 %collective-permute-start.51 = (bf16[2,96,768]{2,1,0:T(8,128)(2,1)S(1)}, bf16[2,96,768]{2,1,0:T(8,128)(2,1)S(1)}, u32[]{:S(2)}, u32[]{:S(2)}) collective-permute-start(bf16[2,96,768]{2,1,0:T(8,128)(2,1)S(1)} %slice.329), channel_id=1, source_target_pairs={{0,2},{1,3},{2,0},{3,1},{4,6},{5,7},{6,4},{7,5},{8,10},{9,11},{10,... | collective-permute-start | bytes 884744 | tf_op jit(solution)/shard_map/ppermute | solution.py:524
  525.6 37.8 %collective-permute-start.52 = (bf16[256,1536]{1,0:T(8,128)(2,1)S(1)}, bf16[256,1536]{1,0:T(8,128)(2,1)S(1)}, u32[]{:S(2)}, u32[]{:S(2)}) collective-permute-start(bf16[256,1536]{1,0:T(8,128)(2,1)S(1)} %slice.330), channel_id=1, source_target_pairs={{0,1},{1,0},{2,3},{3,2},{4,5},{5,4},{6,7},{7,6},{8,9},{9,8},{10,11... | collective-permute-start | bytes 2359304 | tf_op jit(solution)/shard_map/ppermute | solution.py:511
  527.1 36.3 %collective-permute-start.53 = (bf16[2,384,768]{2,1,0:T(8,128)(2,1)S(1)}, bf16[2,384,768]{2,1,0:T(8,128)(2,1)S(1)}, u32[]{:S(2)}, u32[]{:S(2)}) collective-permute-start(bf16[2,384,768]{2,1,0:T(8,128)(2,1)S(1)} %pad_maximum_fusion.7), channel_id=1, source_target_pairs={{0,16},{8,24},{16,0},{24,8},{1,17},{9,25},{17,1},{25,9},{2,18},{10... | collective-permute-start | bytes 3538952 | tf_op jit(solution)/shard_map/ppermute | solution.py:511
  563.7 24.7 %collective-permute-start.54 = (bf16[2,576,384]{2,1,0:T(8,128)(2,1)S(1)}, bf16[2,576,384]{2,1,0:T(8,128)(2,1)S(1)}, u32[]{:S(2)}, u32[]{:S(2)}) collective-permute-start(bf16[2,576,384]{2,1,0:T(8,128)(2,1)S(1)} %combine.1), channel_id=1, source_target_pairs={{0,16},{8,24},{16,0},{24,8},{1,17},{9,25},{17,1},{25,9},{2,18},{10... | collective-permute-start | bytes 2654216 | tf_op jit(solution)/shard_map/ppermute | solution.py:511
  564.6 16.1 %collective-permute-start.55 = (bf16[2,2,384,768]{3,2,1,0:T(8,128)(2,1)S(1)}, bf16[2,2,384,768]{3,2,1,0:T(8,128)(2,1)S(1)}, u32[]{:S(2)}, u32[]{:S(2)}) collective-permute-start(bf16[2,2,384,768]{3,2,1,0:T(8,128)(2,1)S(1)} %maximum_select_fusion.2), channel_id=1, source_target_pairs={{0,8},{8,0},{16,24},{24,16},{1,9},{9,1},{17,25},{25,17},{2,10},{10... | collective-permute-start | bytes 7077896 | tf_op jit(solution)/shard_map/ppermute | solution.py:511
  566.9 3.8 collective-permute-start.56
  570.6 3.8 collective-permute-start.57
  574.4 4.7 collective-permute-start.58
  579.1 1.6 collective-permute-start.59
  588.6 4.9 collective-permute-start.61
  589.2 3.7 collective-permute-start.60
  (50 other events, 340.8 us)

commit v5 on v4

--- a/solution.py
+++ b/solution.py
@@ -698,10 +698,13 @@
     grads, sums, rows, mine[0], arrived, sent, weights = fence((grads, sums, rows, mine[0], arrived, sent, weights))
     other_sums.append(sums)
 
+    sums = small(*[p[1] for p in other_sums])
+    sums, mine[0], arrived, rows, grads, other_sums, own_sums = fence(
+        (sums, mine[0], arrived, rows, grads, other_sums, own_sums)
+    )
+    grad_two_other = to_y(sums)
     blocks = [small(mine[0][j], arrived[j], *[r[j - 1] for r in rows]) for j in (1, 2)]
-    sums = small(*[p[1] for p in other_sums])
-    sums, blocks, grads, other_sums, own_sums = fence((sums, blocks, grads, other_sums, own_sums))
-    grad_two_other = to_y(sums)
+    blocks, grads, normed_two = fence((blocks, grads, normed_two))
     rows = [shift(a, "row", i) for i, a in enumerate(sent[1], 1)]
     along = [shift(blocks[1], "col", -2)]
     grads, *sums = feedforward(normed_two, grad_out, weights, PARTS, grads)
@@ -761,16 +764,16 @@
     first_other, projection_other = to_core(first_halves[1]), to_core(projection_halves[1])
     sent = product(lambda a: rows_of(a, (1 - parity) * own)).astype(BF)
     second_halves = qkv_halves(second)
-    first_part = small(*along)
-    sent, second_halves, first_part, last_along, first_other, projection_other, first_halves, projection_halves = fence(
-        (sent, second_halves, first_part, last_along, first_other, projection_other, first_halves, projection_halves)
+    sent, second_halves, along, last_along, first_other, projection_other, first_halves, projection_halves = fence(
+        (sent, second_halves, along, last_along, first_other, projection_other, first_halves, projection_halves)
     )
     half = own // 2
     grad_one_other = [to_pair(sent[:half])]
     last_along[2] = shift(last_along[2], "col", -2)
     first_rows = small(first_halves[0], first_other)
     g = small(projection_halves[0], projection_other)
-    sent, first_rows, g, second_halves, own_sums = fence((sent, first_rows, g, second_halves, own_sums))
+    sent, first_rows, g, second_halves, own_sums, along = fence((sent, first_rows, g, second_halves, own_sums, along))
+    first_part = small(*along)
     out_kept = middle + total(*[p[0] for p in own_sums])
     first_rows = [first_rows[0]] + to_rows(first_rows)
     projection_rows = [g[:, :, i * block : (i + 1) * block] for i in range(row_size)]

time: 604 us -> 599 us (level)
  transfers between devices with their start and end apart: 62 -> 62, of which waited for: 24 -> 25; matrix products, arithmetic and copies ran while one was open for 10% -> 11% of each run, Pallas kernels for 33% -> 34%
where the time goes in v5:
time: 599 us; the launch traced here: 591 us
  Pallas kernels  207 us (35%)
  waiting for transfers between devices  202 us (34%)
  starting transfers between devices  66.6 us (11%)
  other arithmetic  66.5 us (11%)
  local copies, waits for them, and re-layouts  32.1 us (5%)
  matrix products  14.6 us (2%)
    ppermute x29, waiting for transfers between devices, shift(): return lax.ppermute(a, axis, [(i, (i + by) % n) for i in range(n)])  148 us
    pallas_call x4, Pallas kernels, feedforward(): pl.pallas_call(functools.partial(feedforward_kernel, col_step, sub, rows_...  109 us
    ppermute x30, waiting for transfers between devices, swap(): return lax.ppermute(a, axis, [(i, i ^ bit) for i in range(n)])  45.3 us
    ppermute x29, starting transfers between devices, shift(): return lax.ppermute(a, axis, [(i, (i + by) % n) for i in range(n)])  44.4 us
    pallas_call x2, Pallas kernels, attention_backward(): pl.pallas_call(attention_backward_kernel, grid=(groups,), in_specs=[pl.Bl...  30.8 us
    pallas_call x1, Pallas kernels, attention_forward(): pl.pallas_call(attention_forward_kernel, grid=(groups,), in_specs=[whole(...  27.5 us
    convert_element_type x16, other arithmetic, small(): return total(*parts).astype(BF)  23.6 us
    ppermute x30, starting transfers between devices, swap(): return lax.ppermute(a, axis, [(i, i ^ bit) for i in range(n)])  19.4 us
  transfers between devices with their start and end apart: 62, of which 25 were waited for; matrix products, arithmetic and copies ran while one was open for 11% of the time, Pallas kernels for 34%

profile of v5, /device:TPU:0, one launch (start us, length us, event | category | flops | bytes accessed | tf_op | source)
XLA Modules:
  0.0 590.8 jit_solution(11904948537270233199)
XLA Ops:
  3.7 4.1 collective-permute-start
  9.5 2.1 fusion
  16.9 1.7 dynamic-slice_bitcast_fusion
  19.5 1.9 multiply_sine_fusion
  24.2 2.9 maximum_select_fusion.4.cot_ref.skip_ref
  27.2 19.5 %collective-permute-done.refs_0_ = bf16[2,576,384]{2,1,0:T(8,128)(2,1)} collective-permute-done((bf16[2,576,384]{2,1,0:T(8,128)(2,1)S(1)}, bf16[2,576,384]{2,1,0:T(8,128)(2,1)}, u32[]{:S(2)}, u32[]{:S(2)}) %collective-permute-start) | collective-permute-done | bytes 884768 | tf_op jit(solution)/shard_map/ppermute | solution.py:524
  46.7 21.3 %collective-permute-done.2 = bf16[512,1536]{1,0:T(8,128)(2,1)} collective-permute-done((bf16[512,1536]{1,0:T(8,128)(2,1)}, bf16[512,1536]{1,0:T(8,128)(2,1)}, u32[]{:S(2)}, u32[]{:S(2)}) %collective-permute-start.2) | collective-permute-done | bytes 1572896 | tf_op jit(solution)/shard_map/ppermute | solution.py:511
  70.2 4.4 maximum_select_fusion.n1_ref.a_ref
  74.6 12.5 %collective-permute-done.6 = bf16[384,768]{1,0:T(8,128)(2,1)} collective-permute-done((bf16[384,768]{1,0:T(8,128)(2,1)S(1)}, bf16[384,768]{1,0:T(8,128)(2,1)}, u32[]{:S(2)}, u32[]{:S(2)}) %collective-permute-start.6) | collective-permute-done | bytes 589856 | tf_op jit(solution)/shard_map/ppermute | solution.py:524
  87.1 11.7 %collective-permute-done.7 = bf16[384,768]{1,0:T(8,128)(2,1)} collective-permute-done((bf16[384,768]{1,0:T(8,128)(2,1)}, bf16[384,768]{1,0:T(8,128)(2,1)}, u32[]{:S(2)}, u32[]{:S(2)}) %collective-permute-start.7) | collective-permute-done | bytes 589856 | tf_op jit(solution)/shard_map/ppermute | solution.py:524
  99.7 2.5 pad_maximum_fusion.4
  102.2 2.0 collective-permute-start.12
  109.4 6.2 %assemble.1 = (bf16[1536,1536]{1,0:T(8,128)(2,1)}, bf16[1024,1536]{1,0:T(8,128)(2,1)}) custom-call(s32[1]{0:T(128)} %bitcast.15.core_ref, bf16[2,576,384]{2,1,0:T(8,128)(2,1)} %collective-permute-done.refs_0_, bf16[2,576,384]{2,1,0:T(8,128)(2,1)S(1)} %copy-done.7, bf16[2,576,384]{2,1,0:T(8,128)(2,1)S(1)} %pad_maximum_fusion.8.refs_2_, ...), custom_call_target="tpu_custom_call" | custom-call | flops 1 | bytes 1 | tf_op jit(solution)/shard_map/assemble/pallas_call | solution.py:385
  115.5 27.5 %attention_forward.1 = (bf16[1024,2048]{1,0:T(8,128)(2,1)}, bf16[1024,1024]{1,0:T(8,128)(2,1)S(1)}) custom-call(bf16[1024,1536]{1,0:T(8,128)(2,1)} %maximum_select_fusion.n1_ref.a_ref, bf16[1536,1536]{1,0:T(8,128)(2,1)} %get-tuple-element.332.w_ref, bf16[384,512]{1,0:T(8,128)(2,1)S(1)} %fusion.33.spread_ref, f32[1024,128]{1,0:T(8,128)S(1)} %get-tuple-element.334.cos_ref, ...), custom_call_target="tpu_custom_call" | custom-call | flops 1 | bytes 1 | tf_op jit(solution)/shard_map/attention_forward/pallas_call | solution.py:127
  145.1 1.8 convolution_convert_fusion
  146.9 1.8 fusion.21
  156.6 25.3 %collective-permute-done.15 = bf16[2,384,768]{2,1,0:T(8,128)(2,1)S(1)} collective-permute-done((bf16[2,384,768]{2,1,0:T(8,128)(2,1)S(1)}, bf16[2,384,768]{2,1,0:T(8,128)(2,1)S(1)}, u32[]{:S(2)}, u32[]{:S(2)}) %collective-permute-start.15) | collective-permute-done | bytes 1179680 | tf_op jit(solution)/shard_map/ppermute | solution.py:524
  181.9 6.3 %collective-permute-done.14 = bf16[512,1536]{1,0:T(8,128)(2,1)S(1)} collective-permute-done((bf16[512,1536]{1,0:T(8,128)(2,1)S(1)}, bf16[512,1536]{1,0:T(8,128)(2,1)S(1)}, u32[]{:S(2)}, u32[]{:S(2)}) %collective-permute-start.14) | collective-permute-done | bytes 1572896 | tf_op jit(solution)/shard_map/ppermute | solution.py:511
  192.8 1.7 pad_maximum_fusion.1.refs_1_
  198.9 2.9 collective-permute-start.20
  202.7 1.9 slice.276
  204.6 26.1 %feedforward.4 = (bf16[4,384,768]{2,1,0:T(8,128)(2,1)}, bf16[4,384,768]{2,1,0:T(8,128)(2,1)}, bf16[4,384,768]{2,1,0:T(8,128)(2,1)}, bf16[4,384,768]{2,1,0:T(8,12...) custom-call(bf16[512,1536]{1,0:T(8,128)(2,1)} %copy-done.17, ...), custom_call_target="tpu_custom_call" | custom-call | flops 1 | bytes 1 | tf_op jit(solution)/shard_map/feedforward/pallas_call | solution.py:243
  230.7 2.2 collective-permute-done.22.n2_ref
  234.3 3.1 pad_maximum_fusion.2.refs_0_
  238.7 28.0 %feedforward.5 = (bf16[4,384,768]{2,1,0:T(8,128)(2,1)}, bf16[4,384,768]{2,1,0:T(8,128)(2,1)}, bf16[4,384,768]{2,1,0:T(8,128)(2,1)}, bf16[4,384,768]{2,1,0:T(8,12...) custom-call(bf16[512,1536]{1,0:T(8,128)(2,1)} %collective-permute-done.22.n2_ref, ...), custom_call_target="tpu_custom_call" | custom-call | flops 1 | bytes 1 | tf_op jit(solution)/shard_map/feedforward/pallas_call | solution.py:243
  267.8 1.8 pad_maximum_fusion.3.refs_1_
  270.2 4.0 collective-permute-done.25.refs_3_
  275.6 2.0 collective-permute-done.26
  281.4 26.3 %feedforward.6 = (bf16[4,384,768]{2,1,0:T(8,128)(2,1)}, bf16[4,384,768]{2,1,0:T(8,128)(2,1)}, bf16[4,384,768]{2,1,0:T(8,128)(2,1)}, bf16[4,384,768]{2,1,0:T(8,12...) custom-call(bf16[512,1536]{1,0:T(8,128)(2,1)} %collective-permute-done.22.n2_ref, ...), custom_call_target="tpu_custom_call" | custom-call | flops 1 | bytes 1 | tf_op jit(solution)/shard_map/feedforward/pallas_call | solution.py:243
  309.2 3.2 add_convert_fusion.2
  314.6 3.1 fusion.35
  317.6 6.4 %collective-permute-start.30 = (bf16[384,768]{1,0:T(8,128)(2,1)}, bf16[384,768]{1,0:T(8,128)(2,1)}, u32[]{:S(2)}, u32[]{:S(2)}) collective-permute-start(bf16[384,768]{1,0:T(8,128)(2,1)} %get-tuple-element.475), channel_id=1, source_target_pairs={{0,2},{1,3},{2,0},{3,1},{4,6},{5,7},{6,4},{7,5},{8,10},{9,11},{10,... | collective-permute-start | bytes 1769480 | tf_op jit(solution)/shard_map/ppermute | solution.py:524
  324.1 28.2 %feedforward.7 = (bf16[4,384,768]{2,1,0:T(8,128)(2,1)}, bf16[4,384,768]{2,1,0:T(8,128)(2,1)}, bf16[4,384,768]{2,1,0:T(8,128)(2,1)}, bf16[4,384,768]{2,1,0:T(8,12...) custom-call(bf16[512,1536]{1,0:T(8,128)(2,1)} %copy-done.17, ...), custom_call_target="tpu_custom_call" | custom-call | flops 1 | bytes 1 | tf_op jit(solution)/shard_map/feedforward/pallas_call | solution.py:243
  353.5 6.8 %norm_back.1 = (f32[512,1536]{1,0:T(8,128)}, bf16[512,1536]{1,0:T(8,128)(2,1)}, f32[1,1536]{1,0:T(1,128)}) custom-call(f32[512,1536]{1,0:T(8,128)} %copy-done.8, f32[1,1536]{1,0:T(1,128)} %broadcast_in_dim.41.gain_ref, bf16[512,1536]{1,0:T(8,128)(2,1)} %maximum_select_fusion.4.cot_ref.skip_ref, bf16[512,1536]{1,0:T(8,128)(2,1)} %copy-done.33, ...), custom_call_target="tpu_custom_call" | custom-call | flops 1 | bytes 1 | tf_op jit(solution)/shard_map/norm_back/pallas_call | solution.py:464
  361.1 3.8 collective-permute-start.33
  364.9 1.9 add_convert_fusion.4
  368.4 3.1 fusion.37
  374.2 20.8 %collective-permute-done.35 = bf16[2,384,768]{2,1,0:T(8,128)(2,1)S(1)} collective-permute-done((bf16[2,384,768]{2,1,0:T(8,128)(2,1)S(1)}, bf16[2,384,768]{2,1,0:T(8,128)(2,1)S(1)}, u32[]{:S(2)}, u32[]{:S(2)}) %collective-permute-start.35) | collective-permute-done | bytes 1179680 | tf_op jit(solution)/shard_map/ppermute | solution.py:524
  395.0 5.2 collective-permute-done.33
  400.1 1.8 collective-permute-start.36
  401.9 2.1 collective-permute-start.37
  408.8 3.7 convolution_convert_fusion.1.do_ref
  412.6 15.7 %attention_backward.2.b_ref = bf16[1024,768]{1,0:T(8,128)(2,1)S(1)} custom-call(bf16[1024,2048]{1,0:T(8,128)(2,1)} %get-tuple-element.505.qkv_ref, bf16[1024,1024]{1,0:T(8,128)(2,1)S(1)} %convolution_convert_fusion.1.do_ref, bf16[512,384]{1,0:T(8,128)(2,1)S(1)} %fusion.32.gather_ref, f32[1024,128]{1,0:T(8,128)S(1)} %get-tuple-element.334.cos_ref, ...), custom_call_target="tpu_custom_call" | custom-call | flops 1 | bytes 1 | tf_op jit(solution)/shard_map/attention_backward/pallas_call | solution.py:154
  429.5 2.0 collective-permute-done.38
  431.4 3.3 fusion.41
  436.8 1.6 copy-done.1
  438.4 15.1 %attention_backward.3.b_ref = bf16[1024,768]{1,0:T(8,128)(2,1)S(1)} custom-call(bf16[1024,2048]{1,0:T(8,128)(2,1)} %get-tuple-element.505.qkv_ref, bf16[1024,1024]{1,0:T(8,128)(2,1)S(1)} %copy-done.1, bf16[512,384]{1,0:T(8,128)(2,1)S(1)} %fusion.32.gather_ref, f32[1024,128]{1,0:T(8,128)S(1)} %get-tuple-element.334.cos_ref, ...), custom_call_target="tpu_custom_call" | custom-call | flops 1 | bytes 1 | tf_op jit(solution)/shard_map/attention_backward/pallas_call | solution.py:154
  453.5 5.1 gradient_halves.3
  458.7 7.5 %gradient_halves.4 = bf16[2,4,96,1536]{3,2,1,0:T(8,128)(2,1)S(1)} custom-call(s32[1]{0:T(128)} %bitcast.15.core_ref, bf16[1024,1024]{1,0:T(8,128)(2,1)S(1)} %copy-done.3, bf16[1024,1536]{1,0:T(8,128)(2,1)} %copy-done.18), custom_call_target="tpu_custom_call" | custom-call | flops 1 | bytes 1 | tf_op jit(solution)/shard_map/gradient_halves/pallas_call | solution.py:412
  466.2 3.1 fusion.17
  469.3 5.1 gradient_halves.5
  481.0 3.2 collective-permute-start.45
  486.8 2.2 add_convert_fusion.11
  490.0 20.6 %collective-permute-done.45 = bf16[384,768]{1,0:T(8,128)(2,1)S(1)} collective-permute-done((bf16[384,768]{1,0:T(8,128)(2,1)S(1)}, bf16[384,768]{1,0:T(8,128)(2,1)S(1)}, u32[]{:S(2)}, u32[]{:S(2)}) %collective-permute-start.45) | collective-permute-done | bytes 589856 | tf_op jit(solution)/shard_map/ppermute | solution.py:524
  518.7 1.6 collective-permute-start.51
  520.4 2.2 collective-permute-start.52
  523.0 2.0 add_convert_fusion
  526.7 31.3 %collective-permute-done.51.refs_4_ = bf16[2,96,768]{2,1,0:T(8,128)(2,1)S(1)} collective-permute-done((bf16[2,96,768]{2,1,0:T(8,128)(2,1)S(1)}, bf16[2,96,768]{2,1,0:T(8,128)(2,1)S(1)}, u32[]{:S(2)}, u32[]{:S(2)}) %collective-permute-start.51) | collective-permute-done | bytes 294944 | tf_op jit(solution)/shard_map/ppermute | solution.py:524
  562.9 2.4 collective-permute-done.56
  566.3 2.7 collective-permute-done.57
  570.5 3.2 collective-permute-done.58
  576.2 6.8 %place.1 = (f32[12288,128]{1,0:T(8,128)}, f32[1024,768]{1,0:T(8,128)}) custom-call(bf16[2,2,384,768]{3,2,1,0:T(8,128)(2,1)S(1)} %get-tuple-element.634.refs_0_, bf16[2,2,384,768]{3,2,1,0:T(8,128)(2,1)S(1)} %get-tuple-element.633.refs_1_), custom_call_target="tpu_custom_call" | custom-call | flops 1 | bytes 1 | tf_op jit(solution)/shard_map/place/pallas_call | solution.py:280
  585.4 2.1 collective-permute-done.60
  588.3 2.0 place_attention.1
  (299 shorter events, 102.3 us)
Async XLA Ops:
  3.7 42.9 %collective-permute-start = (bf16[2,576,384]{2,1,0:T(8,128)(2,1)S(1)}, bf16[2,576,384]{2,1,0:T(8,128)(2,1)}, u32[]{:S(2)}, u32[]{:S(2)}) collective-permute-start(bf16[2,576,384]{2,1,0:T(8,128)(2,1)S(1)} %pad_maximum_fusion.8.refs_2_), channel_id=1, source_target_pairs={{0,2},{1,3},{2,0},{3,1},{4,6},{5,7},{6,4},{7,5},{8,10},{9,11},{10,... | collective-permute-start | bytes 2654216 | tf_op jit(solution)/shard_map/ppermute | solution.py:524
  7.8 38.8 %collective-permute-start.1 = (bf16[2,576,384]{2,1,0:T(8,128)(2,1)S(1)}, bf16[2,576,384]{2,1,0:T(8,128)(2,1)}, u32[]{:S(2)}, u32[]{:S(2)}) collective-permute-start(bf16[2,576,384]{2,1,0:T(8,128)(2,1)S(1)} %pad_maximum_fusion.8.refs_2_), channel_id=1, source_target_pairs={{0,4},{4,0},{1,5},{5,1},{2,6},{6,2},{3,7},{7,3},{8,12},{12,8},{9,1... | collective-permute-start | bytes 2654216 | tf_op jit(solution)/shard_map/ppermute | solution.py:524
  14.2 53.7 %collective-permute-start.2 = (bf16[512,1536]{1,0:T(8,128)(2,1)}, bf16[512,1536]{1,0:T(8,128)(2,1)}, u32[]{:S(2)}, u32[]{:S(2)}) collective-permute-start(bf16[512,1536]{1,0:T(8,128)(2,1)} %fusion.2), channel_id=1, source_target_pairs={{0,1},{1,0},{2,3},{3,2},{4,5},{5,4},{6,7},{7,6},{8,9},{9,8},{10,11... | collective-permute-start | bytes 4718600 | tf_op jit(solution)/shard_map/ppermute | solution.py:511
  67.9 30.9 %collective-permute-start.3 = (bf16[2,576,384]{2,1,0:T(8,128)(2,1)}, bf16[2,576,384]{2,1,0:T(8,128)(2,1)}, u32[]{:S(2)}, u32[]{:S(2)}) collective-permute-start(bf16[2,576,384]{2,1,0:T(8,128)(2,1)} %collective-permute-done.refs_0_), channel_id=1, source_target_pairs={{0,4},{4,0},{1,5},{5,1},{2,6},{6,2},{3,7},{7,3},{8,12},{12,8},{9,1... | collective-permute-start | bytes 2654216 | tf_op jit(solution)/shard_map/ppermute | solution.py:524
  67.9 30.9 %collective-permute-start.4 = (bf16[2,576,384]{2,1,0:T(8,128)(2,1)S(1)}, bf16[2,576,384]{2,1,0:T(8,128)(2,1)S(1)}, u32[]{:S(2)}, u32[]{:S(2)}) collective-permute-start(bf16[2,576,384]{2,1,0:T(8,128)(2,1)S(1)} %pad_maximum_fusion.8.refs_2_), channel_id=1, source_target_pairs={{0,8},{8,0},{16,24},{24,16},{1,9},{9,1},{17,25},{25,17},{2,10},{10... | collective-permute-start | bytes 2654216 | tf_op jit(solution)/shard_map/ppermute | solution.py:511
  67.9 31.8 %collective-permute-start.5 = (bf16[2,576,384]{2,1,0:T(8,128)(2,1)}, bf16[2,576,384]{2,1,0:T(8,128)(2,1)S(1)}, u32[]{:S(2)}, u32[]{:S(2)}) collective-permute-start(bf16[2,576,384]{2,1,0:T(8,128)(2,1)} %collective-permute-done.1.refs_6_), channel_id=1, source_target_pairs={{0,8},{8,0},{16,24},{24,16},{1,9},{9,1},{17,25},{25,17},{2,10},{10... | collective-permute-start | bytes 2654216 | tf_op jit(solution)/shard_map/ppermute | solution.py:511
  69.0 18.2 %collective-permute-start.6 = (bf16[384,768]{1,0:T(8,128)(2,1)S(1)}, bf16[384,768]{1,0:T(8,128)(2,1)}, u32[]{:S(2)}, u32[]{:S(2)}) collective-permute-start(bf16[384,768]{1,0:T(8,128)(2,1)S(1)} %pad_maximum_fusion.9), channel_id=1, source_target_pairs={{0,1},{1,2},{2,3},{3,0},{4,5},{5,6},{6,7},{7,4},{8,9},{9,10},{10,1... | collective-permute-start | bytes 1769480 | tf_op jit(solution)/shard_map/ppermute | solution.py:524
  69.0 29.8 %collective-permute-start.7 = (bf16[384,768]{1,0:T(8,128)(2,1)}, bf16[384,768]{1,0:T(8,128)(2,1)}, u32[]{:S(2)}, u32[]{:S(2)}) collective-permute-start(bf16[384,768]{1,0:T(8,128)(2,1)} %pad_maximum_fusion.10), channel_id=1, source_target_pairs={{0,1},{1,2},{2,3},{3,0},{4,5},{5,6},{6,7},{7,4},{8,9},{9,10},{10,1... | collective-permute-start | bytes 1769480 | tf_op jit(solution)/shard_map/ppermute | solution.py:524
  99.7 5.6 collective-permute-start.8
  102.2 41.3 %collective-permute-start.12 = (bf16[2,384,768]{2,1,0:T(8,128)(2,1)}, bf16[2,384,768]{2,1,0:T(8,128)(2,1)}, u32[]{:S(2)}, u32[]{:S(2)}) collective-permute-start(bf16[2,384,768]{2,1,0:T(8,128)(2,1)} %pad_maximum_fusion.4), channel_id=1, source_target_pairs={{0,4},{4,0},{1,5},{5,1},{2,6},{6,2},{3,7},{7,3},{8,12},{12,8},{9,1... | collective-permute-start | bytes 3538952 | tf_op jit(solution)/shard_map/ppermute | solution.py:524
  104.3 2.8 collective-permute-start.9
  104.3 38.8 %collective-permute-start.10 = (bf16[384,768]{1,0:T(8,128)(2,1)S(1)}, bf16[384,768]{1,0:T(8,128)(2,1)}, u32[]{:S(2)}, u32[]{:S(2)}) collective-permute-start(bf16[384,768]{1,0:T(8,128)(2,1)S(1)} %pad_maximum_fusion.9), channel_id=1, source_target_pairs={{0,2},{1,3},{2,0},{3,1},{4,6},{5,7},{6,4},{7,5},{8,10},{9,11},{10,... | collective-permute-start | bytes 1769480 | tf_op jit(solution)/shard_map/ppermute | solution.py:524
  104.3 38.8 %collective-permute-start.11 = (bf16[384,768]{1,0:T(8,128)(2,1)S(1)}, bf16[384,768]{1,0:T(8,128)(2,1)}, u32[]{:S(2)}, u32[]{:S(2)}) collective-permute-start(bf16[384,768]{1,0:T(8,128)(2,1)S(1)} %pad_maximum_fusion.9), channel_id=1, source_target_pairs={{0,3},{1,0},{2,1},{3,2},{4,7},{5,4},{6,5},{7,6},{8,11},{9,8},{10,9... | collective-permute-start | bytes 1769480 | tf_op jit(solution)/shard_map/ppermute | solution.py:524
  106.2 37.3 %collective-permute-start.13 = (bf16[384,768]{1,0:T(8,128)(2,1)}, bf16[384,768]{1,0:T(8,128)(2,1)}, u32[]{:S(2)}, u32[]{:S(2)}) collective-permute-start(bf16[384,768]{1,0:T(8,128)(2,1)} %collective-permute-done.6), channel_id=1, source_target_pairs={{0,4},{4,0},{1,5},{5,1},{2,6},{6,2},{3,7},{7,3},{8,12},{12,8},{9,1... | collective-permute-start | bytes 1769480 | tf_op jit(solution)/shard_map/ppermute | solution.py:524
  149.8 40.4 %copy-start.11 = (bf16[512,1536]{1,0:T(8,128)(2,1)S(1)}, bf16[512,1536]{1,0:T(8,128)(2,1)}, u32[]{:S(2)}) copy-start(bf16[512,1536]{1,0:T(8,128)(2,1)} %copy-done.10) | copy-start | bytes 4718596
  151.3 37.8 %copy-start.14 = (bf16[4,384,768]{2,1,0:T(8,128)(2,1)}, bf16[4,384,768]{2,1,0:T(8,128)(2,1)S(1)}, u32[]{:S(2)}) copy-start(bf16[4,384,768]{2,1,0:T(8,128)(2,1)S(1)} %pad_maximum_fusion.refs_0_) | copy-start | bytes 7077892
  151.3 38.9 %collective-permute-start.16 = (bf16[4,384,768]{2,1,0:T(8,128)(2,1)S(1)}, bf16[4,384,768]{2,1,0:T(8,128)(2,1)}, u32[]{:S(2)}, u32[]{:S(2)}) collective-permute-start(bf16[4,384,768]{2,1,0:T(8,128)(2,1)S(1)} %pad_maximum_fusion.refs_0_), channel_id=1, source_target_pairs={{0,8},{8,0},{16,24},{24,16},{1,9},{9,1},{17,25},{25,17},{2,10},{10... | collective-permute-start | bytes 7077896 | tf_op jit(solution)/shard_map/ppermute | solution.py:511
  151.6 36.6 %collective-permute-start.14 = (bf16[512,1536]{1,0:T(8,128)(2,1)S(1)}, bf16[512,1536]{1,0:T(8,128)(2,1)S(1)}, u32[]{:S(2)}, u32[]{:S(2)}) collective-permute-start(bf16[512,1536]{1,0:T(8,128)(2,1)S(1)} %convolution_convert_fusion), channel_id=1, source_target_pairs={{0,1},{1,0},{2,3},{3,2},{4,5},{5,4},{6,7},{7,6},{8,9},{9,8},{10,11... | collective-permute-start | bytes 4718600 | tf_op jit(solution)/shard_map/ppermute | solution.py:511
  152.6 36.5 %collective-permute-start.17 = (bf16[512,1536]{1,0:T(8,128)(2,1)S(1)}, bf16[512,1536]{1,0:T(8,128)(2,1)S(1)}, u32[]{:S(2)}, u32[]{:S(2)}) collective-permute-start(bf16[512,1536]{1,0:T(8,128)(2,1)S(1)} %copy-done.13), channel_id=1, source_target_pairs={{0,16},{8,24},{16,0},{24,8},{1,17},{9,25},{17,1},{25,9},{2,18},{10... | collective-permute-start | bytes 4718600 | tf_op jit(solution)/shard_map/ppermute | solution.py:511
  154.1 27.8 %collective-permute-start.15 = (bf16[2,384,768]{2,1,0:T(8,128)(2,1)S(1)}, bf16[2,384,768]{2,1,0:T(8,128)(2,1)S(1)}, u32[]{:S(2)}, u32[]{:S(2)}) collective-permute-start(bf16[2,384,768]{2,1,0:T(8,128)(2,1)S(1)} %pad_maximum_fusion.5), channel_id=1, source_target_pairs={{0,4},{4,0},{1,5},{5,1},{2,6},{6,2},{3,7},{7,3},{8,12},{12,8},{9,1... | collective-permute-start | bytes 3538952 | tf_op jit(solution)/shard_map/ppermute | solution.py:524
  196.0 8.6 %collective-permute-start.18 = (bf16[4,384,768]{2,1,0:T(8,128)(2,1)S(1)}, bf16[4,384,768]{2,1,0:T(8,128)(2,1)}, u32[]{:S(2)}, u32[]{:S(2)}) collective-permute-start(bf16[4,384,768]{2,1,0:T(8,128)(2,1)S(1)} %pad_maximum_fusion.1.refs_1_), channel_id=1, source_target_pairs={{0,8},{8,0},{16,24},{24,16},{1,9},{9,1},{17,25},{25,17},{2,10},{10... | collective-permute-start | bytes 7077896 | tf_op jit(solution)/shard_map/ppermute | solution.py:511
  196.0 36.9 %collective-permute-start.22 = (bf16[512,1536]{1,0:T(8,128)(2,1)S(1)}, bf16[512,1536]{1,0:T(8,128)(2,1)}, u32[]{:S(2)}, u32[]{:S(2)}) collective-permute-start(bf16[512,1536]{1,0:T(8,128)(2,1)S(1)} %multiply_convert_fusion.n2_ref), channel_id=1, source_target_pairs={{0,16},{8,24},{16,0},{24,8},{1,17},{9,25},{17,1},{25,9},{2,18},{10... | collective-permute-start | bytes 4718600 | tf_op jit(solution)/shard_map/ppermute | solution.py:511
  197.5 33.2 %collective-permute-start.19 = (bf16[384,768]{1,0:T(8,128)(2,1)}, bf16[384,768]{1,0:T(8,128)(2,1)}, u32[]{:S(2)}, u32[]{:S(2)}) collective-permute-start(bf16[384,768]{1,0:T(8,128)(2,1)} %collective-permute-done.7), channel_id=1, source_target_pairs={{0,4},{4,0},{1,5},{5,1},{2,6},{6,2},{3,7},{7,3},{8,12},{12,8},{9,1... | collective-permute-start | bytes 1769480 | tf_op jit(solution)/shard_map/ppermute | solution.py:524
  198.9 31.8 %collective-permute-start.20 = (bf16[384,768]{1,0:T(8,128)(2,1)}, bf16[384,768]{1,0:T(8,128)(2,1)}, u32[]{:S(2)}, u32[]{:S(2)}) collective-permute-start(bf16[384,768]{1,0:T(8,128)(2,1)} %pad_maximum_fusion.10), channel_id=1, source_target_pairs={{0,2},{1,3},{2,0},{3,1},{4,6},{5,7},{6,4},{7,5},{8,10},{9,11},{10,... | collective-permute-start | bytes 1769480 | tf_op jit(solution)/shard_map/ppermute | solution.py:524
  201.8 28.9 %collective-permute-start.21 = (bf16[384,768]{1,0:T(8,128)(2,1)}, bf16[384,768]{1,0:T(8,128)(2,1)}, u32[]{:S(2)}, u32[]{:S(2)}) collective-permute-start(bf16[384,768]{1,0:T(8,128)(2,1)} %pad_maximum_fusion.10), channel_id=1, source_target_pairs={{0,3},{1,0},{2,1},{3,2},{4,7},{5,4},{6,5},{7,6},{8,11},{9,8},{10,9... | collective-permute-start | bytes 1769480 | tf_op jit(solution)/shard_map/ppermute | solution.py:524
  237.4 29.3 %collective-permute-start.24 = (bf16[4,384,768]{2,1,0:T(8,128)(2,1)}, bf16[4,384,768]{2,1,0:T(8,128)(2,1)}, u32[]{:S(2)}, u32[]{:S(2)}) collective-permute-start(bf16[4,384,768]{2,1,0:T(8,128)(2,1)} %pad_maximum_fusion.2.refs_0_), channel_id=1, source_target_pairs={{0,8},{8,0},{16,24},{24,16},{1,9},{9,1},{17,25},{25,17},{2,10},{10... | collective-permute-start | bytes 7077896 | tf_op jit(solution)/shard_map/ppermute | solution.py:511
  237.4 29.3 %collective-permute-start.23 = (bf16[2,384,768]{2,1,0:T(8,128)(2,1)S(1)}, bf16[2,384,768]{2,1,0:T(8,128)(2,1)}, u32[]{:S(2)}, u32[]{:S(2)}) collective-permute-start(bf16[2,384,768]{2,1,0:T(8,128)(2,1)S(1)} %pad_maximum_fusion.6), channel_id=1, source_target_pairs={{0,4},{4,0},{1,5},{5,1},{2,6},{6,2},{3,7},{7,3},{8,12},{12,8},{9,1... | collective-permute-start | bytes 3538952 | tf_op jit(solution)/shard_map/ppermute | solution.py:524
  269.6 4.6 collective-permute-start.25
  270.0 7.6 %collective-permute-start.26 = (bf16[4,384,768]{2,1,0:T(8,128)(2,1)S(1)}, bf16[4,384,768]{2,1,0:T(8,128)(2,1)S(1)}, u32[]{:S(2)}, u32[]{:S(2)}) collective-permute-start(bf16[4,384,768]{2,1,0:T(8,128)(2,1)S(1)} %copy-done.48), channel_id=1, source_target_pairs={{0,8},{8,0},{16,24},{24,16},{1,9},{9,1},{17,25},{25,17},{2,10},{10... | collective-permute-start | bytes 7077896 | tf_op jit(solution)/shard_map/ppermute | solution.py:511
  280.5 28.7 %collective-permute-start.28 = (bf16[4,384,768]{2,1,0:T(8,128)(2,1)}, bf16[4,384,768]{2,1,0:T(8,128)(2,1)}, u32[]{:S(2)}, u32[]{:S(2)}) collective-permute-start(bf16[4,384,768]{2,1,0:T(8,128)(2,1)} %get-tuple-element.438), channel_id=1, source_target_pairs={{0,8},{8,0},{16,24},{24,16},{1,9},{9,1},{17,25},{25,17},{2,10},{10... | collective-permute-start | bytes 7077896 | tf_op jit(solution)/shard_map/ppermute | solution.py:511
  280.7 28.5 %collective-permute-start.27 = (bf16[2,384,768]{2,1,0:T(8,128)(2,1)}, bf16[2,384,768]{2,1,0:T(8,128)(2,1)}, u32[]{:S(2)}, u32[]{:S(2)}) collective-permute-start(bf16[2,384,768]{2,1,0:T(8,128)(2,1)} %add_convert_fusion.6), channel_id=1, source_target_pairs={{0,4},{4,0},{1,5},{5,1},{2,6},{6,2},{3,7},{7,3},{8,12},{12,8},{9,1... | collective-permute-start | bytes 3538952 | tf_op jit(solution)/shard_map/ppermute | solution.py:524
  312.3 40.0 %collective-permute-start.31 = (bf16[512,1536]{1,0:T(8,128)(2,1)}, bf16[512,1536]{1,0:T(8,128)(2,1)S(1)}, u32[]{:S(2)}, u32[]{:S(2)}) collective-permute-start(bf16[512,1536]{1,0:T(8,128)(2,1)} %add_convert_fusion.2), channel_id=1, source_target_pairs={{0,16},{8,24},{16,0},{24,8},{1,17},{9,25},{17,1},{25,9},{2,18},{10... | collective-permute-start | bytes 4718600 | tf_op jit(solution)/shard_map/ppermute | solution.py:511
  313.9 38.4 %collective-permute-start.29 = (bf16[2,384,768]{2,1,0:T(8,128)(2,1)}, bf16[2,384,768]{2,1,0:T(8,128)(2,1)}, u32[]{:S(2)}, u32[]{:S(2)}) collective-permute-start(bf16[2,384,768]{2,1,0:T(8,128)(2,1)} %add_convert_fusion.5), channel_id=1, source_target_pairs={{0,4},{4,0},{1,5},{5,1},{2,6},{6,2},{3,7},{7,3},{8,12},{12,8},{9,1... | collective-permute-start | bytes 3538952 | tf_op jit(solution)/shard_map/ppermute | solution.py:524
  317.6 34.7 %collective-permute-start.30 = (bf16[384,768]{1,0:T(8,128)(2,1)}, bf16[384,768]{1,0:T(8,128)(2,1)}, u32[]{:S(2)}, u32[]{:S(2)}) collective-permute-start(bf16[384,768]{1,0:T(8,128)(2,1)} %get-tuple-element.475), channel_id=1, source_target_pairs={{0,2},{1,3},{2,0},{3,1},{4,6},{5,7},{6,4},{7,5},{8,10},{9,11},{10,... | collective-permute-start | bytes 1769480 | tf_op jit(solution)/shard_map/ppermute | solution.py:524
  352.4 8.7 %collective-permute-start.32 = (bf16[4,384,768]{2,1,0:T(8,128)(2,1)}, bf16[4,384,768]{2,1,0:T(8,128)(2,1)}, u32[]{:S(2)}, u32[]{:S(2)}) collective-permute-start(bf16[4,384,768]{2,1,0:T(8,128)(2,1)} %get-tuple-element.478), channel_id=1, source_target_pairs={{0,8},{8,0},{16,24},{24,16},{1,9},{9,1},{17,25},{25,17},{2,10},{10... | collective-permute-start | bytes 7077896 | tf_op jit(solution)/shard_map/ppermute | solution.py:511
  361.0 39.1 %collective-permute-start.34 = (bf16[4,384,768]{2,1,0:T(8,128)(2,1)}, bf16[4,384,768]{2,1,0:T(8,128)(2,1)S(1)}, u32[]{:S(2)}, u32[]{:S(2)}) collective-permute-start(bf16[4,384,768]{2,1,0:T(8,128)(2,1)} %get-tuple-element.491), channel_id=1, source_target_pairs={{0,8},{8,0},{16,24},{24,16},{1,9},{9,1},{17,25},{25,17},{2,10},{10... | collective-permute-start | bytes 7077896 | tf_op jit(solution)/shard_map/ppermute | solution.py:511
  361.1 39.0 %collective-permute-start.33 = (bf16[512,1536]{1,0:T(8,128)(2,1)}, bf16[512,1536]{1,0:T(8,128)(2,1)S(1)}, u32[]{:S(2)}, u32[]{:S(2)}) collective-permute-start(bf16[512,1536]{1,0:T(8,128)(2,1)} %get-tuple-element.506), channel_id=1, source_target_pairs={{0,1},{1,0},{2,3},{3,2},{4,5},{5,4},{6,7},{7,6},{8,9},{9,8},{10,11... | collective-permute-start | bytes 4718600 | tf_op jit(solution)/shard_map/ppermute | solution.py:511
  366.8 28.1 %collective-permute-start.35 = (bf16[2,384,768]{2,1,0:T(8,128)(2,1)S(1)}, bf16[2,384,768]{2,1,0:T(8,128)(2,1)S(1)}, u32[]{:S(2)}, u32[]{:S(2)}) collective-permute-start(bf16[2,384,768]{2,1,0:T(8,128)(2,1)S(1)} %add_convert_fusion.4), channel_id=1, source_target_pairs={{0,4},{4,0},{1,5},{5,1},{2,6},{6,2},{3,7},{7,3},{8,12},{12,8},{9,1... | collective-permute-start | bytes 3538952 | tf_op jit(solution)/shard_map/ppermute | solution.py:524
  400.1 28.1 %collective-permute-start.36 = (bf16[384,768]{1,0:T(8,128)(2,1)}, bf16[384,768]{1,0:T(8,128)(2,1)}, u32[]{:S(2)}, u32[]{:S(2)}) collective-permute-start(bf16[384,768]{1,0:T(8,128)(2,1)} %get-tuple-element.511), channel_id=1, source_target_pairs={{0,1},{1,2},{2,3},{3,0},{4,5},{5,6},{6,7},{7,4},{8,9},{9,10},{10,1... | collective-permute-start | bytes 1769480 | tf_op jit(solution)/shard_map/ppermute | solution.py:524
  401.9 27.6 %collective-permute-start.37 = (bf16[384,768]{1,0:T(8,128)(2,1)}, bf16[384,768]{1,0:T(8,128)(2,1)}, u32[]{:S(2)}, u32[]{:S(2)}) collective-permute-start(bf16[384,768]{1,0:T(8,128)(2,1)} %get-tuple-element.512), channel_id=1, source_target_pairs={{0,3},{1,0},{2,1},{3,2},{4,7},{5,4},{6,5},{7,6},{8,11},{9,8},{10,9... | collective-permute-start | bytes 1769480 | tf_op jit(solution)/shard_map/ppermute | solution.py:524
  404.0 27.5 %collective-permute-start.38 = (bf16[2,384,768]{2,1,0:T(8,128)(2,1)}, bf16[2,384,768]{2,1,0:T(8,128)(2,1)}, u32[]{:S(2)}, u32[]{:S(2)}) collective-permute-start(bf16[2,384,768]{2,1,0:T(8,128)(2,1)} %add_convert_fusion.3), channel_id=1, source_target_pairs={{0,4},{4,0},{1,5},{5,1},{2,6},{6,2},{3,7},{7,3},{8,12},{12,8},{9,1... | collective-permute-start | bytes 3538952 | tf_op jit(solution)/shard_map/ppermute | solution.py:524
  407.0 59.2 %collective-permute-start.41 = (bf16[512,1536]{1,0:T(8,128)(2,1)}, bf16[512,1536]{1,0:T(8,128)(2,1)}, u32[]{:S(2)}, u32[]{:S(2)}) collective-permute-start(bf16[512,1536]{1,0:T(8,128)(2,1)} %add_convert_fusion.1), channel_id=1, source_target_pairs={{0,16},{8,24},{16,0},{24,8},{1,17},{9,25},{17,1},{25,9},{2,18},{10... | collective-permute-start | bytes 4718600 | tf_op jit(solution)/shard_map/ppermute | solution.py:511
  434.7 31.4 %collective-permute-start.39 = (bf16[384,768]{1,0:T(8,128)(2,1)}, bf16[384,768]{1,0:T(8,128)(2,1)}, u32[]{:S(2)}, u32[]{:S(2)}) collective-permute-start(bf16[384,768]{1,0:T(8,128)(2,1)} %get-tuple-element.522), channel_id=1, source_target_pairs={{0,3},{1,0},{2,1},{3,2},{4,7},{5,4},{6,5},{7,6},{8,11},{9,8},{10,9... | collective-permute-start | bytes 1769480 | tf_op jit(solution)/shard_map/ppermute | solution.py:524
  436.3 29.9 %collective-permute-start.40 = (bf16[384,768]{1,0:T(8,128)(2,1)}, bf16[384,768]{1,0:T(8,128)(2,1)}, u32[]{:S(2)}, u32[]{:S(2)}) collective-permute-start(bf16[384,768]{1,0:T(8,128)(2,1)} %get-tuple-element.524), channel_id=1, source_target_pairs={{0,1},{1,2},{2,3},{3,0},{4,5},{5,6},{6,7},{7,4},{8,9},{9,10},{10,1... | collective-permute-start | bytes 1769480 | tf_op jit(solution)/shard_map/ppermute | solution.py:524
  474.5 5.1 collective-permute-start.42
  474.7 4.9 collective-permute-start.43
  480.3 32.5 %collective-permute-start.44 = (bf16[256,1536]{1,0:T(8,128)(2,1)S(1)}, bf16[256,1536]{1,0:T(8,128)(2,1)S(1)}, u32[]{:S(2)}, u32[]{:S(2)}) collective-permute-start(bf16[256,1536]{1,0:T(8,128)(2,1)S(1)} %slice.320), channel_id=1, source_target_pairs={{0,1},{1,0},{2,3},{3,2},{4,5},{5,4},{6,7},{7,6},{8,9},{9,8},{10,11... | collective-permute-start | bytes 2359304 | tf_op jit(solution)/shard_map/ppermute | solution.py:511
  481.0 29.6 %collective-permute-start.45 = (bf16[384,768]{1,0:T(8,128)(2,1)S(1)}, bf16[384,768]{1,0:T(8,128)(2,1)S(1)}, u32[]{:S(2)}, u32[]{:S(2)}) collective-permute-start(bf16[384,768]{1,0:T(8,128)(2,1)S(1)} %copy-done.41), channel_id=1, source_target_pairs={{0,2},{1,3},{2,0},{3,1},{4,6},{5,7},{6,4},{7,5},{8,10},{9,11},{10,... | collective-permute-start | bytes 1769480 | tf_op jit(solution)/shard_map/ppermute | solution.py:524
  484.3 26.3 %collective-permute-start.46 = (bf16[384,768]{1,0:T(8,128)(2,1)S(1)}, bf16[384,768]{1,0:T(8,128)(2,1)S(1)}, u32[]{:S(2)}, u32[]{:S(2)}) collective-permute-start(bf16[384,768]{1,0:T(8,128)(2,1)S(1)} %get-tuple-element.664), channel_id=1, source_target_pairs={{0,4},{4,0},{1,5},{5,1},{2,6},{6,2},{3,7},{7,3},{8,12},{12,8},{9,1... | collective-permute-start | bytes 1769480 | tf_op jit(solution)/shard_map/ppermute | solution.py:524
  486.0 26.8 %collective-permute-start.48 = (bf16[2,384,768]{2,1,0:T(8,128)(2,1)S(1)}, bf16[2,384,768]{2,1,0:T(8,128)(2,1)S(1)}, u32[]{:S(2)}, u32[]{:S(2)}) collective-permute-start(bf16[2,384,768]{2,1,0:T(8,128)(2,1)S(1)} %slice_bitcast_fusion), channel_id=1, source_target_pairs={{0,8},{8,0},{16,24},{24,16},{1,9},{9,1},{17,25},{25,17},{2,10},{10... | collective-permute-start | bytes 3538952 | tf_op jit(solution)/shard_map/ppermute | solution.py:511
  486.1 25.9 %collective-permute-start.47 = (bf16[4,96,768]{2,1,0:T(8,128)(2,1)S(1)}, bf16[4,96,768]{2,1,0:T(8,128)(2,1)S(1)}, u32[]{:S(2)}, u32[]{:S(2)}) collective-permute-start(bf16[4,96,768]{2,1,0:T(8,128)(2,1)S(1)} %get-tuple-element.662), channel_id=1, source_target_pairs={{0,4},{4,0},{1,5},{5,1},{2,6},{6,2},{3,7},{7,3},{8,12},{12,8},{9,1... | collective-permute-start | bytes 1769480 | tf_op jit(solution)/shard_map/ppermute | solution.py:524
  515.8 42.2 %collective-permute-start.49 = (bf16[384,768]{1,0:T(8,128)(2,1)S(1)}, bf16[384,768]{1,0:T(8,128)(2,1)S(1)}, u32[]{:S(2)}, u32[]{:S(2)}) collective-permute-start(bf16[384,768]{1,0:T(8,128)(2,1)S(1)} %get-tuple-element.660), channel_id=1, source_target_pairs={{0,4},{4,0},{1,5},{5,1},{2,6},{6,2},{3,7},{7,3},{8,12},{12,8},{9,1... | collective-permute-start | bytes 1769480 | tf_op jit(solution)/shard_map/ppermute | solution.py:524
  517.3 40.7 %collective-permute-start.50 = (bf16[384,768]{1,0:T(8,128)(2,1)S(1)}, bf16[384,768]{1,0:T(8,128)(2,1)S(1)}, u32[]{:S(2)}, u32[]{:S(2)}) collective-permute-start(bf16[384,768]{1,0:T(8,128)(2,1)S(1)} %add_convert_fusion.10), channel_id=1, source_target_pairs={{0,2},{1,3},{2,0},{3,1},{4,6},{5,7},{6,4},{7,5},{8,10},{9,11},{10,... | collective-permute-start | bytes 1769480 | tf_op jit(solution)/shard_map/ppermute | solution.py:524
  518.7 39.3 %collective-permute-start.51 = (bf16[2,96,768]{2,1,0:T(8,128)(2,1)S(1)}, bf16[2,96,768]{2,1,0:T(8,128)(2,1)S(1)}, u32[]{:S(2)}, u32[]{:S(2)}) collective-permute-start(bf16[2,96,768]{2,1,0:T(8,128)(2,1)S(1)} %slice.329), channel_id=1, source_target_pairs={{0,2},{1,3},{2,0},{3,1},{4,6},{5,7},{6,4},{7,5},{8,10},{9,11},{10,... | collective-permute-start | bytes 884744 | tf_op jit(solution)/shard_map/ppermute | solution.py:524
  520.4 37.6 %collective-permute-start.52 = (bf16[256,1536]{1,0:T(8,128)(2,1)S(1)}, bf16[256,1536]{1,0:T(8,128)(2,1)S(1)}, u32[]{:S(2)}, u32[]{:S(2)}) collective-permute-start(bf16[256,1536]{1,0:T(8,128)(2,1)S(1)} %slice.330), channel_id=1, source_target_pairs={{0,1},{1,0},{2,3},{3,2},{4,5},{5,4},{6,7},{7,6},{8,9},{9,8},{10,11... | collective-permute-start | bytes 2359304 | tf_op jit(solution)/shard_map/ppermute | solution.py:511
  522.6 35.4 %collective-permute-start.53 = (bf16[2,384,768]{2,1,0:T(8,128)(2,1)S(1)}, bf16[2,384,768]{2,1,0:T(8,128)(2,1)S(1)}, u32[]{:S(2)}, u32[]{:S(2)}) collective-permute-start(bf16[2,384,768]{2,1,0:T(8,128)(2,1)S(1)} %pad_maximum_fusion.7), channel_id=1, source_target_pairs={{0,16},{8,24},{16,0},{24,8},{1,17},{9,25},{17,1},{25,9},{2,18},{10... | collective-permute-start | bytes 3538952 | tf_op jit(solution)/shard_map/ppermute | solution.py:511
  558.4 24.7 %collective-permute-start.54 = (bf16[2,576,384]{2,1,0:T(8,128)(2,1)S(1)}, bf16[2,576,384]{2,1,0:T(8,128)(2,1)S(1)}, u32[]{:S(2)}, u32[]{:S(2)}) collective-permute-start(bf16[2,576,384]{2,1,0:T(8,128)(2,1)S(1)} %combine.1), channel_id=1, source_target_pairs={{0,16},{8,24},{16,0},{24,8},{1,17},{9,25},{17,1},{25,9},{2,18},{10... | collective-permute-start | bytes 2654216 | tf_op jit(solution)/shard_map/ppermute | solution.py:511
  559.3 16.1 %collective-permute-start.55 = (bf16[2,2,384,768]{3,2,1,0:T(8,128)(2,1)S(1)}, bf16[2,2,384,768]{3,2,1,0:T(8,128)(2,1)S(1)}, u32[]{:S(2)}, u32[]{:S(2)}) collective-permute-start(bf16[2,2,384,768]{3,2,1,0:T(8,128)(2,1)S(1)} %maximum_select_fusion.2), channel_id=1, source_target_pairs={{0,8},{8,0},{16,24},{24,16},{1,9},{9,1},{17,25},{25,17},{2,10},{10... | collective-permute-start | bytes 7077896 | tf_op jit(solution)/shard_map/ppermute | solution.py:511
  561.5 3.8 collective-permute-start.56
  565.3 3.8 collective-permute-start.57
  569.1 4.7 collective-permute-start.58
  573.7 1.6 collective-permute-start.59
  583.3 4.9 collective-permute-start.61
  583.8 3.7 collective-permute-start.60
  (50 other events, 342.3 us)

commit v6 on v5

--- a/solution.py
+++ b/solution.py
@@ -397,11 +397,15 @@
 
 def halves_kernel(gap, core_ref, a_ref, b_ref, out_ref):
     g = dot_tn(a_ref[...], b_ref[...]).astype(BF)
-    if gap:
-        out_ref[0, 0, :HALF] = g[:HALF]
-        out_ref[0, 0, HALF:] = g[LANES // 2 : LANES // 2 + HALF]
-    else:
-        out_ref[0, 0] = g
+    rows = g.shape[0] // 2
+    first = core_ref[0] == 0
+    for h, (low, high) in enumerate(((0, rows), (rows, 0))):
+        piece = jnp.where(first, g[low : low + rows], g[high : high + rows])
+        if gap:
+            out_ref[h, 0, :HALF] = piece[:HALF]
+            out_ref[h, 0, HALF:] = piece[LANES // 2 : LANES // 2 + HALF]
+        else:
+            out_ref[h, 0] = piece
 
 
 def gradient_halves(core, a, b, rows, gap=False):
@@ -413,12 +417,12 @@
         functools.partial(halves_kernel, gap),
         grid_spec=pltpu.PrefetchScalarGridSpec(
             num_scalar_prefetch=1,
-            grid=(2, blocks),
+            grid=(blocks,),
             in_specs=[
-                pl.BlockSpec((tokens, rows), lambda h, i, core: (0, 2 * i + (core[0] + h) % 2)),
-                pl.BlockSpec(b.shape, lambda h, i, core: (0, 0)),
+                pl.BlockSpec((tokens, 2 * rows), lambda i, core: (0, i)),
+                pl.BlockSpec(b.shape, lambda i, core: (0, 0)),
             ],
-            out_specs=pl.BlockSpec((1, 1, kept, columns), lambda h, i, core: (h, i, 0, 0)),
+            out_specs=pl.BlockSpec((2, 1, kept, columns), lambda i, core: (0, i, 0, 0)),
         ),
         out_shape=jax.ShapeDtypeStruct((2, blocks, kept, columns), BF),
         compiler_params=pltpu.CompilerParams(vmem_limit_bytes=48 * 1024 * 1024),

time: 599 us -> 597 us (level)
  no operation moved by 1% of the time
where the time goes in v6:
time: 597 us; the launch traced here: 589 us
  Pallas kernels  205 us (34%)
  waiting for transfers between devices  202 us (34%)
  starting transfers between devices  66.6 us (11%)
  other arithmetic  66.5 us (11%)
  local copies, waits for them, and re-layouts  32.1 us (5%)
  matrix products  14.6 us (2%)
    ppermute x29, waiting for transfers between devices, shift(): return lax.ppermute(a, axis, [(i, (i + by) % n) for i in range(n)])  148 us
    pallas_call x4, Pallas kernels, feedforward(): pl.pallas_call(functools.partial(feedforward_kernel, col_step, sub, rows_...  109 us
    ppermute x30, waiting for transfers between devices, swap(): return lax.ppermute(a, axis, [(i, i ^ bit) for i in range(n)])  45.3 us
    ppermute x29, starting transfers between devices, shift(): return lax.ppermute(a, axis, [(i, (i + by) % n) for i in range(n)])  44.4 us
    pallas_call x2, Pallas kernels, attention_backward(): pl.pallas_call(attention_backward_kernel, grid=(groups,), in_specs=[pl.Bl...  30.8 us
    pallas_call x1, Pallas kernels, attention_forward(): pl.pallas_call(attention_forward_kernel, grid=(groups,), in_specs=[whole(...  27.5 us
    convert_element_type x16, other arithmetic, small(): return total(*parts).astype(BF)  23.6 us
    ppermute x30, starting transfers between devices, swap(): return lax.ppermute(a, axis, [(i, i ^ bit) for i in range(n)])  19.4 us
  transfers between devices with their start and end apart: 62, of which 25 were waited for; matrix products, arithmetic and copies ran while one was open for 11% of the time, Pallas kernels for 34%

profile of v6, /device:TPU:0, one launch (start us, length us, event | category | flops | bytes accessed | tf_op | source)
XLA Modules:
  0.0 588.9 jit_solution(7983539052288944588)
XLA Ops:
  3.7 4.1 collective-permute-start
  9.5 2.1 fusion
  16.9 1.7 dynamic-slice_bitcast_fusion
  19.5 1.9 multiply_sine_fusion
  24.2 2.9 maximum_select_fusion.4.cot_ref.skip_ref
  27.2 19.5 %collective-permute-done.refs_0_ = bf16[2,576,384]{2,1,0:T(8,128)(2,1)} collective-permute-done((bf16[2,576,384]{2,1,0:T(8,128)(2,1)S(1)}, bf16[2,576,384]{2,1,0:T(8,128)(2,1)}, u32[]{:S(2)}, u32[]{:S(2)}) %collective-permute-start) | collective-permute-done | bytes 884768 | tf_op jit(solution)/shard_map/ppermute | solution.py:528
  46.7 21.3 %collective-permute-done.2 = bf16[512,1536]{1,0:T(8,128)(2,1)} collective-permute-done((bf16[512,1536]{1,0:T(8,128)(2,1)}, bf16[512,1536]{1,0:T(8,128)(2,1)}, u32[]{:S(2)}, u32[]{:S(2)}) %collective-permute-start.2) | collective-permute-done | bytes 1572896 | tf_op jit(solution)/shard_map/ppermute | solution.py:515
  70.2 4.4 maximum_select_fusion.n1_ref.a_ref
  74.6 12.5 %collective-permute-done.6 = bf16[384,768]{1,0:T(8,128)(2,1)} collective-permute-done((bf16[384,768]{1,0:T(8,128)(2,1)S(1)}, bf16[384,768]{1,0:T(8,128)(2,1)}, u32[]{:S(2)}, u32[]{:S(2)}) %collective-permute-start.6) | collective-permute-done | bytes 589856 | tf_op jit(solution)/shard_map/ppermute | solution.py:528
  87.1 11.7 %collective-permute-done.7 = bf16[384,768]{1,0:T(8,128)(2,1)} collective-permute-done((bf16[384,768]{1,0:T(8,128)(2,1)}, bf16[384,768]{1,0:T(8,128)(2,1)}, u32[]{:S(2)}, u32[]{:S(2)}) %collective-permute-start.7) | collective-permute-done | bytes 589856 | tf_op jit(solution)/shard_map/ppermute | solution.py:528
  99.7 2.5 pad_maximum_fusion.4
  102.2 2.0 collective-permute-start.12
  109.4 6.2 %assemble.1 = (bf16[1536,1536]{1,0:T(8,128)(2,1)}, bf16[1024,1536]{1,0:T(8,128)(2,1)}) custom-call(s32[1]{0:T(128)} %bitcast.15.core_ref, bf16[2,576,384]{2,1,0:T(8,128)(2,1)} %collective-permute-done.refs_0_, bf16[2,576,384]{2,1,0:T(8,128)(2,1)S(1)} %copy-done.7, bf16[2,576,384]{2,1,0:T(8,128)(2,1)S(1)} %pad_maximum_fusion.8.refs_2_, ...), custom_call_target="tpu_custom_call" | custom-call | flops 1 | bytes 1 | tf_op jit(solution)/shard_map/assemble/pallas_call | solution.py:385
  115.5 27.5 %attention_forward.1 = (bf16[1024,2048]{1,0:T(8,128)(2,1)}, bf16[1024,1024]{1,0:T(8,128)(2,1)S(1)}) custom-call(bf16[1024,1536]{1,0:T(8,128)(2,1)} %maximum_select_fusion.n1_ref.a_ref, bf16[1536,1536]{1,0:T(8,128)(2,1)} %get-tuple-element.332.w_ref, bf16[384,512]{1,0:T(8,128)(2,1)S(1)} %fusion.33.spread_ref, f32[1024,128]{1,0:T(8,128)S(1)} %get-tuple-element.334.cos_ref, ...), custom_call_target="tpu_custom_call" | custom-call | flops 1 | bytes 1 | tf_op jit(solution)/shard_map/attention_forward/pallas_call | solution.py:127
  145.1 1.8 convolution_convert_fusion
  146.9 1.8 fusion.21
  156.6 25.3 %collective-permute-done.15 = bf16[2,384,768]{2,1,0:T(8,128)(2,1)S(1)} collective-permute-done((bf16[2,384,768]{2,1,0:T(8,128)(2,1)S(1)}, bf16[2,384,768]{2,1,0:T(8,128)(2,1)S(1)}, u32[]{:S(2)}, u32[]{:S(2)}) %collective-permute-start.15) | collective-permute-done | bytes 1179680 | tf_op jit(solution)/shard_map/ppermute | solution.py:528
  181.9 6.3 %collective-permute-done.14 = bf16[512,1536]{1,0:T(8,128)(2,1)S(1)} collective-permute-done((bf16[512,1536]{1,0:T(8,128)(2,1)S(1)}, bf16[512,1536]{1,0:T(8,128)(2,1)S(1)}, u32[]{:S(2)}, u32[]{:S(2)}) %collective-permute-start.14) | collective-permute-done | bytes 1572896 | tf_op jit(solution)/shard_map/ppermute | solution.py:515
  192.8 1.7 pad_maximum_fusion.1.refs_1_
  198.9 2.9 collective-permute-start.20
  202.7 1.9 slice.276
  204.6 26.1 %feedforward.4 = (bf16[4,384,768]{2,1,0:T(8,128)(2,1)}, bf16[4,384,768]{2,1,0:T(8,128)(2,1)}, bf16[4,384,768]{2,1,0:T(8,128)(2,1)}, bf16[4,384,768]{2,1,0:T(8,12...) custom-call(bf16[512,1536]{1,0:T(8,128)(2,1)} %copy-done.17, ...), custom_call_target="tpu_custom_call" | custom-call | flops 1 | bytes 1 | tf_op jit(solution)/shard_map/feedforward/pallas_call | solution.py:243
  230.7 2.2 collective-permute-done.22.n2_ref
  234.3 3.1 pad_maximum_fusion.2.refs_0_
  238.7 28.0 %feedforward.5 = (bf16[4,384,768]{2,1,0:T(8,128)(2,1)}, bf16[4,384,768]{2,1,0:T(8,128)(2,1)}, bf16[4,384,768]{2,1,0:T(8,128)(2,1)}, bf16[4,384,768]{2,1,0:T(8,12...) custom-call(bf16[512,1536]{1,0:T(8,128)(2,1)} %collective-permute-done.22.n2_ref, ...), custom_call_target="tpu_custom_call" | custom-call | flops 1 | bytes 1 | tf_op jit(solution)/shard_map/feedforward/pallas_call | solution.py:243
  267.8 1.8 pad_maximum_fusion.3.refs_1_
  270.2 4.0 collective-permute-done.25.refs_3_
  275.6 2.0 collective-permute-done.26
  281.4 26.3 %feedforward.6 = (bf16[4,384,768]{2,1,0:T(8,128)(2,1)}, bf16[4,384,768]{2,1,0:T(8,128)(2,1)}, bf16[4,384,768]{2,1,0:T(8,128)(2,1)}, bf16[4,384,768]{2,1,0:T(8,12...) custom-call(bf16[512,1536]{1,0:T(8,128)(2,1)} %collective-permute-done.22.n2_ref, ...), custom_call_target="tpu_custom_call" | custom-call | flops 1 | bytes 1 | tf_op jit(solution)/shard_map/feedforward/pallas_call | solution.py:243
  309.2 3.2 add_convert_fusion.2
  314.6 3.1 fusion.35
  317.6 6.4 %collective-permute-start.30 = (bf16[384,768]{1,0:T(8,128)(2,1)}, bf16[384,768]{1,0:T(8,128)(2,1)}, u32[]{:S(2)}, u32[]{:S(2)}) collective-permute-start(bf16[384,768]{1,0:T(8,128)(2,1)} %get-tuple-element.475), channel_id=1, source_target_pairs={{0,2},{1,3},{2,0},{3,1},{4,6},{5,7},{6,4},{7,5},{8,10},{9,11},{10,... | collective-permute-start | bytes 1769480 | tf_op jit(solution)/shard_map/ppermute | solution.py:528
  324.1 28.2 %feedforward.7 = (bf16[4,384,768]{2,1,0:T(8,128)(2,1)}, bf16[4,384,768]{2,1,0:T(8,128)(2,1)}, bf16[4,384,768]{2,1,0:T(8,128)(2,1)}, bf16[4,384,768]{2,1,0:T(8,12...) custom-call(bf16[512,1536]{1,0:T(8,128)(2,1)} %copy-done.17, ...), custom_call_target="tpu_custom_call" | custom-call | flops 1 | bytes 1 | tf_op jit(solution)/shard_map/feedforward/pallas_call | solution.py:243
  353.5 6.8 %norm_back.1 = (f32[512,1536]{1,0:T(8,128)}, bf16[512,1536]{1,0:T(8,128)(2,1)}, f32[1,1536]{1,0:T(1,128)}) custom-call(f32[512,1536]{1,0:T(8,128)} %copy-done.8, f32[1,1536]{1,0:T(1,128)} %broadcast_in_dim.41.gain_ref, bf16[512,1536]{1,0:T(8,128)(2,1)} %maximum_select_fusion.4.cot_ref.skip_ref, bf16[512,1536]{1,0:T(8,128)(2,1)} %copy-done.33, ...), custom_call_target="tpu_custom_call" | custom-call | flops 1 | bytes 1 | tf_op jit(solution)/shard_map/norm_back/pallas_call | solution.py:468
  361.1 3.8 collective-permute-start.33
  364.9 1.9 add_convert_fusion.4
  368.4 3.1 fusion.37
  374.2 20.8 %collective-permute-done.35 = bf16[2,384,768]{2,1,0:T(8,128)(2,1)S(1)} collective-permute-done((bf16[2,384,768]{2,1,0:T(8,128)(2,1)S(1)}, bf16[2,384,768]{2,1,0:T(8,128)(2,1)S(1)}, u32[]{:S(2)}, u32[]{:S(2)}) %collective-permute-start.35) | collective-permute-done | bytes 1179680 | tf_op jit(solution)/shard_map/ppermute | solution.py:528
  395.0 5.2 collective-permute-done.33
  400.1 1.8 collective-permute-start.36
  401.9 2.1 collective-permute-start.37
  408.8 3.7 convolution_convert_fusion.1.do_ref
  412.6 15.7 %attention_backward.2.b_ref = bf16[1024,768]{1,0:T(8,128)(2,1)S(1)} custom-call(bf16[1024,2048]{1,0:T(8,128)(2,1)} %get-tuple-element.505.qkv_ref, bf16[1024,1024]{1,0:T(8,128)(2,1)S(1)} %convolution_convert_fusion.1.do_ref, bf16[512,384]{1,0:T(8,128)(2,1)S(1)} %fusion.32.gather_ref, f32[1024,128]{1,0:T(8,128)S(1)} %get-tuple-element.334.cos_ref, ...), custom_call_target="tpu_custom_call" | custom-call | flops 1 | bytes 1 | tf_op jit(solution)/shard_map/attention_backward/pallas_call | solution.py:154
  429.5 2.0 collective-permute-done.38
  431.4 3.3 fusion.41
  436.8 1.6 copy-done.1
  438.4 15.1 %attention_backward.3.b_ref = bf16[1024,768]{1,0:T(8,128)(2,1)S(1)} custom-call(bf16[1024,2048]{1,0:T(8,128)(2,1)} %get-tuple-element.505.qkv_ref, bf16[1024,1024]{1,0:T(8,128)(2,1)S(1)} %copy-done.1, bf16[512,384]{1,0:T(8,128)(2,1)S(1)} %fusion.32.gather_ref, f32[1024,128]{1,0:T(8,128)S(1)} %get-tuple-element.334.cos_ref, ...), custom_call_target="tpu_custom_call" | custom-call | flops 1 | bytes 1 | tf_op jit(solution)/shard_map/attention_backward/pallas_call | solution.py:154
  453.5 4.6 gradient_halves.3
  458.2 6.4 %gradient_halves.4 = bf16[2,4,96,1536]{3,2,1,0:T(8,128)(2,1)S(1)} custom-call(s32[1]{0:T(128)} %bitcast.15.core_ref, bf16[1024,1024]{1,0:T(8,128)(2,1)S(1)} %copy-done.3, bf16[1024,1536]{1,0:T(8,128)(2,1)} %copy-done.18), custom_call_target="tpu_custom_call" | custom-call | flops 1 | bytes 1 | tf_op jit(solution)/shard_map/gradient_halves/pallas_call | solution.py:416
  464.6 3.1 fusion.17
  467.7 4.7 gradient_halves.5
  479.1 3.2 collective-permute-start.45
  484.8 2.2 add_convert_fusion.11
  488.0 20.6 %collective-permute-done.45 = bf16[384,768]{1,0:T(8,128)(2,1)S(1)} collective-permute-done((bf16[384,768]{1,0:T(8,128)(2,1)S(1)}, bf16[384,768]{1,0:T(8,128)(2,1)S(1)}, u32[]{:S(2)}, u32[]{:S(2)}) %collective-permute-start.45) | collective-permute-done | bytes 589856 | tf_op jit(solution)/shard_map/ppermute | solution.py:528
  516.8 1.6 collective-permute-start.51
  518.4 2.2 collective-permute-start.52
  521.1 2.0 add_convert_fusion
  524.7 31.3 %collective-permute-done.51.refs_4_ = bf16[2,96,768]{2,1,0:T(8,128)(2,1)S(1)} collective-permute-done((bf16[2,96,768]{2,1,0:T(8,128)(2,1)S(1)}, bf16[2,96,768]{2,1,0:T(8,128)(2,1)S(1)}, u32[]{:S(2)}, u32[]{:S(2)}) %collective-permute-start.51) | collective-permute-done | bytes 294944 | tf_op jit(solution)/shard_map/ppermute | solution.py:528
  560.9 2.4 collective-permute-done.56
  564.4 2.7 collective-permute-done.57
  568.5 3.2 collective-permute-done.58
  574.2 6.8 %place.1 = (f32[12288,128]{1,0:T(8,128)}, f32[1024,768]{1,0:T(8,128)}) custom-call(bf16[2,2,384,768]{3,2,1,0:T(8,128)(2,1)S(1)} %get-tuple-element.634.refs_0_, bf16[2,2,384,768]{3,2,1,0:T(8,128)(2,1)S(1)} %get-tuple-element.633.refs_1_), custom_call_target="tpu_custom_call" | custom-call | flops 1 | bytes 1 | tf_op jit(solution)/shard_map/place/pallas_call | solution.py:280
  583.4 2.1 collective-permute-done.60
  586.3 2.0 place_attention.1
  (299 shorter events, 102.4 us)
Async XLA Ops:
  3.7 42.9 %collective-permute-start = (bf16[2,576,384]{2,1,0:T(8,128)(2,1)S(1)}, bf16[2,576,384]{2,1,0:T(8,128)(2,1)}, u32[]{:S(2)}, u32[]{:S(2)}) collective-permute-start(bf16[2,576,384]{2,1,0:T(8,128)(2,1)S(1)} %pad_maximum_fusion.8.refs_2_), channel_id=1, source_target_pairs={{0,2},{1,3},{2,0},{3,1},{4,6},{5,7},{6,4},{7,5},{8,10},{9,11},{10,... | collective-permute-start | bytes 2654216 | tf_op jit(solution)/shard_map/ppermute | solution.py:528
  7.8 38.8 %collective-permute-start.1 = (bf16[2,576,384]{2,1,0:T(8,128)(2,1)S(1)}, bf16[2,576,384]{2,1,0:T(8,128)(2,1)}, u32[]{:S(2)}, u32[]{:S(2)}) collective-permute-start(bf16[2,576,384]{2,1,0:T(8,128)(2,1)S(1)} %pad_maximum_fusion.8.refs_2_), channel_id=1, source_target_pairs={{0,4},{4,0},{1,5},{5,1},{2,6},{6,2},{3,7},{7,3},{8,12},{12,8},{9,1... | collective-permute-start | bytes 2654216 | tf_op jit(solution)/shard_map/ppermute | solution.py:528
  14.2 53.7 %collective-permute-start.2 = (bf16[512,1536]{1,0:T(8,128)(2,1)}, bf16[512,1536]{1,0:T(8,128)(2,1)}, u32[]{:S(2)}, u32[]{:S(2)}) collective-permute-start(bf16[512,1536]{1,0:T(8,128)(2,1)} %fusion.2), channel_id=1, source_target_pairs={{0,1},{1,0},{2,3},{3,2},{4,5},{5,4},{6,7},{7,6},{8,9},{9,8},{10,11... | collective-permute-start | bytes 4718600 | tf_op jit(solution)/shard_map/ppermute | solution.py:515
  67.9 30.9 %collective-permute-start.3 = (bf16[2,576,384]{2,1,0:T(8,128)(2,1)}, bf16[2,576,384]{2,1,0:T(8,128)(2,1)}, u32[]{:S(2)}, u32[]{:S(2)}) collective-permute-start(bf16[2,576,384]{2,1,0:T(8,128)(2,1)} %collective-permute-done.refs_0_), channel_id=1, source_target_pairs={{0,4},{4,0},{1,5},{5,1},{2,6},{6,2},{3,7},{7,3},{8,12},{12,8},{9,1... | collective-permute-start | bytes 2654216 | tf_op jit(solution)/shard_map/ppermute | solution.py:528
  67.9 30.9 %collective-permute-start.4 = (bf16[2,576,384]{2,1,0:T(8,128)(2,1)S(1)}, bf16[2,576,384]{2,1,0:T(8,128)(2,1)S(1)}, u32[]{:S(2)}, u32[]{:S(2)}) collective-permute-start(bf16[2,576,384]{2,1,0:T(8,128)(2,1)S(1)} %pad_maximum_fusion.8.refs_2_), channel_id=1, source_target_pairs={{0,8},{8,0},{16,24},{24,16},{1,9},{9,1},{17,25},{25,17},{2,10},{10... | collective-permute-start | bytes 2654216 | tf_op jit(solution)/shard_map/ppermute | solution.py:515
  67.9 31.8 %collective-permute-start.5 = (bf16[2,576,384]{2,1,0:T(8,128)(2,1)}, bf16[2,576,384]{2,1,0:T(8,128)(2,1)S(1)}, u32[]{:S(2)}, u32[]{:S(2)}) collective-permute-start(bf16[2,576,384]{2,1,0:T(8,128)(2,1)} %collective-permute-done.1.refs_6_), channel_id=1, source_target_pairs={{0,8},{8,0},{16,24},{24,16},{1,9},{9,1},{17,25},{25,17},{2,10},{10... | collective-permute-start | bytes 2654216 | tf_op jit(solution)/shard_map/ppermute | solution.py:515
  69.0 18.2 %collective-permute-start.6 = (bf16[384,768]{1,0:T(8,128)(2,1)S(1)}, bf16[384,768]{1,0:T(8,128)(2,1)}, u32[]{:S(2)}, u32[]{:S(2)}) collective-permute-start(bf16[384,768]{1,0:T(8,128)(2,1)S(1)} %pad_maximum_fusion.9), channel_id=1, source_target_pairs={{0,1},{1,2},{2,3},{3,0},{4,5},{5,6},{6,7},{7,4},{8,9},{9,10},{10,1... | collective-permute-start | bytes 1769480 | tf_op jit(solution)/shard_map/ppermute | solution.py:528
  69.0 29.8 %collective-permute-start.7 = (bf16[384,768]{1,0:T(8,128)(2,1)}, bf16[384,768]{1,0:T(8,128)(2,1)}, u32[]{:S(2)}, u32[]{:S(2)}) collective-permute-start(bf16[384,768]{1,0:T(8,128)(2,1)} %pad_maximum_fusion.10), channel_id=1, source_target_pairs={{0,1},{1,2},{2,3},{3,0},{4,5},{5,6},{6,7},{7,4},{8,9},{9,10},{10,1... | collective-permute-start | bytes 1769480 | tf_op jit(solution)/shard_map/ppermute | solution.py:528
  99.7 5.6 collective-permute-start.8
  102.2 41.3 %collective-permute-start.12 = (bf16[2,384,768]{2,1,0:T(8,128)(2,1)}, bf16[2,384,768]{2,1,0:T(8,128)(2,1)}, u32[]{:S(2)}, u32[]{:S(2)}) collective-permute-start(bf16[2,384,768]{2,1,0:T(8,128)(2,1)} %pad_maximum_fusion.4), channel_id=1, source_target_pairs={{0,4},{4,0},{1,5},{5,1},{2,6},{6,2},{3,7},{7,3},{8,12},{12,8},{9,1... | collective-permute-start | bytes 3538952 | tf_op jit(solution)/shard_map/ppermute | solution.py:528
  104.3 2.8 collective-permute-start.9
  104.3 38.8 %collective-permute-start.10 = (bf16[384,768]{1,0:T(8,128)(2,1)S(1)}, bf16[384,768]{1,0:T(8,128)(2,1)}, u32[]{:S(2)}, u32[]{:S(2)}) collective-permute-start(bf16[384,768]{1,0:T(8,128)(2,1)S(1)} %pad_maximum_fusion.9), channel_id=1, source_target_pairs={{0,2},{1,3},{2,0},{3,1},{4,6},{5,7},{6,4},{7,5},{8,10},{9,11},{10,... | collective-permute-start | bytes 1769480 | tf_op jit(solution)/shard_map/ppermute | solution.py:528
  104.3 38.8 %collective-permute-start.11 = (bf16[384,768]{1,0:T(8,128)(2,1)S(1)}, bf16[384,768]{1,0:T(8,128)(2,1)}, u32[]{:S(2)}, u32[]{:S(2)}) collective-permute-start(bf16[384,768]{1,0:T(8,128)(2,1)S(1)} %pad_maximum_fusion.9), channel_id=1, source_target_pairs={{0,3},{1,0},{2,1},{3,2},{4,7},{5,4},{6,5},{7,6},{8,11},{9,8},{10,9... | collective-permute-start | bytes 1769480 | tf_op jit(solution)/shard_map/ppermute | solution.py:528
  106.2 37.3 %collective-permute-start.13 = (bf16[384,768]{1,0:T(8,128)(2,1)}, bf16[384,768]{1,0:T(8,128)(2,1)}, u32[]{:S(2)}, u32[]{:S(2)}) collective-permute-start(bf16[384,768]{1,0:T(8,128)(2,1)} %collective-permute-done.6), channel_id=1, source_target_pairs={{0,4},{4,0},{1,5},{5,1},{2,6},{6,2},{3,7},{7,3},{8,12},{12,8},{9,1... | collective-permute-start | bytes 1769480 | tf_op jit(solution)/shard_map/ppermute | solution.py:528
  149.8 40.4 %copy-start.11 = (bf16[512,1536]{1,0:T(8,128)(2,1)S(1)}, bf16[512,1536]{1,0:T(8,128)(2,1)}, u32[]{:S(2)}) copy-start(bf16[512,1536]{1,0:T(8,128)(2,1)} %copy-done.10) | copy-start | bytes 4718596
  151.3 37.8 %copy-start.14 = (bf16[4,384,768]{2,1,0:T(8,128)(2,1)}, bf16[4,384,768]{2,1,0:T(8,128)(2,1)S(1)}, u32[]{:S(2)}) copy-start(bf16[4,384,768]{2,1,0:T(8,128)(2,1)S(1)} %pad_maximum_fusion.refs_0_) | copy-start | bytes 7077892
  151.3 38.9 %collective-permute-start.16 = (bf16[4,384,768]{2,1,0:T(8,128)(2,1)S(1)}, bf16[4,384,768]{2,1,0:T(8,128)(2,1)}, u32[]{:S(2)}, u32[]{:S(2)}) collective-permute-start(bf16[4,384,768]{2,1,0:T(8,128)(2,1)S(1)} %pad_maximum_fusion.refs_0_), channel_id=1, source_target_pairs={{0,8},{8,0},{16,24},{24,16},{1,9},{9,1},{17,25},{25,17},{2,10},{10... | collective-permute-start | bytes 7077896 | tf_op jit(solution)/shard_map/ppermute | solution.py:515
  151.6 36.6 %collective-permute-start.14 = (bf16[512,1536]{1,0:T(8,128)(2,1)S(1)}, bf16[512,1536]{1,0:T(8,128)(2,1)S(1)}, u32[]{:S(2)}, u32[]{:S(2)}) collective-permute-start(bf16[512,1536]{1,0:T(8,128)(2,1)S(1)} %convolution_convert_fusion), channel_id=1, source_target_pairs={{0,1},{1,0},{2,3},{3,2},{4,5},{5,4},{6,7},{7,6},{8,9},{9,8},{10,11... | collective-permute-start | bytes 4718600 | tf_op jit(solution)/shard_map/ppermute | solution.py:515
  152.6 36.5 %collective-permute-start.17 = (bf16[512,1536]{1,0:T(8,128)(2,1)S(1)}, bf16[512,1536]{1,0:T(8,128)(2,1)S(1)}, u32[]{:S(2)}, u32[]{:S(2)}) collective-permute-start(bf16[512,1536]{1,0:T(8,128)(2,1)S(1)} %copy-done.13), channel_id=1, source_target_pairs={{0,16},{8,24},{16,0},{24,8},{1,17},{9,25},{17,1},{25,9},{2,18},{10... | collective-permute-start | bytes 4718600 | tf_op jit(solution)/shard_map/ppermute | solution.py:515
  154.1 27.8 %collective-permute-start.15 = (bf16[2,384,768]{2,1,0:T(8,128)(2,1)S(1)}, bf16[2,384,768]{2,1,0:T(8,128)(2,1)S(1)}, u32[]{:S(2)}, u32[]{:S(2)}) collective-permute-start(bf16[2,384,768]{2,1,0:T(8,128)(2,1)S(1)} %pad_maximum_fusion.5), channel_id=1, source_target_pairs={{0,4},{4,0},{1,5},{5,1},{2,6},{6,2},{3,7},{7,3},{8,12},{12,8},{9,1... | collective-permute-start | bytes 3538952 | tf_op jit(solution)/shard_map/ppermute | solution.py:528
  196.0 8.6 %collective-permute-start.18 = (bf16[4,384,768]{2,1,0:T(8,128)(2,1)S(1)}, bf16[4,384,768]{2,1,0:T(8,128)(2,1)}, u32[]{:S(2)}, u32[]{:S(2)}) collective-permute-start(bf16[4,384,768]{2,1,0:T(8,128)(2,1)S(1)} %pad_maximum_fusion.1.refs_1_), channel_id=1, source_target_pairs={{0,8},{8,0},{16,24},{24,16},{1,9},{9,1},{17,25},{25,17},{2,10},{10... | collective-permute-start | bytes 7077896 | tf_op jit(solution)/shard_map/ppermute | solution.py:515
  196.0 36.9 %collective-permute-start.22 = (bf16[512,1536]{1,0:T(8,128)(2,1)S(1)}, bf16[512,1536]{1,0:T(8,128)(2,1)}, u32[]{:S(2)}, u32[]{:S(2)}) collective-permute-start(bf16[512,1536]{1,0:T(8,128)(2,1)S(1)} %multiply_convert_fusion.n2_ref), channel_id=1, source_target_pairs={{0,16},{8,24},{16,0},{24,8},{1,17},{9,25},{17,1},{25,9},{2,18},{10... | collective-permute-start | bytes 4718600 | tf_op jit(solution)/shard_map/ppermute | solution.py:515
  197.5 33.2 %collective-permute-start.19 = (bf16[384,768]{1,0:T(8,128)(2,1)}, bf16[384,768]{1,0:T(8,128)(2,1)}, u32[]{:S(2)}, u32[]{:S(2)}) collective-permute-start(bf16[384,768]{1,0:T(8,128)(2,1)} %collective-permute-done.7), channel_id=1, source_target_pairs={{0,4},{4,0},{1,5},{5,1},{2,6},{6,2},{3,7},{7,3},{8,12},{12,8},{9,1... | collective-permute-start | bytes 1769480 | tf_op jit(solution)/shard_map/ppermute | solution.py:528
  198.9 31.8 %collective-permute-start.20 = (bf16[384,768]{1,0:T(8,128)(2,1)}, bf16[384,768]{1,0:T(8,128)(2,1)}, u32[]{:S(2)}, u32[]{:S(2)}) collective-permute-start(bf16[384,768]{1,0:T(8,128)(2,1)} %pad_maximum_fusion.10), channel_id=1, source_target_pairs={{0,2},{1,3},{2,0},{3,1},{4,6},{5,7},{6,4},{7,5},{8,10},{9,11},{10,... | collective-permute-start | bytes 1769480 | tf_op jit(solution)/shard_map/ppermute | solution.py:528
  201.8 28.9 %collective-permute-start.21 = (bf16[384,768]{1,0:T(8,128)(2,1)}, bf16[384,768]{1,0:T(8,128)(2,1)}, u32[]{:S(2)}, u32[]{:S(2)}) collective-permute-start(bf16[384,768]{1,0:T(8,128)(2,1)} %pad_maximum_fusion.10), channel_id=1, source_target_pairs={{0,3},{1,0},{2,1},{3,2},{4,7},{5,4},{6,5},{7,6},{8,11},{9,8},{10,9... | collective-permute-start | bytes 1769480 | tf_op jit(solution)/shard_map/ppermute | solution.py:528
  237.4 29.3 %collective-permute-start.24 = (bf16[4,384,768]{2,1,0:T(8,128)(2,1)}, bf16[4,384,768]{2,1,0:T(8,128)(2,1)}, u32[]{:S(2)}, u32[]{:S(2)}) collective-permute-start(bf16[4,384,768]{2,1,0:T(8,128)(2,1)} %pad_maximum_fusion.2.refs_0_), channel_id=1, source_target_pairs={{0,8},{8,0},{16,24},{24,16},{1,9},{9,1},{17,25},{25,17},{2,10},{10... | collective-permute-start | bytes 7077896 | tf_op jit(solution)/shard_map/ppermute | solution.py:515
  237.4 29.3 %collective-permute-start.23 = (bf16[2,384,768]{2,1,0:T(8,128)(2,1)S(1)}, bf16[2,384,768]{2,1,0:T(8,128)(2,1)}, u32[]{:S(2)}, u32[]{:S(2)}) collective-permute-start(bf16[2,384,768]{2,1,0:T(8,128)(2,1)S(1)} %pad_maximum_fusion.6), channel_id=1, source_target_pairs={{0,4},{4,0},{1,5},{5,1},{2,6},{6,2},{3,7},{7,3},{8,12},{12,8},{9,1... | collective-permute-start | bytes 3538952 | tf_op jit(solution)/shard_map/ppermute | solution.py:528
  269.6 4.6 collective-permute-start.25
  270.0 7.6 %collective-permute-start.26 = (bf16[4,384,768]{2,1,0:T(8,128)(2,1)S(1)}, bf16[4,384,768]{2,1,0:T(8,128)(2,1)S(1)}, u32[]{:S(2)}, u32[]{:S(2)}) collective-permute-start(bf16[4,384,768]{2,1,0:T(8,128)(2,1)S(1)} %copy-done.48), channel_id=1, source_target_pairs={{0,8},{8,0},{16,24},{24,16},{1,9},{9,1},{17,25},{25,17},{2,10},{10... | collective-permute-start | bytes 7077896 | tf_op jit(solution)/shard_map/ppermute | solution.py:515
  280.5 28.7 %collective-permute-start.28 = (bf16[4,384,768]{2,1,0:T(8,128)(2,1)}, bf16[4,384,768]{2,1,0:T(8,128)(2,1)}, u32[]{:S(2)}, u32[]{:S(2)}) collective-permute-start(bf16[4,384,768]{2,1,0:T(8,128)(2,1)} %get-tuple-element.438), channel_id=1, source_target_pairs={{0,8},{8,0},{16,24},{24,16},{1,9},{9,1},{17,25},{25,17},{2,10},{10... | collective-permute-start | bytes 7077896 | tf_op jit(solution)/shard_map/ppermute | solution.py:515
  280.7 28.5 %collective-permute-start.27 = (bf16[2,384,768]{2,1,0:T(8,128)(2,1)}, bf16[2,384,768]{2,1,0:T(8,128)(2,1)}, u32[]{:S(2)}, u32[]{:S(2)}) collective-permute-start(bf16[2,384,768]{2,1,0:T(8,128)(2,1)} %add_convert_fusion.6), channel_id=1, source_target_pairs={{0,4},{4,0},{1,5},{5,1},{2,6},{6,2},{3,7},{7,3},{8,12},{12,8},{9,1... | collective-permute-start | bytes 3538952 | tf_op jit(solution)/shard_map/ppermute | solution.py:528
  312.3 40.0 %collective-permute-start.31 = (bf16[512,1536]{1,0:T(8,128)(2,1)}, bf16[512,1536]{1,0:T(8,128)(2,1)S(1)}, u32[]{:S(2)}, u32[]{:S(2)}) collective-permute-start(bf16[512,1536]{1,0:T(8,128)(2,1)} %add_convert_fusion.2), channel_id=1, source_target_pairs={{0,16},{8,24},{16,0},{24,8},{1,17},{9,25},{17,1},{25,9},{2,18},{10... | collective-permute-start | bytes 4718600 | tf_op jit(solution)/shard_map/ppermute | solution.py:515
  313.9 38.4 %collective-permute-start.29 = (bf16[2,384,768]{2,1,0:T(8,128)(2,1)}, bf16[2,384,768]{2,1,0:T(8,128)(2,1)}, u32[]{:S(2)}, u32[]{:S(2)}) collective-permute-start(bf16[2,384,768]{2,1,0:T(8,128)(2,1)} %add_convert_fusion.5), channel_id=1, source_target_pairs={{0,4},{4,0},{1,5},{5,1},{2,6},{6,2},{3,7},{7,3},{8,12},{12,8},{9,1... | collective-permute-start | bytes 3538952 | tf_op jit(solution)/shard_map/ppermute | solution.py:528
  317.6 34.7 %collective-permute-start.30 = (bf16[384,768]{1,0:T(8,128)(2,1)}, bf16[384,768]{1,0:T(8,128)(2,1)}, u32[]{:S(2)}, u32[]{:S(2)}) collective-permute-start(bf16[384,768]{1,0:T(8,128)(2,1)} %get-tuple-element.475), channel_id=1, source_target_pairs={{0,2},{1,3},{2,0},{3,1},{4,6},{5,7},{6,4},{7,5},{8,10},{9,11},{10,... | collective-permute-start | bytes 1769480 | tf_op jit(solution)/shard_map/ppermute | solution.py:528
  352.4 8.7 %collective-permute-start.32 = (bf16[4,384,768]{2,1,0:T(8,128)(2,1)}, bf16[4,384,768]{2,1,0:T(8,128)(2,1)}, u32[]{:S(2)}, u32[]{:S(2)}) collective-permute-start(bf16[4,384,768]{2,1,0:T(8,128)(2,1)} %get-tuple-element.478), channel_id=1, source_target_pairs={{0,8},{8,0},{16,24},{24,16},{1,9},{9,1},{17,25},{25,17},{2,10},{10... | collective-permute-start | bytes 7077896 | tf_op jit(solution)/shard_map/ppermute | solution.py:515
  361.0 39.1 %collective-permute-start.34 = (bf16[4,384,768]{2,1,0:T(8,128)(2,1)}, bf16[4,384,768]{2,1,0:T(8,128)(2,1)S(1)}, u32[]{:S(2)}, u32[]{:S(2)}) collective-permute-start(bf16[4,384,768]{2,1,0:T(8,128)(2,1)} %get-tuple-element.491), channel_id=1, source_target_pairs={{0,8},{8,0},{16,24},{24,16},{1,9},{9,1},{17,25},{25,17},{2,10},{10... | collective-permute-start | bytes 7077896 | tf_op jit(solution)/shard_map/ppermute | solution.py:515
  361.1 39.0 %collective-permute-start.33 = (bf16[512,1536]{1,0:T(8,128)(2,1)}, bf16[512,1536]{1,0:T(8,128)(2,1)S(1)}, u32[]{:S(2)}, u32[]{:S(2)}) collective-permute-start(bf16[512,1536]{1,0:T(8,128)(2,1)} %get-tuple-element.506), channel_id=1, source_target_pairs={{0,1},{1,0},{2,3},{3,2},{4,5},{5,4},{6,7},{7,6},{8,9},{9,8},{10,11... | collective-permute-start | bytes 4718600 | tf_op jit(solution)/shard_map/ppermute | solution.py:515
  366.8 28.1 %collective-permute-start.35 = (bf16[2,384,768]{2,1,0:T(8,128)(2,1)S(1)}, bf16[2,384,768]{2,1,0:T(8,128)(2,1)S(1)}, u32[]{:S(2)}, u32[]{:S(2)}) collective-permute-start(bf16[2,384,768]{2,1,0:T(8,128)(2,1)S(1)} %add_convert_fusion.4), channel_id=1, source_target_pairs={{0,4},{4,0},{1,5},{5,1},{2,6},{6,2},{3,7},{7,3},{8,12},{12,8},{9,1... | collective-permute-start | bytes 3538952 | tf_op jit(solution)/shard_map/ppermute | solution.py:528
  400.1 28.1 %collective-permute-start.36 = (bf16[384,768]{1,0:T(8,128)(2,1)}, bf16[384,768]{1,0:T(8,128)(2,1)}, u32[]{:S(2)}, u32[]{:S(2)}) collective-permute-start(bf16[384,768]{1,0:T(8,128)(2,1)} %get-tuple-element.511), channel_id=1, source_target_pairs={{0,1},{1,2},{2,3},{3,0},{4,5},{5,6},{6,7},{7,4},{8,9},{9,10},{10,1... | collective-permute-start | bytes 1769480 | tf_op jit(solution)/shard_map/ppermute | solution.py:528
  401.9 27.6 %collective-permute-start.37 = (bf16[384,768]{1,0:T(8,128)(2,1)}, bf16[384,768]{1,0:T(8,128)(2,1)}, u32[]{:S(2)}, u32[]{:S(2)}) collective-permute-start(bf16[384,768]{1,0:T(8,128)(2,1)} %get-tuple-element.512), channel_id=1, source_target_pairs={{0,3},{1,0},{2,1},{3,2},{4,7},{5,4},{6,5},{7,6},{8,11},{9,8},{10,9... | collective-permute-start | bytes 1769480 | tf_op jit(solution)/shard_map/ppermute | solution.py:528
  404.0 27.5 %collective-permute-start.38 = (bf16[2,384,768]{2,1,0:T(8,128)(2,1)}, bf16[2,384,768]{2,1,0:T(8,128)(2,1)}, u32[]{:S(2)}, u32[]{:S(2)}) collective-permute-start(bf16[2,384,768]{2,1,0:T(8,128)(2,1)} %add_convert_fusion.3), channel_id=1, source_target_pairs={{0,4},{4,0},{1,5},{5,1},{2,6},{6,2},{3,7},{7,3},{8,12},{12,8},{9,1... | collective-permute-start | bytes 3538952 | tf_op jit(solution)/shard_map/ppermute | solution.py:528
  407.0 57.6 %collective-permute-start.41 = (bf16[512,1536]{1,0:T(8,128)(2,1)}, bf16[512,1536]{1,0:T(8,128)(2,1)}, u32[]{:S(2)}, u32[]{:S(2)}) collective-permute-start(bf16[512,1536]{1,0:T(8,128)(2,1)} %add_convert_fusion.1), channel_id=1, source_target_pairs={{0,16},{8,24},{16,0},{24,8},{1,17},{9,25},{17,1},{25,9},{2,18},{10... | collective-permute-start | bytes 4718600 | tf_op jit(solution)/shard_map/ppermute | solution.py:515
  434.7 29.9 %collective-permute-start.39 = (bf16[384,768]{1,0:T(8,128)(2,1)}, bf16[384,768]{1,0:T(8,128)(2,1)}, u32[]{:S(2)}, u32[]{:S(2)}) collective-permute-start(bf16[384,768]{1,0:T(8,128)(2,1)} %get-tuple-element.522), channel_id=1, source_target_pairs={{0,3},{1,0},{2,1},{3,2},{4,7},{5,4},{6,5},{7,6},{8,11},{9,8},{10,9... | collective-permute-start | bytes 1769480 | tf_op jit(solution)/shard_map/ppermute | solution.py:528
  436.3 28.3 %collective-permute-start.40 = (bf16[384,768]{1,0:T(8,128)(2,1)}, bf16[384,768]{1,0:T(8,128)(2,1)}, u32[]{:S(2)}, u32[]{:S(2)}) collective-permute-start(bf16[384,768]{1,0:T(8,128)(2,1)} %get-tuple-element.524), channel_id=1, source_target_pairs={{0,1},{1,2},{2,3},{3,0},{4,5},{5,6},{6,7},{7,4},{8,9},{9,10},{10,1... | collective-permute-start | bytes 1769480 | tf_op jit(solution)/shard_map/ppermute | solution.py:528
  472.5 5.1 collective-permute-start.42
  472.7 4.9 collective-permute-start.43
  478.3 32.5 %collective-permute-start.44 = (bf16[256,1536]{1,0:T(8,128)(2,1)S(1)}, bf16[256,1536]{1,0:T(8,128)(2,1)S(1)}, u32[]{:S(2)}, u32[]{:S(2)}) collective-permute-start(bf16[256,1536]{1,0:T(8,128)(2,1)S(1)} %slice.320), channel_id=1, source_target_pairs={{0,1},{1,0},{2,3},{3,2},{4,5},{5,4},{6,7},{7,6},{8,9},{9,8},{10,11... | collective-permute-start | bytes 2359304 | tf_op jit(solution)/shard_map/ppermute | solution.py:515
  479.1 29.6 %collective-permute-start.45 = (bf16[384,768]{1,0:T(8,128)(2,1)S(1)}, bf16[384,768]{1,0:T(8,128)(2,1)S(1)}, u32[]{:S(2)}, u32[]{:S(2)}) collective-permute-start(bf16[384,768]{1,0:T(8,128)(2,1)S(1)} %copy-done.41), channel_id=1, source_target_pairs={{0,2},{1,3},{2,0},{3,1},{4,6},{5,7},{6,4},{7,5},{8,10},{9,11},{10,... | collective-permute-start | bytes 1769480 | tf_op jit(solution)/shard_map/ppermute | solution.py:528
  482.3 26.3 %collective-permute-start.46 = (bf16[384,768]{1,0:T(8,128)(2,1)S(1)}, bf16[384,768]{1,0:T(8,128)(2,1)S(1)}, u32[]{:S(2)}, u32[]{:S(2)}) collective-permute-start(bf16[384,768]{1,0:T(8,128)(2,1)S(1)} %get-tuple-element.664), channel_id=1, source_target_pairs={{0,4},{4,0},{1,5},{5,1},{2,6},{6,2},{3,7},{7,3},{8,12},{12,8},{9,1... | collective-permute-start | bytes 1769480 | tf_op jit(solution)/shard_map/ppermute | solution.py:528
  484.0 26.8 %collective-permute-start.48 = (bf16[2,384,768]{2,1,0:T(8,128)(2,1)S(1)}, bf16[2,384,768]{2,1,0:T(8,128)(2,1)S(1)}, u32[]{:S(2)}, u32[]{:S(2)}) collective-permute-start(bf16[2,384,768]{2,1,0:T(8,128)(2,1)S(1)} %slice_bitcast_fusion), channel_id=1, source_target_pairs={{0,8},{8,0},{16,24},{24,16},{1,9},{9,1},{17,25},{25,17},{2,10},{10... | collective-permute-start | bytes 3538952 | tf_op jit(solution)/shard_map/ppermute | solution.py:515
  484.2 25.9 %collective-permute-start.47 = (bf16[4,96,768]{2,1,0:T(8,128)(2,1)S(1)}, bf16[4,96,768]{2,1,0:T(8,128)(2,1)S(1)}, u32[]{:S(2)}, u32[]{:S(2)}) collective-permute-start(bf16[4,96,768]{2,1,0:T(8,128)(2,1)S(1)} %get-tuple-element.662), channel_id=1, source_target_pairs={{0,4},{4,0},{1,5},{5,1},{2,6},{6,2},{3,7},{7,3},{8,12},{12,8},{9,1... | collective-permute-start | bytes 1769480 | tf_op jit(solution)/shard_map/ppermute | solution.py:528
  513.8 42.2 %collective-permute-start.49 = (bf16[384,768]{1,0:T(8,128)(2,1)S(1)}, bf16[384,768]{1,0:T(8,128)(2,1)S(1)}, u32[]{:S(2)}, u32[]{:S(2)}) collective-permute-start(bf16[384,768]{1,0:T(8,128)(2,1)S(1)} %get-tuple-element.660), channel_id=1, source_target_pairs={{0,4},{4,0},{1,5},{5,1},{2,6},{6,2},{3,7},{7,3},{8,12},{12,8},{9,1... | collective-permute-start | bytes 1769480 | tf_op jit(solution)/shard_map/ppermute | solution.py:528
  515.3 40.7 %collective-permute-start.50 = (bf16[384,768]{1,0:T(8,128)(2,1)S(1)}, bf16[384,768]{1,0:T(8,128)(2,1)S(1)}, u32[]{:S(2)}, u32[]{:S(2)}) collective-permute-start(bf16[384,768]{1,0:T(8,128)(2,1)S(1)} %add_convert_fusion.10), channel_id=1, source_target_pairs={{0,2},{1,3},{2,0},{3,1},{4,6},{5,7},{6,4},{7,5},{8,10},{9,11},{10,... | collective-permute-start | bytes 1769480 | tf_op jit(solution)/shard_map/ppermute | solution.py:528
  516.8 39.3 %collective-permute-start.51 = (bf16[2,96,768]{2,1,0:T(8,128)(2,1)S(1)}, bf16[2,96,768]{2,1,0:T(8,128)(2,1)S(1)}, u32[]{:S(2)}, u32[]{:S(2)}) collective-permute-start(bf16[2,96,768]{2,1,0:T(8,128)(2,1)S(1)} %slice.329), channel_id=1, source_target_pairs={{0,2},{1,3},{2,0},{3,1},{4,6},{5,7},{6,4},{7,5},{8,10},{9,11},{10,... | collective-permute-start | bytes 884744 | tf_op jit(solution)/shard_map/ppermute | solution.py:528
  518.4 37.6 %collective-permute-start.52 = (bf16[256,1536]{1,0:T(8,128)(2,1)S(1)}, bf16[256,1536]{1,0:T(8,128)(2,1)S(1)}, u32[]{:S(2)}, u32[]{:S(2)}) collective-permute-start(bf16[256,1536]{1,0:T(8,128)(2,1)S(1)} %slice.330), channel_id=1, source_target_pairs={{0,1},{1,0},{2,3},{3,2},{4,5},{5,4},{6,7},{7,6},{8,9},{9,8},{10,11... | collective-permute-start | bytes 2359304 | tf_op jit(solution)/shard_map/ppermute | solution.py:515
  520.6 35.4 %collective-permute-start.53 = (bf16[2,384,768]{2,1,0:T(8,128)(2,1)S(1)}, bf16[2,384,768]{2,1,0:T(8,128)(2,1)S(1)}, u32[]{:S(2)}, u32[]{:S(2)}) collective-permute-start(bf16[2,384,768]{2,1,0:T(8,128)(2,1)S(1)} %pad_maximum_fusion.7), channel_id=1, source_target_pairs={{0,16},{8,24},{16,0},{24,8},{1,17},{9,25},{17,1},{25,9},{2,18},{10... | collective-permute-start | bytes 3538952 | tf_op jit(solution)/shard_map/ppermute | solution.py:515
  556.4 24.7 %collective-permute-start.54 = (bf16[2,576,384]{2,1,0:T(8,128)(2,1)S(1)}, bf16[2,576,384]{2,1,0:T(8,128)(2,1)S(1)}, u32[]{:S(2)}, u32[]{:S(2)}) collective-permute-start(bf16[2,576,384]{2,1,0:T(8,128)(2,1)S(1)} %combine.1), channel_id=1, source_target_pairs={{0,16},{8,24},{16,0},{24,8},{1,17},{9,25},{17,1},{25,9},{2,18},{10... | collective-permute-start | bytes 2654216 | tf_op jit(solution)/shard_map/ppermute | solution.py:515
  557.3 16.1 %collective-permute-start.55 = (bf16[2,2,384,768]{3,2,1,0:T(8,128)(2,1)S(1)}, bf16[2,2,384,768]{3,2,1,0:T(8,128)(2,1)S(1)}, u32[]{:S(2)}, u32[]{:S(2)}) collective-permute-start(bf16[2,2,384,768]{3,2,1,0:T(8,128)(2,1)S(1)} %maximum_select_fusion.2), channel_id=1, source_target_pairs={{0,8},{8,0},{16,24},{24,16},{1,9},{9,1},{17,25},{25,17},{2,10},{10... | collective-permute-start | bytes 7077896 | tf_op jit(solution)/shard_map/ppermute | solution.py:515
  559.5 3.8 collective-permute-start.56
  563.3 3.8 collective-permute-start.57
  567.1 4.7 collective-permute-start.58
  571.7 1.6 collective-permute-start.59
  581.3 4.9 collective-permute-start.61
  581.8 3.7 collective-permute-start.60
  (50 other events, 339.1 us)
